TPU v7x, 256 devices: a whole 4x4x8 slice. The times are simulated.
256 devices in a mesh: rows: 64 (over z, y_hi, x), slab: 4 (over y_lo, core).
Axes of the slice: x: 4, y: 4 (y_hi: 2, y_lo: 2; y = y_hi * 2 + y_lo), z: 8, core: 2. Of those that a mesh axis runs over, the one named last changes fastest.
Arguments:
- adj_tiles: bfloat16 [12288, 128, 128], P('rows'), may hold values from 0.0019073486 to 0.030517578
- tile_index: int32 [12288, 2], P('rows'), may hold values from 0 to 255, as said below
- grad_out: bfloat16 [32768, 256], P('rows', 'slab'), may hold values from -6 to 6
- relu_mask: int32 [32768, 256], P('rows', 'slab'), may hold values 0 or 1
- features: bfloat16 [32768, 256], P('rows'), may hold values from -0.09375 to 0.09375
- weight: bfloat16 [256, 256], P(None, 'slab'), may hold values from -0.375 to 0.375
Outputs:
- grad_input: bfloat16 [32768, 256], P('rows', 'slab')
- grad_weight: float32 [256, 256], P('rows', 'slab')
Inputs may be any that keep to these rules, and one draw needn't show every extreme that they name: `tile_index`: row t of a list on index d of rows (rows d * 192 to (d + 1) * 192 - 1) holds a row block in d's own range d * 4 to (d + 1) * 4 - 1 and a column block whose owner (column block // 4) never falls along the list; no list holds more than 12 tiles of one owner, and every list holds exactly 12 tiles of some owner.
All inputs are finite; a program needn't handle non-finite values. No bound on the sum of `relu_mask` on one device may be relied on, other than what follows from the above.
Results may differ from a plain program's by a relative error of at most 0.015.
Values may be sent and summed in bfloat16 or wider, within the bound.
No kernel may reach another device: no remote copies, remote signals or barrier semaphores. Data moves between devices by JAX's collectives and lax.ppermute only.
A program may use at most 64 MiB of HBM per device.

v0:
```python
import jax
import jax.numpy as jnp
from jax import lax
from jax.sharding import PartitionSpec as P

MAX_TILES_PER_ROW = 12


def passed_along(block, axis, distance):
    devices = range(lax.axis_size(axis))
    route = [((i - distance) % len(devices), i) for i in devices]
    return lax.ppermute(block, axis, route)


def apply_tiles(totals, blocks, tiles, targets, columns, valid):
    count_blocks = totals.shape[0]
    picked = blocks[jnp.clip(columns, 0, blocks.shape[0] - 1)]
    products = jnp.einsum("tij,tjc->tic", tiles, picked, preferred_element_type=jnp.float32)
    placing = ((targets[None, :] == jnp.arange(count_blocks)[:, None]) & valid[None, :]).astype(
        jnp.float32
    )
    return totals + jnp.einsum("bt,tic->bic", placing, products, precision=lax.Precision.HIGHEST)


def body(adj_tiles, tile_index, grad_out, relu_mask, features, weight):
    cycle_size = lax.axis_size("rows")
    position = lax.axis_index("rows")
    tile = adj_tiles.shape[1]
    blocks_dev = grad_out.shape[0] // tile
    width = grad_out.shape[1]
    listed = adj_tiles.shape[0]
    g_pre = (grad_out.astype(jnp.float32) * relu_mask.astype(jnp.float32)).astype(jnp.bfloat16)
    owning_devices = tile_index[:, 1] // blocks_dev
    owner_count = jnp.sum(
        (owning_devices[:, None] == jnp.arange(cycle_size)[None, :]).astype(jnp.int32), axis=0
    )
    owner_start = jnp.cumsum(owner_count) - owner_count
    totals = jnp.zeros((blocks_dev, tile, width), jnp.float32)

    def from_owner(totals, held, source):
        first = owner_start[source]
        span = owner_count[source]
        begin = jnp.clip(first, 0, listed - MAX_TILES_PER_ROW)
        tiles = lax.dynamic_slice_in_dim(adj_tiles, begin, MAX_TILES_PER_ROW, 0)
        entries = lax.dynamic_slice_in_dim(tile_index, begin, MAX_TILES_PER_ROW, 0)
        slots = begin + jnp.arange(MAX_TILES_PER_ROW)
        valid = (slots >= first) & (slots < first + span) & jnp.asarray(True)
        return apply_tiles(
            totals,
            held.reshape(blocks_dev, tile, width),
            tiles,
            entries[:, 0] - position * blocks_dev,
            entries[:, 1] - source * blocks_dev,
            valid,
        )

    totals = from_owner(totals, g_pre, position)

    def turn_one(turn, carry):
        held, running = carry
        held = passed_along(held, "rows", 1)
        source = (position - turn) % cycle_size
        return (held, from_owner(running, held, source))

    unused, totals = lax.fori_loop(1, cycle_size, turn_one, (g_pre, totals))
    agg_b = totals.reshape(blocks_dev * tile, width).astype(jnp.bfloat16)
    partial_input = jnp.einsum("rs,is->ri", agg_b, weight, preferred_element_type=jnp.float32)
    grad_input = lax.psum_scatter(
        partial_input.astype(jnp.bfloat16), "slab", scatter_dimension=1, tiled=True
    )
    grad_weight = lax.psum_scatter(
        jnp.einsum("ri,rs->is", features, agg_b, preferred_element_type=jnp.float32),
        "rows",
        scatter_dimension=0,
        tiled=True,
    )
    return (grad_input, grad_weight)


def solution(mesh):
    placed = (
        P("rows", None, None),
        P("rows", None),
        P("rows", "slab"),
        P("rows", "slab"),
        P("rows", None),
        P(None, "slab"),
    )
    return jax.shard_map(
        body,
        mesh=mesh,
        in_specs=placed,
        out_specs=(P("rows", "slab"), P("rows", "slab")),
        check_vma=False,
    )
```

profile of v0, /device:TPU:8, one launch (start us, length us, event | category | flops | bytes accessed | tf_op | source)
XLA Modules:
  0.0 1437.9 jit_solution(16710190480693695005)
XLA Ops:
  17.4 811.5 %while.17 = (s32[]{:T(128)}, bf16[512,64]{0,1:T(8,128)(2,1)S(1)}, f32[4,128,64]{1,0,2:T(4,128)S(1)}, s32[]{:T(128)}, s32[64]{0:T(128)S(1)}, /*index=5*/s32[192,2...) while((s32[]{:T(128)}, bf16[512,64]{0,1:T(8,128)(2,1)S(1)}, ...), condition=%wide.region_3.4_spmd, body=%wide.region_2.3_spmd.sunk | while | flops 29918444 | bytes 2560988 | solution.py:65
  23.2 6.2 collective-permute-done
  36.6 5.7 collective-permute-done
  49.5 5.7 collective-permute-done
  62.3 5.7 collective-permute-done
  75.1 5.7 collective-permute-done
  87.9 5.7 collective-permute-done
  100.7 5.7 collective-permute-done
  113.6 5.7 collective-permute-done
  126.4 5.7 collective-permute-done
  139.2 6.0 collective-permute-done
  152.3 5.7 collective-permute-done
  165.1 5.7 collective-permute-done
  178.0 5.7 collective-permute-done
  190.8 5.7 collective-permute-done
  203.6 5.7 collective-permute-done
  216.4 5.7 collective-permute-done
  229.2 5.7 collective-permute-done
  242.0 5.7 collective-permute-done
  254.9 5.7 collective-permute-done
  267.7 5.8 collective-permute-done
  280.7 5.7 collective-permute-done
  293.6 5.7 collective-permute-done
  306.4 5.7 collective-permute-done
  319.2 5.7 collective-permute-done
  332.0 5.7 collective-permute-done
  344.9 5.7 collective-permute-done
  357.7 5.7 collective-permute-done
  370.5 5.7 collective-permute-done
  383.3 5.7 collective-permute-done
  396.1 5.7 collective-permute-done
  408.9 6.2 collective-permute-done
  422.4 5.7 collective-permute-done
  435.2 5.7 collective-permute-done
  448.0 5.7 collective-permute-done
  460.8 5.7 collective-permute-done
  473.6 5.7 collective-permute-done
  486.5 5.7 collective-permute-done
  499.3 5.7 collective-permute-done
  512.1 5.7 collective-permute-done
  524.9 5.7 collective-permute-done
  537.7 6.1 collective-permute-done
  551.0 5.7 collective-permute-done
  563.8 5.7 collective-permute-done
  576.6 5.7 collective-permute-done
  589.4 5.7 collective-permute-done
  602.3 5.7 collective-permute-done
  615.1 5.7 collective-permute-done
  627.9 5.7 collective-permute-done
  640.7 5.7 collective-permute-done
  653.5 5.7 collective-permute-done
  666.3 6.0 collective-permute-done
  679.5 5.7 collective-permute-done
  692.3 5.7 collective-permute-done
  705.1 5.7 collective-permute-done
  717.9 5.7 collective-permute-done
  730.7 5.7 collective-permute-done
  743.6 5.7 collective-permute-done
  756.4 5.7 collective-permute-done
  769.2 5.7 collective-permute-done
  782.0 5.7 collective-permute-done
  794.8 5.7 collective-permute-done
  807.7 5.7 collective-permute-done
  832.0 596.9 %all-reduce.3.cloned.1.call-done = f32[256,64]{0,1:T(8,128)} async-done(((f32[256,64]{0,1:T(8,128)}), f32[256,64]{0,1:T(8,128)}) %all-reduce.3.cloned.1.call-update) | async-done | bytes 65552
  (791 shorter events, 354.6 us)
Async XLA Ops:
  8.0 1420.9 %all-reduce.3.cloned.1.call-start = ((), (), s32[]{:S(2)}) async-start(), calls=%async_computation.2 | async-start | bytes 131072
  17.4 12.1 collective-permute-start
  32.2 10.1 collective-permute-start
  45.1 10.1 collective-permute-start
  57.9 10.1 collective-permute-start
  70.7 10.1 collective-permute-start
  83.5 10.1 collective-permute-start
  96.3 10.1 collective-permute-start
  109.1 10.1 collective-permute-start
  122.0 10.1 collective-permute-start
  134.8 10.4 collective-permute-start
  147.9 10.1 collective-permute-start
  160.7 10.1 collective-permute-start
  173.5 10.1 collective-permute-start
  186.4 10.1 collective-permute-start
  199.2 10.1 collective-permute-start
  212.0 10.1 collective-permute-start
  224.8 10.1 collective-permute-start
  237.6 10.1 collective-permute-start
  250.4 10.1 collective-permute-start
  263.3 10.2 collective-permute-start
  276.3 10.1 collective-permute-start
  289.2 10.1 collective-permute-start
  302.0 10.1 collective-permute-start
  314.8 10.1 collective-permute-start
  327.6 10.1 collective-permute-start
  340.4 10.1 collective-permute-start
  353.3 10.1 collective-permute-start
  366.1 10.1 collective-permute-start
  378.9 10.1 collective-permute-start
  391.7 10.1 collective-permute-start
  404.5 10.7 collective-permute-start
  417.9 10.1 collective-permute-start
  430.8 10.1 collective-permute-start
  443.6 10.1 collective-permute-start
  456.4 10.1 collective-permute-start
  469.2 10.1 collective-permute-start
  482.0 10.1 collective-permute-start
  494.9 10.1 collective-permute-start
  507.7 10.1 collective-permute-start
  520.5 10.1 collective-permute-start
  533.3 10.5 collective-permute-start
  546.6 10.1 collective-permute-start
  559.4 10.1 collective-permute-start
  572.2 10.1 collective-permute-start
  585.0 10.1 collective-permute-start
  597.8 10.1 collective-permute-start
  610.7 10.1 collective-permute-start
  623.5 10.1 collective-permute-start
  636.3 10.1 collective-permute-start
  649.1 10.1 collective-permute-start
  661.9 10.4 collective-permute-start
  675.0 10.1 collective-permute-start
  687.9 10.1 collective-permute-start
  700.7 10.1 collective-permute-start
  713.5 10.1 collective-permute-start
  726.3 10.1 collective-permute-start
  739.1 10.1 collective-permute-start
  752.0 10.1 collective-permute-start
  764.8 10.1 collective-permute-start
  777.6 10.1 collective-permute-start
  790.4 10.1 collective-permute-start
  803.2 10.1 collective-permute-start
  829.7 600.7 %reduce-scatter.3.cloned.1.call-start = ((), (), s32[]{:S(2)}) async-start(), calls=%async_computation.1 | async-start | bytes 327680 | tf_op jit(solution)/shard_map/reduce_scatter | solution.py:68
  (4 other events, 2456.9 us)
Sparse Core Ops, SparseCore 0:
  829.9 599.0 all-reduce.2
Sparse Core Ops, SparseCore 1:
  833.3 15.5 reduce-scatter.2
where the time goes:
time: 1440 us
  waiting for transfers between devices  955 us (66%)
  local copies, waits for them, and re-layouts  165 us (11%)
  matrix products  137 us (10%)
  loops' own time  115 us (8%)
  other arithmetic  39.4 us (3%)
  between operations  18.2 us (1%)
    unnamed x3, waiting for transfers between devices  597 us
    ppermute x63, waiting for transfers between devices, passed_along(): return lax.ppermute(block, axis, route)  358 us
    another operation x1, loops' own time, body(): unused, totals = lax.fori_loop(1, cycle_size, turn_one, (g_pre, totals))  115 us
    dot_general x64, matrix products, apply_tiles(): jnp.einsum('tij,tjc->tic', tiles, picked, preferred_element_type=jnp.floa...  87.3 us
    dynamic_slice x64, local copies, waits for them, and re-layouts, from_owner(): entries = lax.dynamic_slice_in_dim(tile_index, begin, MAX_TILES_PER_ROW, 0)  48.6 us
    dot_general x64, matrix products, apply_tiles(): jnp.einsum('bt,tic->bic', placing, products, precision=lax.Precision.HIGH...  48.2 us
    dynamic_slice x64, local copies, waits for them, and re-layouts, from_owner(): span = owner_count[source]  38.9 us
    gather x64, local copies, waits for them, and re-layouts, apply_tiles(): picked = blocks[jnp.clip(columns, 0, blocks.shape[0] - 1)]  37.4 us
  transfers between devices with their start and end apart: 65, of which 64 were waited for; matrix products, arithmetic and copies ran while one was open for 11% of the time, Pallas kernels for 0%

commit v1 on v0

v1 whole, which is shorter than its diff:
```python
import jax
import jax.numpy as jnp
from jax import lax
from jax.experimental import pallas as pl
from jax.experimental.pallas import tpu as pltpu
from jax.sharding import Mesh, PartitionSpec as P

ROWS = ("z", "yh", "x")
SLAB = ("yl", "core")
GROUP = 8


def tile_table(tile_index, first_row, block_slot, steps):
    listed = tile_index.shape[0]
    row = tile_index[:, 0] - first_row
    slot, half = block_slot(tile_index[:, 1])
    t = jnp.arange(listed)
    rank = jnp.sum(((row[None, :] == row[:, None]) & (t[None, :] < t[:, None])).astype(jnp.int32), axis=1)
    r4 = jnp.arange(4)
    count = jnp.sum((row[:, None] == r4[None, :]).astype(jnp.int32), axis=0)
    need = (count + GROUP - 1) // GROUP
    ends = jnp.sum(jnp.where(r4[None, :] <= r4[:, None], need[None, :], 0), axis=1)
    starts = ends - need
    place = jnp.sum(jnp.where(row[:, None] == r4[None, :], starts[None, :], 0), axis=1) * GROUP + rank
    value = 1 + t + slot * 256 + half * 65536
    j = jnp.arange(steps * GROUP)
    table = jnp.sum(jnp.where(place[None, :] == j[:, None], value[None, :], 0), axis=1)
    table = jnp.where(table > 0, table - 1, 2 * 65536)
    step_row = jnp.minimum(jnp.sum((ends[None, :] <= jnp.arange(steps)[:, None]).astype(jnp.int32), axis=1), 3)
    return table.astype(jnp.int32), jnp.concatenate([step_row, ends[3:]]).astype(jnp.int32)


def agg_kernel(table, step_row, adj, blocks, out, acc, masks):
    steps = step_row.shape[0] - 1
    lane = lax.broadcasted_iota(jnp.int32, (128, 128), 1)
    masks[0] = jnp.where(lane < 64, 1.0, 0.0).astype(masks.dtype)
    masks[1] = jnp.where(lane < 64, 0.0, 1.0).astype(masks.dtype)
    masks[2] = jnp.zeros((128, 128), masks.dtype)
    acc[...] = jnp.zeros_like(acc)

    def step(s, carry):
        lhs, rhs = [], []
        for u in range(GROUP):
            e = table[s * GROUP + u]
            lhs.append(adj[e & 255])
            rhs.append(blocks[(e >> 8) & 255] * masks[e >> 16])
        acc[step_row[s]] += jnp.dot(
            jnp.concatenate(lhs, axis=1), jnp.concatenate(rhs, axis=0), preferred_element_type=jnp.float32
        )
        return carry

    lax.fori_loop(0, step_row[steps], step, 0)
    agg = [acc[r] + pltpu.roll(acc[r], 64, 1) for r in range(4)]
    for r in range(2):
        out[pl.ds(r * 128, 128), :] = jnp.where(lane < 64, agg[r], agg[r + 2]).astype(out.dtype)


def aggregate(table, step_row, adj, blocks):
    smem = pl.BlockSpec(memory_space=pltpu.SMEM)
    vmem = pl.BlockSpec(memory_space=pltpu.VMEM)
    return pl.pallas_call(
        agg_kernel,
        out_shape=jax.ShapeDtypeStruct((256, 128), jnp.bfloat16),
        in_specs=[smem, smem, vmem, vmem],
        out_specs=vmem,
        scratch_shapes=[pltpu.VMEM((4, 128, 128), jnp.float32), pltpu.VMEM((3, 128, 128), jnp.bfloat16)],
        compiler_params=pltpu.CompilerParams(vmem_limit_bytes=32 * 1024 * 1024),
        name="aggregate",
    )(table, step_row, adj, blocks)


def halves(packed):
    return jnp.concatenate([packed[:, :64], packed[:, 64:]], axis=0)


def body(adj_tiles, tile_index, grad_out, relu_mask, features, weight):
    position = lax.axis_index(ROWS)
    slab = lax.axis_index(SLAB)
    g_pre = (grad_out.astype(jnp.float32) * relu_mask.astype(jnp.float32)).astype(jnp.bfloat16)
    packed = jnp.concatenate([g_pre[:256], g_pre[256:]], axis=1)

    flips = ([(0, 1), (1, 0), (2, 3), (3, 2)], [(0, 2), (2, 0), (1, 3), (3, 1)], [(0, 3), (3, 0), (1, 2), (2, 1)])
    w_parts = [lax.dynamic_slice_in_dim(weight, slab * 64, 64, 0)]
    for k, pairs in enumerate(flips):
        w_parts.append(lax.ppermute(lax.dynamic_slice_in_dim(weight, (slab ^ (k + 1)) * 64, 64, 0), SLAB, pairs))

    gathered = lax.all_gather(packed, "yh", axis=0, tiled=False)
    gathered = lax.all_gather(gathered, "x", axis=0, tiled=False)
    gathered = lax.all_gather(gathered, "z", axis=0, tiled=False)

    def block_slot(column):
        owner, block = column // 4, column % 4
        z, y, x = owner // 8, (owner // 4) % 2, owner % 4
        return ((z * 4 + x) * 2 + y) * 2 + block % 2, block // 2

    steps = adj_tiles.shape[0] // GROUP + 4
    table, step_row = tile_table(tile_index, position * 4, block_slot, steps)
    agg = aggregate(table, step_row, adj_tiles, gathered.reshape(128, 128, 128))

    a_parts = [halves(agg)] + [halves(lax.ppermute(agg, SLAB, pairs)) for pairs in flips]
    grad_input = jnp.einsum(
        "rs,is->ri", jnp.concatenate(a_parts, axis=1), jnp.concatenate(w_parts, axis=1), preferred_element_type=jnp.float32
    ).astype(jnp.bfloat16)

    partial = jnp.einsum("ri,rs->is", features, a_parts[0], preferred_element_type=jnp.float32)
    pieces = lax.all_to_all(partial.reshape(64, 256), ROWS, 0, 0, tiled=True)
    grad_weight = jnp.sum(pieces, axis=0).reshape(4, 64)
    return grad_input, grad_weight


def solution(mesh):
    fine = Mesh(mesh.devices.reshape(8, 2, 4, 2, 2), ROWS + SLAB)
    return jax.shard_map(
        body,
        mesh=fine,
        in_specs=(P(ROWS, None, None), P(ROWS, None), P(ROWS, SLAB), P(ROWS, SLAB), P(ROWS, None), P(None, SLAB)),
        out_specs=(P(ROWS, SLAB), P(ROWS, SLAB)),
        check_vma=False,
    )
```

time: 1440 us -> 131 us (0.09)
  waiting for transfers between devices: 955 us -> 60.6 us
  local copies, waits for them, and re-layouts: 165 us -> 8.44 us
  matrix products: 137 us -> 1.18 us
  loops' own time: 115 us -> 0 us
  other arithmetic: 39.4 us -> 3.33 us
  blocking collectives: 0 us -> 20.6 us
    unnamed x3 -> x1, waiting for transfers between devices: 597 us -> 0.02 us
    ppermute x63 -> x6, waiting for transfers between devices: 358 us -> 2.69 us  [the longest x3 2.69 us: body(): lax.ppermute(agg, SLAB, pairs)]
    dot_general x130 -> x2, matrix products: 137 us -> 1.18 us  [the longest x1 0.98 us: body(): jnp.einsum('rs,is->ri', jnp.concatenate(a_parts, axis=1), jnp.concatenate...]
    dynamic_slice x192 -> x1, local copies, waits for them, and re-layouts: 125 us -> 0.89 us  [body(): w_parts = [lax.dynamic_slice_in_dim(weight, slab * 64, 64, 0)]]
    another operation x1 -> x0, loops' own time: 115 us -> none  [body(): unused, totals = lax.fori_loop(1, cycle_size, turn_one, (g_pre, totals))]
    all_gather x0 -> x1, waiting for transfers between devices: none -> 51.2 us  [body(): gathered = lax.all_gather(gathered, 'z', axis=0, tiled=False)]
    gather x64 -> x0, local copies, waits for them, and re-layouts: 37.4 us -> none  [apply_tiles(): picked = blocks[jnp.clip(columns, 0, blocks.shape[0] - 1)]]
    and x64 -> x0, other arithmetic: 36.2 us -> none  [from_owner(): valid = (slots >= first) & (slots < first + span) & jnp.asarray(True)]
  transfers between devices with their start and end apart: 65 -> 8, of which waited for: 64 -> 3; matrix products, arithmetic and copies ran while one was open for 11% -> 4% of each run, Pallas kernels for 0% -> 5%
where the time goes in v1:
time: 131 us; the launch traced here: 129 us
  waiting for transfers between devices  60.6 us (46%)
  blocking collectives  20.6 us (16%)
  between operations  14.2 us (11%)
  starting transfers between devices  13.8 us (11%)
  local copies, waits for them, and re-layouts  8.44 us (6%)
  Pallas kernels  6.95 us (5%)
  other arithmetic  3.33 us (3%)
    all_gather x1, waiting for transfers between devices, body(): gathered = lax.all_gather(gathered, 'z', axis=0, tiled=False)  51.2 us
    all_gather x1, blocking collectives, body(): gathered = lax.all_gather(gathered, 'x', axis=0, tiled=False)  14.2 us
    all_to_all x1, starting transfers between devices, body(): pieces = lax.all_to_all(partial.reshape(64, 256), ROWS, 0, 0, tiled=True)  9.26 us
    pallas_call x1, Pallas kernels, aggregate(): pl.pallas_call(agg_kernel, out_shape=jax.ShapeDtypeStruct((256, 128), jnp...  6.95 us
    all_to_all x1, waiting for transfers between devices, body(): pieces = lax.all_to_all(partial.reshape(64, 256), ROWS, 0, 0, tiled=True)  6.69 us
    all_gather x1, blocking collectives, body(): gathered = lax.all_gather(packed, 'yh', axis=0, tiled=False)  6.45 us
    unnamed x6, local copies, waits for them, and re-layouts  4.98 us
    ppermute x3, waiting for transfers between devices, body(): lax.ppermute(agg, SLAB, pairs)  2.69 us
  transfers between devices with their start and end apart: 8, of which 3 were waited for; matrix products, arithmetic and copies ran while one was open for 4% of the time, Pallas kernels for 5%

profile of v1, /device:TPU:8, one launch (start us, length us, event | category | flops | bytes accessed | tf_op | source)
XLA Modules:
  0.0 129.1 jit_solution(14919066565566162790)
XLA Ops:
  7.2 0.0 copy-start
  7.2 0.0 all-gather.5.cloned.1.call-start
  7.2 1.0 multiply_convert_fusion
  8.2 6.4 %all-gather = bf16[512,128]{0,1:T(8,128)(2,1)S(1)} all-gather(bf16[256,128]{0,1:T(8,128)(2,1)S(1)} %pad_maximum_fusion), channel_id=2, replica_groups=mesh['z'=8,'yh'=2,'x'=4,'yl'=2,'core'=2] {'yh'}, dimensions={0}, use_global_device_ids=true | all-gather | bytes 196608 | tf_op jit(solution)/shard_map/all_gather | solution.py:87
  14.7 0.1 copy.14
  14.8 14.2 %all-gather.1 = bf16[8,256,128]{2,1,0:T(8,128)(2,1)} all-gather(bf16[2,256,128]{2,1,0:T(8,128)(2,1)S(1)} %bitcast.10), channel_id=3, replica_groups=mesh['z'=8,'yh'=2,'x'=4,'yl'=2,'core'=2] {'x'}, dimensions={0}, use_global_device_ids=true | all-gather | bytes 655360 | tf_op jit(solution)/shard_map/all_gather | solution.py:88
  28.9 0.0 all-gather.5.cloned.1.call-update
  29.0 0.9 constant_dynamic-slice_fusion.2
  29.9 0.1 collective-permute-start.3
  30.0 2.2 %collective-permute-start.4 = (bf16[64,64]{0,1:T(8,128)(2,1)S(1)}, bf16[64,64]{0,1:T(8,128)(2,1)S(1)}, u32[]{:S(2)}, u32[]{:S(2)}) collective-permute-start(bf16[64,64]{0,1:T(8,128)(2,1)S(1)} %get-tuple-element.15), channel_id=1, source_target_pairs={{0,2},{2,0},{1,3},{3,1},{4,6},{6,4},{5,7},{7,5},{8,10},{10,8},{9,1... | collective-permute-start | bytes 24584 | tf_op jit(solution)/shard_map/ppermute | solution.py:85
  32.2 0.1 collective-permute-start.5
  32.3 0.8 slice_subtract_fusion
  33.0 0.1 convert_reduce_fusion.1
  33.2 0.1 select_reduce_fusion.2
  33.3 0.6 slice.41
  33.9 0.1 convert_reduce_fusion.2
  34.0 0.7 pad_add_fusion.step_row
  34.7 0.1 select_reduce_fusion.1
  34.8 0.2 convert_reduce_fusion
  35.0 0.1 select_reduce_fusion
  35.2 51.2 %all-gather.5.cloned.1.call-done = bf16[32,2,256,128]{3,2,1,0:T(8,128)(2,1)} async-done(((bf16[4,2,256,128]{3,2,1,0:T(8,128)(2,1)}), bf16[32,2,256,128]{3,2,1,0:T(8,128)(2,1)}) %all-gather.5.cloned.1.call-update) | async-done | bytes 4194320 | tf_op jit(solution)/shard_map/all_gather | solution.py:89
  86.3 0.0 copy-start.1
  86.3 2.8 %copy-done.1 = bf16[192,128,128]{2,1,0:T(8,128)(2,1)S(1)} copy-done((bf16[192,128,128]{2,1,0:T(8,128)(2,1)S(1)}, bf16[192,128,128]{2,1,0:T(8,128)(2,1)}, u32[]{:S(2)}) %copy-start.1) | copy-done | bytes 6291480
  89.1 0.0 copy-start.2
  89.1 2.2 %copy-done.2 = bf16[32,2,256,128]{3,2,1,0:T(8,128)(2,1)S(1)} copy-done((bf16[32,2,256,128]{3,2,1,0:T(8,128)(2,1)S(1)}, bf16[32,2,256,128]{3,2,1,0:T(8,128)(2,1)}, u32[]{:S(2)}) %copy-start.2) | copy-done | bytes 4194328
  91.3 7.0 %aggregate.1 = bf16[256,128]{1,0:T(8,128)(2,1)S(1)} custom-call(s32[224]{0:T(256)S(1)} %compare_select_fusion.2.table, s32[29]{0:T(128)S(1)} %pad_add_fusion.step_row, bf16[192,128,128]{2,1,0:T(8,128)(2,1)S(1)} %copy-done.1, bf16[128,128,128]{2,1,0:T(8,128)(2,1)S(1)} %bitcast.8), custom_call_target="tpu_custom_call" | custom-call | tf_op jit(solution)/shard_map/aggregate/pallas_call | solution.py:61
  98.3 0.1 fusion.32
  98.4 0.1 collective-permute-start
  98.5 0.6 collective-permute-start.1
  99.1 0.0 copy-done
  99.1 0.2 convolution_bitcast_fusion
  99.3 0.1 copy.15
  99.4 0.7 all_to_all.8
  100.1 9.3 %all-to-all-start = ((f32[64,1,256]{2,1,0:T(1,128)}), f32[64,1,256]{2,1,0:T(1,128)S(1)}, u32[]{:S(2)}, u32[]{:S(2)}) async-start(f32[64,1,256]{2,1,0:T(1,128)} %all_to_all.8), calls=%async_computation | async-start | bytes 131072 | tf_op jit(solution)/shard_map/all_to_all | solution.py:106
  109.4 0.0 collective-permute-done
  109.4 1.4 %collective-permute-start.2 = (bf16[256,128]{1,0:T(8,128)(2,1)S(1)}, bf16[256,128]{1,0:T(8,128)(2,1)S(1)}, u32[]{:S(2)}, u32[]{:S(2)}) collective-permute-start(bf16[256,128]{1,0:T(8,128)(2,1)S(1)} %aggregate.1), channel_id=1, source_target_pairs={{0,3},{3,0},{1,2},{2,1},{4,7},{7,4},{5,6},{6,5},{8,11},{11,8},{9,1... | collective-permute-start | bytes 196616 | tf_op jit(solution)/shard_map/ppermute | solution.py:100
  110.8 0.1 fusion.33
  110.9 0.0 collective-permute-done.1
  110.9 0.1 fusion.34
  111.0 2.7 %collective-permute-done.2 = bf16[256,128]{1,0:T(8,128)(2,1)S(1)} collective-permute-done((bf16[256,128]{1,0:T(8,128)(2,1)S(1)}, bf16[256,128]{1,0:T(8,128)(2,1)S(1)}, u32[]{:S(2)}, u32[]{:S(2)}) %collective-permute-start.2) | collective-permute-done | bytes 65568 | tf_op jit(solution)/shard_map/ppermute | solution.py:100
  113.7 0.1 fusion.35
  113.8 0.0 collective-permute-done.3
  113.8 0.0 collective-permute-done.4
  113.8 0.0 collective-permute-done.5
  113.8 1.0 convolution_convert_fusion
  114.8 6.7 %all-to-all-done = f32[64,1,256]{2,1,0:T(1,128)S(1)} async-done(((f32[64,1,256]{2,1,0:T(1,128)}), f32[64,1,256]{2,1,0:T(1,128)S(1)}, u32[]{:S(2)}, u32[]{:S(2)}) %all-to-all-start) | async-done | bytes 65568 | tf_op jit(solution)/shard_map/all_to_all | solution.py:106
  121.5 0.1 reduce_sum.69
  121.6 0.7 reshape.187
  (7 shorter events, 0.1 us)
Async XLA Ops:
  7.2 91.9 %copy-start = (bf16[512,256]{1,0:T(8,128)(2,1)S(1)}, bf16[512,256]{1,0:T(8,128)(2,1)}, u32[]{:S(2)}) copy-start(bf16[512,256]{1,0:T(8,128)(2,1)} %param.10) | copy-start | bytes 786436
  7.2 79.1 %all-gather.5.cloned.1.call-start = ((), (), s32[]{:S(2)}) async-start(), calls=%async_computation.1 | async-start | bytes 4718592 | tf_op jit(solution)/shard_map/all_gather | solution.py:89
  29.9 83.9 %collective-permute-start.3 = (bf16[64,64]{0,1:T(8,128)(2,1)S(1)}, bf16[64,64]{0,1:T(8,128)(2,1)S(1)}, u32[]{:S(2)}, u32[]{:S(2)}) collective-permute-start(bf16[64,64]{0,1:T(8,128)(2,1)S(1)} %get-tuple-element.13), channel_id=1, source_target_pairs={{0,1},{1,0},{2,3},{3,2},{4,5},{5,4},{6,7},{7,6},{8,9},{9,8},{10,11... | collective-permute-start | bytes 24584 | tf_op jit(solution)/shard_map/ppermute | solution.py:85
  30.0 83.8 %collective-permute-start.4 = (bf16[64,64]{0,1:T(8,128)(2,1)S(1)}, bf16[64,64]{0,1:T(8,128)(2,1)S(1)}, u32[]{:S(2)}, u32[]{:S(2)}) collective-permute-start(bf16[64,64]{0,1:T(8,128)(2,1)S(1)} %get-tuple-element.15), channel_id=1, source_target_pairs={{0,2},{2,0},{1,3},{3,1},{4,6},{6,4},{5,7},{7,5},{8,10},{10,8},{9,1... | collective-permute-start | bytes 24584 | tf_op jit(solution)/shard_map/ppermute | solution.py:85
  32.2 81.6 %collective-permute-start.5 = (bf16[64,64]{0,1:T(8,128)(2,1)S(1)}, bf16[64,64]{0,1:T(8,128)(2,1)S(1)}, u32[]{:S(2)}, u32[]{:S(2)}) collective-permute-start(bf16[64,64]{0,1:T(8,128)(2,1)S(1)} %get-tuple-element.14), channel_id=1, source_target_pairs={{0,3},{3,0},{1,2},{2,1},{4,7},{7,4},{5,6},{6,5},{8,11},{11,8},{9,1... | collective-permute-start | bytes 24584 | tf_op jit(solution)/shard_map/ppermute | solution.py:85
  86.3 2.8 %copy-start.1 = (bf16[192,128,128]{2,1,0:T(8,128)(2,1)S(1)}, bf16[192,128,128]{2,1,0:T(8,128)(2,1)}, u32[]{:S(2)}) copy-start(bf16[192,128,128]{2,1,0:T(8,128)(2,1)} %adj.1) | copy-start | bytes 18874372
  89.1 2.2 %copy-start.2 = (bf16[32,2,256,128]{3,2,1,0:T(8,128)(2,1)S(1)}, bf16[32,2,256,128]{3,2,1,0:T(8,128)(2,1)}, u32[]{:S(2)}) copy-start(bf16[32,2,256,128]{3,2,1,0:T(8,128)(2,1)} %all-gather.5.cloned.1.call-done) | copy-start | bytes 12582916
  98.4 11.1 %collective-permute-start = (bf16[256,128]{1,0:T(8,128)(2,1)S(1)}, bf16[256,128]{1,0:T(8,128)(2,1)S(1)}, u32[]{:S(2)}, u32[]{:S(2)}) collective-permute-start(bf16[256,128]{1,0:T(8,128)(2,1)S(1)} %aggregate.1), channel_id=1, source_target_pairs={{0,1},{1,0},{2,3},{3,2},{4,5},{5,4},{6,7},{7,6},{8,9},{9,8},{10,11... | collective-permute-start | bytes 196616 | tf_op jit(solution)/shard_map/ppermute | solution.py:100
  98.5 12.4 %collective-permute-start.1 = (bf16[256,128]{1,0:T(8,128)(2,1)S(1)}, bf16[256,128]{1,0:T(8,128)(2,1)S(1)}, u32[]{:S(2)}, u32[]{:S(2)}) collective-permute-start(bf16[256,128]{1,0:T(8,128)(2,1)S(1)} %aggregate.1), channel_id=1, source_target_pairs={{0,2},{2,0},{1,3},{3,1},{4,6},{6,4},{5,7},{7,5},{8,10},{10,8},{9,1... | collective-permute-start | bytes 196616 | tf_op jit(solution)/shard_map/ppermute | solution.py:100
  100.1 21.3 %all-to-all-start = ((f32[64,1,256]{2,1,0:T(1,128)}), f32[64,1,256]{2,1,0:T(1,128)S(1)}, u32[]{:S(2)}, u32[]{:S(2)}) async-start(f32[64,1,256]{2,1,0:T(1,128)} %all_to_all.8), calls=%async_computation | async-start | bytes 131072 | tf_op jit(solution)/shard_map/all_to_all | solution.py:106
  109.4 4.3 %collective-permute-start.2 = (bf16[256,128]{1,0:T(8,128)(2,1)S(1)}, bf16[256,128]{1,0:T(8,128)(2,1)S(1)}, u32[]{:S(2)}, u32[]{:S(2)}) collective-permute-start(bf16[256,128]{1,0:T(8,128)(2,1)S(1)} %aggregate.1), channel_id=1, source_target_pairs={{0,3},{3,0},{1,2},{2,1},{4,7},{7,4},{5,6},{6,5},{8,11},{11,8},{9,1... | collective-permute-start | bytes 196616 | tf_op jit(solution)/shard_map/ppermute | solution.py:100
Sparse Core Ops, SparseCore 0:
  29.1 57.1 all-gather.4

commit v2 on v1

v2 whole, which is shorter than its diff:
```python
import jax
import jax.numpy as jnp
from jax import lax
from jax.experimental import pallas as pl
from jax.experimental.pallas import tpu as pltpu
from jax.sharding import Mesh, PartitionSpec as P

NZ, NY, NX, NL, NC = 8, 2, 4, 2, 2
ROWS = ("z", "yh", "x")
SLAB = ("yl", "core")
ALL = ROWS + SLAB
GROUP = 8
SLOTS = 4
FLIPS = ([(0, 1), (1, 0), (2, 3), (3, 2)], [(0, 2), (2, 0), (1, 3), (3, 1)], [(0, 3), (3, 0), (1, 2), (2, 1)])


def device(z, y, x, l, c):
    return ((((z % NZ) * NY + y % NY) * NX + x % NX) * NL + l) * NC + c


def places():
    return [(z, y, x, l, c) for z in range(NZ) for y in range(NY) for x in range(NX) for l in range(NL) for c in range(NC)]


def from_rows(value, dz=0, dy=0):
    pairs = [(device(z + dz, y + dy, x, l, c), device(z, y, x, l, c)) for z, y, x, l, c in places()]
    return lax.ppermute(value, ALL, pairs)


def from_axis(value, second, step):
    pairs = []
    for z, y, x, l, c in places():
        along_x = (c == 0) != second
        source = device(z, y, x + step, l, c) if along_x else device(z + step, y, x, l, c)
        pairs.append((source, device(z, y, x, l, c)))
    return lax.ppermute(value, ALL, pairs)


def gather_near(packed):
    four = jnp.stack([packed, from_rows(packed, dy=1), from_rows(packed, dz=4), from_rows(packed, dz=4, dy=1)])
    early = jnp.stack([four, from_axis(four, False, 1), from_axis(four, False, -1), from_axis(four, False, 2)])
    plus, minus = from_axis(early, True, 1), from_axis(early, True, -1)
    return early, plus, minus


def gather_far(plus, minus):
    return [from_axis(plus[:2], True, 1), from_axis(minus[2:], True, -1)]


def where_held(column):
    owner, block = column // 4, column % 4
    core = lax.axis_index("core")
    dz = (owner // (NY * NX) - lax.axis_index("z")) % NZ
    dy = (owner // NX - lax.axis_index("yh")) % NY
    dx = (owner - lax.axis_index("x")) % NX
    ring = jnp.where(core == 0, dx, dz % 4)
    late = jnp.where(core == 0, dz % 4, dx)
    a = jnp.where(ring == 2, 3, jnp.where(ring == 3, 2, ring))
    upper = (dz >= 3) & (dz <= 6)
    swapped = (core == 0) & (late == 2) & (a >= 2)
    e = dy + 2 * (upper != swapped).astype(jnp.int32)
    stage = jnp.where(late == 0, 0, jnp.where(late == 2, 2, 1))
    place = (a * 4 + e) * 2 + block % 2 + jnp.where(late == 3, 32, 0)
    return stage, place, block // 2


def tile_table(row, valid, place, half, steps):
    t = jnp.arange(row.shape[0])
    row = jnp.where(valid, row, -1)
    r4 = jnp.arange(4)
    rank = jnp.sum(((row[None, :] == row[:, None]) & (t[None, :] < t[:, None])).astype(jnp.int32), axis=1)
    count = jnp.sum((row[:, None] == r4[None, :]).astype(jnp.int32), axis=0)
    need = (count + GROUP - 1) // GROUP
    ends = jnp.sum(jnp.where(r4[None, :] <= r4[:, None], need[None, :], 0), axis=1)
    starts = ends - need
    slot = jnp.sum(jnp.where(row[:, None] == r4[None, :], starts[None, :], 0), axis=1) * GROUP + rank
    slot = jnp.where(valid, slot, -1)
    value = 1 + t + place * 256 + half * 65536
    j = jnp.arange(steps * GROUP)
    table = jnp.sum(jnp.where(slot[None, :] == j[:, None], value[None, :], 0), axis=1)
    table = jnp.where(table > 0, table - 1, 2 * 65536)
    step_row = jnp.minimum(jnp.sum((ends[None, :] <= jnp.arange(steps)[:, None]).astype(jnp.int32), axis=1), 3)
    return table.astype(jnp.int32), jnp.concatenate([step_row, ends[3:]]).astype(jnp.int32)


def add_tiles(table, step_row, adj, sources, acc, blocks, tiles, masks, block_sems, tile_sems):
    steps = step_row[step_row.shape[0] - 1]
    each = blocks.shape[0] // len(sources)
    copies = [
        pltpu.make_async_copy(src, blocks.at[pl.ds(k * each, each)], block_sems.at[k]) for k, src in enumerate(sources)
    ]
    for copy in copies:
        copy.start()

    def fetch(s):
        slot = lax.rem(s, SLOTS)
        for u in range(GROUP):
            pltpu.make_async_copy(adj.at[table[s * GROUP + u] & 255], tiles.at[slot, u], tile_sems.at[slot]).start()

    for s in range(SLOTS - 1):
        @pl.when(s < steps)
        def _():
            fetch(s)

    lane = lax.broadcasted_iota(jnp.int32, (128, 128), 1)
    masks[0] = jnp.where(lane < 64, 1.0, 0.0).astype(masks.dtype)
    masks[1] = jnp.where(lane < 64, 0.0, 1.0).astype(masks.dtype)
    masks[2] = jnp.zeros((128, 128), masks.dtype)
    for copy in copies:
        copy.wait()

    def step(s, carry):
        @pl.when(s + SLOTS - 1 < steps)
        def _():
            fetch(s + SLOTS - 1)

        slot = lax.rem(s, SLOTS)
        pltpu.make_async_copy(adj.at[pl.ds(0, GROUP)], tiles.at[slot], tile_sems.at[slot]).wait()
        lhs, rhs = [], []
        for u in range(GROUP):
            e = table[s * GROUP + u]
            lhs.append(tiles[slot, u])
            rhs.append(blocks[(e >> 8) & 255] * masks[e >> 16])
        acc[step_row[s]] += jnp.dot(
            jnp.concatenate(lhs, axis=1), jnp.concatenate(rhs, axis=0), preferred_element_type=jnp.float32
        )
        return carry

    lax.fori_loop(0, steps, step, 0)
    return lane


def pre_kernel(grad_out, relu_mask, out):
    g = grad_out[...].astype(jnp.float32) * relu_mask[...].astype(jnp.float32)
    out[...] = jnp.concatenate([g[:, :256], g[:, 256:]], axis=0).T.astype(out.dtype)


def masked(grad_out, relu_mask):
    vmem = pl.BlockSpec(memory_space=pltpu.VMEM)
    return pl.pallas_call(
        pre_kernel,
        out_shape=jax.ShapeDtypeStruct((256, 128), jnp.bfloat16),
        in_specs=[vmem, vmem],
        out_specs=vmem,
        name="masked",
    )(grad_out.T, relu_mask.T)


def first_kernel(table, step_row, adj, source, acc, *scratch):
    acc[...] = jnp.zeros_like(acc)
    add_tiles(table, step_row, adj, [source], acc, *scratch)


def middle_kernel(table, step_row, adj, source_a, source_b, before, acc, *scratch):
    acc[...] = before[...]
    add_tiles(table, step_row, adj, [source_a, source_b], acc, *scratch)


def last_kernel(table, step_row, adj, source_a, source_b, before, features, out, partial, acc, *scratch):
    acc[...] = before[...]
    lane = add_tiles(table, step_row, adj, [source_a, source_b], acc, *scratch)
    agg = [acc[r] + pltpu.roll(acc[r], 64, 1) for r in range(4)]
    for r in range(2):
        out[pl.ds(r * 128, 128), :] = jnp.where(lane < 64, agg[r], agg[r + 2]).astype(out.dtype)
    rounded = jnp.concatenate([v.astype(jnp.bfloat16) for v in agg], axis=0)
    product = jnp.dot(features[...], rounded, preferred_element_type=jnp.float32)
    low = lax.broadcasted_iota(jnp.int32, (64, 128), 1) < 64
    for p in range(2):
        partial[:, p, :] = jnp.where(low, product[p * 128 : p * 128 + 64], product[p * 128 + 64 : p * 128 + 128])


def call(kernel, table, step_row, adj, sources, others, out_shape, keep_acc, name):
    smem = pl.BlockSpec(memory_space=pltpu.SMEM)
    vmem = pl.BlockSpec(memory_space=pltpu.VMEM)
    anywhere = pl.BlockSpec(memory_space=pl.ANY)
    sources = [s.reshape(-1, 128, 128) for s in sources]
    held = sum(s.shape[0] for s in sources)
    return pl.pallas_call(
        kernel,
        out_shape=out_shape,
        in_specs=[smem, smem, anywhere] + [anywhere] * len(sources) + [vmem] * len(others),
        out_specs=jax.tree.map(lambda _: vmem, out_shape),
        scratch_shapes=([pltpu.VMEM((4, 128, 128), jnp.float32)] if keep_acc else []) + [
            pltpu.VMEM((held, 128, 128), jnp.bfloat16),
            pltpu.VMEM((SLOTS, GROUP, 128, 128), jnp.bfloat16),
            pltpu.VMEM((3, 128, 128), jnp.bfloat16),
            pltpu.SemaphoreType.DMA((len(sources),)),
            pltpu.SemaphoreType.DMA((SLOTS,)),
        ],
        compiler_params=pltpu.CompilerParams(vmem_limit_bytes=16 * 1024 * 1024),
        cost_estimate=pl.CostEstimate(flops=2 * 64 * 128 * 128 * 128, bytes_accessed=8 * 1024 * 1024, transcendentals=0),
        name=name,
    )(table, step_row, adj, *sources, *others)


def halves(packed):
    return jnp.concatenate([packed[:, :64], packed[:, 64:]], axis=0)


def body(adj_tiles, tile_index, grad_out, relu_mask, features, weight):
    position = lax.axis_index(ROWS)
    slab = lax.axis_index(SLAB)
    early, plus, minus = gather_near(masked(grad_out, relu_mask))

    steps = adj_tiles.shape[0] // GROUP + 4
    stage, place, half = where_held(tile_index[:, 1])
    row = tile_index[:, 0] - position * 4
    tables = [tile_table(row, stage == k, place, half, steps) for k in range(3)]
    f_rows = features.reshape(512, 64, 4).transpose(2, 1, 0).reshape(256, 512)

    sums = jax.ShapeDtypeStruct((4, 128, 128), jnp.float32)
    acc = call(first_kernel, *tables[0], adj_tiles, [early], [], sums, False, "early_tiles")
    weight, acc, plus, minus, f_rows, tables = lax.optimization_barrier((weight, acc, plus, minus, f_rows, tables))
    far = gather_far(plus, minus)
    w_parts = [lax.dynamic_slice_in_dim(weight, slab * 64, 64, 0)]
    for k, pairs in enumerate(FLIPS):
        w_parts.append(lax.ppermute(lax.dynamic_slice_in_dim(weight, (slab ^ (k + 1)) * 64, 64, 0), SLAB, pairs))
    acc = call(middle_kernel, *tables[1], adj_tiles, [plus, minus], [acc], sums, False, "near_tiles")
    outs = (jax.ShapeDtypeStruct((256, 128), jnp.bfloat16), jax.ShapeDtypeStruct((64, 2, 128), jnp.float32))
    agg, partial = call(last_kernel, *tables[2], adj_tiles, far, [acc, f_rows], outs, True, "far_tiles")

    pieces = lax.all_to_all(partial, ROWS, 0, 0, tiled=True)
    a_parts = [halves(agg)] + [halves(lax.ppermute(agg, SLAB, pairs)) for pairs in FLIPS]
    grad_input = jnp.einsum(
        "rs,is->ri", jnp.concatenate(a_parts, axis=1), jnp.concatenate(w_parts, axis=1), preferred_element_type=jnp.float32
    ).astype(jnp.bfloat16)
    grad_weight = jnp.sum(pieces, axis=0).reshape(4, 64)
    return grad_input, grad_weight


def solution(mesh):
    fine = Mesh(mesh.devices.reshape(NZ, NY, NX, NL, NC), ALL)
    return jax.shard_map(
        body,
        mesh=fine,
        in_specs=(P(ROWS, None, None), P(ROWS, None), P(ROWS, SLAB), P(ROWS, SLAB), P(ROWS, None), P(None, SLAB)),
        out_specs=(P(ROWS, SLAB), P(ROWS, SLAB)),
        check_vma=False,
    )
```

time: 131 us -> 102 us (0.78)
  waiting for transfers between devices: 60.6 us -> 25.9 us
  blocking collectives: 20.6 us -> 0 us
  starting transfers between devices: 13.8 us -> 32 us
  Pallas kernels: 6.95 us -> 22.6 us
  between operations: 14.2 us -> 0.91 us
  local copies, waits for them, and re-layouts: 8.44 us -> 11.4 us
  other arithmetic: 3.33 us -> 6.06 us
    all_gather x1 -> x0, waiting for transfers between devices: 51.2 us -> none  [body(): gathered = lax.all_gather(gathered, 'z', axis=0, tiled=False)]
    all_gather x2 -> x0, blocking collectives: 20.6 us -> none  [the longest x1 14.2 us: body(): gathered = lax.all_gather(gathered, 'x', axis=0, tiled=False)]
    ppermute x0 -> x10, starting transfers between devices: none -> 19.4 us  [the longest x3 10.2 us: from_rows(): return lax.ppermute(value, ALL, pairs)]
    ppermute x0 -> x10, waiting for transfers between devices: none -> 16.8 us  [the longest x7 11.1 us: from_axis(): return lax.ppermute(value, ALL, pairs)]
    pallas_call x1 -> x4, Pallas kernels: 6.95 us -> 22.6 us  [the longest x3 20.9 us: call(): pl.pallas_call(kernel, out_shape=out_shape, in_specs=[smem, smem, anywher...]
    all_to_all x1, starting transfers between devices: 9.26 us -> 7.03 us  [body(): pieces = lax.all_to_all(partial, ROWS, 0, 0, tiled=True)]
    slice x1 -> x2, local copies, waits for them, and re-layouts: 0.01 us -> 1.7 us  [gather_far(): return [from_axis(plus[:2], True, 1), from_axis(minus[2:], True, -1)]]
    unnamed x6 -> x7, local copies, waits for them, and re-layouts: 4.98 us -> 6.66 us
  transfers between devices with their start and end apart: 8 -> 17, of which waited for: 3 -> 6; matrix products, arithmetic and copies ran while one was open for 4% -> 10% of each run, Pallas kernels for 5% -> 21%
where the time goes in v2:
time: 102 us; the launch traced here: 99.9 us
  starting transfers between devices  32 us (31%)
  waiting for transfers between devices  25.9 us (25%)
  Pallas kernels  22.6 us (22%)
  local copies, waits for them, and re-layouts  11.4 us (11%)
  other arithmetic  6.06 us (6%)
    pallas_call x3, Pallas kernels, call(): pl.pallas_call(kernel, out_shape=out_shape, in_specs=[smem, smem, anywher...  20.9 us
    ppermute x7, waiting for transfers between devices, from_axis(): return lax.ppermute(value, ALL, pairs)  11.1 us
    ppermute x3, starting transfers between devices, from_rows(): return lax.ppermute(value, ALL, pairs)  10.2 us
    ppermute x7, starting transfers between devices, from_axis(): return lax.ppermute(value, ALL, pairs)  9.25 us
    all_to_all x1, starting transfers between devices, body(): pieces = lax.all_to_all(partial, ROWS, 0, 0, tiled=True)  7.03 us
    all_to_all x1, waiting for transfers between devices, body(): pieces = lax.all_to_all(partial, ROWS, 0, 0, tiled=True)  7 us
    unnamed x7, local copies, waits for them, and re-layouts  6.66 us
    ppermute x3, waiting for transfers between devices, from_rows(): return lax.ppermute(value, ALL, pairs)  5.69 us
  transfers between devices with their start and end apart: 17, of which 6 were waited for; matrix products, arithmetic and copies ran while one was open for 10% of the time, Pallas kernels for 21%

profile of v2, /device:TPU:8, one launch (start us, length us, event | category | flops | bytes accessed | tf_op | source)
XLA Modules:
  0.0 99.9 jit_solution(16370884706692988015)
XLA Ops:
  0.6 1.7 %masked.1 = bf16[256,128]{1,0:T(8,128)(2,1)} custom-call(bf16[64,512]{1,0:T(8,128)(2,1)} %bitcast.39, s32[64,512]{1,0:T(8,128)} %bitcast.35), custom_call_target="tpu_custom_call" | custom-call | tf_op jit(solution)/shard_map/masked/pallas_call | solution.py:140
  2.3 2.3 %collective-permute-start = (bf16[256,128]{1,0:T(8,128)(2,1)}, bf16[256,128]{1,0:T(8,128)(2,1)S(1)}, u32[]{:S(2)}, u32[]{:S(2)}) collective-permute-start(bf16[256,128]{1,0:T(8,128)(2,1)} %masked.1), channel_id=1, source_target_pairs={{16,0},{17,1},{18,2},{19,3},{20,4},{21,5},{22,6},{23,7},{24,8},{25... | collective-permute-start | bytes 196616 | tf_op jit(solution)/shard_map/ppermute | solution.py:27
  4.6 7.2 %collective-permute-start.1 = (bf16[256,128]{1,0:T(8,128)(2,1)}, bf16[256,128]{1,0:T(8,128)(2,1)S(1)}, u32[]{:S(2)}, u32[]{:S(2)}) collective-permute-start(bf16[256,128]{1,0:T(8,128)(2,1)} %masked.1), channel_id=1, source_target_pairs={{128,0},{129,1},{130,2},{131,3},{132,4},{133,5},{134,6},{135,7},{1... | collective-permute-start | bytes 196616 | tf_op jit(solution)/shard_map/ppermute | solution.py:27
  11.8 0.7 collective-permute-start.2
  12.5 0.8 compare_select_fusion.9
  13.3 0.1 convert_reduce_fusion.5
  13.4 0.1 select_reduce_fusion.8
  13.5 0.1 convert_reduce_fusion.8
  13.6 0.7 slice.47
  14.3 0.1 convert_reduce_fusion.3
  14.4 0.1 select_reduce_fusion.6
  14.6 0.1 convert_reduce_fusion.6
  14.6 0.1 convert_reduce_fusion.4
  14.8 0.1 select_reduce_fusion.7
  14.9 0.1 convert_reduce_fusion.7
  15.0 0.6 slice.48
  15.6 0.6 slice.49
  16.1 0.1 select_reduce_fusion.3
  16.3 0.2 convert_reduce_fusion
  16.5 0.1 select_reduce_fusion.4
  16.6 0.1 select_reduce_fusion.5
  16.7 1.3 %pad_add_fusion.1 = (s32[29]{0:T(128)S(1)}, s32[29]{0:T(128)S(1)}) fusion(s32[1]{0:T(128)} %slice.48, s32[28]{0:T(128)S(1)} %broadcast_minimum_fusion.1, s32[1]{0:T(128)} %slice.49, s32[28]{0:T(128)S(1)} %broadcast_minimum_fusion), kind=kLoop, calls=%fused_computation.152 | loop fusion | flops 58 | bytes 464 | tf_op jit(solution)/shard_map/concatenate | solution.py:83
  18.0 5.7 %collective-permute-done.2 = bf16[256,128]{1,0:T(8,128)(2,1)S(1)} collective-permute-done((bf16[256,128]{1,0:T(8,128)(2,1)}, bf16[256,128]{1,0:T(8,128)(2,1)S(1)}, u32[]{:S(2)}, u32[]{:S(2)}) %collective-permute-start.2) | collective-permute-done | bytes 65568 | tf_op jit(solution)/shard_map/ppermute | solution.py:27
  23.7 0.9 fusion.37
  24.5 2.8 %collective-permute-start.3 = (bf16[4,256,128]{2,1,0:T(8,128)(2,1)S(1)}, bf16[4,256,128]{2,1,0:T(8,128)(2,1)S(1)}, u32[]{:S(2)}, u32[]{:S(2)}) collective-permute-start(bf16[4,256,128]{2,1,0:T(8,128)(2,1)S(1)} %get-tuple-element.35), channel_id=1, source_target_pairs={{4,0},{33,1},{6,2},{35,3},{8,4},{37,5},{10,6},{39,7},{12,8},{41,9}... | collective-permute-start | bytes 786440 | tf_op jit(solution)/shard_map/ppermute | solution.py:36
  27.4 2.3 %collective-permute-start.5 = (bf16[4,256,128]{2,1,0:T(8,128)(2,1)S(1)}, bf16[4,256,128]{2,1,0:T(8,128)(2,1)S(1)}, u32[]{:S(2)}, u32[]{:S(2)}) collective-permute-start(bf16[4,256,128]{2,1,0:T(8,128)(2,1)S(1)} %get-tuple-element.35), channel_id=1, source_target_pairs={{8,0},{65,1},{10,2},{67,3},{12,4},{69,5},{14,6},{71,7},{0,8},{73,9... | collective-permute-start | bytes 786440 | tf_op jit(solution)/shard_map/ppermute | solution.py:36
  29.7 0.8 pad_add_fusion.step_row
  30.4 1.1 %copy.11 = bf16[512,256]{0,1:T(8,128)(2,1)S(1)} copy(bf16[512,256]{1,0:T(8,128)(2,1)} %param.10) | data formatting | bytes 524288 | tf_op args[4]
  31.5 0.1 reshape.375
  31.6 0.0 copy-start.2
  31.7 0.2 convert_reduce_fusion.1
  31.8 0.2 convert_reduce_fusion.2
  32.0 5.7 %collective-permute-done.4 = bf16[4,256,128]{2,1,0:T(8,128)(2,1)S(1)} collective-permute-done((bf16[4,256,128]{2,1,0:T(8,128)(2,1)S(1)}, bf16[4,256,128]{2,1,0:T(8,128)(2,1)S(1)}, u32[]{:S(2)}, u32[]{:S(2)}) %collective-permute-start.4) | collective-permute-done | bytes 262176 | tf_op jit(solution)/shard_map/ppermute | solution.py:36
  37.8 0.1 pad_maximum_fusion
  37.9 0.1 collective-permute-start.6
  38.0 2.0 %collective-permute-start.7 = (bf16[4,4,256,128]{3,2,1,0:T(8,128)(2,1)S(1)}, bf16[4,4,256,128]{3,2,1,0:T(8,128)(2,1)S(1)}, u32[]{:S(2)}, u32[]{:S(2)}) collective-permute-start(bf16[4,4,256,128]{3,2,1,0:T(8,128)(2,1)S(1)} %pad_maximum_fusion), channel_id=1, source_target_pairs={{224,0},{13,1},{226,2},{15,3},{228,4},{1,5},{230,6},{3,7},{232,8},... | collective-permute-start | bytes 3145736 | tf_op jit(solution)/shard_map/ppermute | solution.py:36
  40.1 0.2 select_reduce_fusion
  40.3 2.8 %copy-done = bf16[192,128,128]{2,1,0:T(8,128)(2,1)S(1)} copy-done((bf16[192,128,128]{2,1,0:T(8,128)(2,1)S(1)}, bf16[192,128,128]{2,1,0:T(8,128)(2,1)}, u32[]{:S(2)}) %copy-start) | copy-done | bytes 6291480
  43.1 5.6 %early_tiles.1.before = f32[4,128,128]{2,1,0:T(8,128)S(1)} custom-call(s32[224]{0:T(256)S(1)} %compare_select_fusion.28.table, s32[29]{0:T(128)S(1)} %pad_add_fusion.step_row, bf16[192,128,128]{2,1,0:T(8,128)(2,1)S(1)} %copy-done, bf16[32,128,128]{2,1,0:T(8,128)(2,1)S(1)} %bitcast.25), custom_call_target="tpu_custom_call" | custom-call | flops 268435456 | bytes 8388608 | tf_op jit(solution)/shard_map/early_tiles/pallas_call | solution.py:178
  48.7 4.1 %collective-permute-done.6 = bf16[4,4,256,128]{3,2,1,0:T(8,128)(2,1)S(1)} collective-permute-done((bf16[4,4,256,128]{3,2,1,0:T(8,128)(2,1)S(1)}, bf16[4,4,256,128]{3,2,1,0:T(8,128)(2,1)S(1)}, u32[]{:S(2)}, u32[]{:S(2)}) %collective-permute-start.6) | collective-permute-done | bytes 1048608 | tf_op jit(solution)/shard_map/ppermute | solution.py:36
  52.8 1.3 %collective-permute-done.7 = bf16[4,4,256,128]{3,2,1,0:T(8,128)(2,1)S(1)} collective-permute-done((bf16[4,4,256,128]{3,2,1,0:T(8,128)(2,1)S(1)}, bf16[4,4,256,128]{3,2,1,0:T(8,128)(2,1)S(1)}, u32[]{:S(2)}, u32[]{:S(2)}) %collective-permute-start.7) | collective-permute-done | bytes 1048608 | tf_op jit(solution)/shard_map/ppermute | solution.py:36
  54.1 0.8 slice.50
  54.9 0.9 slice.51
  55.8 2.0 %collective-permute-start.9 = (bf16[2,4,256,128]{3,2,1,0:T(8,128)(2,1)}, bf16[2,4,256,128]{3,2,1,0:T(8,128)(2,1)}, u32[]{:S(2)}, u32[]{:S(2)}) collective-permute-start(bf16[2,4,256,128]{3,2,1,0:T(8,128)(2,1)} %slice.51), channel_id=1, source_target_pairs={{224,0},{13,1},{226,2},{15,3},{228,4},{1,5},{230,6},{3,7},{232,8},... | collective-permute-start | bytes 1572872 | tf_op jit(solution)/shard_map/ppermute | solution.py:36
  57.8 0.1 constant_dynamic-slice_fusion.3
  57.9 0.1 collective-permute-start.13
  58.0 0.7 collective-permute-start.14
  58.8 1.1 %collective-permute-start.15 = (bf16[64,64]{0,1:T(8,128)(2,1)S(1)}, bf16[64,64]{0,1:T(8,128)(2,1)S(1)}, u32[]{:S(2)}, u32[]{:S(2)}) collective-permute-start(bf16[64,64]{0,1:T(8,128)(2,1)S(1)} %get-tuple-element.45), channel_id=1, source_target_pairs={{0,3},{3,0},{1,2},{2,1},{4,7},{7,4},{5,6},{6,5},{8,11},{11,8},{9,1... | collective-permute-start | bytes 24584 | tf_op jit(solution)/shard_map/ppermute | solution.py:217
  59.9 2.8 %copy-done.1 = bf16[192,128,128]{2,1,0:T(8,128)(2,1)S(1)} copy-done((bf16[192,128,128]{2,1,0:T(8,128)(2,1)S(1)}, bf16[192,128,128]{2,1,0:T(8,128)(2,1)}, u32[]{:S(2)}) %copy-start.1) | copy-done | bytes 6291480
  62.7 9.4 %near_tiles.1.before = f32[4,128,128]{2,1,0:T(8,128)S(1)} custom-call(s32[224]{0:T(256)S(1)} %get-tuple-element.17.table, s32[29]{0:T(128)S(1)} %get-tuple-element.18.step_row, bf16[192,128,128]{2,1,0:T(8,128)(2,1)S(1)} %copy-done.1, bf16[32,128,128]{2,1,0:T(8,128)(2,1)S(1)} %bitcast.26, bf16[32,128,128]{2,1,0:T(8,128)(2,1)S(1)} %bitcast.27, ...), custom_call_target="tpu_custom_call" | custom-call | flops 268435456 | bytes 8388608 | tf_op jit(solution)/shard_map/near_tiles/pallas_call | solution.py:178
  72.1 5.9 %far_tiles.1 = (bf16[256,128]{1,0:T(8,128)(2,1)S(1)}, f32[64,2,128]{2,1,0:T(2,128)}) custom-call(s32[224]{0:T(256)S(1)} %get-tuple-element.13.table, s32[29]{0:T(128)S(1)} %get-tuple-element.14.step_row, bf16[192,128,128]{2,1,0:T(8,128)(2,1)S(1)} %copy-done.1, bf16[16,128,128]{2,1,0:T(8,128)(2,1)S(1)} %bitcast.29, bf16[16,128,128]{2,1,0:T(8,128)(2,1)} %bitcast.19.source_b, ...), custom_call_target="tpu_custom_call" | custom-call | flops 268435456 | bytes 8388608 | tf_op jit(solution)/shard_map/far_tiles/pallas_call | solution.py:178
  78.0 1.2 %collective-permute-start.10 = (bf16[256,128]{1,0:T(8,128)(2,1)S(1)}, bf16[256,128]{1,0:T(8,128)(2,1)S(1)}, u32[]{:S(2)}, u32[]{:S(2)}) collective-permute-start(bf16[256,128]{1,0:T(8,128)(2,1)S(1)} %get-tuple-element.21), channel_id=1, source_target_pairs={{0,1},{1,0},{2,3},{3,2},{4,5},{5,4},{6,7},{7,6},{8,9},{9,8},{10,11... | collective-permute-start | bytes 196616 | tf_op jit(solution)/shard_map/ppermute | solution.py:223
  79.3 0.7 collective-permute-start.11
  79.9 0.1 fusion.38
  80.0 7.0 %all-to-all-start = ((f32[64,2,128]{2,1,0:T(2,128)}), f32[64,2,128]{2,1,0:T(2,128)S(1)}, u32[]{:S(2)}, u32[]{:S(2)}) async-start(f32[64,2,128]{2,1,0:T(2,128)} %get-tuple-element.23), calls=%async_computation | async-start | bytes 131072 | tf_op jit(solution)/shard_map/all_to_all | solution.py:222
  87.1 1.7 %collective-permute-start.12 = (bf16[256,128]{1,0:T(8,128)(2,1)S(1)}, bf16[256,128]{1,0:T(8,128)(2,1)S(1)}, u32[]{:S(2)}, u32[]{:S(2)}) collective-permute-start(bf16[256,128]{1,0:T(8,128)(2,1)S(1)} %get-tuple-element.21), channel_id=1, source_target_pairs={{0,3},{3,0},{1,2},{2,1},{4,7},{7,4},{5,6},{6,5},{8,11},{11,8},{9,1... | collective-permute-start | bytes 196616 | tf_op jit(solution)/shard_map/ppermute | solution.py:223
  88.8 0.1 fusion.39
  88.9 0.1 fusion.40
  89.0 2.0 %collective-permute-done.12 = bf16[256,128]{1,0:T(8,128)(2,1)S(1)} collective-permute-done((bf16[256,128]{1,0:T(8,128)(2,1)S(1)}, bf16[256,128]{1,0:T(8,128)(2,1)S(1)}, u32[]{:S(2)}, u32[]{:S(2)}) %collective-permute-start.12) | collective-permute-done | bytes 65568 | tf_op jit(solution)/shard_map/ppermute | solution.py:223
  91.0 0.1 fusion.41
  91.1 1.0 convolution_convert_fusion
  92.1 7.0 %all-to-all-done = f32[64,2,128]{2,1,0:T(2,128)S(1)} async-done(((f32[64,2,128]{2,1,0:T(2,128)}), f32[64,2,128]{2,1,0:T(2,128)S(1)}, u32[]{:S(2)}, u32[]{:S(2)}) %all-to-all-start) | async-done | bytes 65568 | tf_op jit(solution)/shard_map/all_to_all | solution.py:222
  99.1 0.1 reduce_sum.189
  99.2 0.7 reshape.381
  (33 shorter events, 0.3 us)
Async XLA Ops:
  2.3 15.6 %collective-permute-start = (bf16[256,128]{1,0:T(8,128)(2,1)}, bf16[256,128]{1,0:T(8,128)(2,1)S(1)}, u32[]{:S(2)}, u32[]{:S(2)}) collective-permute-start(bf16[256,128]{1,0:T(8,128)(2,1)} %masked.1), channel_id=1, source_target_pairs={{16,0},{17,1},{18,2},{19,3},{20,4},{21,5},{22,6},{23,7},{24,8},{25... | collective-permute-start | bytes 196616 | tf_op jit(solution)/shard_map/ppermute | solution.py:27
  4.6 13.4 %collective-permute-start.1 = (bf16[256,128]{1,0:T(8,128)(2,1)}, bf16[256,128]{1,0:T(8,128)(2,1)S(1)}, u32[]{:S(2)}, u32[]{:S(2)}) collective-permute-start(bf16[256,128]{1,0:T(8,128)(2,1)} %masked.1), channel_id=1, source_target_pairs={{128,0},{129,1},{130,2},{131,3},{132,4},{133,5},{134,6},{135,7},{1... | collective-permute-start | bytes 196616 | tf_op jit(solution)/shard_map/ppermute | solution.py:27
  11.8 11.9 %collective-permute-start.2 = (bf16[256,128]{1,0:T(8,128)(2,1)}, bf16[256,128]{1,0:T(8,128)(2,1)S(1)}, u32[]{:S(2)}, u32[]{:S(2)}) collective-permute-start(bf16[256,128]{1,0:T(8,128)(2,1)} %masked.1), channel_id=1, source_target_pairs={{144,0},{145,1},{146,2},{147,3},{148,4},{149,5},{150,6},{151,7},{1... | collective-permute-start | bytes 196616 | tf_op jit(solution)/shard_map/ppermute | solution.py:27
  24.5 7.5 %collective-permute-start.3 = (bf16[4,256,128]{2,1,0:T(8,128)(2,1)S(1)}, bf16[4,256,128]{2,1,0:T(8,128)(2,1)S(1)}, u32[]{:S(2)}, u32[]{:S(2)}) collective-permute-start(bf16[4,256,128]{2,1,0:T(8,128)(2,1)S(1)} %get-tuple-element.35), channel_id=1, source_target_pairs={{4,0},{33,1},{6,2},{35,3},{8,4},{37,5},{10,6},{39,7},{12,8},{41,9}... | collective-permute-start | bytes 786440 | tf_op jit(solution)/shard_map/ppermute | solution.py:36
  27.4 10.4 %collective-permute-start.4 = (bf16[4,256,128]{2,1,0:T(8,128)(2,1)S(1)}, bf16[4,256,128]{2,1,0:T(8,128)(2,1)S(1)}, u32[]{:S(2)}, u32[]{:S(2)}) collective-permute-start(bf16[4,256,128]{2,1,0:T(8,128)(2,1)S(1)} %get-tuple-element.35), channel_id=1, source_target_pairs={{12,0},{225,1},{14,2},{227,3},{0,4},{229,5},{2,6},{231,7},{4,8},{2... | collective-permute-start | bytes 786440 | tf_op jit(solution)/shard_map/ppermute | solution.py:36
  27.4 10.4 %collective-permute-start.5 = (bf16[4,256,128]{2,1,0:T(8,128)(2,1)S(1)}, bf16[4,256,128]{2,1,0:T(8,128)(2,1)S(1)}, u32[]{:S(2)}, u32[]{:S(2)}) collective-permute-start(bf16[4,256,128]{2,1,0:T(8,128)(2,1)S(1)} %get-tuple-element.35), channel_id=1, source_target_pairs={{8,0},{65,1},{10,2},{67,3},{12,4},{69,5},{14,6},{71,7},{0,8},{73,9... | collective-permute-start | bytes 786440 | tf_op jit(solution)/shard_map/ppermute | solution.py:36
  31.6 26.2 %copy-start.2 = (bf16[256,64]{0,1:T(8,128)(2,1)S(1)}, bf16[256,64]{0,1:T(8,128)(2,1)}, u32[]{:S(2)}) copy-start(bf16[256,64]{0,1:T(8,128)(2,1)} %param.11) | copy-start | bytes 98308
  37.9 14.9 %collective-permute-start.6 = (bf16[4,4,256,128]{3,2,1,0:T(8,128)(2,1)S(1)}, bf16[4,4,256,128]{3,2,1,0:T(8,128)(2,1)S(1)}, u32[]{:S(2)}, u32[]{:S(2)}) collective-permute-start(bf16[4,4,256,128]{3,2,1,0:T(8,128)(2,1)S(1)} %pad_maximum_fusion), channel_id=1, source_target_pairs={{32,0},{5,1},{34,2},{7,3},{36,4},{9,5},{38,6},{11,7},{40,8},{13,9}... | collective-permute-start | bytes 3145736 | tf_op jit(solution)/shard_map/ppermute | solution.py:36
  38.0 16.1 %collective-permute-start.7 = (bf16[4,4,256,128]{3,2,1,0:T(8,128)(2,1)S(1)}, bf16[4,4,256,128]{3,2,1,0:T(8,128)(2,1)S(1)}, u32[]{:S(2)}, u32[]{:S(2)}) collective-permute-start(bf16[4,4,256,128]{3,2,1,0:T(8,128)(2,1)S(1)} %pad_maximum_fusion), channel_id=1, source_target_pairs={{224,0},{13,1},{226,2},{15,3},{228,4},{1,5},{230,6},{3,7},{232,8},... | collective-permute-start | bytes 3145736 | tf_op jit(solution)/shard_map/ppermute | solution.py:36
  40.3 2.8 %copy-start = (bf16[192,128,128]{2,1,0:T(8,128)(2,1)S(1)}, bf16[192,128,128]{2,1,0:T(8,128)(2,1)}, u32[]{:S(2)}) copy-start(bf16[192,128,128]{2,1,0:T(8,128)(2,1)} %adj.5) | copy-start | bytes 18874372
  54.9 17.1 %collective-permute-start.8 = (bf16[2,4,256,128]{3,2,1,0:T(8,128)(2,1)}, bf16[2,4,256,128]{3,2,1,0:T(8,128)(2,1)S(1)}, u32[]{:S(2)}, u32[]{:S(2)}) collective-permute-start(bf16[2,4,256,128]{3,2,1,0:T(8,128)(2,1)} %slice.50), channel_id=1, source_target_pairs={{32,0},{5,1},{34,2},{7,3},{36,4},{9,5},{38,6},{11,7},{40,8},{13,9}... | collective-permute-start | bytes 1572872 | tf_op jit(solution)/shard_map/ppermute | solution.py:36
  55.8 16.3 %collective-permute-start.9 = (bf16[2,4,256,128]{3,2,1,0:T(8,128)(2,1)}, bf16[2,4,256,128]{3,2,1,0:T(8,128)(2,1)}, u32[]{:S(2)}, u32[]{:S(2)}) collective-permute-start(bf16[2,4,256,128]{3,2,1,0:T(8,128)(2,1)} %slice.51), channel_id=1, source_target_pairs={{224,0},{13,1},{226,2},{15,3},{228,4},{1,5},{230,6},{3,7},{232,8},... | collective-permute-start | bytes 1572872 | tf_op jit(solution)/shard_map/ppermute | solution.py:36
  57.9 33.2 %collective-permute-start.13 = (bf16[64,64]{0,1:T(8,128)(2,1)S(1)}, bf16[64,64]{0,1:T(8,128)(2,1)S(1)}, u32[]{:S(2)}, u32[]{:S(2)}) collective-permute-start(bf16[64,64]{0,1:T(8,128)(2,1)S(1)} %get-tuple-element.47), channel_id=1, source_target_pairs={{0,1},{1,0},{2,3},{3,2},{4,5},{5,4},{6,7},{7,6},{8,9},{9,8},{10,11... | collective-permute-start | bytes 24584 | tf_op jit(solution)/shard_map/ppermute | solution.py:217
  58.0 33.1 %collective-permute-start.14 = (bf16[64,64]{0,1:T(8,128)(2,1)S(1)}, bf16[64,64]{0,1:T(8,128)(2,1)S(1)}, u32[]{:S(2)}, u32[]{:S(2)}) collective-permute-start(bf16[64,64]{0,1:T(8,128)(2,1)S(1)} %get-tuple-element.46), channel_id=1, source_target_pairs={{0,2},{2,0},{1,3},{3,1},{4,6},{6,4},{5,7},{7,5},{8,10},{10,8},{9,1... | collective-permute-start | bytes 24584 | tf_op jit(solution)/shard_map/ppermute | solution.py:217
  58.8 32.4 %collective-permute-start.15 = (bf16[64,64]{0,1:T(8,128)(2,1)S(1)}, bf16[64,64]{0,1:T(8,128)(2,1)S(1)}, u32[]{:S(2)}, u32[]{:S(2)}) collective-permute-start(bf16[64,64]{0,1:T(8,128)(2,1)S(1)} %get-tuple-element.45), channel_id=1, source_target_pairs={{0,3},{3,0},{1,2},{2,1},{4,7},{7,4},{5,6},{6,5},{8,11},{11,8},{9,1... | collective-permute-start | bytes 24584 | tf_op jit(solution)/shard_map/ppermute | solution.py:217
  59.9 2.8 %copy-start.1 = (bf16[192,128,128]{2,1,0:T(8,128)(2,1)S(1)}, bf16[192,128,128]{2,1,0:T(8,128)(2,1)}, u32[]{:S(2)}) copy-start(bf16[192,128,128]{2,1,0:T(8,128)(2,1)} %adj.5) | copy-start | bytes 18874372
  78.0 9.0 %collective-permute-start.10 = (bf16[256,128]{1,0:T(8,128)(2,1)S(1)}, bf16[256,128]{1,0:T(8,128)(2,1)S(1)}, u32[]{:S(2)}, u32[]{:S(2)}) collective-permute-start(bf16[256,128]{1,0:T(8,128)(2,1)S(1)} %get-tuple-element.21), channel_id=1, source_target_pairs={{0,1},{1,0},{2,3},{3,2},{4,5},{5,4},{6,7},{7,6},{8,9},{9,8},{10,11... | collective-permute-start | bytes 196616 | tf_op jit(solution)/shard_map/ppermute | solution.py:223
  79.3 9.6 %collective-permute-start.11 = (bf16[256,128]{1,0:T(8,128)(2,1)S(1)}, bf16[256,128]{1,0:T(8,128)(2,1)S(1)}, u32[]{:S(2)}, u32[]{:S(2)}) collective-permute-start(bf16[256,128]{1,0:T(8,128)(2,1)S(1)} %get-tuple-element.21), channel_id=1, source_target_pairs={{0,2},{2,0},{1,3},{3,1},{4,6},{6,4},{5,7},{7,5},{8,10},{10,8},{9,1... | collective-permute-start | bytes 196616 | tf_op jit(solution)/shard_map/ppermute | solution.py:223
  80.0 19.1 %all-to-all-start = ((f32[64,2,128]{2,1,0:T(2,128)}), f32[64,2,128]{2,1,0:T(2,128)S(1)}, u32[]{:S(2)}, u32[]{:S(2)}) async-start(f32[64,2,128]{2,1,0:T(2,128)} %get-tuple-element.23), calls=%async_computation | async-start | bytes 131072 | tf_op jit(solution)/shard_map/all_to_all | solution.py:222
  87.1 3.9 %collective-permute-start.12 = (bf16[256,128]{1,0:T(8,128)(2,1)S(1)}, bf16[256,128]{1,0:T(8,128)(2,1)S(1)}, u32[]{:S(2)}, u32[]{:S(2)}) collective-permute-start(bf16[256,128]{1,0:T(8,128)(2,1)S(1)} %get-tuple-element.21), channel_id=1, source_target_pairs={{0,3},{3,0},{1,2},{2,1},{4,7},{7,4},{5,6},{6,5},{8,11},{11,8},{9,1... | collective-permute-start | bytes 196616 | tf_op jit(solution)/shard_map/ppermute | solution.py:223

commit v3 on v2

v3 whole, which is shorter than its diff:
```python
import jax
import jax.numpy as jnp
from jax import lax
from jax.experimental import pallas as pl
from jax.experimental.pallas import tpu as pltpu
from jax.sharding import Mesh, PartitionSpec as P

NZ, NY, NX, NL, NC = 8, 2, 4, 2, 2
ROWS = ("z", "yh", "x")
SLAB = ("yl", "core")
ALL = ROWS + SLAB
GROUP = 4
FLIPS = ([(0, 1), (1, 0), (2, 3), (3, 2)], [(0, 2), (2, 0), (1, 3), (3, 1)], [(0, 3), (3, 0), (1, 2), (2, 1)])


def device(z, y, x, l, c):
    return ((((z % NZ) * NY + y % NY) * NX + x % NX) * NL + l) * NC + c


def places():
    return [(z, y, x, l, c) for z in range(NZ) for y in range(NY) for x in range(NX) for l in range(NL) for c in range(NC)]


def from_rows(value, dz=0, dy=0):
    pairs = [(device(z + dz, y + dy, x, l, c), device(z, y, x, l, c)) for z, y, x, l, c in places()]
    return lax.ppermute(value, ALL, pairs)


def from_axis(value, second, step):
    pairs = []
    for z, y, x, l, c in places():
        along_x = (c == 0) != second
        z_step = -step if step == 2 and z % 2 else step
        source = device(z, y, x + step, l, c) if along_x else device(z + z_step, y, x, l, c)
        pairs.append((source, device(z, y, x, l, c)))
    return lax.ppermute(value, ALL, pairs)


def gather_near(packed):
    far_y, far = from_rows(packed, dz=4, dy=1), from_rows(packed, dz=4)
    four = jnp.stack([packed, from_rows(again(packed), dy=1), far, far_y])
    early = jnp.stack([four, from_axis(four, False, 1), from_axis(four, False, -1), from_axis(four, False, 2)])
    plus, minus = from_axis(early, True, 1), from_axis(early, True, -1)
    return early, plus, minus


def gather_far(plus, minus):
    return [from_axis(plus[:2], True, 1), from_axis(minus[2:], True, -1)]


def where_held(column):
    owner, block = column // 4, column % 4
    core = lax.axis_index("core")
    dz = (owner // (NY * NX) - lax.axis_index("z")) % NZ
    dy = (owner // NX - lax.axis_index("yh")) % NY
    dx = (owner - lax.axis_index("x")) % NX
    ring = jnp.where(core == 0, dx, dz % 4)
    late = jnp.where(core == 0, dz % 4, dx)
    a = jnp.where(ring == 2, 3, jnp.where(ring == 3, 2, ring))
    upper = (dz >= 3) & (dz <= 6)
    swapped = jnp.where(core == 0, (late == 2) & (a >= 2), (ring == 2) & (lax.axis_index("z") % 2 == 1))
    e = dy + 2 * (upper != swapped).astype(jnp.int32)
    source = jnp.where(late == 0, 0, jnp.where(late == 1, 1, jnp.where(late == 3, 2, 3 + a // 2)))
    place = (jnp.where(late == 2, a % 2, a) * 4 + e) * 2 + block % 2
    return source, place, block // 2


def tile_table(row, source, place, half, count):
    listed = row.shape[0]
    t = jnp.arange(listed)
    r4, sources = jnp.arange(4), jnp.arange(count)
    key = source * 4 + row
    rank = jnp.sum(((key[None, :] == key[:, None]) & (t[None, :] < t[:, None])).astype(jnp.int32), axis=1)
    held = jnp.sum((key[:, None] == jnp.arange(count * 4)[None, :]).astype(jnp.int32), axis=0).reshape(count, 4)
    need = jnp.max((held + GROUP - 1) // GROUP, axis=1)
    bounds = jnp.sum(jnp.where(sources[None, :] < jnp.arange(count + 1)[:, None], need[None, :], 0), axis=1)
    begin = jnp.sum(jnp.where(source[:, None] == sources[None, :], bounds[None, :count], 0), axis=1)
    slot = ((begin + rank // GROUP) * 4 + row) * GROUP + rank % GROUP
    value = 1 + t + place * 256 + half * 65536
    j = jnp.arange((listed // GROUP + count) * 4 * GROUP)
    table = jnp.sum(jnp.where(slot[None, :] == j[:, None], value[None, :], 0), axis=1)
    return jnp.where(table > 0, table - 1, 2 * 65536).astype(jnp.int32), bounds.astype(jnp.int32)


def add_tiles(table, first, last, adj, blocks, acc, masks):
    def step(s, carry):
        for r in range(4):
            lhs, rhs = [], []
            for u in range(GROUP):
                e = table[(s * 4 + r) * GROUP + u]
                lhs.append(adj[e & 255])
                rhs.append(blocks[(e >> 8) & 255] * masks[e >> 16])
            acc[r] += jnp.dot(
                jnp.concatenate(lhs, axis=1), jnp.concatenate(rhs, axis=0), preferred_element_type=jnp.float32
            )
        return carry

    lax.fori_loop(first, last, step, 0)


def set_masks(masks):
    lane = lax.broadcasted_iota(jnp.int32, (128, 128), 1)
    masks[0] = jnp.where(lane < 64, 1.0, 0.0).astype(masks.dtype)
    masks[1] = jnp.where(lane < 64, 0.0, 1.0).astype(masks.dtype)
    masks[2] = jnp.zeros((128, 128), masks.dtype)
    return lane


def pre_kernel(grad_out, relu_mask, out):
    g = grad_out[...].astype(jnp.float32) * relu_mask[...].astype(jnp.float32)
    out[...] = jnp.concatenate([g[:, :256], g[:, 256:]], axis=0).T.astype(out.dtype)


def masked(grad_out, relu_mask):
    vmem = pl.BlockSpec(memory_space=pltpu.VMEM)
    return pl.pallas_call(
        pre_kernel,
        out_shape=jax.ShapeDtypeStruct((256, 128), jnp.bfloat16),
        in_specs=[vmem, vmem],
        out_specs=vmem,
        name="masked",
    )(grad_out.T, relu_mask.T)


def again_kernel(value, out):
    out[...] = value[...]


def again(value):
    vmem = pl.BlockSpec(memory_space=pltpu.VMEM)
    shape = jax.ShapeDtypeStruct(value.shape, value.dtype)
    return pl.pallas_call(again_kernel, out_shape=shape, in_specs=[vmem], out_specs=vmem, name="again")(value)


def first_kernel(table, bounds, adj, source, acc, masks):
    set_masks(masks)
    acc[...] = jnp.zeros_like(acc)
    add_tiles(table, bounds[0], bounds[1], adj, source, acc, masks)


def middle_kernel(table, bounds, adj, source_a, source_b, before, acc, masks):
    set_masks(masks)
    acc[...] = before[...]
    add_tiles(table, bounds[1], bounds[2], adj, source_a, acc, masks)
    add_tiles(table, bounds[2], bounds[3], adj, source_b, acc, masks)


def last_kernel(table, bounds, adj, source_a, source_b, before, features, out, partial, acc, masks):
    lane = set_masks(masks)
    acc[...] = before[...]
    add_tiles(table, bounds[3], bounds[4], adj, source_a, acc, masks)
    add_tiles(table, bounds[4], bounds[5], adj, source_b, acc, masks)
    agg = [acc[r] + pltpu.roll(acc[r], 64, 1) for r in range(4)]
    for r in range(2):
        out[pl.ds(r * 128, 128), :] = jnp.where(lane < 64, agg[r], agg[r + 2]).astype(out.dtype)
    rounded = jnp.concatenate([v.astype(jnp.bfloat16) for v in agg], axis=0)
    product = jnp.dot(features[...], rounded, preferred_element_type=jnp.float32)
    low = lax.broadcasted_iota(jnp.int32, (64, 128), 1) < 64
    for p in range(2):
        partial[:, p, :] = jnp.where(low, product[p * 128 : p * 128 + 64], product[p * 128 + 64 : p * 128 + 128])


def call(kernel, table, bounds, adj, sources, others, out_shape, keep_acc, name):
    smem = pl.BlockSpec(memory_space=pltpu.SMEM)
    vmem = pl.BlockSpec(memory_space=pltpu.VMEM)
    sources = [s.reshape(-1, 128, 128) for s in sources]
    return pl.pallas_call(
        kernel,
        out_shape=out_shape,
        in_specs=[smem, smem, vmem] + [vmem] * len(sources) + [vmem] * len(others),
        out_specs=jax.tree.map(lambda _: vmem, out_shape),
        scratch_shapes=([pltpu.VMEM((4, 128, 128), jnp.float32)] if keep_acc else []) + [
            pltpu.VMEM((3, 128, 128), jnp.bfloat16),
        ],
        compiler_params=pltpu.CompilerParams(vmem_limit_bytes=24 * 1024 * 1024),
        cost_estimate=pl.CostEstimate(flops=2 * 64 * 128 * 128 * 128, bytes_accessed=8 * 1024 * 1024, transcendentals=0),
        name=name,
    )(table, bounds, adj, *sources, *others)


def halves(packed):
    return jnp.concatenate([packed[:, :64], packed[:, 64:]], axis=0)


def body(adj_tiles, tile_index, grad_out, relu_mask, features, weight):
    position = lax.axis_index(ROWS)
    slab = lax.axis_index(SLAB)
    early, plus, minus = gather_near(masked(grad_out, relu_mask))

    source, place, half = where_held(tile_index[:, 1])
    tables = tile_table(tile_index[:, 0] - position * 4, source, place, half, 5)
    f_rows = features.reshape(512, 64, 4).transpose(2, 1, 0).reshape(256, 512)

    sums = jax.ShapeDtypeStruct((4, 128, 128), jnp.float32)
    acc = call(first_kernel, *tables, adj_tiles, [early], [], sums, False, "early_tiles")
    weight, acc, plus, minus, f_rows, tables = lax.optimization_barrier((weight, acc, plus, minus, f_rows, tables))
    far = gather_far(plus, minus)
    w_parts = [lax.dynamic_slice_in_dim(weight, slab * 64, 64, 0)]
    for k, pairs in enumerate(FLIPS):
        w_parts.append(lax.ppermute(lax.dynamic_slice_in_dim(weight, (slab ^ (k + 1)) * 64, 64, 0), SLAB, pairs))
    acc = call(middle_kernel, *tables, adj_tiles, [plus, minus], [acc], sums, False, "near_tiles")
    outs = (jax.ShapeDtypeStruct((256, 128), jnp.bfloat16), jax.ShapeDtypeStruct((64, 2, 128), jnp.float32))
    agg, partial = call(last_kernel, *tables, adj_tiles, far, [acc, f_rows], outs, True, "far_tiles")

    pieces = lax.all_to_all(partial, ROWS, 0, 0, tiled=True)
    a_parts = [halves(agg)] + [halves(lax.ppermute(agg, SLAB, pairs)) for pairs in FLIPS]
    grad_input = jnp.einsum(
        "rs,is->ri", jnp.concatenate(a_parts, axis=1), jnp.concatenate(w_parts, axis=1), preferred_element_type=jnp.float32
    ).astype(jnp.bfloat16)
    grad_weight = jnp.sum(pieces, axis=0).reshape(4, 64)
    return grad_input, grad_weight


def solution(mesh):
    fine = Mesh(mesh.devices.reshape(NZ, NY, NX, NL, NC), ALL)
    return jax.shard_map(
        body,
        mesh=fine,
        in_specs=(P(ROWS, None, None), P(ROWS, None), P(ROWS, SLAB), P(ROWS, SLAB), P(ROWS, None), P(None, SLAB)),
        out_specs=(P(ROWS, SLAB), P(ROWS, SLAB)),
        check_vma=False,
    )
```

time: 102 us -> 91.9 us (0.901)
  Pallas kernels: 22.6 us -> 12.1 us
  waiting for transfers between devices: 25.9 us -> 32 us
  other arithmetic: 6.06 us -> 2.76 us
  local copies, waits for them, and re-layouts: 11.4 us -> 9.65 us
    pallas_call x3 -> x4, Pallas kernels: 20.9 us -> 10.4 us  [the longest x3 8.92 us: call(): pl.pallas_call(kernel, out_shape=out_shape, in_specs=[smem, smem, vmem] +...]
    ppermute x7, waiting for transfers between devices: 11.1 us -> 17.4 us  [from_axis(): return lax.ppermute(value, ALL, pairs)]
    concatenate x2 -> x0, other arithmetic: 2.04 us -> none  [tile_table(): jnp.concatenate([step_row, ends[3:]]).astype(jnp.int32)]
    slice x3 -> x0, local copies, waits for them, and re-layouts: 1.82 us -> none  [tile_table(): ends[3:]]
    reduce_sum x15 -> x4, other arithmetic: 1.77 us -> 0.5 us  [the longest x1 0.18 us: tile_table(): jnp.sum(((key[None, :] == key[:, None]) & (t[None, :] < t[:, None])).asty...]
  transfers between devices with their start and end apart: 17 -> 17, of which waited for: 6 -> 8; matrix products, arithmetic and copies ran while one was open for 10% -> 6% of each run, Pallas kernels for 21% -> 12%
where the time goes in v3:
time: 91.9 us; the launch traced here: 90.3 us
  starting transfers between devices  32 us (35%)
  waiting for transfers between devices  32 us (35%)
  Pallas kernels  12.1 us (13%)
  local copies, waits for them, and re-layouts  9.65 us (11%)
  other arithmetic  2.76 us (3%)
  matrix products  0.98 us (1%)
    ppermute x7, waiting for transfers between devices, from_axis(): return lax.ppermute(value, ALL, pairs)  17.4 us
    ppermute x7, starting transfers between devices, from_axis(): return lax.ppermute(value, ALL, pairs)  10.3 us
    ppermute x3, starting transfers between devices, from_rows(): return lax.ppermute(value, ALL, pairs)  10.2 us
    pallas_call x3, Pallas kernels, call(): pl.pallas_call(kernel, out_shape=out_shape, in_specs=[smem, smem, vmem] +...  8.92 us
    all_to_all x1, waiting for transfers between devices, body(): pieces = lax.all_to_all(partial, ROWS, 0, 0, tiled=True)  7.01 us
    unnamed x7, local copies, waits for them, and re-layouts  6.66 us
    all_to_all x1, starting transfers between devices, body(): pieces = lax.all_to_all(partial, ROWS, 0, 0, tiled=True)  6.05 us
    ppermute x3, waiting for transfers between devices, from_rows(): return lax.ppermute(value, ALL, pairs)  5.39 us
  transfers between devices with their start and end apart: 17, of which 8 were waited for; matrix products, arithmetic and copies ran while one was open for 6% of the time, Pallas kernels for 12%

profile of v3, /device:TPU:8, one launch (start us, length us, event | category | flops | bytes accessed | tf_op | source)
XLA Modules:
  0.0 90.3 jit_solution(17185337416800665696)
XLA Ops:
  0.6 1.7 %masked.1.value = bf16[256,128]{1,0:T(8,128)(2,1)} custom-call(bf16[64,512]{1,0:T(8,128)(2,1)} %bitcast.40, s32[64,512]{1,0:T(8,128)} %bitcast.36), custom_call_target="tpu_custom_call" | custom-call | tf_op jit(solution)/shard_map/masked/pallas_call | solution.py:116
  2.3 7.2 %collective-permute-start.1 = (bf16[256,128]{1,0:T(8,128)(2,1)}, bf16[256,128]{1,0:T(8,128)(2,1)S(1)}, u32[]{:S(2)}, u32[]{:S(2)}) collective-permute-start(bf16[256,128]{1,0:T(8,128)(2,1)} %masked.1.value), channel_id=1, source_target_pairs={{128,0},{129,1},{130,2},{131,3},{132,4},{133,5},{134,6},{135,7},{1... | collective-permute-start | bytes 196616 | tf_op jit(solution)/shard_map/ppermute | solution.py:26
  9.5 1.7 %collective-permute-start.2 = (bf16[256,128]{1,0:T(8,128)(2,1)}, bf16[256,128]{1,0:T(8,128)(2,1)S(1)}, u32[]{:S(2)}, u32[]{:S(2)}) collective-permute-start(bf16[256,128]{1,0:T(8,128)(2,1)} %masked.1.value), channel_id=1, source_target_pairs={{144,0},{145,1},{146,2},{147,3},{148,4},{149,5},{150,6},{151,7},{1... | collective-permute-start | bytes 196616 | tf_op jit(solution)/shard_map/ppermute | solution.py:26
  11.2 1.5 %again.1 = bf16[256,128]{1,0:T(8,128)(2,1)} custom-call(bf16[256,128]{1,0:T(8,128)(2,1)} %masked.1.value), custom_call_target="tpu_custom_call" | custom-call | tf_op jit(solution)/shard_map/again/pallas_call | solution.py:132
  12.7 1.2 %collective-permute-start = (bf16[256,128]{1,0:T(8,128)(2,1)}, bf16[256,128]{1,0:T(8,128)(2,1)S(1)}, u32[]{:S(2)}, u32[]{:S(2)}) collective-permute-start(bf16[256,128]{1,0:T(8,128)(2,1)} %again.1), channel_id=1, source_target_pairs={{16,0},{17,1},{18,2},{19,3},{20,4},{21,5},{22,6},{23,7},{24,8},{25... | collective-permute-start | bytes 196616 | tf_op jit(solution)/shard_map/ppermute | solution.py:26
  14.0 0.8 multiply_add_fusion.1
  14.8 0.1 convert_reduce_fusion.1
  14.9 4.4 %collective-permute-done = bf16[256,128]{1,0:T(8,128)(2,1)S(1)} collective-permute-done((bf16[256,128]{1,0:T(8,128)(2,1)}, bf16[256,128]{1,0:T(8,128)(2,1)S(1)}, u32[]{:S(2)}, u32[]{:S(2)}) %collective-permute-start) | collective-permute-done | bytes 65568 | tf_op jit(solution)/shard_map/ppermute | solution.py:26
  19.3 0.0 collective-permute-done.1
  19.3 1.0 %collective-permute-done.2 = bf16[256,128]{1,0:T(8,128)(2,1)S(1)} collective-permute-done((bf16[256,128]{1,0:T(8,128)(2,1)}, bf16[256,128]{1,0:T(8,128)(2,1)S(1)}, u32[]{:S(2)}, u32[]{:S(2)}) %collective-permute-start.2) | collective-permute-done | bytes 65568 | tf_op jit(solution)/shard_map/ppermute | solution.py:26
  20.3 0.9 fusion.43
  21.2 2.8 %collective-permute-start.3 = (bf16[4,256,128]{2,1,0:T(8,128)(2,1)S(1)}, bf16[4,256,128]{2,1,0:T(8,128)(2,1)S(1)}, u32[]{:S(2)}, u32[]{:S(2)}) collective-permute-start(bf16[4,256,128]{2,1,0:T(8,128)(2,1)S(1)} %get-tuple-element.27), channel_id=1, source_target_pairs={{4,0},{33,1},{6,2},{35,3},{8,4},{37,5},{10,6},{39,7},{12,8},{41,9}... | collective-permute-start | bytes 786440 | tf_op jit(solution)/shard_map/ppermute | solution.py:36
  24.0 0.0 collective-permute-start.4
  24.0 2.3 %collective-permute-start.5 = (bf16[4,256,128]{2,1,0:T(8,128)(2,1)S(1)}, bf16[4,256,128]{2,1,0:T(8,128)(2,1)S(1)}, u32[]{:S(2)}, u32[]{:S(2)}) collective-permute-start(bf16[4,256,128]{2,1,0:T(8,128)(2,1)S(1)} %get-tuple-element.27), channel_id=1, source_target_pairs={{8,0},{65,1},{10,2},{67,3},{12,4},{69,5},{14,6},{71,7},{0,8},{73,9... | collective-permute-start | bytes 786440 | tf_op jit(solution)/shard_map/ppermute | solution.py:36
  26.3 0.1 sub.125
  26.4 1.1 %copy.11 = bf16[512,256]{0,1:T(8,128)(2,1)S(1)} copy(bf16[512,256]{1,0:T(8,128)(2,1)} %param.10) | data formatting | bytes 524288 | tf_op args[4]
  27.5 0.1 reshape.299
  27.6 0.0 copy-start.2
  27.6 0.1 fusion.24
  27.7 0.1 select_reduce_fusion.2.bounds
  27.9 0.0 collective-permute-done.3
  27.9 6.5 %collective-permute-done.4 = bf16[4,256,128]{2,1,0:T(8,128)(2,1)S(1)} collective-permute-done((bf16[4,256,128]{2,1,0:T(8,128)(2,1)S(1)}, bf16[4,256,128]{2,1,0:T(8,128)(2,1)S(1)}, u32[]{:S(2)}, u32[]{:S(2)}) %collective-permute-start.4) | collective-permute-done | bytes 262176 | tf_op jit(solution)/shard_map/ppermute | solution.py:36
  34.4 0.0 collective-permute-done.5
  34.4 0.1 pad_maximum_fusion
  34.5 3.1 %collective-permute-start.6 = (bf16[4,4,256,128]{3,2,1,0:T(8,128)(2,1)S(1)}, bf16[4,4,256,128]{3,2,1,0:T(8,128)(2,1)S(1)}, u32[]{:S(2)}, u32[]{:S(2)}) collective-permute-start(bf16[4,4,256,128]{3,2,1,0:T(8,128)(2,1)S(1)} %pad_maximum_fusion), channel_id=1, source_target_pairs={{32,0},{5,1},{34,2},{7,3},{36,4},{9,5},{38,6},{11,7},{40,8},{13,9}... | collective-permute-start | bytes 3145736 | tf_op jit(solution)/shard_map/ppermute | solution.py:36
  37.7 0.0 collective-permute-start.7
  37.7 0.1 select_reduce_fusion.1
  37.8 0.2 convert_reduce_fusion
  38.0 0.1 select_reduce_fusion
  38.2 0.0 copy-start
  38.2 2.8 %copy-done = bf16[192,128,128]{2,1,0:T(8,128)(2,1)S(1)} copy-done((bf16[192,128,128]{2,1,0:T(8,128)(2,1)S(1)}, bf16[192,128,128]{2,1,0:T(8,128)(2,1)}, u32[]{:S(2)}) %copy-start) | copy-done | bytes 6291480
  41.0 1.9 %early_tiles.1.before = f32[4,128,128]{2,1,0:T(8,128)S(1)} custom-call(s32[848]{0:T(1024)S(1)} %add_select_fusion.1.table, s32[6]{0:T(128)S(1)} %select_reduce_fusion.2.bounds, bf16[192,128,128]{2,1,0:T(8,128)(2,1)S(1)} %copy-done, bf16[32,128,128]{2,1,0:T(8,128)(2,1)S(1)} %bitcast.25), custom_call_target="tpu_custom_call" | custom-call | flops 268435456 | bytes 8388608 | tf_op jit(solution)/shard_map/early_tiles/pallas_call | solution.py:167
  42.9 7.1 %collective-permute-done.6 = bf16[4,4,256,128]{3,2,1,0:T(8,128)(2,1)S(1)} collective-permute-done((bf16[4,4,256,128]{3,2,1,0:T(8,128)(2,1)S(1)}, bf16[4,4,256,128]{3,2,1,0:T(8,128)(2,1)S(1)}, u32[]{:S(2)}, u32[]{:S(2)}) %collective-permute-start.6) | collective-permute-done | bytes 1048608 | tf_op jit(solution)/shard_map/ppermute | solution.py:36
  50.0 3.7 %collective-permute-done.7 = bf16[4,4,256,128]{3,2,1,0:T(8,128)(2,1)S(1)} collective-permute-done((bf16[4,4,256,128]{3,2,1,0:T(8,128)(2,1)S(1)}, bf16[4,4,256,128]{3,2,1,0:T(8,128)(2,1)S(1)}, u32[]{:S(2)}, u32[]{:S(2)}) %collective-permute-start.7) | collective-permute-done | bytes 1048608 | tf_op jit(solution)/shard_map/ppermute | solution.py:36
  53.7 0.8 slice.42
  54.5 0.0 collective-permute-start.8
  54.5 0.9 slice.43
  55.4 2.0 %collective-permute-start.9 = (bf16[2,4,256,128]{3,2,1,0:T(8,128)(2,1)}, bf16[2,4,256,128]{3,2,1,0:T(8,128)(2,1)}, u32[]{:S(2)}, u32[]{:S(2)}) collective-permute-start(bf16[2,4,256,128]{3,2,1,0:T(8,128)(2,1)} %slice.43), channel_id=1, source_target_pairs={{224,0},{13,1},{226,2},{15,3},{228,4},{1,5},{230,6},{3,7},{232,8},... | collective-permute-start | bytes 1572872 | tf_op jit(solution)/shard_map/ppermute | solution.py:36
  57.4 0.1 constant_dynamic-slice_fusion.1
  57.5 0.1 collective-permute-start.13
  57.6 1.4 %collective-permute-start.14 = (bf16[64,64]{0,1:T(8,128)(2,1)S(1)}, bf16[64,64]{0,1:T(8,128)(2,1)S(1)}, u32[]{:S(2)}, u32[]{:S(2)}) collective-permute-start(bf16[64,64]{0,1:T(8,128)(2,1)S(1)} %get-tuple-element.38), channel_id=1, source_target_pairs={{0,2},{2,0},{1,3},{3,1},{4,6},{6,4},{5,7},{7,5},{8,10},{10,8},{9,1... | collective-permute-start | bytes 24584 | tf_op jit(solution)/shard_map/ppermute | solution.py:200
  59.0 0.4 collective-permute-start.15
  59.5 2.8 %copy-done.1 = bf16[192,128,128]{2,1,0:T(8,128)(2,1)S(1)} copy-done((bf16[192,128,128]{2,1,0:T(8,128)(2,1)S(1)}, bf16[192,128,128]{2,1,0:T(8,128)(2,1)}, u32[]{:S(2)}) %copy-start.1) | copy-done | bytes 6291480
  62.2 3.7 %near_tiles.1.before = f32[4,128,128]{2,1,0:T(8,128)S(1)} custom-call(s32[848]{0:T(1024)S(1)} %add_select_fusion.1.table, s32[6]{0:T(128)S(1)} %select_reduce_fusion.2.bounds, bf16[192,128,128]{2,1,0:T(8,128)(2,1)S(1)} %copy-done.1, bf16[32,128,128]{2,1,0:T(8,128)(2,1)S(1)} %bitcast.26, bf16[32,128,128]{2,1,0:T(8,128)(2,1)S(1)} %bitcast.27, ...), custom_call_target="tpu_custom_call" | custom-call | flops 268435456 | bytes 8388608 | tf_op jit(solution)/shard_map/near_tiles/pallas_call | solution.py:167
  66.0 0.0 collective-permute-done.8
  66.0 0.1 collective-permute-done.9
  66.1 3.3 %far_tiles.1 = (bf16[256,128]{1,0:T(8,128)(2,1)S(1)}, f32[64,2,128]{2,1,0:T(2,128)}) custom-call(s32[848]{0:T(1024)S(1)} %add_select_fusion.1.table, s32[6]{0:T(128)S(1)} %select_reduce_fusion.2.bounds, bf16[192,128,128]{2,1,0:T(8,128)(2,1)S(1)} %copy-done.1, bf16[16,128,128]{2,1,0:T(8,128)(2,1)S(1)} %bitcast.29, bf16[16,128,128]{2,1,0:T(8,128)(2,1)} %bitcast.18.source_b, ...), custom_call_target="tpu_custom_call" | custom-call | flops 268435456 | bytes 8388608 | tf_op jit(solution)/shard_map/far_tiles/pallas_call | solution.py:167
  69.4 0.6 collective-permute-start.10
  70.0 1.3 %collective-permute-start.11 = (bf16[256,128]{1,0:T(8,128)(2,1)S(1)}, bf16[256,128]{1,0:T(8,128)(2,1)S(1)}, u32[]{:S(2)}, u32[]{:S(2)}) collective-permute-start(bf16[256,128]{1,0:T(8,128)(2,1)S(1)} %get-tuple-element.17), channel_id=1, source_target_pairs={{0,2},{2,0},{1,3},{3,1},{4,6},{6,4},{5,7},{7,5},{8,10},{10,8},{9,1... | collective-permute-start | bytes 196616 | tf_op jit(solution)/shard_map/ppermute | solution.py:206
  71.4 0.1 fusion.44
  71.4 6.0 %all-to-all-start = ((f32[64,2,128]{2,1,0:T(2,128)}), f32[64,2,128]{2,1,0:T(2,128)S(1)}, u32[]{:S(2)}, u32[]{:S(2)}) async-start(f32[64,2,128]{2,1,0:T(2,128)} %get-tuple-element.19), calls=%async_computation | async-start | bytes 131072 | tf_op jit(solution)/shard_map/all_to_all | solution.py:205
  77.5 0.0 collective-permute-done.10
  77.5 1.6 %collective-permute-start.12 = (bf16[256,128]{1,0:T(8,128)(2,1)S(1)}, bf16[256,128]{1,0:T(8,128)(2,1)S(1)}, u32[]{:S(2)}, u32[]{:S(2)}) collective-permute-start(bf16[256,128]{1,0:T(8,128)(2,1)S(1)} %get-tuple-element.17), channel_id=1, source_target_pairs={{0,3},{3,0},{1,2},{2,1},{4,7},{7,4},{5,6},{6,5},{8,11},{11,8},{9,1... | collective-permute-start | bytes 196616 | tf_op jit(solution)/shard_map/ppermute | solution.py:206
  79.1 0.1 fusion.45
  79.2 0.0 collective-permute-done.11
  79.2 0.1 fusion.46
  79.3 2.1 %collective-permute-done.12 = bf16[256,128]{1,0:T(8,128)(2,1)S(1)} collective-permute-done((bf16[256,128]{1,0:T(8,128)(2,1)S(1)}, bf16[256,128]{1,0:T(8,128)(2,1)S(1)}, u32[]{:S(2)}, u32[]{:S(2)}) %collective-permute-start.12) | collective-permute-done | bytes 65568 | tf_op jit(solution)/shard_map/ppermute | solution.py:206
  81.4 0.1 fusion.47
  81.5 0.0 collective-permute-done.14
  81.5 0.0 collective-permute-done.15
  81.6 1.0 %convolution_convert_fusion = bf16[512,64]{0,1:T(8,128)(2,1)} fusion(bf16[256,64]{1,0:T(8,128)(2,1)S(1)} %get-tuple-element.35, bf16[256,64]{1,0:T(8,128)(2,1)S(1)} %get-tuple-element.34, bf16[256,64]{1,0:T(8,128)(2,1)S(1)} %get-tuple-element.33, bf16[256,64]{1,0:T(8,128)(2,1)S(1)} %get-tuple-element.32, bf16[256,64]{1,0:T(8,128)(2,1)S(1)} %get-tuple-element.31, ...), kind=kOutput, calls=%fused_computation | convolution fusion | flops 19038208 | bytes 360448 | tf_op jit(solution)/shard_map/rs,is->ri/dot_general | solution.py:207
  82.5 7.0 %all-to-all-done = f32[64,2,128]{2,1,0:T(2,128)S(1)} async-done(((f32[64,2,128]{2,1,0:T(2,128)}), f32[64,2,128]{2,1,0:T(2,128)S(1)}, u32[]{:S(2)}, u32[]{:S(2)}) %all-to-all-start) | async-done | bytes 65568 | tf_op jit(solution)/shard_map/all_to_all | solution.py:205
  89.5 0.1 reduce_sum.59
  89.6 0.7 reshape.305
  (8 shorter events, 0.1 us)
Async XLA Ops:
  2.3 17.0 %collective-permute-start.1 = (bf16[256,128]{1,0:T(8,128)(2,1)}, bf16[256,128]{1,0:T(8,128)(2,1)S(1)}, u32[]{:S(2)}, u32[]{:S(2)}) collective-permute-start(bf16[256,128]{1,0:T(8,128)(2,1)} %masked.1.value), channel_id=1, source_target_pairs={{128,0},{129,1},{130,2},{131,3},{132,4},{133,5},{134,6},{135,7},{1... | collective-permute-start | bytes 196616 | tf_op jit(solution)/shard_map/ppermute | solution.py:26
  9.5 10.8 %collective-permute-start.2 = (bf16[256,128]{1,0:T(8,128)(2,1)}, bf16[256,128]{1,0:T(8,128)(2,1)S(1)}, u32[]{:S(2)}, u32[]{:S(2)}) collective-permute-start(bf16[256,128]{1,0:T(8,128)(2,1)} %masked.1.value), channel_id=1, source_target_pairs={{144,0},{145,1},{146,2},{147,3},{148,4},{149,5},{150,6},{151,7},{1... | collective-permute-start | bytes 196616 | tf_op jit(solution)/shard_map/ppermute | solution.py:26
  12.7 6.5 %collective-permute-start = (bf16[256,128]{1,0:T(8,128)(2,1)}, bf16[256,128]{1,0:T(8,128)(2,1)S(1)}, u32[]{:S(2)}, u32[]{:S(2)}) collective-permute-start(bf16[256,128]{1,0:T(8,128)(2,1)} %again.1), channel_id=1, source_target_pairs={{16,0},{17,1},{18,2},{19,3},{20,4},{21,5},{22,6},{23,7},{24,8},{25... | collective-permute-start | bytes 196616 | tf_op jit(solution)/shard_map/ppermute | solution.py:26
  21.2 6.7 %collective-permute-start.3 = (bf16[4,256,128]{2,1,0:T(8,128)(2,1)S(1)}, bf16[4,256,128]{2,1,0:T(8,128)(2,1)S(1)}, u32[]{:S(2)}, u32[]{:S(2)}) collective-permute-start(bf16[4,256,128]{2,1,0:T(8,128)(2,1)S(1)} %get-tuple-element.27), channel_id=1, source_target_pairs={{4,0},{33,1},{6,2},{35,3},{8,4},{37,5},{10,6},{39,7},{12,8},{41,9}... | collective-permute-start | bytes 786440 | tf_op jit(solution)/shard_map/ppermute | solution.py:36
  24.0 10.4 %collective-permute-start.4 = (bf16[4,256,128]{2,1,0:T(8,128)(2,1)S(1)}, bf16[4,256,128]{2,1,0:T(8,128)(2,1)S(1)}, u32[]{:S(2)}, u32[]{:S(2)}) collective-permute-start(bf16[4,256,128]{2,1,0:T(8,128)(2,1)S(1)} %get-tuple-element.27), channel_id=1, source_target_pairs={{12,0},{225,1},{14,2},{227,3},{0,4},{229,5},{2,6},{231,7},{4,8},{2... | collective-permute-start | bytes 786440 | tf_op jit(solution)/shard_map/ppermute | solution.py:36
  24.0 10.4 %collective-permute-start.5 = (bf16[4,256,128]{2,1,0:T(8,128)(2,1)S(1)}, bf16[4,256,128]{2,1,0:T(8,128)(2,1)S(1)}, u32[]{:S(2)}, u32[]{:S(2)}) collective-permute-start(bf16[4,256,128]{2,1,0:T(8,128)(2,1)S(1)} %get-tuple-element.27), channel_id=1, source_target_pairs={{8,0},{65,1},{10,2},{67,3},{12,4},{69,5},{14,6},{71,7},{0,8},{73,9... | collective-permute-start | bytes 786440 | tf_op jit(solution)/shard_map/ppermute | solution.py:36
  27.6 29.8 %copy-start.2 = (bf16[256,64]{0,1:T(8,128)(2,1)S(1)}, bf16[256,64]{0,1:T(8,128)(2,1)}, u32[]{:S(2)}) copy-start(bf16[256,64]{0,1:T(8,128)(2,1)} %param.11) | copy-start | bytes 98308
  34.5 15.4 %collective-permute-start.6 = (bf16[4,4,256,128]{3,2,1,0:T(8,128)(2,1)S(1)}, bf16[4,4,256,128]{3,2,1,0:T(8,128)(2,1)S(1)}, u32[]{:S(2)}, u32[]{:S(2)}) collective-permute-start(bf16[4,4,256,128]{3,2,1,0:T(8,128)(2,1)S(1)} %pad_maximum_fusion), channel_id=1, source_target_pairs={{32,0},{5,1},{34,2},{7,3},{36,4},{9,5},{38,6},{11,7},{40,8},{13,9}... | collective-permute-start | bytes 3145736 | tf_op jit(solution)/shard_map/ppermute | solution.py:36
  37.7 16.0 %collective-permute-start.7 = (bf16[4,4,256,128]{3,2,1,0:T(8,128)(2,1)S(1)}, bf16[4,4,256,128]{3,2,1,0:T(8,128)(2,1)S(1)}, u32[]{:S(2)}, u32[]{:S(2)}) collective-permute-start(bf16[4,4,256,128]{3,2,1,0:T(8,128)(2,1)S(1)} %pad_maximum_fusion), channel_id=1, source_target_pairs={{224,0},{13,1},{226,2},{15,3},{228,4},{1,5},{230,6},{3,7},{232,8},... | collective-permute-start | bytes 3145736 | tf_op jit(solution)/shard_map/ppermute | solution.py:36
  38.2 2.8 %copy-start = (bf16[192,128,128]{2,1,0:T(8,128)(2,1)S(1)}, bf16[192,128,128]{2,1,0:T(8,128)(2,1)}, u32[]{:S(2)}) copy-start(bf16[192,128,128]{2,1,0:T(8,128)(2,1)} %adj.5) | copy-start | bytes 18874372
  54.5 11.5 %collective-permute-start.8 = (bf16[2,4,256,128]{3,2,1,0:T(8,128)(2,1)}, bf16[2,4,256,128]{3,2,1,0:T(8,128)(2,1)S(1)}, u32[]{:S(2)}, u32[]{:S(2)}) collective-permute-start(bf16[2,4,256,128]{3,2,1,0:T(8,128)(2,1)} %slice.42), channel_id=1, source_target_pairs={{32,0},{5,1},{34,2},{7,3},{36,4},{9,5},{38,6},{11,7},{40,8},{13,9}... | collective-permute-start | bytes 1572872 | tf_op jit(solution)/shard_map/ppermute | solution.py:36
  55.4 10.7 %collective-permute-start.9 = (bf16[2,4,256,128]{3,2,1,0:T(8,128)(2,1)}, bf16[2,4,256,128]{3,2,1,0:T(8,128)(2,1)}, u32[]{:S(2)}, u32[]{:S(2)}) collective-permute-start(bf16[2,4,256,128]{3,2,1,0:T(8,128)(2,1)} %slice.43), channel_id=1, source_target_pairs={{224,0},{13,1},{226,2},{15,3},{228,4},{1,5},{230,6},{3,7},{232,8},... | collective-permute-start | bytes 1572872 | tf_op jit(solution)/shard_map/ppermute | solution.py:36
  57.5 24.0 %collective-permute-start.13 = (bf16[64,64]{0,1:T(8,128)(2,1)S(1)}, bf16[64,64]{0,1:T(8,128)(2,1)S(1)}, u32[]{:S(2)}, u32[]{:S(2)}) collective-permute-start(bf16[64,64]{0,1:T(8,128)(2,1)S(1)} %get-tuple-element.39), channel_id=1, source_target_pairs={{0,1},{1,0},{2,3},{3,2},{4,5},{5,4},{6,7},{7,6},{8,9},{9,8},{10,11... | collective-permute-start | bytes 24584 | tf_op jit(solution)/shard_map/ppermute | solution.py:200
  57.6 23.9 %collective-permute-start.14 = (bf16[64,64]{0,1:T(8,128)(2,1)S(1)}, bf16[64,64]{0,1:T(8,128)(2,1)S(1)}, u32[]{:S(2)}, u32[]{:S(2)}) collective-permute-start(bf16[64,64]{0,1:T(8,128)(2,1)S(1)} %get-tuple-element.38), channel_id=1, source_target_pairs={{0,2},{2,0},{1,3},{3,1},{4,6},{6,4},{5,7},{7,5},{8,10},{10,8},{9,1... | collective-permute-start | bytes 24584 | tf_op jit(solution)/shard_map/ppermute | solution.py:200
  59.0 22.5 %collective-permute-start.15 = (bf16[64,64]{0,1:T(8,128)(2,1)S(1)}, bf16[64,64]{0,1:T(8,128)(2,1)S(1)}, u32[]{:S(2)}, u32[]{:S(2)}) collective-permute-start(bf16[64,64]{0,1:T(8,128)(2,1)S(1)} %get-tuple-element.37), channel_id=1, source_target_pairs={{0,3},{3,0},{1,2},{2,1},{4,7},{7,4},{5,6},{6,5},{8,11},{11,8},{9,1... | collective-permute-start | bytes 24584 | tf_op jit(solution)/shard_map/ppermute | solution.py:200
  59.5 2.8 %copy-start.1 = (bf16[192,128,128]{2,1,0:T(8,128)(2,1)S(1)}, bf16[192,128,128]{2,1,0:T(8,128)(2,1)}, u32[]{:S(2)}) copy-start(bf16[192,128,128]{2,1,0:T(8,128)(2,1)} %adj.5) | copy-start | bytes 18874372
  69.4 8.1 %collective-permute-start.10 = (bf16[256,128]{1,0:T(8,128)(2,1)S(1)}, bf16[256,128]{1,0:T(8,128)(2,1)S(1)}, u32[]{:S(2)}, u32[]{:S(2)}) collective-permute-start(bf16[256,128]{1,0:T(8,128)(2,1)S(1)} %get-tuple-element.17), channel_id=1, source_target_pairs={{0,1},{1,0},{2,3},{3,2},{4,5},{5,4},{6,7},{7,6},{8,9},{9,8},{10,11... | collective-permute-start | bytes 196616 | tf_op jit(solution)/shard_map/ppermute | solution.py:206
  70.0 9.2 %collective-permute-start.11 = (bf16[256,128]{1,0:T(8,128)(2,1)S(1)}, bf16[256,128]{1,0:T(8,128)(2,1)S(1)}, u32[]{:S(2)}, u32[]{:S(2)}) collective-permute-start(bf16[256,128]{1,0:T(8,128)(2,1)S(1)} %get-tuple-element.17), channel_id=1, source_target_pairs={{0,2},{2,0},{1,3},{3,1},{4,6},{6,4},{5,7},{7,5},{8,10},{10,8},{9,1... | collective-permute-start | bytes 196616 | tf_op jit(solution)/shard_map/ppermute | solution.py:206
  71.4 18.1 %all-to-all-start = ((f32[64,2,128]{2,1,0:T(2,128)}), f32[64,2,128]{2,1,0:T(2,128)S(1)}, u32[]{:S(2)}, u32[]{:S(2)}) async-start(f32[64,2,128]{2,1,0:T(2,128)} %get-tuple-element.19), calls=%async_computation | async-start | bytes 131072 | tf_op jit(solution)/shard_map/all_to_all | solution.py:205
  77.5 3.9 %collective-permute-start.12 = (bf16[256,128]{1,0:T(8,128)(2,1)S(1)}, bf16[256,128]{1,0:T(8,128)(2,1)S(1)}, u32[]{:S(2)}, u32[]{:S(2)}) collective-permute-start(bf16[256,128]{1,0:T(8,128)(2,1)S(1)} %get-tuple-element.17), channel_id=1, source_target_pairs={{0,3},{3,0},{1,2},{2,1},{4,7},{7,4},{5,6},{6,5},{8,11},{11,8},{9,1... | collective-permute-start | bytes 196616 | tf_op jit(solution)/shard_map/ppermute | solution.py:206

commit v4 on v3

--- a/solution.py
+++ b/solution.py
@@ -36,16 +36,39 @@
     return lax.ppermute(value, ALL, pairs)
 
 
-def gather_near(packed):
+def exchange(value, second_pairs):
+    pairs = []
+    for z, y, x, l, c in places():
+        at = z if c == 0 else x
+        step = 1 if (at % 2 == 0) != second_pairs else -1
+        source = device(z + step, y, x, l, c) if c == 0 else device(z, y, x + step, l, c)
+        pairs.append((source, device(z, y, x, l, c)))
+    return lax.ppermute(value, ALL, pairs)
+
+
+def odd_place():
+    return jnp.where(lax.axis_index("core") == 0, lax.axis_index("z"), lax.axis_index("x")) % 2 == 1
+
+
+def gather_early(packed, later):
     far_y, far = from_rows(packed, dz=4, dy=1), from_rows(packed, dz=4)
-    four = jnp.stack([packed, from_rows(again(packed), dy=1), far, far_y])
-    early = jnp.stack([four, from_axis(four, False, 1), from_axis(four, False, -1), from_axis(four, False, 2)])
-    plus, minus = from_axis(early, True, 1), from_axis(early, True, -1)
-    return early, plus, minus
+    again, later = lax.optimization_barrier((packed, later))
+    four = jnp.stack([packed, from_rows(again, dy=1), far, far_y])
+    low = jnp.stack([four, from_axis(four, False, 1)])
+    high = jnp.stack([from_axis(four, False, -1), from_axis(four, False, 2)])
+    return low, high, later
+
+
+def gather_near(low, high):
+    odd = odd_place()
+    forwarded = [from_axis(low, True, 1), from_axis(high, True, -1)]
+    low, high = lax.optimization_barrier((low, high))
+    others = [exchange(jnp.where(odd, high, low), False), exchange(jnp.where(odd, low, high), True)]
+    return forwarded, others
 
 
 def gather_far(plus, minus):
-    return [from_axis(plus[:2], True, 1), from_axis(minus[2:], True, -1)]
+    return [from_axis(plus, True, 1), from_axis(minus, True, -1)]
 
 
 def where_held(column):
@@ -60,8 +83,11 @@
     upper = (dz >= 3) & (dz <= 6)
     swapped = jnp.where(core == 0, (late == 2) & (a >= 2), (ring == 2) & (lax.axis_index("z") % 2 == 1))
     e = dy + 2 * (upper != swapped).astype(jnp.int32)
-    source = jnp.where(late == 0, 0, jnp.where(late == 1, 1, jnp.where(late == 3, 2, 3 + a // 2)))
-    place = (jnp.where(late == 2, a % 2, a) * 4 + e) * 2 + block % 2
+    high, odd = a // 2, odd_place().astype(jnp.int32)
+    after = jnp.where(high == 0, 2, 4 + odd)
+    before = jnp.where(high == 1, 3, 5 - odd)
+    source = jnp.where(late == 0, high, jnp.where(late == 1, after, jnp.where(late == 3, before, 6 + high)))
+    place = (a % 2 * 4 + e) * 2 + block % 2
     return source, place, block // 2
 
 
@@ -122,45 +148,45 @@
     )(grad_out.T, relu_mask.T)
 
 
-def again_kernel(value, out):
-    out[...] = value[...]
-
-
-def again(value):
-    vmem = pl.BlockSpec(memory_space=pltpu.VMEM)
-    shape = jax.ShapeDtypeStruct(value.shape, value.dtype)
-    return pl.pallas_call(again_kernel, out_shape=shape, in_specs=[vmem], out_specs=vmem, name="again")(value)
-
-
-def first_kernel(table, bounds, adj, source, acc, masks):
+def add_sources(table, bounds, adj, sources, first, acc, masks):
+    for k, source in enumerate(sources):
+        add_tiles(table, bounds[first + k], bounds[first + k + 1], adj, source, acc, masks)
+
+
+def first_kernel(table, bounds, adj, *refs):
+    *sources, acc, kept, masks = refs
     set_masks(masks)
     acc[...] = jnp.zeros_like(acc)
-    add_tiles(table, bounds[0], bounds[1], adj, source, acc, masks)
-
-
-def middle_kernel(table, bounds, adj, source_a, source_b, before, acc, masks):
+    add_sources(table, bounds, adj, sources, 0, acc, masks)
+
+
+def middle_kernel(table, bounds, adj, *refs):
+    *sources, before, acc, masks = refs
     set_masks(masks)
     acc[...] = before[...]
-    add_tiles(table, bounds[1], bounds[2], adj, source_a, acc, masks)
-    add_tiles(table, bounds[2], bounds[3], adj, source_b, acc, masks)
-
-
-def last_kernel(table, bounds, adj, source_a, source_b, before, features, out, partial, acc, masks):
+    add_sources(table, bounds, adj, sources, 2, acc, masks)
+
+
+def last_kernel(table, bounds, adj, *refs):
+    *sources, before, features, weights, out, out_a, out_b, out_c, partial, acc, masks = refs
     lane = set_masks(masks)
     acc[...] = before[...]
-    add_tiles(table, bounds[3], bounds[4], adj, source_a, acc, masks)
-    add_tiles(table, bounds[4], bounds[5], adj, source_b, acc, masks)
+    add_sources(table, bounds, adj, sources, 6, acc, masks)
     agg = [acc[r] + pltpu.roll(acc[r], 64, 1) for r in range(4)]
-    for r in range(2):
-        out[pl.ds(r * 128, 128), :] = jnp.where(lane < 64, agg[r], agg[r + 2]).astype(out.dtype)
     rounded = jnp.concatenate([v.astype(jnp.bfloat16) for v in agg], axis=0)
     product = jnp.dot(features[...], rounded, preferred_element_type=jnp.float32)
     low = lax.broadcasted_iota(jnp.int32, (64, 128), 1) < 64
     for p in range(2):
         partial[:, p, :] = jnp.where(low, product[p * 128 : p * 128 + 64], product[p * 128 + 64 : p * 128 + 128])
-
-
-def call(kernel, table, bounds, adj, sources, others, out_shape, keep_acc, name):
+    for r in range(2):
+        packed = jnp.where(lane < 64, agg[r], agg[r + 2]).astype(out.dtype)
+        for ref in (out, out_a, out_b, out_c):
+            ref[pl.ds(r * 128, 128), :] = packed
+    for k, ref in enumerate((out_a, out_b, out_c)):
+        ref[pl.ds(256, 64), :] = weights[k]
+
+
+def call(kernel, table, bounds, adj, sources, others, out_shape, keep_acc, name, aliases={}):
     smem = pl.BlockSpec(memory_space=pltpu.SMEM)
     vmem = pl.BlockSpec(memory_space=pltpu.VMEM)
     sources = [s.reshape(-1, 128, 128) for s in sources]
@@ -172,8 +198,9 @@
         scratch_shapes=([pltpu.VMEM((4, 128, 128), jnp.float32)] if keep_acc else []) + [
             pltpu.VMEM((3, 128, 128), jnp.bfloat16),
         ],
-        compiler_params=pltpu.CompilerParams(vmem_limit_bytes=24 * 1024 * 1024),
+        compiler_params=pltpu.CompilerParams(vmem_limit_bytes=8 * 1024 * 1024),
         cost_estimate=pl.CostEstimate(flops=2 * 64 * 128 * 128 * 128, bytes_accessed=8 * 1024 * 1024, transcendentals=0),
+        input_output_aliases=aliases,
         name=name,
     )(table, bounds, adj, *sources, *others)
 
@@ -185,28 +212,30 @@
 def body(adj_tiles, tile_index, grad_out, relu_mask, features, weight):
     position = lax.axis_index(ROWS)
     slab = lax.axis_index(SLAB)
-    early, plus, minus = gather_near(masked(grad_out, relu_mask))
-
     source, place, half = where_held(tile_index[:, 1])
-    tables = tile_table(tile_index[:, 0] - position * 4, source, place, half, 5)
+    low, high, source = gather_early(masked(grad_out, relu_mask), source)
+    forwarded, others = gather_near(low, high)
+
+    tables = tile_table(tile_index[:, 0] - position * 4, source, place, half, 8)
     f_rows = features.reshape(512, 64, 4).transpose(2, 1, 0).reshape(256, 512)
+    w_parts = [lax.dynamic_slice_in_dim(weight, (slab ^ k) * 64, 64, 0) for k in range(4)]
+    w_sent = jnp.pad(jnp.stack(w_parts[1:]), ((0, 0), (0, 0), (0, 64)))
 
     sums = jax.ShapeDtypeStruct((4, 128, 128), jnp.float32)
-    acc = call(first_kernel, *tables, adj_tiles, [early], [], sums, False, "early_tiles")
-    weight, acc, plus, minus, f_rows, tables = lax.optimization_barrier((weight, acc, plus, minus, f_rows, tables))
-    far = gather_far(plus, minus)
-    w_parts = [lax.dynamic_slice_in_dim(weight, slab * 64, 64, 0)]
-    for k, pairs in enumerate(FLIPS):
-        w_parts.append(lax.ppermute(lax.dynamic_slice_in_dim(weight, (slab ^ (k + 1)) * 64, 64, 0), SLAB, pairs))
-    acc = call(middle_kernel, *tables, adj_tiles, [plus, minus], [acc], sums, False, "near_tiles")
-    outs = (jax.ShapeDtypeStruct((256, 128), jnp.bfloat16), jax.ShapeDtypeStruct((64, 2, 128), jnp.float32))
-    agg, partial = call(last_kernel, *tables, adj_tiles, far, [acc, f_rows], outs, True, "far_tiles")
+    kept = jax.ShapeDtypeStruct(adj_tiles.shape, adj_tiles.dtype)
+    acc, adj = call(first_kernel, *tables, adj_tiles, [low, high], [], (sums, kept), False, "early_tiles", {2: 1})
+    forwarded, acc, f_rows, w_sent = lax.optimization_barrier((forwarded, acc, f_rows, w_sent))
+    far = gather_far(*forwarded)
+    acc = call(middle_kernel, *tables, adj, forwarded + others, [acc], sums, False, "near_tiles")
+    message = jax.ShapeDtypeStruct((320, 128), jnp.bfloat16)
+    outs = (jax.ShapeDtypeStruct((256, 128), jnp.bfloat16), message, message, message, jax.ShapeDtypeStruct((64, 2, 128), jnp.float32))
+    agg, *messages, partial = call(last_kernel, *tables, adj, far, [acc, f_rows, w_sent], outs, True, "far_tiles")
 
     pieces = lax.all_to_all(partial, ROWS, 0, 0, tiled=True)
-    a_parts = [halves(agg)] + [halves(lax.ppermute(agg, SLAB, pairs)) for pairs in FLIPS]
-    grad_input = jnp.einsum(
-        "rs,is->ri", jnp.concatenate(a_parts, axis=1), jnp.concatenate(w_parts, axis=1), preferred_element_type=jnp.float32
-    ).astype(jnp.bfloat16)
+    arrived = [lax.ppermute(m, SLAB, pairs) for m, pairs in zip(messages, FLIPS)]
+    a_all = jnp.concatenate([halves(agg)] + [halves(m[:256]) for m in arrived], axis=1)
+    w_all = jnp.concatenate([w_parts[0]] + [m[256:, :64] for m in arrived], axis=1)
+    grad_input = jnp.einsum("rs,is->ri", a_all, w_all, preferred_element_type=jnp.float32).astype(jnp.bfloat16)
     grad_weight = jnp.sum(pieces, axis=0).reshape(4, 64)
     return grad_input, grad_weight
 

time: 91.9 us -> 94.5 us (1.028)
  local copies, waits for them, and re-layouts: 9.65 us -> 19.8 us
  waiting for transfers between devices: 32 us -> 24.4 us
  starting transfers between devices: 32 us -> 33.6 us
  Pallas kernels: 12.1 us -> 10.9 us
    unnamed x7 -> x19, local copies, waits for them, and re-layouts: 6.66 us -> 18.2 us
    ppermute x7, waiting for transfers between devices: 17.4 us -> 6.73 us  [from_axis(): return lax.ppermute(value, ALL, pairs)]
    all_to_all x1, waiting for transfers between devices: 7.01 us -> 10.8 us  [body(): pieces = lax.all_to_all(partial, ROWS, 0, 0, tiled=True)]
    ppermute x6 -> x5, waiting for transfers between devices: 2.13 us -> 0.01 us  [the longest x3 0.01 us: body(): lax.ppermute(m, SLAB, pairs)]
    all_to_all x1, starting transfers between devices: 6.05 us -> 7.96 us  [body(): pieces = lax.all_to_all(partial, ROWS, 0, 0, tiled=True)]
    slice x2 -> x3, local copies, waits for them, and re-layouts: 1.69 us -> 0.01 us  [body(): m[256:, :64]]
    pallas_call x1 -> x0, Pallas kernels: 1.5 us -> none  [again(): pl.pallas_call(again_kernel, out_shape=shape, in_specs=[vmem], out_specs=...]
    ppermute x3, waiting for transfers between devices: 5.39 us -> 6.88 us  [from_rows(): return lax.ppermute(value, ALL, pairs)]
  transfers between devices with their start and end apart: 17 -> 16, of which waited for: 8 -> 6; matrix products, arithmetic and copies ran while one was open for 6% -> 4% of each run, Pallas kernels for 12% -> 7%
where the time goes in v4:
time: 94.5 us; the launch traced here: 93.6 us
  starting transfers between devices  33.6 us (36%)
  waiting for transfers between devices  24.4 us (26%)
  local copies, waits for them, and re-layouts  19.8 us (21%)
  Pallas kernels  10.9 us (12%)
  other arithmetic  3.01 us (3%)
  matrix products  0.96 us (1%)
    unnamed x19, local copies, waits for them, and re-layouts  18.2 us
    ppermute x7, starting transfers between devices, from_axis(): return lax.ppermute(value, ALL, pairs)  11.2 us
    all_to_all x1, waiting for transfers between devices, body(): pieces = lax.all_to_all(partial, ROWS, 0, 0, tiled=True)  10.8 us
    ppermute x3, starting transfers between devices, from_rows(): return lax.ppermute(value, ALL, pairs)  10.2 us
    pallas_call x3, Pallas kernels, call(): pl.pallas_call(kernel, out_shape=out_shape, in_specs=[smem, smem, vmem] +...  9.22 us
    all_to_all x1, starting transfers between devices, body(): pieces = lax.all_to_all(partial, ROWS, 0, 0, tiled=True)  7.96 us
    ppermute x3, waiting for transfers between devices, from_rows(): return lax.ppermute(value, ALL, pairs)  6.88 us
    ppermute x7, waiting for transfers between devices, from_axis(): return lax.ppermute(value, ALL, pairs)  6.73 us
  transfers between devices with their start and end apart: 16, of which 6 were waited for; matrix products, arithmetic and copies ran while one was open for 4% of the time, Pallas kernels for 7%

profile of v4, /device:TPU:8, one launch (start us, length us, event | category | flops | bytes accessed | tf_op | source)
XLA Modules:
  0.0 93.6 jit_solution(2632508933048935438)
XLA Ops:
  0.7 8.1 %copy.29.adj = bf16[192,128,128]{2,1,0:T(8,128)(2,1)} copy(bf16[192,128,128]{2,1,0:T(8,128)(2,1)} %param.6) | data formatting | bytes 12582912
  8.8 1.7 %masked.1 = bf16[256,128]{1,0:T(8,128)(2,1)} custom-call(bf16[64,512]{1,0:T(8,128)(2,1)} %bitcast.51, s32[64,512]{1,0:T(8,128)} %bitcast.44), custom_call_target="tpu_custom_call" | custom-call | tf_op jit(solution)/shard_map/masked/pallas_call | solution.py:142
  10.5 7.2 %collective-permute-start.1 = (bf16[256,128]{1,0:T(8,128)(2,1)}, bf16[256,128]{1,0:T(8,128)(2,1)S(1)}, u32[]{:S(2)}, u32[]{:S(2)}) collective-permute-start(bf16[256,128]{1,0:T(8,128)(2,1)} %masked.1), channel_id=1, source_target_pairs={{128,0},{129,1},{130,2},{131,3},{132,4},{133,5},{134,6},{135,7},{1... | collective-permute-start | bytes 196616 | tf_op jit(solution)/shard_map/ppermute | solution.py:26
  17.7 1.7 %collective-permute-start.2 = (bf16[256,128]{1,0:T(8,128)(2,1)}, bf16[256,128]{1,0:T(8,128)(2,1)S(1)}, u32[]{:S(2)}, u32[]{:S(2)}) collective-permute-start(bf16[256,128]{1,0:T(8,128)(2,1)} %masked.1), channel_id=1, source_target_pairs={{144,0},{145,1},{146,2},{147,3},{148,4},{149,5},{150,6},{151,7},{1... | collective-permute-start | bytes 196616 | tf_op jit(solution)/shard_map/ppermute | solution.py:26
  19.4 1.3 %collective-permute-start = (bf16[256,128]{1,0:T(8,128)(2,1)}, bf16[256,128]{1,0:T(8,128)(2,1)S(1)}, u32[]{:S(2)}, u32[]{:S(2)}) collective-permute-start(bf16[256,128]{1,0:T(8,128)(2,1)} %masked.1), channel_id=1, source_target_pairs={{16,0},{17,1},{18,2},{19,3},{20,4},{21,5},{22,6},{23,7},{24,8},{25... | collective-permute-start | bytes 196616 | tf_op jit(solution)/shard_map/ppermute | solution.py:26
  20.8 0.1 convert_reduce_fusion.1
  20.9 0.2 convert_reduce_fusion
  21.1 0.1 sub.105
  21.2 0.1 fusion.29
  21.3 0.1 select_reduce_fusion.2.bounds
  21.4 0.1 select_reduce_fusion.1
  21.6 3.9 %collective-permute-done = bf16[256,128]{1,0:T(8,128)(2,1)S(1)} collective-permute-done((bf16[256,128]{1,0:T(8,128)(2,1)}, bf16[256,128]{1,0:T(8,128)(2,1)S(1)}, u32[]{:S(2)}, u32[]{:S(2)}) %collective-permute-start) | collective-permute-done | bytes 65568 | tf_op jit(solution)/shard_map/ppermute | solution.py:26
  25.5 0.0 collective-permute-done.1
  25.5 2.9 %collective-permute-done.2 = bf16[256,128]{1,0:T(8,128)(2,1)S(1)} collective-permute-done((bf16[256,128]{1,0:T(8,128)(2,1)}, bf16[256,128]{1,0:T(8,128)(2,1)S(1)}, u32[]{:S(2)}, u32[]{:S(2)}) %collective-permute-start.2) | collective-permute-done | bytes 65568 | tf_op jit(solution)/shard_map/ppermute | solution.py:26
  28.4 0.9 fusion.43
  29.3 1.6 %collective-permute-start.4 = (bf16[4,256,128]{2,1,0:T(8,128)(2,1)S(1)}, bf16[4,256,128]{2,1,0:T(8,128)(2,1)S(1)}, u32[]{:S(2)}, u32[]{:S(2)}) collective-permute-start(bf16[4,256,128]{2,1,0:T(8,128)(2,1)S(1)} %get-tuple-element.40), channel_id=1, source_target_pairs={{12,0},{225,1},{14,2},{227,3},{0,4},{229,5},{2,6},{231,7},{4,8},{2... | collective-permute-start | bytes 786440 | tf_op jit(solution)/shard_map/ppermute | solution.py:36
  30.9 2.7 %collective-permute-start.5 = (bf16[4,256,128]{2,1,0:T(8,128)(2,1)S(1)}, bf16[4,256,128]{2,1,0:T(8,128)(2,1)S(1)}, u32[]{:S(2)}, u32[]{:S(2)}) collective-permute-start(bf16[4,256,128]{2,1,0:T(8,128)(2,1)S(1)} %get-tuple-element.40), channel_id=1, source_target_pairs={{8,0},{65,1},{10,2},{67,3},{12,4},{69,5},{14,6},{71,7},{0,8},{73,9... | collective-permute-start | bytes 786440 | tf_op jit(solution)/shard_map/ppermute | solution.py:36
  33.6 0.1 constant_dynamic-slice_fusion.2
  33.7 0.1 copy.22
  33.8 0.1 copy.23
  33.9 0.1 copy.24
  34.0 1.5 %collective-permute-start.3 = (bf16[4,256,128]{2,1,0:T(8,128)(2,1)S(1)}, bf16[4,256,128]{2,1,0:T(8,128)(2,1)S(1)}, u32[]{:S(2)}, u32[]{:S(2)}) collective-permute-start(bf16[4,256,128]{2,1,0:T(8,128)(2,1)S(1)} %get-tuple-element.40), channel_id=1, source_target_pairs={{4,0},{33,1},{6,2},{35,3},{8,4},{37,5},{10,6},{39,7},{12,8},{41,9}... | collective-permute-start | bytes 786440 | tf_op jit(solution)/shard_map/ppermute | solution.py:36
  35.6 0.1 copy.20
  35.7 0.1 reshape.275
  35.9 0.1 select_reduce_fusion
  36.0 1.0 %collective-permute-done.4 = bf16[4,256,128]{2,1,0:T(8,128)(2,1)S(1)} collective-permute-done((bf16[4,256,128]{2,1,0:T(8,128)(2,1)S(1)}, bf16[4,256,128]{2,1,0:T(8,128)(2,1)S(1)}, u32[]{:S(2)}, u32[]{:S(2)}) %collective-permute-start.4) | collective-permute-done | bytes 262176 | tf_op jit(solution)/shard_map/ppermute | solution.py:36
  37.0 4.3 %collective-permute-done.5 = bf16[4,256,128]{2,1,0:T(8,128)(2,1)S(1)} collective-permute-done((bf16[4,256,128]{2,1,0:T(8,128)(2,1)S(1)}, bf16[4,256,128]{2,1,0:T(8,128)(2,1)S(1)}, u32[]{:S(2)}, u32[]{:S(2)}) %collective-permute-start.5) | collective-permute-done | bytes 262176 | tf_op jit(solution)/shard_map/ppermute | solution.py:36
  41.3 0.1 pad_maximum_fusion.1
  41.4 0.8 collective-permute-start.7
  42.1 0.0 collective-permute-done.3
  42.1 0.1 pad_maximum_fusion
  42.2 2.6 %collective-permute-start.6 = (bf16[2,4,256,128]{3,2,1,0:T(8,128)(2,1)S(1)}, bf16[2,4,256,128]{3,2,1,0:T(8,128)(2,1)S(1)}, u32[]{:S(2)}, u32[]{:S(2)}) collective-permute-start(bf16[2,4,256,128]{3,2,1,0:T(8,128)(2,1)S(1)} %pad_maximum_fusion), channel_id=1, source_target_pairs={{32,0},{5,1},{34,2},{7,3},{36,4},{9,5},{38,6},{11,7},{40,8},{13,9}... | collective-permute-start | bytes 1572872 | tf_op jit(solution)/shard_map/ppermute | solution.py:36
  44.8 1.1 %broadcast_select_fusion = (bf16[2,4,256,128]{3,2,1,0:T(8,128)(2,1)}, bf16[2,4,256,128]{3,2,1,0:T(8,128)(2,1)}) fusion(bf16[2,4,256,128]{3,2,1,0:T(8,128)(2,1)S(1)} %pad_maximum_fusion, bf16[2,4,256,128]{3,2,1,0:T(8,128)(2,1)S(1)} %pad_maximum_fusion.1, pred[]{:T(512)S(6)} %eq.123), kind=kLoop, calls=%fused_computation.5 | loop fusion | flops 524288 | bytes 2097153 | tf_op jit(solution)/shard_map/jit(_where)/select_n | solution.py:66
  45.9 0.0 collective-permute-start.10
  45.9 1.9 %collective-permute-start.11 = (bf16[2,4,256,128]{3,2,1,0:T(8,128)(2,1)}, bf16[2,4,256,128]{3,2,1,0:T(8,128)(2,1)S(1)}, u32[]{:S(2)}, u32[]{:S(2)}) collective-permute-start(bf16[2,4,256,128]{3,2,1,0:T(8,128)(2,1)} %get-tuple-element.37), channel_id=1, source_target_pairs={{224,0},{13,1},{226,2},{15,3},{228,4},{9,5},{230,6},{11,7},{232,8}... | collective-permute-start | bytes 1572872 | tf_op jit(solution)/shard_map/ppermute | solution.py:46
  47.8 2.8 %copy-done = bf16[192,128,128]{2,1,0:T(8,128)(2,1)S(1)} copy-done((bf16[192,128,128]{2,1,0:T(8,128)(2,1)S(1)}, bf16[192,128,128]{2,1,0:T(8,128)(2,1)}, u32[]{:S(2)}) %copy-start) | copy-done | bytes 6291480
  50.6 1.9 %early_tiles.1 = (f32[4,128,128]{2,1,0:T(8,128)S(1)}, bf16[192,128,128]{2,1,0:T(8,128)(2,1)S(1)}) custom-call(s32[896]{0:T(1024)S(1)} %add_select_fusion.1.table, s32[9]{0:T(128)S(1)} %select_reduce_fusion.2.bounds, bf16[192,128,128]{2,1,0:T(8,128)(2,1)S(1)} %copy-done, bf16[16,128,128]{2,1,0:T(8,128)(2,1)S(1)} %bitcast.30, ...), custom_call_target="tpu_custom_call", output_to_operand_aliasing={{1}: (2, {})} | custom-call | flops 268435456 | bytes 8388608 | tf_op jit(solution)/shard_map/early_tiles/pallas_call | solution.py:193
  52.5 2.6 %copy-done.1 = bf16[192,128,128]{2,1,0:T(8,128)(2,1)} copy-done((bf16[192,128,128]{2,1,0:T(8,128)(2,1)}, bf16[192,128,128]{2,1,0:T(8,128)(2,1)S(1)}, u32[]{:S(2)}) %copy-start.1) | copy-done | bytes 6291480
  55.2 0.7 copy-done.3
  55.9 0.0 collective-permute-done.7
  55.9 0.0 collective-permute-done.6
  55.9 1.4 %collective-permute-start.8 = (bf16[2,4,256,128]{3,2,1,0:T(8,128)(2,1)S(1)}, bf16[2,4,256,128]{3,2,1,0:T(8,128)(2,1)S(1)}, u32[]{:S(2)}, u32[]{:S(2)}) collective-permute-start(bf16[2,4,256,128]{3,2,1,0:T(8,128)(2,1)S(1)} %collective-permute-done.6), channel_id=1, source_target_pairs={{32,0},{5,1},{34,2},{7,3},{36,4},{9,5},{38,6},{11,7},{40,8},{13,9}... | collective-permute-start | bytes 1572872 | tf_op jit(solution)/shard_map/ppermute | solution.py:36
  57.2 0.7 collective-permute-start.9
  57.9 0.1 copy.26
  58.0 0.0 collective-permute-done.10
  58.0 0.0 collective-permute-done.11
  58.0 2.8 %copy-done.2 = bf16[192,128,128]{2,1,0:T(8,128)(2,1)S(1)} copy-done((bf16[192,128,128]{2,1,0:T(8,128)(2,1)S(1)}, bf16[192,128,128]{2,1,0:T(8,128)(2,1)}, u32[]{:S(2)}) %copy-start.2) | copy-done | bytes 6291480
  60.8 0.9 %copy-done.4 = f32[4,128,128]{2,1,0:T(8,128)S(1)} copy-done((f32[4,128,128]{2,1,0:T(8,128)S(1)}, f32[4,128,128]{2,1,0:T(8,128)}, u32[]{:S(2)}) %copy-start.4) | copy-done | bytes 262168
  61.7 4.5 %near_tiles.1.refs_2_ = f32[4,128,128]{2,1,0:T(8,128)S(1)} custom-call(s32[896]{0:T(1024)S(1)} %add_select_fusion.1.table, s32[9]{0:T(128)S(1)} %select_reduce_fusion.2.bounds, bf16[192,128,128]{2,1,0:T(8,128)(2,1)S(1)} %copy-done.2, bf16[16,128,128]{2,1,0:T(8,128)(2,1)S(1)} %bitcast.33, bf16[16,128,128]{2,1,0:T(8,128)(2,1)S(1)} %bitcast.32, ...), custom_call_target="tpu_custom_call" | custom-call | flops 268435456 | bytes 8388608 | tf_op jit(solution)/shard_map/near_tiles/pallas_call | solution.py:193
  66.2 1.4 %collective-permute-done.9 = bf16[2,4,256,128]{3,2,1,0:T(8,128)(2,1)S(1)} collective-permute-done((bf16[2,4,256,128]{3,2,1,0:T(8,128)(2,1)S(1)}, bf16[2,4,256,128]{3,2,1,0:T(8,128)(2,1)S(1)}, u32[]{:S(2)}, u32[]{:S(2)}) %collective-permute-start.9) | collective-permute-done | bytes 524320 | tf_op jit(solution)/shard_map/ppermute | solution.py:36
  67.6 2.8 %far_tiles.1 = (bf16[256,128]{1,0:T(8,128)(2,1)S(1)}, bf16[320,128]{1,0:T(8,128)(2,1)S(1)}, bf16[320,128]{1,0:T(8,128)(2,1)S(1)}, bf16[320,128]{1,0:T(8,128)(2,1)S(1)}, f32[64,2,128]{2,1,0:T(2,128)}) custom-call(s32[896]{0:T(1024)S(1)} %add_select_fusion.1.table, s32[9]{0:T(128)S(1)} %select_reduce_fusion.2.bounds, bf16[192,128,128]{2,1,0:T(8,128)(2,1)S(1)} %copy-done.2, ...), custom_call_target="tpu_custom_call" | custom-call | flops 268435456 | bytes 8388608 | tf_op jit(solution)/shard_map/far_tiles/pallas_call | solution.py:193
  70.4 2.1 %collective-permute-start.13 = (bf16[320,128]{1,0:T(8,128)(2,1)S(1)}, bf16[320,128]{1,0:T(8,128)(2,1)S(1)}, u32[]{:S(2)}, u32[]{:S(2)}) collective-permute-start(bf16[320,128]{1,0:T(8,128)(2,1)S(1)} %get-tuple-element.31), channel_id=1, source_target_pairs={{0,2},{2,0},{1,3},{3,1},{4,6},{6,4},{5,7},{7,5},{8,10},{10,8},{9,1... | collective-permute-start | bytes 245768 | tf_op jit(solution)/shard_map/ppermute | solution.py:235
  72.6 0.1 collective-permute-start.14
  72.7 0.1 fusion.47
  72.8 8.0 %all-to-all-start = ((f32[64,2,128]{2,1,0:T(2,128)}), f32[64,2,128]{2,1,0:T(2,128)S(1)}, u32[]{:S(2)}, u32[]{:S(2)}) async-start(f32[64,2,128]{2,1,0:T(2,128)} %get-tuple-element.33), calls=%async_computation | async-start | bytes 131072 | tf_op jit(solution)/shard_map/all_to_all | solution.py:234
  80.8 0.1 fusion.44
  80.9 0.0 collective-permute-done.13
  80.9 0.1 fusion.45
  81.0 0.0 collective-permute-done.14
  81.0 0.1 fusion.46
  81.1 1.0 %convolution_convert_fusion = bf16[512,64]{0,1:T(8,128)(2,1)} fusion(bf16[256,64]{1,0:T(8,128)(2,1)S(1)} %get-tuple-element.46, bf16[256,64]{1,0:T(8,128)(2,1)S(1)} %get-tuple-element.45, bf16[256,64]{1,0:T(8,128)(2,1)S(1)} %get-tuple-element.44, bf16[256,64]{1,0:T(8,128)(2,1)S(1)} %get-tuple-element.43, bf16[256,64]{1,0:T(8,128)(2,1)S(1)} %get-tuple-element.42, ...), kind=kOutput, calls=%fused_computation | convolution fusion | flops 19038208 | bytes 360448 | tf_op jit(solution)/shard_map/rs,is->ri/dot_general | solution.py:238
  82.1 10.8 %all-to-all-done = f32[64,2,128]{2,1,0:T(2,128)S(1)} async-done(((f32[64,2,128]{2,1,0:T(2,128)}), f32[64,2,128]{2,1,0:T(2,128)S(1)}, u32[]{:S(2)}, u32[]{:S(2)}) %all-to-all-start) | async-done | bytes 65568 | tf_op jit(solution)/shard_map/all_to_all | solution.py:234
  92.9 0.1 reduce_sum.59
  92.9 0.7 reshape.283
  (26 shorter events, 0.2 us)
Async XLA Ops:
  0.6 18.8 %copy-start.7 = (s32[192,2]{0,1:T(2,128)S(1)}, s32[192,2]{0,1:T(2,128)}, u32[]{:S(2)}) copy-start(s32[192,2]{0,1:T(2,128)} %param.7) | copy-start | bytes 4612
  0.6 34.9 %copy-start.5 = (bf16[512,256]{1,0:T(8,128)(2,1)S(1)}, bf16[512,256]{1,0:T(8,128)(2,1)}, u32[]{:S(2)}) copy-start(bf16[512,256]{1,0:T(8,128)(2,1)} %param.10) | copy-start | bytes 786436
  0.7 33.0 %copy-start.6 = (bf16[256,64]{0,1:T(8,128)(2,1)S(1)}, bf16[256,64]{0,1:T(8,128)(2,1)}, u32[]{:S(2)}) copy-start(bf16[256,64]{0,1:T(8,128)(2,1)} %param.11) | copy-start | bytes 98308
  10.5 15.0 %collective-permute-start.1 = (bf16[256,128]{1,0:T(8,128)(2,1)}, bf16[256,128]{1,0:T(8,128)(2,1)S(1)}, u32[]{:S(2)}, u32[]{:S(2)}) collective-permute-start(bf16[256,128]{1,0:T(8,128)(2,1)} %masked.1), channel_id=1, source_target_pairs={{128,0},{129,1},{130,2},{131,3},{132,4},{133,5},{134,6},{135,7},{1... | collective-permute-start | bytes 196616 | tf_op jit(solution)/shard_map/ppermute | solution.py:26
  17.7 10.8 %collective-permute-start.2 = (bf16[256,128]{1,0:T(8,128)(2,1)}, bf16[256,128]{1,0:T(8,128)(2,1)S(1)}, u32[]{:S(2)}, u32[]{:S(2)}) collective-permute-start(bf16[256,128]{1,0:T(8,128)(2,1)} %masked.1), channel_id=1, source_target_pairs={{144,0},{145,1},{146,2},{147,3},{148,4},{149,5},{150,6},{151,7},{1... | collective-permute-start | bytes 196616 | tf_op jit(solution)/shard_map/ppermute | solution.py:26
  19.4 6.1 %collective-permute-start = (bf16[256,128]{1,0:T(8,128)(2,1)}, bf16[256,128]{1,0:T(8,128)(2,1)S(1)}, u32[]{:S(2)}, u32[]{:S(2)}) collective-permute-start(bf16[256,128]{1,0:T(8,128)(2,1)} %masked.1), channel_id=1, source_target_pairs={{16,0},{17,1},{18,2},{19,3},{20,4},{21,5},{22,6},{23,7},{24,8},{25... | collective-permute-start | bytes 196616 | tf_op jit(solution)/shard_map/ppermute | solution.py:26
  29.3 7.7 %collective-permute-start.4 = (bf16[4,256,128]{2,1,0:T(8,128)(2,1)S(1)}, bf16[4,256,128]{2,1,0:T(8,128)(2,1)S(1)}, u32[]{:S(2)}, u32[]{:S(2)}) collective-permute-start(bf16[4,256,128]{2,1,0:T(8,128)(2,1)S(1)} %get-tuple-element.40), channel_id=1, source_target_pairs={{12,0},{225,1},{14,2},{227,3},{0,4},{229,5},{2,6},{231,7},{4,8},{2... | collective-permute-start | bytes 786440 | tf_op jit(solution)/shard_map/ppermute | solution.py:36
  30.9 10.4 %collective-permute-start.5 = (bf16[4,256,128]{2,1,0:T(8,128)(2,1)S(1)}, bf16[4,256,128]{2,1,0:T(8,128)(2,1)S(1)}, u32[]{:S(2)}, u32[]{:S(2)}) collective-permute-start(bf16[4,256,128]{2,1,0:T(8,128)(2,1)S(1)} %get-tuple-element.40), channel_id=1, source_target_pairs={{8,0},{65,1},{10,2},{67,3},{12,4},{69,5},{14,6},{71,7},{0,8},{73,9... | collective-permute-start | bytes 786440 | tf_op jit(solution)/shard_map/ppermute | solution.py:36
  34.0 8.1 %collective-permute-start.3 = (bf16[4,256,128]{2,1,0:T(8,128)(2,1)S(1)}, bf16[4,256,128]{2,1,0:T(8,128)(2,1)S(1)}, u32[]{:S(2)}, u32[]{:S(2)}) collective-permute-start(bf16[4,256,128]{2,1,0:T(8,128)(2,1)S(1)} %get-tuple-element.40), channel_id=1, source_target_pairs={{4,0},{33,1},{6,2},{35,3},{8,4},{37,5},{10,6},{39,7},{12,8},{41,9}... | collective-permute-start | bytes 786440 | tf_op jit(solution)/shard_map/ppermute | solution.py:36
  41.4 14.5 %collective-permute-start.7 = (bf16[2,4,256,128]{3,2,1,0:T(8,128)(2,1)S(1)}, bf16[2,4,256,128]{3,2,1,0:T(8,128)(2,1)S(1)}, u32[]{:S(2)}, u32[]{:S(2)}) collective-permute-start(bf16[2,4,256,128]{3,2,1,0:T(8,128)(2,1)S(1)} %pad_maximum_fusion.1), channel_id=1, source_target_pairs={{224,0},{13,1},{226,2},{15,3},{228,4},{1,5},{230,6},{3,7},{232,8},... | collective-permute-start | bytes 1572872 | tf_op jit(solution)/shard_map/ppermute | solution.py:36
  42.2 13.7 %collective-permute-start.6 = (bf16[2,4,256,128]{3,2,1,0:T(8,128)(2,1)S(1)}, bf16[2,4,256,128]{3,2,1,0:T(8,128)(2,1)S(1)}, u32[]{:S(2)}, u32[]{:S(2)}) collective-permute-start(bf16[2,4,256,128]{3,2,1,0:T(8,128)(2,1)S(1)} %pad_maximum_fusion), channel_id=1, source_target_pairs={{32,0},{5,1},{34,2},{7,3},{36,4},{9,5},{38,6},{11,7},{40,8},{13,9}... | collective-permute-start | bytes 1572872 | tf_op jit(solution)/shard_map/ppermute | solution.py:36
  45.9 12.1 %collective-permute-start.10 = (bf16[2,4,256,128]{3,2,1,0:T(8,128)(2,1)}, bf16[2,4,256,128]{3,2,1,0:T(8,128)(2,1)S(1)}, u32[]{:S(2)}, u32[]{:S(2)}) collective-permute-start(bf16[2,4,256,128]{3,2,1,0:T(8,128)(2,1)} %get-tuple-element.38), channel_id=1, source_target_pairs={{32,0},{5,1},{34,2},{7,3},{36,4},{1,5},{38,6},{3,7},{40,8},{13,9},... | collective-permute-start | bytes 1572872 | tf_op jit(solution)/shard_map/ppermute | solution.py:46
  45.9 12.1 %collective-permute-start.11 = (bf16[2,4,256,128]{3,2,1,0:T(8,128)(2,1)}, bf16[2,4,256,128]{3,2,1,0:T(8,128)(2,1)S(1)}, u32[]{:S(2)}, u32[]{:S(2)}) collective-permute-start(bf16[2,4,256,128]{3,2,1,0:T(8,128)(2,1)} %get-tuple-element.37), channel_id=1, source_target_pairs={{224,0},{13,1},{226,2},{15,3},{228,4},{9,5},{230,6},{11,7},{232,8}... | collective-permute-start | bytes 1572872 | tf_op jit(solution)/shard_map/ppermute | solution.py:46
  47.8 2.8 %copy-start = (bf16[192,128,128]{2,1,0:T(8,128)(2,1)S(1)}, bf16[192,128,128]{2,1,0:T(8,128)(2,1)}, u32[]{:S(2)}) copy-start(bf16[192,128,128]{2,1,0:T(8,128)(2,1)} %copy.29.adj) | copy-start | bytes 18874372
  52.5 2.7 %copy-start.1 = (bf16[192,128,128]{2,1,0:T(8,128)(2,1)}, bf16[192,128,128]{2,1,0:T(8,128)(2,1)S(1)}, u32[]{:S(2)}) copy-start(bf16[192,128,128]{2,1,0:T(8,128)(2,1)S(1)} %get-tuple-element.20.adj) | copy-start | bytes 18874372
  55.2 0.7 copy-start.3
  55.9 10.3 %collective-permute-start.8 = (bf16[2,4,256,128]{3,2,1,0:T(8,128)(2,1)S(1)}, bf16[2,4,256,128]{3,2,1,0:T(8,128)(2,1)S(1)}, u32[]{:S(2)}, u32[]{:S(2)}) collective-permute-start(bf16[2,4,256,128]{3,2,1,0:T(8,128)(2,1)S(1)} %collective-permute-done.6), channel_id=1, source_target_pairs={{32,0},{5,1},{34,2},{7,3},{36,4},{9,5},{38,6},{11,7},{40,8},{13,9}... | collective-permute-start | bytes 1572872 | tf_op jit(solution)/shard_map/ppermute | solution.py:36
  57.2 10.4 %collective-permute-start.9 = (bf16[2,4,256,128]{3,2,1,0:T(8,128)(2,1)S(1)}, bf16[2,4,256,128]{3,2,1,0:T(8,128)(2,1)S(1)}, u32[]{:S(2)}, u32[]{:S(2)}) collective-permute-start(bf16[2,4,256,128]{3,2,1,0:T(8,128)(2,1)S(1)} %collective-permute-done.7), channel_id=1, source_target_pairs={{224,0},{13,1},{226,2},{15,3},{228,4},{1,5},{230,6},{3,7},{232,8},... | collective-permute-start | bytes 1572872 | tf_op jit(solution)/shard_map/ppermute | solution.py:36
  58.0 2.8 %copy-start.2 = (bf16[192,128,128]{2,1,0:T(8,128)(2,1)S(1)}, bf16[192,128,128]{2,1,0:T(8,128)(2,1)}, u32[]{:S(2)}) copy-start(bf16[192,128,128]{2,1,0:T(8,128)(2,1)} %copy-done.1) | copy-start | bytes 18874372
  60.8 0.9 %copy-start.4 = (f32[4,128,128]{2,1,0:T(8,128)S(1)}, f32[4,128,128]{2,1,0:T(8,128)}, u32[]{:S(2)}) copy-start(f32[4,128,128]{2,1,0:T(8,128)} %copy-done.3) | copy-start | bytes 786436
  70.4 10.4 %collective-permute-start.12 = (bf16[320,128]{1,0:T(8,128)(2,1)S(1)}, bf16[320,128]{1,0:T(8,128)(2,1)S(1)}, u32[]{:S(2)}, u32[]{:S(2)}) collective-permute-start(bf16[320,128]{1,0:T(8,128)(2,1)S(1)} %get-tuple-element.30), channel_id=1, source_target_pairs={{0,1},{1,0},{2,3},{3,2},{4,5},{5,4},{6,7},{7,6},{8,9},{9,8},{10,11... | collective-permute-start | bytes 245768 | tf_op jit(solution)/shard_map/ppermute | solution.py:235
  70.4 10.4 %collective-permute-start.13 = (bf16[320,128]{1,0:T(8,128)(2,1)S(1)}, bf16[320,128]{1,0:T(8,128)(2,1)S(1)}, u32[]{:S(2)}, u32[]{:S(2)}) collective-permute-start(bf16[320,128]{1,0:T(8,128)(2,1)S(1)} %get-tuple-element.31), channel_id=1, source_target_pairs={{0,2},{2,0},{1,3},{3,1},{4,6},{6,4},{5,7},{7,5},{8,10},{10,8},{9,1... | collective-permute-start | bytes 245768 | tf_op jit(solution)/shard_map/ppermute | solution.py:235
  72.6 8.4 %collective-permute-start.14 = (bf16[320,128]{1,0:T(8,128)(2,1)S(1)}, bf16[320,128]{1,0:T(8,128)(2,1)S(1)}, u32[]{:S(2)}, u32[]{:S(2)}) collective-permute-start(bf16[320,128]{1,0:T(8,128)(2,1)S(1)} %get-tuple-element.32), channel_id=1, source_target_pairs={{0,3},{3,0},{1,2},{2,1},{4,7},{7,4},{5,6},{6,5},{8,11},{11,8},{9,1... | collective-permute-start | bytes 245768 | tf_op jit(solution)/shard_map/ppermute | solution.py:235
  72.8 20.0 %all-to-all-start = ((f32[64,2,128]{2,1,0:T(2,128)}), f32[64,2,128]{2,1,0:T(2,128)S(1)}, u32[]{:S(2)}, u32[]{:S(2)}) async-start(f32[64,2,128]{2,1,0:T(2,128)} %get-tuple-element.33), calls=%async_computation | async-start | bytes 131072 | tf_op jit(solution)/shard_map/all_to_all | solution.py:234

commit v5 on v4

--- a/solution.py
+++ b/solution.py
@@ -154,7 +154,7 @@
 
 
 def first_kernel(table, bounds, adj, *refs):
-    *sources, acc, kept, masks = refs
+    *sources, acc, masks = refs
     set_masks(masks)
     acc[...] = jnp.zeros_like(acc)
     add_sources(table, bounds, adj, sources, 0, acc, masks)
@@ -186,7 +186,7 @@
         ref[pl.ds(256, 64), :] = weights[k]
 
 
-def call(kernel, table, bounds, adj, sources, others, out_shape, keep_acc, name, aliases={}):
+def call(kernel, table, bounds, adj, sources, others, out_shape, keep_acc, name):
     smem = pl.BlockSpec(memory_space=pltpu.SMEM)
     vmem = pl.BlockSpec(memory_space=pltpu.VMEM)
     sources = [s.reshape(-1, 128, 128) for s in sources]
@@ -200,7 +200,6 @@
         ],
         compiler_params=pltpu.CompilerParams(vmem_limit_bytes=8 * 1024 * 1024),
         cost_estimate=pl.CostEstimate(flops=2 * 64 * 128 * 128 * 128, bytes_accessed=8 * 1024 * 1024, transcendentals=0),
-        input_output_aliases=aliases,
         name=name,
     )(table, bounds, adj, *sources, *others)
 
@@ -222,21 +221,21 @@
     w_sent = jnp.pad(jnp.stack(w_parts[1:]), ((0, 0), (0, 0), (0, 64)))
 
     sums = jax.ShapeDtypeStruct((4, 128, 128), jnp.float32)
-    kept = jax.ShapeDtypeStruct(adj_tiles.shape, adj_tiles.dtype)
-    acc, adj = call(first_kernel, *tables, adj_tiles, [low, high], [], (sums, kept), False, "early_tiles", {2: 1})
+    acc = call(first_kernel, *tables, adj_tiles, [low, high], [], sums, False, "early_tiles")
     forwarded, acc, f_rows, w_sent = lax.optimization_barrier((forwarded, acc, f_rows, w_sent))
     far = gather_far(*forwarded)
-    acc = call(middle_kernel, *tables, adj, forwarded + others, [acc], sums, False, "near_tiles")
+    acc = call(middle_kernel, *tables, adj_tiles, forwarded + others, [acc], sums, False, "near_tiles")
     message = jax.ShapeDtypeStruct((320, 128), jnp.bfloat16)
     outs = (jax.ShapeDtypeStruct((256, 128), jnp.bfloat16), message, message, message, jax.ShapeDtypeStruct((64, 2, 128), jnp.float32))
-    agg, *messages, partial = call(last_kernel, *tables, adj, far, [acc, f_rows, w_sent], outs, True, "far_tiles")
+    agg, *messages, partial = call(last_kernel, *tables, adj_tiles, far, [acc, f_rows, w_sent], outs, True, "far_tiles")
 
     pieces = lax.all_to_all(partial, ROWS, 0, 0, tiled=True)
     arrived = [lax.ppermute(m, SLAB, pairs) for m, pairs in zip(messages, FLIPS)]
     a_all = jnp.concatenate([halves(agg)] + [halves(m[:256]) for m in arrived], axis=1)
     w_all = jnp.concatenate([w_parts[0]] + [m[256:, :64] for m in arrived], axis=1)
     grad_input = jnp.einsum("rs,is->ri", a_all, w_all, preferred_element_type=jnp.float32).astype(jnp.bfloat16)
-    grad_weight = jnp.sum(pieces, axis=0).reshape(4, 64)
+    total = jnp.sum(pieces, axis=0)
+    grad_weight = jnp.concatenate([total[p : p + 1, k : k + 64] for p in range(2) for k in (0, 64)], axis=0)
     return grad_input, grad_weight
 
 

time: 94.5 us -> 83.1 us (0.88)
  local copies, waits for them, and re-layouts: 19.8 us -> 8.54 us
  waiting for transfers between devices: 24.4 us -> 21.1 us
  Pallas kernels: 10.9 us -> 12.4 us
  other arithmetic: 3.01 us -> 4.31 us
    unnamed x19 -> x6, local copies, waits for them, and re-layouts: 18.2 us -> 6.75 us
    all_to_all x1, waiting for transfers between devices: 10.8 us -> 4.51 us  [body(): pieces = lax.all_to_all(partial, ROWS, 0, 0, tiled=True)]
    ppermute x3, waiting for transfers between devices: 0.01 us -> 4.22 us  [body(): lax.ppermute(m, SLAB, pairs)]
    ppermute x7, waiting for transfers between devices: 6.73 us -> 4.46 us  [from_axis(): return lax.ppermute(value, ALL, pairs)]
    ppermute x2, waiting for transfers between devices: 0.01 us -> 1.75 us  [exchange(): return lax.ppermute(value, ALL, pairs)]
    pallas_call x3, Pallas kernels: 9.22 us -> 10.8 us  [call(): pl.pallas_call(kernel, out_shape=out_shape, in_specs=[smem, smem, vmem] +...]
  transfers between devices with their start and end apart: 16 -> 16, of which waited for: 6 -> 9; matrix products, arithmetic and copies ran while one was open for 4% -> 8% of each run, Pallas kernels for 7% -> 9%
where the time goes in v5:
time: 83.1 us; the launch traced here: 82 us
  starting transfers between devices  33.8 us (41%)
  waiting for transfers between devices  21.1 us (25%)
  Pallas kernels  12.4 us (15%)
  local copies, waits for them, and re-layouts  8.54 us (10%)
  other arithmetic  4.31 us (5%)
  matrix products  0.96 us (1%)
  between operations  0.87 us (1%)
    ppermute x7, starting transfers between devices, from_axis(): return lax.ppermute(value, ALL, pairs)  11.3 us
    pallas_call x3, Pallas kernels, call(): pl.pallas_call(kernel, out_shape=out_shape, in_specs=[smem, smem, vmem] +...  10.8 us
    ppermute x3, starting transfers between devices, from_rows(): return lax.ppermute(value, ALL, pairs)  10.2 us
    all_to_all x1, starting transfers between devices, body(): pieces = lax.all_to_all(partial, ROWS, 0, 0, tiled=True)  8.3 us
    unnamed x6, local copies, waits for them, and re-layouts  6.75 us
    ppermute x3, waiting for transfers between devices, from_rows(): return lax.ppermute(value, ALL, pairs)  6.13 us
    all_to_all x1, waiting for transfers between devices, body(): pieces = lax.all_to_all(partial, ROWS, 0, 0, tiled=True)  4.51 us
    ppermute x7, waiting for transfers between devices, from_axis(): return lax.ppermute(value, ALL, pairs)  4.46 us
  transfers between devices with their start and end apart: 16, of which 9 were waited for; matrix products, arithmetic and copies ran while one was open for 8% of the time, Pallas kernels for 9%

profile of v5, /device:TPU:8, one launch (start us, length us, event | category | flops | bytes accessed | tf_op | source)
XLA Modules:
  0.0 82.0 jit_solution(12479100213964259500)
XLA Ops:
  0.6 1.7 %masked.1 = bf16[256,128]{1,0:T(8,128)(2,1)} custom-call(bf16[64,512]{1,0:T(8,128)(2,1)} %bitcast.50, s32[64,512]{1,0:T(8,128)} %bitcast.43), custom_call_target="tpu_custom_call" | custom-call | tf_op jit(solution)/shard_map/masked/pallas_call | solution.py:142
  2.3 7.2 %collective-permute-start.1 = (bf16[256,128]{1,0:T(8,128)(2,1)}, bf16[256,128]{1,0:T(8,128)(2,1)S(1)}, u32[]{:S(2)}, u32[]{:S(2)}) collective-permute-start(bf16[256,128]{1,0:T(8,128)(2,1)} %masked.1), channel_id=1, source_target_pairs={{128,0},{129,1},{130,2},{131,3},{132,4},{133,5},{134,6},{135,7},{1... | collective-permute-start | bytes 196616 | tf_op jit(solution)/shard_map/ppermute | solution.py:26
  9.5 1.7 %collective-permute-start.2 = (bf16[256,128]{1,0:T(8,128)(2,1)}, bf16[256,128]{1,0:T(8,128)(2,1)S(1)}, u32[]{:S(2)}, u32[]{:S(2)}) collective-permute-start(bf16[256,128]{1,0:T(8,128)(2,1)} %masked.1), channel_id=1, source_target_pairs={{144,0},{145,1},{146,2},{147,3},{148,4},{149,5},{150,6},{151,7},{1... | collective-permute-start | bytes 196616 | tf_op jit(solution)/shard_map/ppermute | solution.py:26
  11.2 0.8 slice_subtract_fusion
  12.0 1.3 %collective-permute-start = (bf16[256,128]{1,0:T(8,128)(2,1)}, bf16[256,128]{1,0:T(8,128)(2,1)S(1)}, u32[]{:S(2)}, u32[]{:S(2)}) collective-permute-start(bf16[256,128]{1,0:T(8,128)(2,1)} %masked.1), channel_id=1, source_target_pairs={{16,0},{17,1},{18,2},{19,3},{20,4},{21,5},{22,6},{23,7},{24,8},{25... | collective-permute-start | bytes 196616 | tf_op jit(solution)/shard_map/ppermute | solution.py:26
  13.4 0.1 convert_reduce_fusion.1
  13.5 0.2 convert_reduce_fusion
  13.7 0.1 sub.105
  13.8 0.1 fusion.29
  13.9 0.1 select_reduce_fusion.2.bounds
  14.0 0.1 select_reduce_fusion.1
  14.2 3.9 %collective-permute-done = bf16[256,128]{1,0:T(8,128)(2,1)S(1)} collective-permute-done((bf16[256,128]{1,0:T(8,128)(2,1)}, bf16[256,128]{1,0:T(8,128)(2,1)S(1)}, u32[]{:S(2)}, u32[]{:S(2)}) %collective-permute-start) | collective-permute-done | bytes 65568 | tf_op jit(solution)/shard_map/ppermute | solution.py:26
  18.1 0.0 collective-permute-done.1
  18.1 2.2 %collective-permute-done.2 = bf16[256,128]{1,0:T(8,128)(2,1)S(1)} collective-permute-done((bf16[256,128]{1,0:T(8,128)(2,1)}, bf16[256,128]{1,0:T(8,128)(2,1)S(1)}, u32[]{:S(2)}, u32[]{:S(2)}) %collective-permute-start.2) | collective-permute-done | bytes 65568 | tf_op jit(solution)/shard_map/ppermute | solution.py:26
  20.3 0.9 %fusion.43 = (bf16[1,4,256,128]{3,2,1,0:T(8,128)(2,1)S(1)}, bf16[4,256,128]{2,1,0:T(8,128)(2,1)S(1)}) fusion(bf16[1,256,128]{2,1,0:T(8,128)(2,1)S(1)} %bitcast.45, bf16[1,256,128]{2,1,0:T(8,128)(2,1)S(1)} %bitcast.44, bf16[1,256,128]{2,1,0:T(8,128)(2,1)S(1)} %bitcast.46, bf16[1,256,128]{2,1,0:T(8,128)(2,1)} %bitcast.39), kind=kLoop, calls=%fused_computation.129 | loop fusion | flops 393216 | bytes 786432 | tf_op jit(solution)/shard_map/stack | solution.py:57
  21.2 1.6 %collective-permute-start.5 = (bf16[4,256,128]{2,1,0:T(8,128)(2,1)S(1)}, bf16[4,256,128]{2,1,0:T(8,128)(2,1)S(1)}, u32[]{:S(2)}, u32[]{:S(2)}) collective-permute-start(bf16[4,256,128]{2,1,0:T(8,128)(2,1)S(1)} %get-tuple-element.36), channel_id=1, source_target_pairs={{12,0},{225,1},{14,2},{227,3},{0,4},{229,5},{2,6},{231,7},{4,8},{2... | collective-permute-start | bytes 786440 | tf_op jit(solution)/shard_map/ppermute | solution.py:36
  22.7 2.7 %collective-permute-start.6 = (bf16[4,256,128]{2,1,0:T(8,128)(2,1)S(1)}, bf16[4,256,128]{2,1,0:T(8,128)(2,1)S(1)}, u32[]{:S(2)}, u32[]{:S(2)}) collective-permute-start(bf16[4,256,128]{2,1,0:T(8,128)(2,1)S(1)} %get-tuple-element.36), channel_id=1, source_target_pairs={{8,0},{65,1},{10,2},{67,3},{12,4},{69,5},{14,6},{71,7},{0,8},{73,9... | collective-permute-start | bytes 786440 | tf_op jit(solution)/shard_map/ppermute | solution.py:36
  25.5 0.9 %constant_dynamic-slice_fusion.2 = (bf16[64,64]{0,1:T(8,128)(2,1)S(1)}, bf16[64,64]{0,1:T(8,128)(2,1)S(1)}, bf16[64,64]{0,1:T(8,128)(2,1)S(1)}, bf16[64,64]{0,1:T(8,128)(2,1)S(1)}) fusion(bf16[256,64]{0,1:T(8,128)(2,1)} %param.11, s32[]{:T(128)S(6)} %select_n.270, s32[]{:T(128)S(6)} %select_n.265, s32[]{:T(128)S(6)} %select_n.264, s32[]{:T(128)S(6)} %select_n.266), kind=kLoop, calls=%fused_computation.118 | loop fusion | bytes 65552 | tf_op jit(solution)/shard_map/dynamic_slice | solution.py:220
  26.4 0.1 copy.21
  26.5 0.1 copy.22
  26.6 0.1 copy.23
  26.7 1.5 %collective-permute-start.3 = (bf16[4,256,128]{2,1,0:T(8,128)(2,1)S(1)}, bf16[4,256,128]{2,1,0:T(8,128)(2,1)S(1)}, u32[]{:S(2)}, u32[]{:S(2)}) collective-permute-start(bf16[4,256,128]{2,1,0:T(8,128)(2,1)S(1)} %get-tuple-element.36), channel_id=1, source_target_pairs={{4,0},{33,1},{6,2},{35,3},{8,4},{37,5},{10,6},{39,7},{12,8},{41,9}... | collective-permute-start | bytes 786440 | tf_op jit(solution)/shard_map/ppermute | solution.py:36
  28.2 1.1 %copy.19 = bf16[512,256]{0,1:T(8,128)(2,1)S(1)} copy(bf16[512,256]{1,0:T(8,128)(2,1)} %param.10) | data formatting | bytes 524288 | tf_op args[4]
  29.3 0.1 reshape.272
  29.4 0.1 select_reduce_fusion
  29.6 0.0 collective-permute-done.5
  29.6 3.6 %collective-permute-done.6 = bf16[4,256,128]{2,1,0:T(8,128)(2,1)S(1)} collective-permute-done((bf16[4,256,128]{2,1,0:T(8,128)(2,1)S(1)}, bf16[4,256,128]{2,1,0:T(8,128)(2,1)S(1)}, u32[]{:S(2)}, u32[]{:S(2)}) %collective-permute-start.6) | collective-permute-done | bytes 262176 | tf_op jit(solution)/shard_map/ppermute | solution.py:36
  33.2 0.1 pad_maximum_fusion.1
  33.2 0.8 collective-permute-start.7
  34.0 0.0 collective-permute-done.3
  34.0 0.1 pad_maximum_fusion
  34.0 2.6 %collective-permute-start.4 = (bf16[2,4,256,128]{3,2,1,0:T(8,128)(2,1)S(1)}, bf16[2,4,256,128]{3,2,1,0:T(8,128)(2,1)S(1)}, u32[]{:S(2)}, u32[]{:S(2)}) collective-permute-start(bf16[2,4,256,128]{3,2,1,0:T(8,128)(2,1)S(1)} %pad_maximum_fusion), channel_id=1, source_target_pairs={{32,0},{5,1},{34,2},{7,3},{36,4},{9,5},{38,6},{11,7},{40,8},{13,9}... | collective-permute-start | bytes 1572872 | tf_op jit(solution)/shard_map/ppermute | solution.py:36
  36.7 1.0 %broadcast_select_fusion = (bf16[2,4,256,128]{3,2,1,0:T(8,128)(2,1)}, bf16[2,4,256,128]{3,2,1,0:T(8,128)(2,1)}) fusion(bf16[2,4,256,128]{3,2,1,0:T(8,128)(2,1)S(1)} %pad_maximum_fusion, bf16[2,4,256,128]{3,2,1,0:T(8,128)(2,1)S(1)} %pad_maximum_fusion.1, pred[]{:T(512)S(6)} %eq.123), kind=kLoop, calls=%fused_computation.5 | loop fusion | flops 524288 | bytes 2097153 | tf_op jit(solution)/shard_map/jit(_where)/select_n | solution.py:66
  37.7 0.0 collective-permute-start.10
  37.7 2.0 %collective-permute-start.11 = (bf16[2,4,256,128]{3,2,1,0:T(8,128)(2,1)}, bf16[2,4,256,128]{3,2,1,0:T(8,128)(2,1)}, u32[]{:S(2)}, u32[]{:S(2)}) collective-permute-start(bf16[2,4,256,128]{3,2,1,0:T(8,128)(2,1)} %get-tuple-element.33), channel_id=1, source_target_pairs={{224,0},{13,1},{226,2},{15,3},{228,4},{9,5},{230,6},{11,7},{232,8}... | collective-permute-start | bytes 1572872 | tf_op jit(solution)/shard_map/ppermute | solution.py:46
  39.7 2.8 %copy-done = bf16[192,128,128]{2,1,0:T(8,128)(2,1)S(1)} copy-done((bf16[192,128,128]{2,1,0:T(8,128)(2,1)S(1)}, bf16[192,128,128]{2,1,0:T(8,128)(2,1)}, u32[]{:S(2)}) %copy-start) | copy-done | bytes 6291480
  42.5 2.9 %early_tiles.1.refs_4_ = f32[4,128,128]{2,1,0:T(8,128)S(1)} custom-call(s32[896]{0:T(1024)S(1)} %add_select_fusion.1.table, s32[9]{0:T(128)S(1)} %select_reduce_fusion.2.bounds, bf16[192,128,128]{2,1,0:T(8,128)(2,1)S(1)} %copy-done, bf16[16,128,128]{2,1,0:T(8,128)(2,1)S(1)} %bitcast.30, bf16[16,128,128]{2,1,0:T(8,128)(2,1)S(1)} %bitcast.29), custom_call_target="tpu_custom_call" | custom-call | flops 268435456 | bytes 8388608 | tf_op jit(solution)/shard_map/early_tiles/pallas_call | solution.py:193
  45.4 0.0 collective-permute-done.7
  45.5 0.0 collective-permute-done.4
  45.5 1.6 %collective-permute-start.8 = (bf16[2,4,256,128]{3,2,1,0:T(8,128)(2,1)S(1)}, bf16[2,4,256,128]{3,2,1,0:T(8,128)(2,1)S(1)}, u32[]{:S(2)}, u32[]{:S(2)}) collective-permute-start(bf16[2,4,256,128]{3,2,1,0:T(8,128)(2,1)S(1)} %collective-permute-done.4), channel_id=1, source_target_pairs={{32,0},{5,1},{34,2},{7,3},{36,4},{9,5},{38,6},{11,7},{40,8},{13,9}... | collective-permute-start | bytes 1572872 | tf_op jit(solution)/shard_map/ppermute | solution.py:36
  47.1 0.5 collective-permute-start.9
  47.6 0.1 copy.25
  47.7 1.3 %collective-permute-done.10 = bf16[2,4,256,128]{3,2,1,0:T(8,128)(2,1)S(1)} collective-permute-done((bf16[2,4,256,128]{3,2,1,0:T(8,128)(2,1)}, bf16[2,4,256,128]{3,2,1,0:T(8,128)(2,1)S(1)}, u32[]{:S(2)}, u32[]{:S(2)}) %collective-permute-start.10) | collective-permute-done | bytes 524320 | tf_op jit(solution)/shard_map/ppermute | solution.py:46
  48.9 0.5 collective-permute-done.11
  49.4 2.8 %copy-done.1 = bf16[192,128,128]{2,1,0:T(8,128)(2,1)S(1)} copy-done((bf16[192,128,128]{2,1,0:T(8,128)(2,1)S(1)}, bf16[192,128,128]{2,1,0:T(8,128)(2,1)}, u32[]{:S(2)}) %copy-start.1) | copy-done | bytes 6291480
  52.2 4.4 %near_tiles.1.refs_2_ = f32[4,128,128]{2,1,0:T(8,128)S(1)} custom-call(s32[896]{0:T(1024)S(1)} %add_select_fusion.1.table, s32[9]{0:T(128)S(1)} %select_reduce_fusion.2.bounds, bf16[192,128,128]{2,1,0:T(8,128)(2,1)S(1)} %copy-done.1, bf16[16,128,128]{2,1,0:T(8,128)(2,1)S(1)} %bitcast.33, bf16[16,128,128]{2,1,0:T(8,128)(2,1)S(1)} %bitcast.32, ...), custom_call_target="tpu_custom_call" | custom-call | flops 268435456 | bytes 8388608 | tf_op jit(solution)/shard_map/near_tiles/pallas_call | solution.py:193
  56.6 0.0 collective-permute-done.8
  56.6 0.9 %collective-permute-done.9 = bf16[2,4,256,128]{3,2,1,0:T(8,128)(2,1)S(1)} collective-permute-done((bf16[2,4,256,128]{3,2,1,0:T(8,128)(2,1)S(1)}, bf16[2,4,256,128]{3,2,1,0:T(8,128)(2,1)S(1)}, u32[]{:S(2)}, u32[]{:S(2)}) %collective-permute-start.9) | collective-permute-done | bytes 524320 | tf_op jit(solution)/shard_map/ppermute | solution.py:36
  57.5 3.5 %far_tiles.1 = (bf16[256,128]{1,0:T(8,128)(2,1)S(1)}, bf16[320,128]{1,0:T(8,128)(2,1)S(1)}, bf16[320,128]{1,0:T(8,128)(2,1)S(1)}, bf16[320,128]{1,0:T(8,128)(2,1)S(1)}, f32[64,2,128]{2,1,0:T(2,128)}) custom-call(s32[896]{0:T(1024)S(1)} %add_select_fusion.1.table, s32[9]{0:T(128)S(1)} %select_reduce_fusion.2.bounds, bf16[192,128,128]{2,1,0:T(8,128)(2,1)S(1)} %copy-done.1, ...), custom_call_target="tpu_custom_call" | custom-call | flops 268435456 | bytes 8388608 | tf_op jit(solution)/shard_map/far_tiles/pallas_call | solution.py:193
  60.9 8.3 %all-to-all-start = ((f32[64,2,128]{2,1,0:T(2,128)}), f32[64,2,128]{2,1,0:T(2,128)S(1)}, u32[]{:S(2)}, u32[]{:S(2)}) async-start(f32[64,2,128]{2,1,0:T(2,128)} %get-tuple-element.29), calls=%async_computation | async-start | bytes 131072 | tf_op jit(solution)/shard_map/all_to_all | solution.py:232
  69.2 0.1 collective-permute-start.12
  69.3 1.5 %collective-permute-start.13 = (bf16[320,128]{1,0:T(8,128)(2,1)S(1)}, bf16[320,128]{1,0:T(8,128)(2,1)S(1)}, u32[]{:S(2)}, u32[]{:S(2)}) collective-permute-start(bf16[320,128]{1,0:T(8,128)(2,1)S(1)} %get-tuple-element.27), channel_id=1, source_target_pairs={{0,2},{2,0},{1,3},{3,1},{4,6},{6,4},{5,7},{7,5},{8,10},{10,8},{9,1... | collective-permute-start | bytes 245768 | tf_op jit(solution)/shard_map/ppermute | solution.py:233
  70.8 0.4 collective-permute-start.14
  71.2 0.1 fusion.47
  71.3 0.1 fusion.44
  71.4 3.4 %collective-permute-done.13 = bf16[320,128]{1,0:T(8,128)(2,1)S(1)} collective-permute-done((bf16[320,128]{1,0:T(8,128)(2,1)S(1)}, bf16[320,128]{1,0:T(8,128)(2,1)S(1)}, u32[]{:S(2)}, u32[]{:S(2)}) %collective-permute-start.13) | collective-permute-done | bytes 81952 | tf_op jit(solution)/shard_map/ppermute | solution.py:233
  74.8 0.1 fusion.45
  74.9 0.8 collective-permute-done.14
  75.7 0.1 fusion.46
  75.8 1.0 %convolution_convert_fusion = bf16[512,64]{0,1:T(8,128)(2,1)} fusion(bf16[256,64]{1,0:T(8,128)(2,1)S(1)} %get-tuple-element.42, bf16[256,64]{1,0:T(8,128)(2,1)S(1)} %get-tuple-element.41, bf16[256,64]{1,0:T(8,128)(2,1)S(1)} %get-tuple-element.40, bf16[256,64]{1,0:T(8,128)(2,1)S(1)} %get-tuple-element.39, bf16[256,64]{1,0:T(8,128)(2,1)S(1)} %get-tuple-element.38, ...), kind=kOutput, calls=%fused_computation | convolution fusion | flops 19038208 | bytes 360448 | tf_op jit(solution)/shard_map/rs,is->ri/dot_general | solution.py:236
  76.8 4.5 %all-to-all-done = f32[64,2,128]{2,1,0:T(2,128)S(1)} async-done(((f32[64,2,128]{2,1,0:T(2,128)}), f32[64,2,128]{2,1,0:T(2,128)S(1)}, u32[]{:S(2)}, u32[]{:S(2)}) %all-to-all-start) | async-done | bytes 65568 | tf_op jit(solution)/shard_map/all_to_all | solution.py:232
  81.3 0.1 reduce_sum.59
  81.4 0.1 fusion.48
  81.4 0.6 pad_maximum_fusion.3
  (14 shorter events, 0.2 us)
Async XLA Ops:
  2.3 15.8 %collective-permute-start.1 = (bf16[256,128]{1,0:T(8,128)(2,1)}, bf16[256,128]{1,0:T(8,128)(2,1)S(1)}, u32[]{:S(2)}, u32[]{:S(2)}) collective-permute-start(bf16[256,128]{1,0:T(8,128)(2,1)} %masked.1), channel_id=1, source_target_pairs={{128,0},{129,1},{130,2},{131,3},{132,4},{133,5},{134,6},{135,7},{1... | collective-permute-start | bytes 196616 | tf_op jit(solution)/shard_map/ppermute | solution.py:26
  9.5 10.8 %collective-permute-start.2 = (bf16[256,128]{1,0:T(8,128)(2,1)}, bf16[256,128]{1,0:T(8,128)(2,1)S(1)}, u32[]{:S(2)}, u32[]{:S(2)}) collective-permute-start(bf16[256,128]{1,0:T(8,128)(2,1)} %masked.1), channel_id=1, source_target_pairs={{144,0},{145,1},{146,2},{147,3},{148,4},{149,5},{150,6},{151,7},{1... | collective-permute-start | bytes 196616 | tf_op jit(solution)/shard_map/ppermute | solution.py:26
  12.0 6.1 %collective-permute-start = (bf16[256,128]{1,0:T(8,128)(2,1)}, bf16[256,128]{1,0:T(8,128)(2,1)S(1)}, u32[]{:S(2)}, u32[]{:S(2)}) collective-permute-start(bf16[256,128]{1,0:T(8,128)(2,1)} %masked.1), channel_id=1, source_target_pairs={{16,0},{17,1},{18,2},{19,3},{20,4},{21,5},{22,6},{23,7},{24,8},{25... | collective-permute-start | bytes 196616 | tf_op jit(solution)/shard_map/ppermute | solution.py:26
  21.2 8.4 %collective-permute-start.5 = (bf16[4,256,128]{2,1,0:T(8,128)(2,1)S(1)}, bf16[4,256,128]{2,1,0:T(8,128)(2,1)S(1)}, u32[]{:S(2)}, u32[]{:S(2)}) collective-permute-start(bf16[4,256,128]{2,1,0:T(8,128)(2,1)S(1)} %get-tuple-element.36), channel_id=1, source_target_pairs={{12,0},{225,1},{14,2},{227,3},{0,4},{229,5},{2,6},{231,7},{4,8},{2... | collective-permute-start | bytes 786440 | tf_op jit(solution)/shard_map/ppermute | solution.py:36
  22.7 10.4 %collective-permute-start.6 = (bf16[4,256,128]{2,1,0:T(8,128)(2,1)S(1)}, bf16[4,256,128]{2,1,0:T(8,128)(2,1)S(1)}, u32[]{:S(2)}, u32[]{:S(2)}) collective-permute-start(bf16[4,256,128]{2,1,0:T(8,128)(2,1)S(1)} %get-tuple-element.36), channel_id=1, source_target_pairs={{8,0},{65,1},{10,2},{67,3},{12,4},{69,5},{14,6},{71,7},{0,8},{73,9... | collective-permute-start | bytes 786440 | tf_op jit(solution)/shard_map/ppermute | solution.py:36
  26.7 7.3 %collective-permute-start.3 = (bf16[4,256,128]{2,1,0:T(8,128)(2,1)S(1)}, bf16[4,256,128]{2,1,0:T(8,128)(2,1)S(1)}, u32[]{:S(2)}, u32[]{:S(2)}) collective-permute-start(bf16[4,256,128]{2,1,0:T(8,128)(2,1)S(1)} %get-tuple-element.36), channel_id=1, source_target_pairs={{4,0},{33,1},{6,2},{35,3},{8,4},{37,5},{10,6},{39,7},{12,8},{41,9}... | collective-permute-start | bytes 786440 | tf_op jit(solution)/shard_map/ppermute | solution.py:36
  33.2 12.2 %collective-permute-start.7 = (bf16[2,4,256,128]{3,2,1,0:T(8,128)(2,1)S(1)}, bf16[2,4,256,128]{3,2,1,0:T(8,128)(2,1)S(1)}, u32[]{:S(2)}, u32[]{:S(2)}) collective-permute-start(bf16[2,4,256,128]{3,2,1,0:T(8,128)(2,1)S(1)} %pad_maximum_fusion.1), channel_id=1, source_target_pairs={{224,0},{13,1},{226,2},{15,3},{228,4},{1,5},{230,6},{3,7},{232,8},... | collective-permute-start | bytes 1572872 | tf_op jit(solution)/shard_map/ppermute | solution.py:36
  34.0 11.4 %collective-permute-start.4 = (bf16[2,4,256,128]{3,2,1,0:T(8,128)(2,1)S(1)}, bf16[2,4,256,128]{3,2,1,0:T(8,128)(2,1)S(1)}, u32[]{:S(2)}, u32[]{:S(2)}) collective-permute-start(bf16[2,4,256,128]{3,2,1,0:T(8,128)(2,1)S(1)} %pad_maximum_fusion), channel_id=1, source_target_pairs={{32,0},{5,1},{34,2},{7,3},{36,4},{9,5},{38,6},{11,7},{40,8},{13,9}... | collective-permute-start | bytes 1572872 | tf_op jit(solution)/shard_map/ppermute | solution.py:36
  37.7 11.2 %collective-permute-start.10 = (bf16[2,4,256,128]{3,2,1,0:T(8,128)(2,1)}, bf16[2,4,256,128]{3,2,1,0:T(8,128)(2,1)S(1)}, u32[]{:S(2)}, u32[]{:S(2)}) collective-permute-start(bf16[2,4,256,128]{3,2,1,0:T(8,128)(2,1)} %get-tuple-element.34), channel_id=1, source_target_pairs={{32,0},{5,1},{34,2},{7,3},{36,4},{1,5},{38,6},{3,7},{40,8},{13,9},... | collective-permute-start | bytes 1572872 | tf_op jit(solution)/shard_map/ppermute | solution.py:46
  37.7 11.7 %collective-permute-start.11 = (bf16[2,4,256,128]{3,2,1,0:T(8,128)(2,1)}, bf16[2,4,256,128]{3,2,1,0:T(8,128)(2,1)}, u32[]{:S(2)}, u32[]{:S(2)}) collective-permute-start(bf16[2,4,256,128]{3,2,1,0:T(8,128)(2,1)} %get-tuple-element.33), channel_id=1, source_target_pairs={{224,0},{13,1},{226,2},{15,3},{228,4},{9,5},{230,6},{11,7},{232,8}... | collective-permute-start | bytes 1572872 | tf_op jit(solution)/shard_map/ppermute | solution.py:46
  39.7 2.8 %copy-start = (bf16[192,128,128]{2,1,0:T(8,128)(2,1)S(1)}, bf16[192,128,128]{2,1,0:T(8,128)(2,1)}, u32[]{:S(2)}) copy-start(bf16[192,128,128]{2,1,0:T(8,128)(2,1)} %adj.5) | copy-start | bytes 18874372
  45.5 11.1 %collective-permute-start.8 = (bf16[2,4,256,128]{3,2,1,0:T(8,128)(2,1)S(1)}, bf16[2,4,256,128]{3,2,1,0:T(8,128)(2,1)S(1)}, u32[]{:S(2)}, u32[]{:S(2)}) collective-permute-start(bf16[2,4,256,128]{3,2,1,0:T(8,128)(2,1)S(1)} %collective-permute-done.4), channel_id=1, source_target_pairs={{32,0},{5,1},{34,2},{7,3},{36,4},{9,5},{38,6},{11,7},{40,8},{13,9}... | collective-permute-start | bytes 1572872 | tf_op jit(solution)/shard_map/ppermute | solution.py:36
  47.1 10.4 %collective-permute-start.9 = (bf16[2,4,256,128]{3,2,1,0:T(8,128)(2,1)S(1)}, bf16[2,4,256,128]{3,2,1,0:T(8,128)(2,1)S(1)}, u32[]{:S(2)}, u32[]{:S(2)}) collective-permute-start(bf16[2,4,256,128]{3,2,1,0:T(8,128)(2,1)S(1)} %collective-permute-done.7), channel_id=1, source_target_pairs={{224,0},{13,1},{226,2},{15,3},{228,4},{1,5},{230,6},{3,7},{232,8},... | collective-permute-start | bytes 1572872 | tf_op jit(solution)/shard_map/ppermute | solution.py:36
  49.4 2.8 %copy-start.1 = (bf16[192,128,128]{2,1,0:T(8,128)(2,1)S(1)}, bf16[192,128,128]{2,1,0:T(8,128)(2,1)}, u32[]{:S(2)}) copy-start(bf16[192,128,128]{2,1,0:T(8,128)(2,1)} %adj.5) | copy-start | bytes 18874372
  60.9 20.4 %all-to-all-start = ((f32[64,2,128]{2,1,0:T(2,128)}), f32[64,2,128]{2,1,0:T(2,128)S(1)}, u32[]{:S(2)}, u32[]{:S(2)}) async-start(f32[64,2,128]{2,1,0:T(2,128)} %get-tuple-element.29), calls=%async_computation | async-start | bytes 131072 | tf_op jit(solution)/shard_map/all_to_all | solution.py:232
  69.2 2.1 %collective-permute-start.12 = (bf16[320,128]{1,0:T(8,128)(2,1)S(1)}, bf16[320,128]{1,0:T(8,128)(2,1)S(1)}, u32[]{:S(2)}, u32[]{:S(2)}) collective-permute-start(bf16[320,128]{1,0:T(8,128)(2,1)S(1)} %get-tuple-element.26), channel_id=1, source_target_pairs={{0,1},{1,0},{2,3},{3,2},{4,5},{5,4},{6,7},{7,6},{8,9},{9,8},{10,11... | collective-permute-start | bytes 245768 | tf_op jit(solution)/shard_map/ppermute | solution.py:233
  69.3 5.5 %collective-permute-start.13 = (bf16[320,128]{1,0:T(8,128)(2,1)S(1)}, bf16[320,128]{1,0:T(8,128)(2,1)S(1)}, u32[]{:S(2)}, u32[]{:S(2)}) collective-permute-start(bf16[320,128]{1,0:T(8,128)(2,1)S(1)} %get-tuple-element.27), channel_id=1, source_target_pairs={{0,2},{2,0},{1,3},{3,1},{4,6},{6,4},{5,7},{7,5},{8,10},{10,8},{9,1... | collective-permute-start | bytes 245768 | tf_op jit(solution)/shard_map/ppermute | solution.py:233
  70.8 4.9 %collective-permute-start.14 = (bf16[320,128]{1,0:T(8,128)(2,1)S(1)}, bf16[320,128]{1,0:T(8,128)(2,1)S(1)}, u32[]{:S(2)}, u32[]{:S(2)}) collective-permute-start(bf16[320,128]{1,0:T(8,128)(2,1)S(1)} %get-tuple-element.28), channel_id=1, source_target_pairs={{0,3},{3,0},{1,2},{2,1},{4,7},{7,4},{5,6},{6,5},{8,11},{11,8},{9,1... | collective-permute-start | bytes 245768 | tf_op jit(solution)/shard_map/ppermute | solution.py:233

commit v6 on v5

--- a/solution.py
+++ b/solution.py
@@ -10,6 +10,7 @@
 SLAB = ("yl", "core")
 ALL = ROWS + SLAB
 GROUP = 4
+GROUPS = 4
 FLIPS = ([(0, 1), (1, 0), (2, 3), (3, 2)], [(0, 2), (2, 0), (1, 3), (3, 1)], [(0, 3), (3, 0), (1, 2), (2, 1)])
 
 
@@ -50,13 +51,13 @@
     return jnp.where(lax.axis_index("core") == 0, lax.axis_index("z"), lax.axis_index("x")) % 2 == 1
 
 
-def gather_early(packed, later):
+def gather_early(packed, position):
     far_y, far = from_rows(packed, dz=4, dy=1), from_rows(packed, dz=4)
-    again, later = lax.optimization_barrier((packed, later))
+    again, position = lax.optimization_barrier((packed, position))
     four = jnp.stack([packed, from_rows(again, dy=1), far, far_y])
     low = jnp.stack([four, from_axis(four, False, 1)])
     high = jnp.stack([from_axis(four, False, -1), from_axis(four, False, 2)])
-    return low, high, later
+    return low, high, position
 
 
 def gather_near(low, high):
@@ -94,42 +95,52 @@
 def tile_table(row, source, place, half, count):
     listed = row.shape[0]
     t = jnp.arange(listed)
-    r4, sources = jnp.arange(4), jnp.arange(count)
+    keys, sources = jnp.arange(count * 4), jnp.arange(count)
     key = source * 4 + row
     rank = jnp.sum(((key[None, :] == key[:, None]) & (t[None, :] < t[:, None])).astype(jnp.int32), axis=1)
-    held = jnp.sum((key[:, None] == jnp.arange(count * 4)[None, :]).astype(jnp.int32), axis=0).reshape(count, 4)
-    need = jnp.max((held + GROUP - 1) // GROUP, axis=1)
-    bounds = jnp.sum(jnp.where(sources[None, :] < jnp.arange(count + 1)[:, None], need[None, :], 0), axis=1)
-    begin = jnp.sum(jnp.where(source[:, None] == sources[None, :], bounds[None, :count], 0), axis=1)
-    slot = ((begin + rank // GROUP) * 4 + row) * GROUP + rank % GROUP
-    value = 1 + t + place * 256 + half * 65536
-    j = jnp.arange((listed // GROUP + count) * 4 * GROUP)
+    held = jnp.sum((key[:, None] == keys[None, :]).astype(jnp.int32), axis=0)
+    need = (held + GROUP - 1) // GROUP
+    total = jnp.sum(jnp.where(keys[None, :] // 4 == sources[:, None], need[None, :], 0), axis=1)
+    turns = (total + GROUPS - 1) // GROUPS
+    bounds = jnp.sum(jnp.where(sources[None, :] < jnp.arange(count + 1)[:, None], turns[None, :], 0), axis=1)
+    ahead = (keys[None, :] // 4 == keys[:, None] // 4) & (keys[None, :] < keys[:, None])
+    begin = jnp.sum(jnp.where(ahead, need[None, :], 0), axis=1)
+    begin = begin + GROUPS * jnp.sum(jnp.where(keys[:, None] // 4 == sources[None, :], bounds[None, :count], 0), axis=1)
+    group = jnp.sum(jnp.where(key[:, None] == keys[None, :], begin[None, :], 0), axis=1) + rank // GROUP
+    slot = group * GROUP + rank % GROUP
+    value = 1 + t + place * 256 + half * 65536 + row * 262144
+    most = listed // (GROUP * GROUPS) + (3 * count + 1) // 2
+    j = jnp.arange(most * GROUPS * GROUP)
     table = jnp.sum(jnp.where(slot[None, :] == j[:, None], value[None, :], 0), axis=1)
     return jnp.where(table > 0, table - 1, 2 * 65536).astype(jnp.int32), bounds.astype(jnp.int32)
 
 
 def add_tiles(table, first, last, adj, blocks, acc, masks):
     def step(s, carry):
-        for r in range(4):
+        products = []
+        for g in range(GROUPS):
             lhs, rhs = [], []
             for u in range(GROUP):
-                e = table[(s * 4 + r) * GROUP + u]
+                e = table[(s * GROUPS + g) * GROUP + u]
                 lhs.append(adj[e & 255])
-                rhs.append(blocks[(e >> 8) & 255] * masks[e >> 16])
-            acc[r] += jnp.dot(
-                jnp.concatenate(lhs, axis=1), jnp.concatenate(rhs, axis=0), preferred_element_type=jnp.float32
+                block = blocks[(e >> 8) & 255].reshape(8, 16, 128) * masks[(e >> 16) & 3][None]
+                rhs.append(block.reshape(128, 128))
+            products.append(
+                jnp.dot(jnp.concatenate(lhs, axis=1), jnp.concatenate(rhs, axis=0), preferred_element_type=jnp.float32)
             )
+        for g, product in enumerate(products):
+            acc[table[(s * GROUPS + g) * GROUP] >> 18] += product
         return carry
 
     lax.fori_loop(first, last, step, 0)
 
 
 def set_masks(masks):
-    lane = lax.broadcasted_iota(jnp.int32, (128, 128), 1)
+    lane = lax.broadcasted_iota(jnp.int32, (16, 128), 1)
     masks[0] = jnp.where(lane < 64, 1.0, 0.0).astype(masks.dtype)
     masks[1] = jnp.where(lane < 64, 0.0, 1.0).astype(masks.dtype)
-    masks[2] = jnp.zeros((128, 128), masks.dtype)
-    return lane
+    masks[2] = jnp.zeros((16, 128), masks.dtype)
+    return lax.broadcasted_iota(jnp.int32, (128, 128), 1)
 
 
 def pre_kernel(grad_out, relu_mask, out):
@@ -169,6 +180,7 @@
 
 def last_kernel(table, bounds, adj, *refs):
     *sources, before, features, weights, out, out_a, out_b, out_c, partial, acc, masks = refs
+    outs = (out, out_a, out_b, out_c)
     lane = set_masks(masks)
     acc[...] = before[...]
     add_sources(table, bounds, adj, sources, 6, acc, masks)
@@ -180,10 +192,10 @@
         partial[:, p, :] = jnp.where(low, product[p * 128 : p * 128 + 64], product[p * 128 + 64 : p * 128 + 128])
     for r in range(2):
         packed = jnp.where(lane < 64, agg[r], agg[r + 2]).astype(out.dtype)
-        for ref in (out, out_a, out_b, out_c):
+        for ref in outs:
             ref[pl.ds(r * 128, 128), :] = packed
-    for k, ref in enumerate((out_a, out_b, out_c)):
-        ref[pl.ds(256, 64), :] = weights[k]
+    for k, ref in enumerate(outs):
+        ref[pl.ds(256, 64), :] = weights[:, pl.ds(pl.multiple_of((lax.axis_index("yl") ^ (k >> 1)) * 128, 128), 128)]
 
 
 def call(kernel, table, bounds, adj, sources, others, out_shape, keep_acc, name):
@@ -196,9 +208,9 @@
         in_specs=[smem, smem, vmem] + [vmem] * len(sources) + [vmem] * len(others),
         out_specs=jax.tree.map(lambda _: vmem, out_shape),
         scratch_shapes=([pltpu.VMEM((4, 128, 128), jnp.float32)] if keep_acc else []) + [
-            pltpu.VMEM((3, 128, 128), jnp.bfloat16),
+            pltpu.VMEM((3, 16, 128), jnp.bfloat16),
         ],
-        compiler_params=pltpu.CompilerParams(vmem_limit_bytes=8 * 1024 * 1024),
+        compiler_params=pltpu.CompilerParams(vmem_limit_bytes=4 * 1024 * 1024),
         cost_estimate=pl.CostEstimate(flops=2 * 64 * 128 * 128 * 128, bytes_accessed=8 * 1024 * 1024, transcendentals=0),
         name=name,
     )(table, bounds, adj, *sources, *others)
@@ -210,30 +222,29 @@
 
 def body(adj_tiles, tile_index, grad_out, relu_mask, features, weight):
     position = lax.axis_index(ROWS)
-    slab = lax.axis_index(SLAB)
     source, place, half = where_held(tile_index[:, 1])
-    low, high, source = gather_early(masked(grad_out, relu_mask), source)
+    low, high, position = gather_early(masked(grad_out, relu_mask), position)
     forwarded, others = gather_near(low, high)
 
     tables = tile_table(tile_index[:, 0] - position * 4, source, place, half, 8)
     f_rows = features.reshape(512, 64, 4).transpose(2, 1, 0).reshape(256, 512)
-    w_parts = [lax.dynamic_slice_in_dim(weight, (slab ^ k) * 64, 64, 0) for k in range(4)]
-    w_sent = jnp.pad(jnp.stack(w_parts[1:]), ((0, 0), (0, 0), (0, 64)))
+    low, high, tables, f_rows = lax.optimization_barrier((low, high, tables, f_rows))
 
     sums = jax.ShapeDtypeStruct((4, 128, 128), jnp.float32)
     acc = call(first_kernel, *tables, adj_tiles, [low, high], [], sums, False, "early_tiles")
-    forwarded, acc, f_rows, w_sent = lax.optimization_barrier((forwarded, acc, f_rows, w_sent))
+    forwarded, acc = lax.optimization_barrier((forwarded, acc))
     far = gather_far(*forwarded)
     acc = call(middle_kernel, *tables, adj_tiles, forwarded + others, [acc], sums, False, "near_tiles")
     message = jax.ShapeDtypeStruct((320, 128), jnp.bfloat16)
-    outs = (jax.ShapeDtypeStruct((256, 128), jnp.bfloat16), message, message, message, jax.ShapeDtypeStruct((64, 2, 128), jnp.float32))
-    agg, *messages, partial = call(last_kernel, *tables, adj_tiles, far, [acc, f_rows, w_sent], outs, True, "far_tiles")
+    outs = (message, message, message, message, jax.ShapeDtypeStruct((64, 2, 128), jnp.float32))
+    *messages, partial = call(last_kernel, *tables, adj_tiles, far, [acc, f_rows, weight.T], outs, True, "far_tiles")
 
     pieces = lax.all_to_all(partial, ROWS, 0, 0, tiled=True)
-    arrived = [lax.ppermute(m, SLAB, pairs) for m, pairs in zip(messages, FLIPS)]
-    a_all = jnp.concatenate([halves(agg)] + [halves(m[:256]) for m in arrived], axis=1)
-    w_all = jnp.concatenate([w_parts[0]] + [m[256:, :64] for m in arrived], axis=1)
-    grad_input = jnp.einsum("rs,is->ri", a_all, w_all, preferred_element_type=jnp.float32).astype(jnp.bfloat16)
+    arrived = messages[:1] + [lax.ppermute(m, SLAB, pairs) for m, pairs in zip(messages[1:], FLIPS)]
+    a_all = jnp.concatenate([halves(m[:256]) for m in arrived], axis=1)
+    w_all = jnp.concatenate([m[256:] for m in arrived], axis=0)
+    w_all = jnp.where(lax.axis_index("core") == 0, w_all[:, :64], w_all[:, 64:])
+    grad_input = jnp.einsum("rs,si->ri", a_all, w_all, preferred_element_type=jnp.float32).astype(jnp.bfloat16)
     total = jnp.sum(pieces, axis=0)
     grad_weight = jnp.concatenate([total[p : p + 1, k : k + 64] for p in range(2) for k in (0, 64)], axis=0)
     return grad_input, grad_weight

time: 83.1 us -> 83.7 us (level)
  waiting for transfers between devices: 21.1 us -> 29.1 us
  local copies, waits for them, and re-layouts: 8.54 us -> 4.44 us
  Pallas kernels: 12.4 us -> 9.62 us
    all_to_all x1, waiting for transfers between devices: 4.51 us -> 10.7 us  [body(): pieces = lax.all_to_all(partial, ROWS, 0, 0, tiled=True)]
    ppermute x7, waiting for transfers between devices: 4.46 us -> 10.1 us  [from_axis(): return lax.ppermute(value, ALL, pairs)]
    ppermute x3, waiting for transfers between devices: 4.22 us -> 0.01 us  [body(): lax.ppermute(m, SLAB, pairs)]
    unnamed x6 -> x5, local copies, waits for them, and re-layouts: 6.75 us -> 3.88 us
    pallas_call x3, Pallas kernels: 10.8 us -> 7.94 us  [call(): pl.pallas_call(kernel, out_shape=out_shape, in_specs=[smem, smem, vmem] +...]
    ppermute x7, starting transfers between devices: 11.3 us -> 12.5 us  [from_axis(): return lax.ppermute(value, ALL, pairs)]
    dynamic_slice x4 -> x0, local copies, waits for them, and re-layouts: 1.16 us -> none  [body(): lax.dynamic_slice_in_dim(weight, (slab ^ k) * 64, 64, 0)]
    select_n x1, other arithmetic: 1.04 us -> 0.07 us  [gather_near(): jnp.where(odd, low, high)]
  transfers between devices with their start and end apart: 16 -> 16, of which waited for: 9 -> 10; matrix products, arithmetic and copies ran while one was open for 8% -> 6% of each run, Pallas kernels for 9% -> 6%
where the time goes in v6:
time: 83.7 us; the launch traced here: 83.1 us
  starting transfers between devices  34.5 us (41%)
  waiting for transfers between devices  29.1 us (35%)
  Pallas kernels  9.62 us (11%)
  local copies, waits for them, and re-layouts  4.44 us (5%)
  other arithmetic  3.64 us (4%)
  matrix products  1.02 us (1%)
  between operations  0.84 us (1%)
    ppermute x7, starting transfers between devices, from_axis(): return lax.ppermute(value, ALL, pairs)  12.5 us
    all_to_all x1, waiting for transfers between devices, body(): pieces = lax.all_to_all(partial, ROWS, 0, 0, tiled=True)  10.7 us
    ppermute x3, starting transfers between devices, from_rows(): return lax.ppermute(value, ALL, pairs)  10.2 us
    ppermute x7, waiting for transfers between devices, from_axis(): return lax.ppermute(value, ALL, pairs)  10.1 us
    pallas_call x3, Pallas kernels, call(): pl.pallas_call(kernel, out_shape=out_shape, in_specs=[smem, smem, vmem] +...  7.94 us
    all_to_all x1, starting transfers between devices, body(): pieces = lax.all_to_all(partial, ROWS, 0, 0, tiled=True)  7.61 us
    ppermute x3, waiting for transfers between devices, from_rows(): return lax.ppermute(value, ALL, pairs)  6.01 us
    unnamed x5, local copies, waits for them, and re-layouts  3.88 us
  transfers between devices with their start and end apart: 16, of which 10 were waited for; matrix products, arithmetic and copies ran while one was open for 6% of the time, Pallas kernels for 6%

profile of v6, /device:TPU:8, one launch (start us, length us, event | category | flops | bytes accessed | tf_op | source)
XLA Modules:
  0.0 83.1 jit_solution(7957821291491740919)
XLA Ops:
  0.6 1.7 %masked.1 = bf16[256,128]{1,0:T(8,128)(2,1)} custom-call(bf16[64,512]{1,0:T(8,128)(2,1)} %bitcast.48, s32[64,512]{1,0:T(8,128)} %bitcast.44), custom_call_target="tpu_custom_call" | custom-call | tf_op jit(solution)/shard_map/masked/pallas_call | solution.py:153
  2.3 7.2 %collective-permute-start.1 = (bf16[256,128]{1,0:T(8,128)(2,1)}, bf16[256,128]{1,0:T(8,128)(2,1)S(1)}, u32[]{:S(2)}, u32[]{:S(2)}) collective-permute-start(bf16[256,128]{1,0:T(8,128)(2,1)} %masked.1), channel_id=1, source_target_pairs={{128,0},{129,1},{130,2},{131,3},{132,4},{133,5},{134,6},{135,7},{1... | collective-permute-start | bytes 196616 | tf_op jit(solution)/shard_map/ppermute | solution.py:27
  9.5 1.7 %collective-permute-start.2 = (bf16[256,128]{1,0:T(8,128)(2,1)}, bf16[256,128]{1,0:T(8,128)(2,1)S(1)}, u32[]{:S(2)}, u32[]{:S(2)}) collective-permute-start(bf16[256,128]{1,0:T(8,128)(2,1)} %masked.1), channel_id=1, source_target_pairs={{144,0},{145,1},{146,2},{147,3},{148,4},{149,5},{150,6},{151,7},{1... | collective-permute-start | bytes 196616 | tf_op jit(solution)/shard_map/ppermute | solution.py:27
  11.2 1.2 %collective-permute-start = (bf16[256,128]{1,0:T(8,128)(2,1)}, bf16[256,128]{1,0:T(8,128)(2,1)S(1)}, u32[]{:S(2)}, u32[]{:S(2)}) collective-permute-start(bf16[256,128]{1,0:T(8,128)(2,1)} %masked.1), channel_id=1, source_target_pairs={{16,0},{17,1},{18,2},{19,3},{20,4},{21,5},{22,6},{23,7},{24,8},{25... | collective-permute-start | bytes 196616 | tf_op jit(solution)/shard_map/ppermute | solution.py:27
  12.5 0.8 fusion.32
  13.3 0.1 convert_reduce_fusion.1
  13.4 0.1 select_reduce_fusion.5
  13.5 0.2 select_reduce_fusion.2
  13.7 0.1 select_reduce_fusion.4.bounds
  13.8 0.1 select_reduce_fusion.3
  13.9 0.2 convert_reduce_fusion
  14.2 0.1 select_reduce_fusion.1
  14.3 2.9 %collective-permute-done = bf16[256,128]{1,0:T(8,128)(2,1)S(1)} collective-permute-done((bf16[256,128]{1,0:T(8,128)(2,1)}, bf16[256,128]{1,0:T(8,128)(2,1)S(1)}, u32[]{:S(2)}, u32[]{:S(2)}) %collective-permute-start) | collective-permute-done | bytes 65568 | tf_op jit(solution)/shard_map/ppermute | solution.py:27
  17.2 0.0 collective-permute-done.1
  17.2 3.1 %collective-permute-done.2 = bf16[256,128]{1,0:T(8,128)(2,1)S(1)} collective-permute-done((bf16[256,128]{1,0:T(8,128)(2,1)}, bf16[256,128]{1,0:T(8,128)(2,1)S(1)}, u32[]{:S(2)}, u32[]{:S(2)}) %collective-permute-start.2) | collective-permute-done | bytes 65568 | tf_op jit(solution)/shard_map/ppermute | solution.py:27
  20.3 0.9 %fusion.38 = (bf16[1,4,256,128]{3,2,1,0:T(8,128)(2,1)S(1)}, bf16[4,256,128]{2,1,0:T(8,128)(2,1)S(1)}) fusion(bf16[1,256,128]{2,1,0:T(8,128)(2,1)S(1)} %bitcast.46, bf16[1,256,128]{2,1,0:T(8,128)(2,1)S(1)} %bitcast.45, bf16[1,256,128]{2,1,0:T(8,128)(2,1)S(1)} %bitcast.47, bf16[1,256,128]{2,1,0:T(8,128)(2,1)} %bitcast.40), kind=kLoop, calls=%fused_computation.162 | loop fusion | flops 393216 | bytes 786432 | tf_op jit(solution)/shard_map/stack | solution.py:58
  21.2 1.6 %collective-permute-start.4 = (bf16[4,256,128]{2,1,0:T(8,128)(2,1)S(1)}, bf16[4,256,128]{2,1,0:T(8,128)(2,1)S(1)}, u32[]{:S(2)}, u32[]{:S(2)}) collective-permute-start(bf16[4,256,128]{2,1,0:T(8,128)(2,1)S(1)} %get-tuple-element.44), channel_id=1, source_target_pairs={{12,0},{225,1},{14,2},{227,3},{0,4},{229,5},{2,6},{231,7},{4,8},{2... | collective-permute-start | bytes 786440 | tf_op jit(solution)/shard_map/ppermute | solution.py:37
  22.7 2.7 %collective-permute-start.5 = (bf16[4,256,128]{2,1,0:T(8,128)(2,1)S(1)}, bf16[4,256,128]{2,1,0:T(8,128)(2,1)S(1)}, u32[]{:S(2)}, u32[]{:S(2)}) collective-permute-start(bf16[4,256,128]{2,1,0:T(8,128)(2,1)S(1)} %get-tuple-element.44), channel_id=1, source_target_pairs={{8,0},{65,1},{10,2},{67,3},{12,4},{69,5},{14,6},{71,7},{0,8},{73,9... | collective-permute-start | bytes 786440 | tf_op jit(solution)/shard_map/ppermute | solution.py:37
  25.5 1.4 %collective-permute-start.3 = (bf16[4,256,128]{2,1,0:T(8,128)(2,1)S(1)}, bf16[4,256,128]{2,1,0:T(8,128)(2,1)S(1)}, u32[]{:S(2)}, u32[]{:S(2)}) collective-permute-start(bf16[4,256,128]{2,1,0:T(8,128)(2,1)S(1)} %get-tuple-element.44), channel_id=1, source_target_pairs={{4,0},{33,1},{6,2},{35,3},{8,4},{37,5},{10,6},{39,7},{12,8},{41,9}... | collective-permute-start | bytes 786440 | tf_op jit(solution)/shard_map/ppermute | solution.py:37
  26.9 1.1 %copy.11 = bf16[512,256]{0,1:T(8,128)(2,1)S(1)} copy(bf16[512,256]{1,0:T(8,128)(2,1)} %param.10) | data formatting | bytes 524288 | tf_op args[4]
  28.0 0.1 reshape.419
  28.1 0.1 select_reduce_fusion
  28.3 0.6 collective-permute-done.4
  28.8 4.3 %collective-permute-done.5 = bf16[4,256,128]{2,1,0:T(8,128)(2,1)S(1)} collective-permute-done((bf16[4,256,128]{2,1,0:T(8,128)(2,1)S(1)}, bf16[4,256,128]{2,1,0:T(8,128)(2,1)S(1)}, u32[]{:S(2)}, u32[]{:S(2)}) %collective-permute-start.5) | collective-permute-done | bytes 262176 | tf_op jit(solution)/shard_map/ppermute | solution.py:37
  33.2 0.1 pad_maximum_fusion.1
  33.2 0.8 collective-permute-start.7
  34.0 0.0 collective-permute-done.3
  34.0 0.1 pad_maximum_fusion
  34.0 2.6 %collective-permute-start.6 = (bf16[2,4,256,128]{3,2,1,0:T(8,128)(2,1)S(1)}, bf16[2,4,256,128]{3,2,1,0:T(8,128)(2,1)S(1)}, u32[]{:S(2)}, u32[]{:S(2)}) collective-permute-start(bf16[2,4,256,128]{3,2,1,0:T(8,128)(2,1)S(1)} %pad_maximum_fusion), channel_id=1, source_target_pairs={{32,0},{5,1},{34,2},{7,3},{36,4},{9,5},{38,6},{11,7},{40,8},{13,9}... | collective-permute-start | bytes 1572872 | tf_op jit(solution)/shard_map/ppermute | solution.py:37
  36.7 0.1 broadcast_select_fusion
  36.7 0.1 collective-permute-start.10
  36.8 1.8 %collective-permute-start.11 = (bf16[2,4,256,128]{3,2,1,0:T(8,128)(2,1)S(1)}, bf16[2,4,256,128]{3,2,1,0:T(8,128)(2,1)S(1)}, u32[]{:S(2)}, u32[]{:S(2)}) collective-permute-start(bf16[2,4,256,128]{3,2,1,0:T(8,128)(2,1)S(1)} %get-tuple-element.41), channel_id=1, source_target_pairs={{224,0},{13,1},{226,2},{15,3},{228,4},{9,5},{230,6},{11,7},{232,8}... | collective-permute-start | bytes 1572872 | tf_op jit(solution)/shard_map/ppermute | solution.py:47
  38.6 0.0 copy-start
  38.6 2.8 %copy-done = bf16[192,128,128]{2,1,0:T(8,128)(2,1)S(1)} copy-done((bf16[192,128,128]{2,1,0:T(8,128)(2,1)S(1)}, bf16[192,128,128]{2,1,0:T(8,128)(2,1)}, u32[]{:S(2)}) %copy-start) | copy-done | bytes 6291480
  41.4 1.8 %early_tiles.1.refs_4_ = f32[4,128,128]{2,1,0:T(8,128)S(1)} custom-call(s32[384]{0:T(512)S(1)} %add_select_fusion.table, s32[9]{0:T(128)S(1)} %select_reduce_fusion.4.bounds, bf16[192,128,128]{2,1,0:T(8,128)(2,1)S(1)} %copy-done, bf16[16,128,128]{2,1,0:T(8,128)(2,1)S(1)} %bitcast.29, bf16[16,128,128]{2,1,0:T(8,128)(2,1)S(1)} %bitcast.28), custom_call_target="tpu_custom_call" | custom-call | flops 268435456 | bytes 8388608 | tf_op jit(solution)/shard_map/early_tiles/pallas_call | solution.py:205
  43.3 0.0 copy-start.1
  43.3 0.4 collective-permute-done.7
  43.7 0.0 collective-permute-done.6
  43.7 3.4 %collective-permute-start.8 = (bf16[2,4,256,128]{3,2,1,0:T(8,128)(2,1)S(1)}, bf16[2,4,256,128]{3,2,1,0:T(8,128)(2,1)S(1)}, u32[]{:S(2)}, u32[]{:S(2)}) collective-permute-start(bf16[2,4,256,128]{3,2,1,0:T(8,128)(2,1)S(1)} %collective-permute-done.6), channel_id=1, source_target_pairs={{32,0},{5,1},{34,2},{7,3},{36,4},{9,5},{38,6},{11,7},{40,8},{13,9}... | collective-permute-start | bytes 1572872 | tf_op jit(solution)/shard_map/ppermute | solution.py:37
  47.1 0.0 collective-permute-start.9
  47.1 1.8 %collective-permute-done.10 = bf16[2,4,256,128]{3,2,1,0:T(8,128)(2,1)S(1)} collective-permute-done((bf16[2,4,256,128]{3,2,1,0:T(8,128)(2,1)S(1)}, bf16[2,4,256,128]{3,2,1,0:T(8,128)(2,1)S(1)}, u32[]{:S(2)}, u32[]{:S(2)}) %collective-permute-start.10) | collective-permute-done | bytes 524320 | tf_op jit(solution)/shard_map/ppermute | solution.py:47
  48.9 0.4 collective-permute-done.11
  49.3 3.3 %near_tiles.1.refs_2_ = f32[4,128,128]{2,1,0:T(8,128)S(1)} custom-call(s32[384]{0:T(512)S(1)} %add_select_fusion.table, s32[9]{0:T(128)S(1)} %select_reduce_fusion.4.bounds, bf16[192,128,128]{2,1,0:T(8,128)(2,1)S(1)} %copy-done, bf16[16,128,128]{2,1,0:T(8,128)(2,1)S(1)} %bitcast.32, bf16[16,128,128]{2,1,0:T(8,128)(2,1)S(1)} %bitcast.31, ...), custom_call_target="tpu_custom_call" | custom-call | flops 268435456 | bytes 8388608 | tf_op jit(solution)/shard_map/near_tiles/pallas_call | solution.py:205
  52.7 2.0 %collective-permute-done.8 = bf16[2,4,256,128]{3,2,1,0:T(8,128)(2,1)S(1)} collective-permute-done((bf16[2,4,256,128]{3,2,1,0:T(8,128)(2,1)S(1)}, bf16[2,4,256,128]{3,2,1,0:T(8,128)(2,1)S(1)}, u32[]{:S(2)}, u32[]{:S(2)}) %collective-permute-start.8) | collective-permute-done | bytes 524320 | tf_op jit(solution)/shard_map/ppermute | solution.py:37
  54.6 2.8 %collective-permute-done.9 = bf16[2,4,256,128]{3,2,1,0:T(8,128)(2,1)S(1)} collective-permute-done((bf16[2,4,256,128]{3,2,1,0:T(8,128)(2,1)S(1)}, bf16[2,4,256,128]{3,2,1,0:T(8,128)(2,1)S(1)}, u32[]{:S(2)}, u32[]{:S(2)}) %collective-permute-start.9) | collective-permute-done | bytes 524320 | tf_op jit(solution)/shard_map/ppermute | solution.py:37
  57.5 0.0 copy-done.1
  57.5 2.8 %far_tiles.1 = (bf16[320,128]{1,0:T(8,128)(2,1)S(1)}, bf16[320,128]{1,0:T(8,128)(2,1)S(1)}, bf16[320,128]{1,0:T(8,128)(2,1)S(1)}, bf16[320,128]{1,0:T(8,128)(2,1)S(1)}, f32[64,2,128]{2,1,0:T(2,128)}) custom-call(s32[384]{0:T(512)S(1)} %add_select_fusion.table, s32[9]{0:T(128)S(1)} %select_reduce_fusion.4.bounds, bf16[192,128,128]{2,1,0:T(8,128)(2,1)S(1)} %copy-done, ...), custom_call_target="tpu_custom_call" | custom-call | flops 268435456 | bytes 8388608 | tf_op jit(solution)/shard_map/far_tiles/pallas_call | solution.py:205
  60.2 0.0 collective-permute-start.12
  60.2 2.2 %collective-permute-start.13 = (bf16[320,128]{1,0:T(8,128)(2,1)S(1)}, bf16[320,128]{1,0:T(8,128)(2,1)S(1)}, u32[]{:S(2)}, u32[]{:S(2)}) collective-permute-start(bf16[320,128]{1,0:T(8,128)(2,1)S(1)} %get-tuple-element.33), channel_id=1, source_target_pairs={{0,2},{2,0},{1,3},{3,1},{4,6},{6,4},{5,7},{7,5},{8,10},{10,8},{9,1... | collective-permute-start | bytes 245768 | tf_op jit(solution)/shard_map/ppermute | solution.py:243
  62.4 0.1 collective-permute-start.14
  62.6 0.1 fusion.39
  62.7 7.6 %all-to-all-start = ((f32[64,2,128]{2,1,0:T(2,128)}), f32[64,2,128]{2,1,0:T(2,128)S(1)}, u32[]{:S(2)}, u32[]{:S(2)}) async-start(f32[64,2,128]{2,1,0:T(2,128)} %get-tuple-element.35), calls=%async_computation | async-start | bytes 131072 | tf_op jit(solution)/shard_map/all_to_all | solution.py:242
  70.3 0.0 collective-permute-done.12
  70.3 0.0 collective-permute-done.13
  70.3 0.0 collective-permute-done.14
  70.4 0.1 fusion.40
  70.5 0.1 fusion.41
  70.6 0.1 fusion.42
  70.6 1.0 %convolution_convert_fusion = bf16[512,64]{0,1:T(8,128)(2,1)} fusion(bf16[256,64]{1,0:T(8,128)(2,1)S(1)} %get-tuple-element.52, bf16[256,64]{1,0:T(8,128)(2,1)S(1)} %get-tuple-element.51, bf16[256,64]{1,0:T(8,128)(2,1)S(1)} %get-tuple-element.50, bf16[256,64]{1,0:T(8,128)(2,1)S(1)} %get-tuple-element.49, bf16[256,64]{1,0:T(8,128)(2,1)S(1)} %get-tuple-element.48, ...), kind=kOutput, calls=%fused_computation | convolution fusion | flops 18923520 | bytes 720897 | tf_op jit(solution)/shard_map/rs,si->ri/dot_general | solution.py:247
  71.7 10.7 %all-to-all-done = f32[64,2,128]{2,1,0:T(2,128)S(1)} async-done(((f32[64,2,128]{2,1,0:T(2,128)}), f32[64,2,128]{2,1,0:T(2,128)S(1)}, u32[]{:S(2)}, u32[]{:S(2)}) %all-to-all-start) | async-done | bytes 65568 | tf_op jit(solution)/shard_map/all_to_all | solution.py:242
  82.4 0.1 reduce_sum.89
  82.4 0.1 fusion.43
  82.5 0.6 pad_maximum_fusion.4
  (13 shorter events, 0.2 us)
Async XLA Ops:
  2.3 14.9 %collective-permute-start.1 = (bf16[256,128]{1,0:T(8,128)(2,1)}, bf16[256,128]{1,0:T(8,128)(2,1)S(1)}, u32[]{:S(2)}, u32[]{:S(2)}) collective-permute-start(bf16[256,128]{1,0:T(8,128)(2,1)} %masked.1), channel_id=1, source_target_pairs={{128,0},{129,1},{130,2},{131,3},{132,4},{133,5},{134,6},{135,7},{1... | collective-permute-start | bytes 196616 | tf_op jit(solution)/shard_map/ppermute | solution.py:27
  9.5 10.8 %collective-permute-start.2 = (bf16[256,128]{1,0:T(8,128)(2,1)}, bf16[256,128]{1,0:T(8,128)(2,1)S(1)}, u32[]{:S(2)}, u32[]{:S(2)}) collective-permute-start(bf16[256,128]{1,0:T(8,128)(2,1)} %masked.1), channel_id=1, source_target_pairs={{144,0},{145,1},{146,2},{147,3},{148,4},{149,5},{150,6},{151,7},{1... | collective-permute-start | bytes 196616 | tf_op jit(solution)/shard_map/ppermute | solution.py:27
  11.2 6.0 %collective-permute-start = (bf16[256,128]{1,0:T(8,128)(2,1)}, bf16[256,128]{1,0:T(8,128)(2,1)S(1)}, u32[]{:S(2)}, u32[]{:S(2)}) collective-permute-start(bf16[256,128]{1,0:T(8,128)(2,1)} %masked.1), channel_id=1, source_target_pairs={{16,0},{17,1},{18,2},{19,3},{20,4},{21,5},{22,6},{23,7},{24,8},{25... | collective-permute-start | bytes 196616 | tf_op jit(solution)/shard_map/ppermute | solution.py:27
  21.2 7.7 %collective-permute-start.4 = (bf16[4,256,128]{2,1,0:T(8,128)(2,1)S(1)}, bf16[4,256,128]{2,1,0:T(8,128)(2,1)S(1)}, u32[]{:S(2)}, u32[]{:S(2)}) collective-permute-start(bf16[4,256,128]{2,1,0:T(8,128)(2,1)S(1)} %get-tuple-element.44), channel_id=1, source_target_pairs={{12,0},{225,1},{14,2},{227,3},{0,4},{229,5},{2,6},{231,7},{4,8},{2... | collective-permute-start | bytes 786440 | tf_op jit(solution)/shard_map/ppermute | solution.py:37
  22.7 10.4 %collective-permute-start.5 = (bf16[4,256,128]{2,1,0:T(8,128)(2,1)S(1)}, bf16[4,256,128]{2,1,0:T(8,128)(2,1)S(1)}, u32[]{:S(2)}, u32[]{:S(2)}) collective-permute-start(bf16[4,256,128]{2,1,0:T(8,128)(2,1)S(1)} %get-tuple-element.44), channel_id=1, source_target_pairs={{8,0},{65,1},{10,2},{67,3},{12,4},{69,5},{14,6},{71,7},{0,8},{73,9... | collective-permute-start | bytes 786440 | tf_op jit(solution)/shard_map/ppermute | solution.py:37
  25.5 8.5 %collective-permute-start.3 = (bf16[4,256,128]{2,1,0:T(8,128)(2,1)S(1)}, bf16[4,256,128]{2,1,0:T(8,128)(2,1)S(1)}, u32[]{:S(2)}, u32[]{:S(2)}) collective-permute-start(bf16[4,256,128]{2,1,0:T(8,128)(2,1)S(1)} %get-tuple-element.44), channel_id=1, source_target_pairs={{4,0},{33,1},{6,2},{35,3},{8,4},{37,5},{10,6},{39,7},{12,8},{41,9}... | collective-permute-start | bytes 786440 | tf_op jit(solution)/shard_map/ppermute | solution.py:37
  33.2 10.5 %collective-permute-start.7 = (bf16[2,4,256,128]{3,2,1,0:T(8,128)(2,1)S(1)}, bf16[2,4,256,128]{3,2,1,0:T(8,128)(2,1)S(1)}, u32[]{:S(2)}, u32[]{:S(2)}) collective-permute-start(bf16[2,4,256,128]{3,2,1,0:T(8,128)(2,1)S(1)} %pad_maximum_fusion.1), channel_id=1, source_target_pairs={{224,0},{13,1},{226,2},{15,3},{228,4},{1,5},{230,6},{3,7},{232,8},... | collective-permute-start | bytes 1572872 | tf_op jit(solution)/shard_map/ppermute | solution.py:37
  34.0 9.7 %collective-permute-start.6 = (bf16[2,4,256,128]{3,2,1,0:T(8,128)(2,1)S(1)}, bf16[2,4,256,128]{3,2,1,0:T(8,128)(2,1)S(1)}, u32[]{:S(2)}, u32[]{:S(2)}) collective-permute-start(bf16[2,4,256,128]{3,2,1,0:T(8,128)(2,1)S(1)} %pad_maximum_fusion), channel_id=1, source_target_pairs={{32,0},{5,1},{34,2},{7,3},{36,4},{9,5},{38,6},{11,7},{40,8},{13,9}... | collective-permute-start | bytes 1572872 | tf_op jit(solution)/shard_map/ppermute | solution.py:37
  36.7 12.2 %collective-permute-start.10 = (bf16[2,4,256,128]{3,2,1,0:T(8,128)(2,1)S(1)}, bf16[2,4,256,128]{3,2,1,0:T(8,128)(2,1)S(1)}, u32[]{:S(2)}, u32[]{:S(2)}) collective-permute-start(bf16[2,4,256,128]{3,2,1,0:T(8,128)(2,1)S(1)} %get-tuple-element.42), channel_id=1, source_target_pairs={{32,0},{5,1},{34,2},{7,3},{36,4},{1,5},{38,6},{3,7},{40,8},{13,9},... | collective-permute-start | bytes 1572872 | tf_op jit(solution)/shard_map/ppermute | solution.py:47
  36.8 12.5 %collective-permute-start.11 = (bf16[2,4,256,128]{3,2,1,0:T(8,128)(2,1)S(1)}, bf16[2,4,256,128]{3,2,1,0:T(8,128)(2,1)S(1)}, u32[]{:S(2)}, u32[]{:S(2)}) collective-permute-start(bf16[2,4,256,128]{3,2,1,0:T(8,128)(2,1)S(1)} %get-tuple-element.41), channel_id=1, source_target_pairs={{224,0},{13,1},{226,2},{15,3},{228,4},{9,5},{230,6},{11,7},{232,8}... | collective-permute-start | bytes 1572872 | tf_op jit(solution)/shard_map/ppermute | solution.py:47
  38.6 2.8 %copy-start = (bf16[192,128,128]{2,1,0:T(8,128)(2,1)S(1)}, bf16[192,128,128]{2,1,0:T(8,128)(2,1)}, u32[]{:S(2)}) copy-start(bf16[192,128,128]{2,1,0:T(8,128)(2,1)} %adj.5) | copy-start | bytes 18874372
  43.3 14.2 %copy-start.1 = (bf16[256,64]{0,1:T(8,128)(2,1)S(1)}, bf16[256,64]{0,1:T(8,128)(2,1)}, u32[]{:S(2)}) copy-start(bf16[256,64]{0,1:T(8,128)(2,1)} %param.11) | copy-start | bytes 98308
  43.7 10.9 %collective-permute-start.8 = (bf16[2,4,256,128]{3,2,1,0:T(8,128)(2,1)S(1)}, bf16[2,4,256,128]{3,2,1,0:T(8,128)(2,1)S(1)}, u32[]{:S(2)}, u32[]{:S(2)}) collective-permute-start(bf16[2,4,256,128]{3,2,1,0:T(8,128)(2,1)S(1)} %collective-permute-done.6), channel_id=1, source_target_pairs={{32,0},{5,1},{34,2},{7,3},{36,4},{9,5},{38,6},{11,7},{40,8},{13,9}... | collective-permute-start | bytes 1572872 | tf_op jit(solution)/shard_map/ppermute | solution.py:37
  47.1 10.4 %collective-permute-start.9 = (bf16[2,4,256,128]{3,2,1,0:T(8,128)(2,1)S(1)}, bf16[2,4,256,128]{3,2,1,0:T(8,128)(2,1)S(1)}, u32[]{:S(2)}, u32[]{:S(2)}) collective-permute-start(bf16[2,4,256,128]{3,2,1,0:T(8,128)(2,1)S(1)} %collective-permute-done.7), channel_id=1, source_target_pairs={{224,0},{13,1},{226,2},{15,3},{228,4},{1,5},{230,6},{3,7},{232,8},... | collective-permute-start | bytes 1572872 | tf_op jit(solution)/shard_map/ppermute | solution.py:37
  60.2 10.1 %collective-permute-start.12 = (bf16[320,128]{1,0:T(8,128)(2,1)S(1)}, bf16[320,128]{1,0:T(8,128)(2,1)S(1)}, u32[]{:S(2)}, u32[]{:S(2)}) collective-permute-start(bf16[320,128]{1,0:T(8,128)(2,1)S(1)} %get-tuple-element.32), channel_id=1, source_target_pairs={{0,1},{1,0},{2,3},{3,2},{4,5},{5,4},{6,7},{7,6},{8,9},{9,8},{10,11... | collective-permute-start | bytes 245768 | tf_op jit(solution)/shard_map/ppermute | solution.py:243
  60.2 10.1 %collective-permute-start.13 = (bf16[320,128]{1,0:T(8,128)(2,1)S(1)}, bf16[320,128]{1,0:T(8,128)(2,1)S(1)}, u32[]{:S(2)}, u32[]{:S(2)}) collective-permute-start(bf16[320,128]{1,0:T(8,128)(2,1)S(1)} %get-tuple-element.33), channel_id=1, source_target_pairs={{0,2},{2,0},{1,3},{3,1},{4,6},{6,4},{5,7},{7,5},{8,10},{10,8},{9,1... | collective-permute-start | bytes 245768 | tf_op jit(solution)/shard_map/ppermute | solution.py:243
  62.4 7.9 %collective-permute-start.14 = (bf16[320,128]{1,0:T(8,128)(2,1)S(1)}, bf16[320,128]{1,0:T(8,128)(2,1)S(1)}, u32[]{:S(2)}, u32[]{:S(2)}) collective-permute-start(bf16[320,128]{1,0:T(8,128)(2,1)S(1)} %get-tuple-element.34), channel_id=1, source_target_pairs={{0,3},{3,0},{1,2},{2,1},{4,7},{7,4},{5,6},{6,5},{8,11},{11,8},{9,1... | collective-permute-start | bytes 245768 | tf_op jit(solution)/shard_map/ppermute | solution.py:243
  62.7 19.7 %all-to-all-start = ((f32[64,2,128]{2,1,0:T(2,128)}), f32[64,2,128]{2,1,0:T(2,128)S(1)}, u32[]{:S(2)}, u32[]{:S(2)}) async-start(f32[64,2,128]{2,1,0:T(2,128)} %get-tuple-element.35), calls=%async_computation | async-start | bytes 131072 | tf_op jit(solution)/shard_map/all_to_all | solution.py:242

commit v7 on v6

--- a/solution.py
+++ b/solution.py
@@ -11,7 +11,7 @@
 ALL = ROWS + SLAB
 GROUP = 4
 GROUPS = 4
-FLIPS = ([(0, 1), (1, 0), (2, 3), (3, 2)], [(0, 2), (2, 0), (1, 3), (3, 1)], [(0, 3), (3, 0), (1, 2), (2, 1)])
+OTHER = [(0, 1), (1, 0)]
 
 
 def device(z, y, x, l, c):
@@ -52,11 +52,13 @@
 
 
 def gather_early(packed, position):
-    far_y, far = from_rows(packed, dz=4, dy=1), from_rows(packed, dz=4)
+    far, far_y = from_rows(packed, dz=4), from_rows(packed, dz=4, dy=1)
     again, position = lax.optimization_barrier((packed, position))
-    four = jnp.stack([packed, from_rows(again, dy=1), far, far_y])
-    low = jnp.stack([four, from_axis(four, False, 1)])
-    high = jnp.stack([from_axis(four, False, -1), from_axis(four, False, 2)])
+    near_y = from_rows(again, dy=1)
+    pairs = [jnp.stack([packed, far]), jnp.stack([near_y, far_y])]
+    one, back, two = [[from_axis(pair, False, step) for pair in pairs] for step in (1, -1, 2)]
+    low = jnp.stack(pairs + one).reshape(2, 4, 256, 128)
+    high = jnp.stack(back + two).reshape(2, 4, 256, 128)
     return low, high, position
 
 
@@ -83,7 +85,7 @@
     a = jnp.where(ring == 2, 3, jnp.where(ring == 3, 2, ring))
     upper = (dz >= 3) & (dz <= 6)
     swapped = jnp.where(core == 0, (late == 2) & (a >= 2), (ring == 2) & (lax.axis_index("z") % 2 == 1))
-    e = dy + 2 * (upper != swapped).astype(jnp.int32)
+    e = 2 * dy + (upper != swapped).astype(jnp.int32)
     high, odd = a // 2, odd_place().astype(jnp.int32)
     after = jnp.where(high == 0, 2, 4 + odd)
     before = jnp.where(high == 1, 3, 5 - odd)
@@ -179,8 +181,7 @@
 
 
 def last_kernel(table, bounds, adj, *refs):
-    *sources, before, features, weights, out, out_a, out_b, out_c, partial, acc, masks = refs
-    outs = (out, out_a, out_b, out_c)
+    *sources, before, features, weights, out, partial, acc, masks = refs
     lane = set_masks(masks)
     acc[...] = before[...]
     add_sources(table, bounds, adj, sources, 6, acc, masks)
@@ -191,11 +192,10 @@
     for p in range(2):
         partial[:, p, :] = jnp.where(low, product[p * 128 : p * 128 + 64], product[p * 128 + 64 : p * 128 + 128])
     for r in range(2):
-        packed = jnp.where(lane < 64, agg[r], agg[r + 2]).astype(out.dtype)
-        for ref in outs:
-            ref[pl.ds(r * 128, 128), :] = packed
-    for k, ref in enumerate(outs):
-        ref[pl.ds(256, 64), :] = weights[:, pl.ds(pl.multiple_of((lax.axis_index("yl") ^ (k >> 1)) * 128, 128), 128)]
+        out[pl.ds(r * 128, 128), :] = jnp.where(lane < 64, agg[r], agg[r + 2]).astype(out.dtype)
+    for k in range(2):
+        lanes = pl.multiple_of((lax.axis_index("yl") ^ (1 - k)) * 128, 128)
+        out[pl.ds(256 + k * 64, 64), :] = weights[:, pl.ds(lanes, 128)]
 
 
 def call(kernel, table, bounds, adj, sources, others, out_shape, keep_acc, name):
@@ -235,14 +235,15 @@
     forwarded, acc = lax.optimization_barrier((forwarded, acc))
     far = gather_far(*forwarded)
     acc = call(middle_kernel, *tables, adj_tiles, forwarded + others, [acc], sums, False, "near_tiles")
-    message = jax.ShapeDtypeStruct((320, 128), jnp.bfloat16)
-    outs = (message, message, message, message, jax.ShapeDtypeStruct((64, 2, 128), jnp.float32))
-    *messages, partial = call(last_kernel, *tables, adj_tiles, far, [acc, f_rows, weight.T], outs, True, "far_tiles")
-
+    outs = (jax.ShapeDtypeStruct((384, 128), jnp.bfloat16), jax.ShapeDtypeStruct((64, 2, 128), jnp.float32))
+    own, partial = call(last_kernel, *tables, adj_tiles, far, [acc, f_rows, weight.T], outs, True, "far_tiles")
+
+    other_core = lax.ppermute(own, "core", OTHER)
     pieces = lax.all_to_all(partial, ROWS, 0, 0, tiled=True)
-    arrived = messages[:1] + [lax.ppermute(m, SLAB, pairs) for m, pairs in zip(messages[1:], FLIPS)]
+    other_chip = lax.ppermute(jnp.stack([own[:320], other_core[:320]]), "yl", OTHER)
+    arrived = [own, other_core, other_chip[0], other_chip[1]]
     a_all = jnp.concatenate([halves(m[:256]) for m in arrived], axis=1)
-    w_all = jnp.concatenate([m[256:] for m in arrived], axis=0)
+    w_all = jnp.concatenate([own[320:], other_core[320:], other_chip[0, 256:], other_chip[1, 256:]], axis=0)
     w_all = jnp.where(lax.axis_index("core") == 0, w_all[:, :64], w_all[:, 64:])
     grad_input = jnp.einsum("rs,si->ri", a_all, w_all, preferred_element_type=jnp.float32).astype(jnp.bfloat16)
     total = jnp.sum(pieces, axis=0)

time: 83.7 us -> 85.2 us (1.018)
  starting transfers between devices: 34.5 us -> 41.6 us
  waiting for transfers between devices: 29.1 us -> 22.4 us
    ppermute x7 -> x10, starting transfers between devices: 12.5 us -> 17.9 us  [from_axis(): return lax.ppermute(value, ALL, pairs)]
    ppermute x3, waiting for transfers between devices: 6.01 us -> 2.94 us  [from_rows(): return lax.ppermute(value, ALL, pairs)]
    ppermute x2, starting transfers between devices: 1.89 us -> 4.27 us  [exchange(): return lax.ppermute(value, ALL, pairs)]
    ppermute x7 -> x10, waiting for transfers between devices: 10.1 us -> 7.96 us  [from_axis(): return lax.ppermute(value, ALL, pairs)]
    ppermute x2, waiting for transfers between devices: 2.24 us -> 1.21 us  [exchange(): return lax.ppermute(value, ALL, pairs)]
    ppermute x3 -> x2, starting transfers between devices: 2.33 us -> 1.61 us  [the longest x1 1.6 us: body(): lax.ppermute(jnp.stack([own[:320], other_core[:320]]), 'yl', OTHER)]
  transfers between devices with their start and end apart: 16 -> 18, of which waited for: 10 -> 7; matrix products, arithmetic and copies ran while one was open for 6% -> 6% of each run, Pallas kernels for 6% -> 6%
where the time goes in v7:
time: 85.2 us; the launch traced here: 83.9 us
  starting transfers between devices  41.6 us (49%)
  waiting for transfers between devices  22.4 us (26%)
  Pallas kernels  9.84 us (12%)
  local copies, waits for them, and re-layouts  4.46 us (5%)
  other arithmetic  3.68 us (4%)
  matrix products  1.02 us (1%)
  between operations  0.87 us (1%)
    ppermute x10, starting transfers between devices, from_axis(): return lax.ppermute(value, ALL, pairs)  17.9 us
    all_to_all x1, waiting for transfers between devices, body(): pieces = lax.all_to_all(partial, ROWS, 0, 0, tiled=True)  10.3 us
    ppermute x3, starting transfers between devices, from_rows(): return lax.ppermute(value, ALL, pairs)  10.2 us
    pallas_call x3, Pallas kernels, call(): pl.pallas_call(kernel, out_shape=out_shape, in_specs=[smem, smem, vmem] +...  8.16 us
    ppermute x10, waiting for transfers between devices, from_axis(): return lax.ppermute(value, ALL, pairs)  7.96 us
    all_to_all x1, starting transfers between devices, body(): pieces = lax.all_to_all(partial, ROWS, 0, 0, tiled=True)  7.67 us
    ppermute x2, starting transfers between devices, exchange(): return lax.ppermute(value, ALL, pairs)  4.27 us
    unnamed x5, local copies, waits for them, and re-layouts  3.88 us
  transfers between devices with their start and end apart: 18, of which 7 were waited for; matrix products, arithmetic and copies ran while one was open for 6% of the time, Pallas kernels for 6%

profile of v7, /device:TPU:8, one launch (start us, length us, event | category | flops | bytes accessed | tf_op | source)
XLA Modules:
  0.0 83.9 jit_solution(2964571387621653065)
XLA Ops:
  0.6 1.7 %masked.1 = bf16[256,128]{1,0:T(8,128)(2,1)} custom-call(bf16[64,512]{1,0:T(8,128)(2,1)} %bitcast.71, s32[64,512]{1,0:T(8,128)} %bitcast.64), custom_call_target="tpu_custom_call" | custom-call | tf_op jit(solution)/shard_map/masked/pallas_call | solution.py:155
  2.3 8.9 %collective-permute-start.2 = (bf16[256,128]{1,0:T(8,128)(2,1)}, bf16[256,128]{1,0:T(8,128)(2,1)S(1)}, u32[]{:S(2)}, u32[]{:S(2)}) collective-permute-start(bf16[256,128]{1,0:T(8,128)(2,1)} %masked.1), channel_id=1, source_target_pairs={{144,0},{145,1},{146,2},{147,3},{148,4},{149,5},{150,6},{151,7},{1... | collective-permute-start | bytes 196616 | tf_op jit(solution)/shard_map/ppermute | solution.py:27
  11.2 0.0 collective-permute-start
  11.2 1.2 %collective-permute-start.1 = (bf16[256,128]{1,0:T(8,128)(2,1)}, bf16[256,128]{1,0:T(8,128)(2,1)S(1)}, u32[]{:S(2)}, u32[]{:S(2)}) collective-permute-start(bf16[256,128]{1,0:T(8,128)(2,1)} %masked.1), channel_id=1, source_target_pairs={{16,0},{17,1},{18,2},{19,3},{20,4},{21,5},{22,6},{23,7},{24,8},{25... | collective-permute-start | bytes 196616 | tf_op jit(solution)/shard_map/ppermute | solution.py:27
  12.5 0.8 fusion.33
  13.3 0.1 convert_reduce_fusion.1
  13.4 0.1 select_reduce_fusion.5
  13.5 0.2 select_reduce_fusion.2
  13.7 0.1 select_reduce_fusion.4.bounds
  13.8 0.1 select_reduce_fusion.3
  13.9 0.2 convert_reduce_fusion
  14.2 0.1 select_reduce_fusion.1
  14.3 2.9 %collective-permute-done.1 = bf16[256,128]{1,0:T(8,128)(2,1)S(1)} collective-permute-done((bf16[256,128]{1,0:T(8,128)(2,1)}, bf16[256,128]{1,0:T(8,128)(2,1)S(1)}, u32[]{:S(2)}, u32[]{:S(2)}) %collective-permute-start.1) | collective-permute-done | bytes 65568 | tf_op jit(solution)/shard_map/ppermute | solution.py:27
  17.2 0.0 collective-permute-done.2
  17.2 1.6 %collective-permute-start.6 = (bf16[2,256,128]{2,1,0:T(8,128)(2,1)S(1)}, bf16[2,256,128]{2,1,0:T(8,128)(2,1)S(1)}, u32[]{:S(2)}, u32[]{:S(2)}) collective-permute-start(bf16[2,256,128]{2,1,0:T(8,128)(2,1)S(1)} %get-tuple-element.44), channel_id=1, source_target_pairs={{12,0},{225,1},{14,2},{227,3},{0,4},{229,5},{2,6},{231,7},{4,8},{2... | collective-permute-start | bytes 393224 | tf_op jit(solution)/shard_map/ppermute | solution.py:37
  18.8 2.7 %collective-permute-start.8 = (bf16[2,256,128]{2,1,0:T(8,128)(2,1)S(1)}, bf16[2,256,128]{2,1,0:T(8,128)(2,1)S(1)}, u32[]{:S(2)}, u32[]{:S(2)}) collective-permute-start(bf16[2,256,128]{2,1,0:T(8,128)(2,1)S(1)} %get-tuple-element.44), channel_id=1, source_target_pairs={{8,0},{65,1},{10,2},{67,3},{12,4},{69,5},{14,6},{71,7},{0,8},{73,9... | collective-permute-start | bytes 393224 | tf_op jit(solution)/shard_map/ppermute | solution.py:37
  21.5 0.0 collective-permute-done
  21.5 0.9 %fusion.40 = (bf16[1,2,256,128]{3,2,1,0:T(8,128)(2,1)S(1)}, bf16[2,256,128]{2,1,0:T(8,128)(2,1)S(1)}) fusion(bf16[1,256,128]{2,1,0:T(8,128)(2,1)S(1)} %bitcast.72, bf16[1,256,128]{2,1,0:T(8,128)(2,1)} %bitcast.63), kind=kLoop, calls=%fused_computation.172 | loop fusion | flops 65536 | bytes 393216 | tf_op jit(solution)/shard_map/stack | solution.py:60
  22.4 0.1 collective-permute-start.5
  22.5 2.9 %collective-permute-start.7 = (bf16[2,256,128]{2,1,0:T(8,128)(2,1)S(1)}, bf16[2,256,128]{2,1,0:T(8,128)(2,1)S(1)}, u32[]{:S(2)}, u32[]{:S(2)}) collective-permute-start(bf16[2,256,128]{2,1,0:T(8,128)(2,1)S(1)} %get-tuple-element.42), channel_id=1, source_target_pairs={{8,0},{65,1},{10,2},{67,3},{12,4},{69,5},{14,6},{71,7},{0,8},{73,9... | collective-permute-start | bytes 393224 | tf_op jit(solution)/shard_map/ppermute | solution.py:37
  25.4 1.3 %collective-permute-start.4 = (bf16[2,256,128]{2,1,0:T(8,128)(2,1)S(1)}, bf16[2,256,128]{2,1,0:T(8,128)(2,1)S(1)}, u32[]{:S(2)}, u32[]{:S(2)}) collective-permute-start(bf16[2,256,128]{2,1,0:T(8,128)(2,1)S(1)} %get-tuple-element.44), channel_id=1, source_target_pairs={{4,0},{33,1},{6,2},{35,3},{8,4},{37,5},{10,6},{39,7},{12,8},{41,9}... | collective-permute-start | bytes 393224 | tf_op jit(solution)/shard_map/ppermute | solution.py:37
  26.7 0.0 collective-permute-done.6
  26.7 0.1 collective-permute-start.3
  26.8 0.1 select_reduce_fusion
  26.9 1.1 %copy.11 = bf16[512,256]{0,1:T(8,128)(2,1)S(1)} copy(bf16[512,256]{1,0:T(8,128)(2,1)} %param.10) | data formatting | bytes 524288 | tf_op args[4]
  28.0 0.1 reshape.430
  28.1 0.0 collective-permute-done.8
  28.1 1.9 %collective-permute-done.5 = bf16[2,256,128]{2,1,0:T(8,128)(2,1)S(1)} collective-permute-done((bf16[2,256,128]{2,1,0:T(8,128)(2,1)S(1)}, bf16[2,256,128]{2,1,0:T(8,128)(2,1)S(1)}, u32[]{:S(2)}, u32[]{:S(2)}) %collective-permute-start.5) | collective-permute-done | bytes 131104 | tf_op jit(solution)/shard_map/ppermute | solution.py:37
  30.1 0.0 collective-permute-done.7
  30.1 0.1 pad_maximum_fusion.1
  30.1 1.1 %collective-permute-start.10 = (bf16[2,4,256,128]{3,2,1,0:T(8,128)(2,1)S(1)}, bf16[2,4,256,128]{3,2,1,0:T(8,128)(2,1)S(1)}, u32[]{:S(2)}, u32[]{:S(2)}) collective-permute-start(bf16[2,4,256,128]{3,2,1,0:T(8,128)(2,1)S(1)} %bitcast.47), channel_id=1, source_target_pairs={{224,0},{13,1},{226,2},{15,3},{228,4},{1,5},{230,6},{3,7},{232,8},... | collective-permute-start | bytes 1572872 | tf_op jit(solution)/shard_map/ppermute | solution.py:37
  31.2 0.0 collective-permute-done.4
  31.2 1.1 %collective-permute-done.3 = bf16[2,256,128]{2,1,0:T(8,128)(2,1)S(1)} collective-permute-done((bf16[2,256,128]{2,1,0:T(8,128)(2,1)S(1)}, bf16[2,256,128]{2,1,0:T(8,128)(2,1)S(1)}, u32[]{:S(2)}, u32[]{:S(2)}) %collective-permute-start.3) | collective-permute-done | bytes 131104 | tf_op jit(solution)/shard_map/ppermute | solution.py:37
  32.3 0.1 pad_maximum_fusion
  32.4 6.0 %collective-permute-start.9 = (bf16[2,4,256,128]{3,2,1,0:T(8,128)(2,1)S(1)}, bf16[2,4,256,128]{3,2,1,0:T(8,128)(2,1)S(1)}, u32[]{:S(2)}, u32[]{:S(2)}) collective-permute-start(bf16[2,4,256,128]{3,2,1,0:T(8,128)(2,1)S(1)} %bitcast.50), channel_id=1, source_target_pairs={{32,0},{5,1},{34,2},{7,3},{36,4},{9,5},{38,6},{11,7},{40,8},{13,9}... | collective-permute-start | bytes 1572872 | tf_op jit(solution)/shard_map/ppermute | solution.py:37
  38.4 0.1 broadcast_select_fusion
  38.5 0.1 collective-permute-start.13
  38.6 4.2 %collective-permute-start.14 = (bf16[2,4,256,128]{3,2,1,0:T(8,128)(2,1)S(1)}, bf16[2,4,256,128]{3,2,1,0:T(8,128)(2,1)S(1)}, u32[]{:S(2)}, u32[]{:S(2)}) collective-permute-start(bf16[2,4,256,128]{3,2,1,0:T(8,128)(2,1)S(1)} %get-tuple-element.35), channel_id=1, source_target_pairs={{224,0},{13,1},{226,2},{15,3},{228,4},{9,5},{230,6},{11,7},{232,8}... | collective-permute-start | bytes 1572872 | tf_op jit(solution)/shard_map/ppermute | solution.py:47
  42.8 2.8 %copy-done = bf16[192,128,128]{2,1,0:T(8,128)(2,1)S(1)} copy-done((bf16[192,128,128]{2,1,0:T(8,128)(2,1)S(1)}, bf16[192,128,128]{2,1,0:T(8,128)(2,1)}, u32[]{:S(2)}) %copy-start) | copy-done | bytes 6291480
  45.6 1.8 %early_tiles.1.refs_4_ = f32[4,128,128]{2,1,0:T(8,128)S(1)} custom-call(s32[384]{0:T(512)S(1)} %add_select_fusion.table, s32[9]{0:T(128)S(1)} %select_reduce_fusion.4.bounds, bf16[192,128,128]{2,1,0:T(8,128)(2,1)S(1)} %copy-done, bf16[16,128,128]{2,1,0:T(8,128)(2,1)S(1)} %bitcast.52, bf16[16,128,128]{2,1,0:T(8,128)(2,1)S(1)} %bitcast.49), custom_call_target="tpu_custom_call" | custom-call | flops 268435456 | bytes 8388608 | tf_op jit(solution)/shard_map/early_tiles/pallas_call | solution.py:205
  47.4 0.0 copy-start.1
  47.4 0.0 collective-permute-done.10
  47.4 0.0 collective-permute-done.9
  47.4 1.4 %collective-permute-start.11 = (bf16[2,4,256,128]{3,2,1,0:T(8,128)(2,1)S(1)}, bf16[2,4,256,128]{3,2,1,0:T(8,128)(2,1)S(1)}, u32[]{:S(2)}, u32[]{:S(2)}) collective-permute-start(bf16[2,4,256,128]{3,2,1,0:T(8,128)(2,1)S(1)} %collective-permute-done.9), channel_id=1, source_target_pairs={{32,0},{5,1},{34,2},{7,3},{36,4},{9,5},{38,6},{11,7},{40,8},{13,9}... | collective-permute-start | bytes 1572872 | tf_op jit(solution)/shard_map/ppermute | solution.py:37
  48.8 0.7 collective-permute-start.12
  49.6 0.0 collective-permute-done.13
  49.6 1.2 %collective-permute-done.14 = bf16[2,4,256,128]{3,2,1,0:T(8,128)(2,1)S(1)} collective-permute-done((bf16[2,4,256,128]{3,2,1,0:T(8,128)(2,1)S(1)}, bf16[2,4,256,128]{3,2,1,0:T(8,128)(2,1)S(1)}, u32[]{:S(2)}, u32[]{:S(2)}) %collective-permute-start.14) | collective-permute-done | bytes 524320 | tf_op jit(solution)/shard_map/ppermute | solution.py:47
  50.8 3.5 %near_tiles.1.refs_2_ = f32[4,128,128]{2,1,0:T(8,128)S(1)} custom-call(s32[384]{0:T(512)S(1)} %add_select_fusion.table, s32[9]{0:T(128)S(1)} %select_reduce_fusion.4.bounds, bf16[192,128,128]{2,1,0:T(8,128)(2,1)S(1)} %copy-done, bf16[16,128,128]{2,1,0:T(8,128)(2,1)S(1)} %bitcast.55, bf16[16,128,128]{2,1,0:T(8,128)(2,1)S(1)} %bitcast.54, ...), custom_call_target="tpu_custom_call" | custom-call | flops 268435456 | bytes 8388608 | tf_op jit(solution)/shard_map/near_tiles/pallas_call | solution.py:205
  54.3 2.4 %collective-permute-done.11 = bf16[2,4,256,128]{3,2,1,0:T(8,128)(2,1)S(1)} collective-permute-done((bf16[2,4,256,128]{3,2,1,0:T(8,128)(2,1)S(1)}, bf16[2,4,256,128]{3,2,1,0:T(8,128)(2,1)S(1)}, u32[]{:S(2)}, u32[]{:S(2)}) %collective-permute-start.11) | collective-permute-done | bytes 524320 | tf_op jit(solution)/shard_map/ppermute | solution.py:37
  56.7 2.5 %collective-permute-done.12 = bf16[2,4,256,128]{3,2,1,0:T(8,128)(2,1)S(1)} collective-permute-done((bf16[2,4,256,128]{3,2,1,0:T(8,128)(2,1)S(1)}, bf16[2,4,256,128]{3,2,1,0:T(8,128)(2,1)S(1)}, u32[]{:S(2)}, u32[]{:S(2)}) %collective-permute-start.12) | collective-permute-done | bytes 524320 | tf_op jit(solution)/shard_map/ppermute | solution.py:37
  59.2 2.8 %far_tiles.1 = (bf16[384,128]{1,0:T(8,128)(2,1)S(1)}, f32[64,2,128]{2,1,0:T(2,128)}) custom-call(s32[384]{0:T(512)S(1)} %add_select_fusion.table, s32[9]{0:T(128)S(1)} %select_reduce_fusion.4.bounds, bf16[192,128,128]{2,1,0:T(8,128)(2,1)S(1)} %copy-done, bf16[16,128,128]{2,1,0:T(8,128)(2,1)S(1)} %bitcast.57, bf16[16,128,128]{2,1,0:T(8,128)(2,1)S(1)} %bitcast.59, ...), custom_call_target="tpu_custom_call" | custom-call | flops 268435456 | bytes 8388608 | tf_op jit(solution)/shard_map/far_tiles/pallas_call | solution.py:205
  62.0 0.0 collective-permute-start.15
  62.0 0.1 fusion.41
  62.2 7.7 %all-to-all-start = ((f32[64,2,128]{2,1,0:T(2,128)}), f32[64,2,128]{2,1,0:T(2,128)S(1)}, u32[]{:S(2)}, u32[]{:S(2)}) async-start(f32[64,2,128]{2,1,0:T(2,128)} %get-tuple-element.29), calls=%async_computation | async-start | bytes 131072 | tf_op jit(solution)/shard_map/all_to_all | solution.py:242
  69.8 0.0 collective-permute-done.15
  69.9 1.6 %collective-permute-start.16 = (bf16[2,320,128]{2,1,0:T(8,128)(2,1)S(1)}, bf16[2,320,128]{2,1,0:T(8,128)(2,1)S(1)}, u32[]{:S(2)}, u32[]{:S(2)}) collective-permute-start(bf16[2,320,128]{2,1,0:T(8,128)(2,1)S(1)} %pad_maximum_fusion.2), channel_id=1, source_target_pairs={{0,2},{2,0},{1,3},{3,1},{4,6},{6,4},{5,7},{7,5},{8,10},{10,8},{9,1... | collective-permute-start | bytes 491528 | tf_op jit(solution)/shard_map/ppermute | solution.py:243
  71.5 0.1 fusion.42
  71.6 10.3 %all-to-all-done = f32[64,2,128]{2,1,0:T(2,128)S(1)} async-done(((f32[64,2,128]{2,1,0:T(2,128)}), f32[64,2,128]{2,1,0:T(2,128)S(1)}, u32[]{:S(2)}, u32[]{:S(2)}) %all-to-all-start) | async-done | bytes 65568 | tf_op jit(solution)/shard_map/all_to_all | solution.py:242
  81.9 0.1 reduce_sum.89
  82.0 0.1 fusion.45
  82.1 0.6 pad_maximum_fusion.6
  82.7 0.1 fusion.43
  82.8 0.1 fusion.44
  82.9 1.0 %convolution_convert_fusion = bf16[512,64]{0,1:T(8,128)(2,1)} fusion(bf16[256,64]{1,0:T(8,128)(2,1)S(1)} %get-tuple-element.52, bf16[256,64]{1,0:T(8,128)(2,1)S(1)} %get-tuple-element.51, bf16[256,64]{1,0:T(8,128)(2,1)S(1)} %get-tuple-element.50, bf16[256,64]{1,0:T(8,128)(2,1)S(1)} %get-tuple-element.49, bf16[256,64]{1,0:T(8,128)(2,1)S(1)} %get-tuple-element.48, ...), kind=kOutput, calls=%fused_computation | convolution fusion | flops 18923520 | bytes 720897 | tf_op jit(solution)/shard_map/rs,si->ri/dot_general | solution.py:248
  (20 shorter events, 0.3 us)
Async XLA Ops:
  2.3 14.9 %collective-permute-start.2 = (bf16[256,128]{1,0:T(8,128)(2,1)}, bf16[256,128]{1,0:T(8,128)(2,1)S(1)}, u32[]{:S(2)}, u32[]{:S(2)}) collective-permute-start(bf16[256,128]{1,0:T(8,128)(2,1)} %masked.1), channel_id=1, source_target_pairs={{144,0},{145,1},{146,2},{147,3},{148,4},{149,5},{150,6},{151,7},{1... | collective-permute-start | bytes 196616 | tf_op jit(solution)/shard_map/ppermute | solution.py:27
  11.2 10.3 %collective-permute-start = (bf16[256,128]{1,0:T(8,128)(2,1)}, bf16[256,128]{1,0:T(8,128)(2,1)S(1)}, u32[]{:S(2)}, u32[]{:S(2)}) collective-permute-start(bf16[256,128]{1,0:T(8,128)(2,1)} %masked.1), channel_id=1, source_target_pairs={{128,0},{129,1},{130,2},{131,3},{132,4},{133,5},{134,6},{135,7},{1... | collective-permute-start | bytes 196616 | tf_op jit(solution)/shard_map/ppermute | solution.py:27
  11.2 6.0 %collective-permute-start.1 = (bf16[256,128]{1,0:T(8,128)(2,1)}, bf16[256,128]{1,0:T(8,128)(2,1)S(1)}, u32[]{:S(2)}, u32[]{:S(2)}) collective-permute-start(bf16[256,128]{1,0:T(8,128)(2,1)} %masked.1), channel_id=1, source_target_pairs={{16,0},{17,1},{18,2},{19,3},{20,4},{21,5},{22,6},{23,7},{24,8},{25... | collective-permute-start | bytes 196616 | tf_op jit(solution)/shard_map/ppermute | solution.py:27
  17.2 9.4 %collective-permute-start.6 = (bf16[2,256,128]{2,1,0:T(8,128)(2,1)S(1)}, bf16[2,256,128]{2,1,0:T(8,128)(2,1)S(1)}, u32[]{:S(2)}, u32[]{:S(2)}) collective-permute-start(bf16[2,256,128]{2,1,0:T(8,128)(2,1)S(1)} %get-tuple-element.44), channel_id=1, source_target_pairs={{12,0},{225,1},{14,2},{227,3},{0,4},{229,5},{2,6},{231,7},{4,8},{2... | collective-permute-start | bytes 393224 | tf_op jit(solution)/shard_map/ppermute | solution.py:37
  18.8 9.3 %collective-permute-start.8 = (bf16[2,256,128]{2,1,0:T(8,128)(2,1)S(1)}, bf16[2,256,128]{2,1,0:T(8,128)(2,1)S(1)}, u32[]{:S(2)}, u32[]{:S(2)}) collective-permute-start(bf16[2,256,128]{2,1,0:T(8,128)(2,1)S(1)} %get-tuple-element.44), channel_id=1, source_target_pairs={{8,0},{65,1},{10,2},{67,3},{12,4},{69,5},{14,6},{71,7},{0,8},{73,9... | collective-permute-start | bytes 393224 | tf_op jit(solution)/shard_map/ppermute | solution.py:37
  22.4 7.7 %collective-permute-start.5 = (bf16[2,256,128]{2,1,0:T(8,128)(2,1)S(1)}, bf16[2,256,128]{2,1,0:T(8,128)(2,1)S(1)}, u32[]{:S(2)}, u32[]{:S(2)}) collective-permute-start(bf16[2,256,128]{2,1,0:T(8,128)(2,1)S(1)} %get-tuple-element.42), channel_id=1, source_target_pairs={{12,0},{225,1},{14,2},{227,3},{0,4},{229,5},{2,6},{231,7},{4,8},{2... | collective-permute-start | bytes 393224 | tf_op jit(solution)/shard_map/ppermute | solution.py:37
  22.5 7.6 %collective-permute-start.7 = (bf16[2,256,128]{2,1,0:T(8,128)(2,1)S(1)}, bf16[2,256,128]{2,1,0:T(8,128)(2,1)S(1)}, u32[]{:S(2)}, u32[]{:S(2)}) collective-permute-start(bf16[2,256,128]{2,1,0:T(8,128)(2,1)S(1)} %get-tuple-element.42), channel_id=1, source_target_pairs={{8,0},{65,1},{10,2},{67,3},{12,4},{69,5},{14,6},{71,7},{0,8},{73,9... | collective-permute-start | bytes 393224 | tf_op jit(solution)/shard_map/ppermute | solution.py:37
  25.4 5.8 %collective-permute-start.4 = (bf16[2,256,128]{2,1,0:T(8,128)(2,1)S(1)}, bf16[2,256,128]{2,1,0:T(8,128)(2,1)S(1)}, u32[]{:S(2)}, u32[]{:S(2)}) collective-permute-start(bf16[2,256,128]{2,1,0:T(8,128)(2,1)S(1)} %get-tuple-element.44), channel_id=1, source_target_pairs={{4,0},{33,1},{6,2},{35,3},{8,4},{37,5},{10,6},{39,7},{12,8},{41,9}... | collective-permute-start | bytes 393224 | tf_op jit(solution)/shard_map/ppermute | solution.py:37
  26.7 5.7 %collective-permute-start.3 = (bf16[2,256,128]{2,1,0:T(8,128)(2,1)S(1)}, bf16[2,256,128]{2,1,0:T(8,128)(2,1)S(1)}, u32[]{:S(2)}, u32[]{:S(2)}) collective-permute-start(bf16[2,256,128]{2,1,0:T(8,128)(2,1)S(1)} %get-tuple-element.42), channel_id=1, source_target_pairs={{4,0},{33,1},{6,2},{35,3},{8,4},{37,5},{10,6},{39,7},{12,8},{41,9}... | collective-permute-start | bytes 393224 | tf_op jit(solution)/shard_map/ppermute | solution.py:37
  30.1 17.3 %collective-permute-start.10 = (bf16[2,4,256,128]{3,2,1,0:T(8,128)(2,1)S(1)}, bf16[2,4,256,128]{3,2,1,0:T(8,128)(2,1)S(1)}, u32[]{:S(2)}, u32[]{:S(2)}) collective-permute-start(bf16[2,4,256,128]{3,2,1,0:T(8,128)(2,1)S(1)} %bitcast.47), channel_id=1, source_target_pairs={{224,0},{13,1},{226,2},{15,3},{228,4},{1,5},{230,6},{3,7},{232,8},... | collective-permute-start | bytes 1572872 | tf_op jit(solution)/shard_map/ppermute | solution.py:37
  32.4 15.0 %collective-permute-start.9 = (bf16[2,4,256,128]{3,2,1,0:T(8,128)(2,1)S(1)}, bf16[2,4,256,128]{3,2,1,0:T(8,128)(2,1)S(1)}, u32[]{:S(2)}, u32[]{:S(2)}) collective-permute-start(bf16[2,4,256,128]{3,2,1,0:T(8,128)(2,1)S(1)} %bitcast.50), channel_id=1, source_target_pairs={{32,0},{5,1},{34,2},{7,3},{36,4},{9,5},{38,6},{11,7},{40,8},{13,9}... | collective-permute-start | bytes 1572872 | tf_op jit(solution)/shard_map/ppermute | solution.py:37
  38.5 11.0 %collective-permute-start.13 = (bf16[2,4,256,128]{3,2,1,0:T(8,128)(2,1)S(1)}, bf16[2,4,256,128]{3,2,1,0:T(8,128)(2,1)S(1)}, u32[]{:S(2)}, u32[]{:S(2)}) collective-permute-start(bf16[2,4,256,128]{3,2,1,0:T(8,128)(2,1)S(1)} %get-tuple-element.36), channel_id=1, source_target_pairs={{32,0},{5,1},{34,2},{7,3},{36,4},{1,5},{38,6},{3,7},{40,8},{13,9},... | collective-permute-start | bytes 1572872 | tf_op jit(solution)/shard_map/ppermute | solution.py:47
  38.6 12.1 %collective-permute-start.14 = (bf16[2,4,256,128]{3,2,1,0:T(8,128)(2,1)S(1)}, bf16[2,4,256,128]{3,2,1,0:T(8,128)(2,1)S(1)}, u32[]{:S(2)}, u32[]{:S(2)}) collective-permute-start(bf16[2,4,256,128]{3,2,1,0:T(8,128)(2,1)S(1)} %get-tuple-element.35), channel_id=1, source_target_pairs={{224,0},{13,1},{226,2},{15,3},{228,4},{9,5},{230,6},{11,7},{232,8}... | collective-permute-start | bytes 1572872 | tf_op jit(solution)/shard_map/ppermute | solution.py:47
  42.8 2.8 %copy-start = (bf16[192,128,128]{2,1,0:T(8,128)(2,1)S(1)}, bf16[192,128,128]{2,1,0:T(8,128)(2,1)}, u32[]{:S(2)}) copy-start(bf16[192,128,128]{2,1,0:T(8,128)(2,1)} %adj.5) | copy-start | bytes 18874372
  47.4 11.8 %copy-start.1 = (bf16[256,64]{0,1:T(8,128)(2,1)S(1)}, bf16[256,64]{0,1:T(8,128)(2,1)}, u32[]{:S(2)}) copy-start(bf16[256,64]{0,1:T(8,128)(2,1)} %param.11) | copy-start | bytes 98308
  47.4 9.3 %collective-permute-start.11 = (bf16[2,4,256,128]{3,2,1,0:T(8,128)(2,1)S(1)}, bf16[2,4,256,128]{3,2,1,0:T(8,128)(2,1)S(1)}, u32[]{:S(2)}, u32[]{:S(2)}) collective-permute-start(bf16[2,4,256,128]{3,2,1,0:T(8,128)(2,1)S(1)} %collective-permute-done.9), channel_id=1, source_target_pairs={{32,0},{5,1},{34,2},{7,3},{36,4},{9,5},{38,6},{11,7},{40,8},{13,9}... | collective-permute-start | bytes 1572872 | tf_op jit(solution)/shard_map/ppermute | solution.py:37
  48.8 10.4 %collective-permute-start.12 = (bf16[2,4,256,128]{3,2,1,0:T(8,128)(2,1)S(1)}, bf16[2,4,256,128]{3,2,1,0:T(8,128)(2,1)S(1)}, u32[]{:S(2)}, u32[]{:S(2)}) collective-permute-start(bf16[2,4,256,128]{3,2,1,0:T(8,128)(2,1)S(1)} %collective-permute-done.10), channel_id=1, source_target_pairs={{224,0},{13,1},{226,2},{15,3},{228,4},{1,5},{230,6},{3,7},{232,8},... | collective-permute-start | bytes 1572872 | tf_op jit(solution)/shard_map/ppermute | solution.py:37
  62.0 7.8 %collective-permute-start.15 = (bf16[384,128]{1,0:T(8,128)(2,1)S(1)}, bf16[384,128]{1,0:T(8,128)(2,1)S(1)}, u32[]{:S(2)}, u32[]{:S(2)}) collective-permute-start(bf16[384,128]{1,0:T(8,128)(2,1)S(1)} %get-tuple-element.28), channel_id=1, source_target_pairs={{0,1},{1,0},{2,3},{3,2},{4,5},{5,4},{6,7},{7,6},{8,9},{9,8},{10,11... | collective-permute-start | bytes 294920 | tf_op jit(solution)/shard_map/ppermute | solution.py:241
  62.2 19.7 %all-to-all-start = ((f32[64,2,128]{2,1,0:T(2,128)}), f32[64,2,128]{2,1,0:T(2,128)S(1)}, u32[]{:S(2)}, u32[]{:S(2)}) async-start(f32[64,2,128]{2,1,0:T(2,128)} %get-tuple-element.29), calls=%async_computation | async-start | bytes 131072 | tf_op jit(solution)/shard_map/all_to_all | solution.py:242
  69.9 12.8 %collective-permute-start.16 = (bf16[2,320,128]{2,1,0:T(8,128)(2,1)S(1)}, bf16[2,320,128]{2,1,0:T(8,128)(2,1)S(1)}, u32[]{:S(2)}, u32[]{:S(2)}) collective-permute-start(bf16[2,320,128]{2,1,0:T(8,128)(2,1)S(1)} %pad_maximum_fusion.2), channel_id=1, source_target_pairs={{0,2},{2,0},{1,3},{3,1},{4,6},{6,4},{5,7},{7,5},{8,10},{10,8},{9,1... | collective-permute-start | bytes 491528 | tf_op jit(solution)/shard_map/ppermute | solution.py:243

commit v8 on v6

--- a/solution.py
+++ b/solution.py
@@ -55,7 +55,7 @@
     far_y, far = from_rows(packed, dz=4, dy=1), from_rows(packed, dz=4)
     again, position = lax.optimization_barrier((packed, position))
     four = jnp.stack([packed, from_rows(again, dy=1), far, far_y])
-    low = jnp.stack([four, from_axis(four, False, 1)])
+    low = jnp.stack([lax.optimization_barrier(four), from_axis(four, False, 1)])
     high = jnp.stack([from_axis(four, False, -1), from_axis(four, False, 2)])
     return low, high, position
 
@@ -195,7 +195,10 @@
         for ref in outs:
             ref[pl.ds(r * 128, 128), :] = packed
     for k, ref in enumerate(outs):
-        ref[pl.ds(256, 64), :] = weights[:, pl.ds(pl.multiple_of((lax.axis_index("yl") ^ (k >> 1)) * 128, 128), 128)]
+        lanes = pl.multiple_of((lax.axis_index("yl") ^ (k >> 1)) * 128, 128)
+        of_chip = weights[:, pl.ds(lanes, 128)].astype(jnp.float32)
+        of_core = jnp.where((lax.axis_index("core") ^ (k & 1)) == 0, of_chip, pltpu.roll(of_chip, 64, 1))
+        ref[pl.ds(256, 64), :] = of_core.astype(ref.dtype)
 
 
 def call(kernel, table, bounds, adj, sources, others, out_shape, keep_acc, name):
@@ -242,8 +245,7 @@
     pieces = lax.all_to_all(partial, ROWS, 0, 0, tiled=True)
     arrived = messages[:1] + [lax.ppermute(m, SLAB, pairs) for m, pairs in zip(messages[1:], FLIPS)]
     a_all = jnp.concatenate([halves(m[:256]) for m in arrived], axis=1)
-    w_all = jnp.concatenate([m[256:] for m in arrived], axis=0)
-    w_all = jnp.where(lax.axis_index("core") == 0, w_all[:, :64], w_all[:, 64:])
+    w_all = jnp.concatenate([m[256:, :64] for m in arrived], axis=0)
     grad_input = jnp.einsum("rs,si->ri", a_all, w_all, preferred_element_type=jnp.float32).astype(jnp.bfloat16)
     total = jnp.sum(pieces, axis=0)
     grad_weight = jnp.concatenate([total[p : p + 1, k : k + 64] for p in range(2) for k in (0, 64)], axis=0)

time: 83.7 us -> 82 us (0.980)
  waiting for transfers between devices: 29.1 us -> 27.8 us
    all_to_all x1, waiting for transfers between devices: 10.7 us -> 4.87 us  [body(): pieces = lax.all_to_all(partial, ROWS, 0, 0, tiled=True)]
    ppermute x3, waiting for transfers between devices: 0.01 us -> 4.24 us  [body(): lax.ppermute(m, SLAB, pairs)]
  transfers between devices with their start and end apart: 16 -> 16, of which waited for: 10 -> 12; matrix products, arithmetic and copies ran while one was open for 6% -> 6% of each run, Pallas kernels for 6% -> 6%
where the time goes in v8:
time: 82 us; the launch traced here: 81.2 us
  starting transfers between devices  34 us (41%)
  waiting for transfers between devices  27.8 us (34%)
  Pallas kernels  9.62 us (12%)
  local copies, waits for them, and re-layouts  4.44 us (5%)
  other arithmetic  3.62 us (4%)
  matrix products  0.98 us (1%)
    ppermute x7, starting transfers between devices, from_axis(): return lax.ppermute(value, ALL, pairs)  12.5 us
    ppermute x7, waiting for transfers between devices, from_axis(): return lax.ppermute(value, ALL, pairs)  10.4 us
    ppermute x3, starting transfers between devices, from_rows(): return lax.ppermute(value, ALL, pairs)  10.2 us
    pallas_call x3, Pallas kernels, call(): pl.pallas_call(kernel, out_shape=out_shape, in_specs=[smem, smem, vmem] +...  7.94 us
    all_to_all x1, starting transfers between devices, body(): pieces = lax.all_to_all(partial, ROWS, 0, 0, tiled=True)  7.77 us
    ppermute x3, waiting for transfers between devices, from_rows(): return lax.ppermute(value, ALL, pairs)  6.01 us
    all_to_all x1, waiting for transfers between devices, body(): pieces = lax.all_to_all(partial, ROWS, 0, 0, tiled=True)  4.87 us
    ppermute x3, waiting for transfers between devices, body(): lax.ppermute(m, SLAB, pairs)  4.24 us
  transfers between devices with their start and end apart: 16, of which 12 were waited for; matrix products, arithmetic and copies ran while one was open for 6% of the time, Pallas kernels for 6%

profile of v8, /device:TPU:8, one launch (start us, length us, event | category | flops | bytes accessed | tf_op | source)
XLA Modules:
  0.0 81.2 jit_solution(6200180672897478148)
XLA Ops:
  0.6 1.7 %masked.1 = bf16[256,128]{1,0:T(8,128)(2,1)} custom-call(bf16[64,512]{1,0:T(8,128)(2,1)} %bitcast.45, s32[64,512]{1,0:T(8,128)} %bitcast.44), custom_call_target="tpu_custom_call" | custom-call | tf_op jit(solution)/shard_map/masked/pallas_call | solution.py:153
  2.3 7.2 %collective-permute-start.1 = (bf16[256,128]{1,0:T(8,128)(2,1)}, bf16[256,128]{1,0:T(8,128)(2,1)S(1)}, u32[]{:S(2)}, u32[]{:S(2)}) collective-permute-start(bf16[256,128]{1,0:T(8,128)(2,1)} %masked.1), channel_id=1, source_target_pairs={{128,0},{129,1},{130,2},{131,3},{132,4},{133,5},{134,6},{135,7},{1... | collective-permute-start | bytes 196616 | tf_op jit(solution)/shard_map/ppermute | solution.py:27
  9.5 1.7 %collective-permute-start.2 = (bf16[256,128]{1,0:T(8,128)(2,1)}, bf16[256,128]{1,0:T(8,128)(2,1)S(1)}, u32[]{:S(2)}, u32[]{:S(2)}) collective-permute-start(bf16[256,128]{1,0:T(8,128)(2,1)} %masked.1), channel_id=1, source_target_pairs={{144,0},{145,1},{146,2},{147,3},{148,4},{149,5},{150,6},{151,7},{1... | collective-permute-start | bytes 196616 | tf_op jit(solution)/shard_map/ppermute | solution.py:27
  11.2 1.2 %collective-permute-start = (bf16[256,128]{1,0:T(8,128)(2,1)}, bf16[256,128]{1,0:T(8,128)(2,1)S(1)}, u32[]{:S(2)}, u32[]{:S(2)}) collective-permute-start(bf16[256,128]{1,0:T(8,128)(2,1)} %masked.1), channel_id=1, source_target_pairs={{16,0},{17,1},{18,2},{19,3},{20,4},{21,5},{22,6},{23,7},{24,8},{25... | collective-permute-start | bytes 196616 | tf_op jit(solution)/shard_map/ppermute | solution.py:27
  12.5 0.8 fusion.37
  13.3 0.1 convert_reduce_fusion.1
  13.4 0.1 select_reduce_fusion.5
  13.5 0.2 select_reduce_fusion.2
  13.7 0.1 select_reduce_fusion.4.bounds
  13.8 0.1 select_reduce_fusion.3
  13.9 0.2 convert_reduce_fusion
  14.2 0.1 select_reduce_fusion.1
  14.3 2.9 %collective-permute-done = bf16[256,128]{1,0:T(8,128)(2,1)S(1)} collective-permute-done((bf16[256,128]{1,0:T(8,128)(2,1)}, bf16[256,128]{1,0:T(8,128)(2,1)S(1)}, u32[]{:S(2)}, u32[]{:S(2)}) %collective-permute-start) | collective-permute-done | bytes 65568 | tf_op jit(solution)/shard_map/ppermute | solution.py:27
  17.2 0.0 collective-permute-done.1
  17.2 3.1 %collective-permute-done.2 = bf16[256,128]{1,0:T(8,128)(2,1)S(1)} collective-permute-done((bf16[256,128]{1,0:T(8,128)(2,1)}, bf16[256,128]{1,0:T(8,128)(2,1)S(1)}, u32[]{:S(2)}, u32[]{:S(2)}) %collective-permute-start.2) | collective-permute-done | bytes 65568 | tf_op jit(solution)/shard_map/ppermute | solution.py:27
  20.3 0.9 %pad_maximum_fusion.2 = bf16[4,256,128]{2,1,0:T(8,128)(2,1)S(1)} fusion(bf16[1,256,128]{2,1,0:T(8,128)(2,1)S(1)} %bitcast.47, bf16[1,256,128]{2,1,0:T(8,128)(2,1)S(1)} %bitcast.46, bf16[1,256,128]{2,1,0:T(8,128)(2,1)S(1)} %bitcast.48, bf16[1,256,128]{2,1,0:T(8,128)(2,1)} %bitcast.43), kind=kLoop, calls=%fused_computation.7 | loop fusion | flops 393216 | bytes 524288 | tf_op jit(solution)/shard_map/stack | solution.py:57
  21.2 1.6 %collective-permute-start.4 = (bf16[4,256,128]{2,1,0:T(8,128)(2,1)S(1)}, bf16[4,256,128]{2,1,0:T(8,128)(2,1)S(1)}, u32[]{:S(2)}, u32[]{:S(2)}) collective-permute-start(bf16[4,256,128]{2,1,0:T(8,128)(2,1)S(1)} %pad_maximum_fusion.2), channel_id=1, source_target_pairs={{12,0},{225,1},{14,2},{227,3},{0,4},{229,5},{2,6},{231,7},{4,8},{2... | collective-permute-start | bytes 786440 | tf_op jit(solution)/shard_map/ppermute | solution.py:37
  22.7 2.7 %collective-permute-start.5 = (bf16[4,256,128]{2,1,0:T(8,128)(2,1)S(1)}, bf16[4,256,128]{2,1,0:T(8,128)(2,1)S(1)}, u32[]{:S(2)}, u32[]{:S(2)}) collective-permute-start(bf16[4,256,128]{2,1,0:T(8,128)(2,1)S(1)} %pad_maximum_fusion.2), channel_id=1, source_target_pairs={{8,0},{65,1},{10,2},{67,3},{12,4},{69,5},{14,6},{71,7},{0,8},{73,9... | collective-permute-start | bytes 786440 | tf_op jit(solution)/shard_map/ppermute | solution.py:37
  25.5 1.4 %collective-permute-start.3 = (bf16[4,256,128]{2,1,0:T(8,128)(2,1)S(1)}, bf16[4,256,128]{2,1,0:T(8,128)(2,1)S(1)}, u32[]{:S(2)}, u32[]{:S(2)}) collective-permute-start(bf16[4,256,128]{2,1,0:T(8,128)(2,1)S(1)} %pad_maximum_fusion.2), channel_id=1, source_target_pairs={{4,0},{33,1},{6,2},{35,3},{8,4},{37,5},{10,6},{39,7},{12,8},{41,9}... | collective-permute-start | bytes 786440 | tf_op jit(solution)/shard_map/ppermute | solution.py:37
  26.9 1.1 %copy.11 = bf16[512,256]{0,1:T(8,128)(2,1)S(1)} copy(bf16[512,256]{1,0:T(8,128)(2,1)} %param.10) | data formatting | bytes 524288 | tf_op args[4]
  28.0 0.1 reshape.419
  28.1 0.1 select_reduce_fusion
  28.3 0.6 collective-permute-done.4
  28.8 4.3 %collective-permute-done.5 = bf16[4,256,128]{2,1,0:T(8,128)(2,1)S(1)} collective-permute-done((bf16[4,256,128]{2,1,0:T(8,128)(2,1)S(1)}, bf16[4,256,128]{2,1,0:T(8,128)(2,1)S(1)}, u32[]{:S(2)}, u32[]{:S(2)}) %collective-permute-start.5) | collective-permute-done | bytes 262176 | tf_op jit(solution)/shard_map/ppermute | solution.py:37
  33.2 0.1 pad_maximum_fusion.1
  33.2 0.8 collective-permute-start.7
  34.0 0.0 collective-permute-done.3
  34.0 0.1 pad_maximum_fusion
  34.0 2.6 %collective-permute-start.6 = (bf16[2,4,256,128]{3,2,1,0:T(8,128)(2,1)S(1)}, bf16[2,4,256,128]{3,2,1,0:T(8,128)(2,1)S(1)}, u32[]{:S(2)}, u32[]{:S(2)}) collective-permute-start(bf16[2,4,256,128]{3,2,1,0:T(8,128)(2,1)S(1)} %pad_maximum_fusion), channel_id=1, source_target_pairs={{32,0},{5,1},{34,2},{7,3},{36,4},{9,5},{38,6},{11,7},{40,8},{13,9}... | collective-permute-start | bytes 1572872 | tf_op jit(solution)/shard_map/ppermute | solution.py:37
  36.7 0.1 broadcast_select_fusion
  36.7 0.1 collective-permute-start.10
  36.8 1.8 %collective-permute-start.11 = (bf16[2,4,256,128]{3,2,1,0:T(8,128)(2,1)S(1)}, bf16[2,4,256,128]{3,2,1,0:T(8,128)(2,1)S(1)}, u32[]{:S(2)}, u32[]{:S(2)}) collective-permute-start(bf16[2,4,256,128]{3,2,1,0:T(8,128)(2,1)S(1)} %get-tuple-element.41), channel_id=1, source_target_pairs={{224,0},{13,1},{226,2},{15,3},{228,4},{9,5},{230,6},{11,7},{232,8}... | collective-permute-start | bytes 1572872 | tf_op jit(solution)/shard_map/ppermute | solution.py:47
  38.6 0.0 copy-start
  38.6 2.8 %copy-done = bf16[192,128,128]{2,1,0:T(8,128)(2,1)S(1)} copy-done((bf16[192,128,128]{2,1,0:T(8,128)(2,1)S(1)}, bf16[192,128,128]{2,1,0:T(8,128)(2,1)}, u32[]{:S(2)}) %copy-start) | copy-done | bytes 6291480
  41.4 1.8 %early_tiles.1.refs_4_ = f32[4,128,128]{2,1,0:T(8,128)S(1)} custom-call(s32[384]{0:T(512)S(1)} %add_select_fusion.table, s32[9]{0:T(128)S(1)} %select_reduce_fusion.4.bounds, bf16[192,128,128]{2,1,0:T(8,128)(2,1)S(1)} %copy-done, bf16[16,128,128]{2,1,0:T(8,128)(2,1)S(1)} %bitcast.28, bf16[16,128,128]{2,1,0:T(8,128)(2,1)S(1)} %bitcast.27), custom_call_target="tpu_custom_call" | custom-call | flops 268435456 | bytes 8388608 | tf_op jit(solution)/shard_map/early_tiles/pallas_call | solution.py:208
  43.2 0.0 copy-start.1
  43.3 0.4 collective-permute-done.7
  43.7 0.0 collective-permute-done.6
  43.7 3.4 %collective-permute-start.8 = (bf16[2,4,256,128]{3,2,1,0:T(8,128)(2,1)S(1)}, bf16[2,4,256,128]{3,2,1,0:T(8,128)(2,1)S(1)}, u32[]{:S(2)}, u32[]{:S(2)}) collective-permute-start(bf16[2,4,256,128]{3,2,1,0:T(8,128)(2,1)S(1)} %collective-permute-done.6), channel_id=1, source_target_pairs={{32,0},{5,1},{34,2},{7,3},{36,4},{9,5},{38,6},{11,7},{40,8},{13,9}... | collective-permute-start | bytes 1572872 | tf_op jit(solution)/shard_map/ppermute | solution.py:37
  47.0 0.0 collective-permute-start.9
  47.1 1.8 %collective-permute-done.10 = bf16[2,4,256,128]{3,2,1,0:T(8,128)(2,1)S(1)} collective-permute-done((bf16[2,4,256,128]{3,2,1,0:T(8,128)(2,1)S(1)}, bf16[2,4,256,128]{3,2,1,0:T(8,128)(2,1)S(1)}, u32[]{:S(2)}, u32[]{:S(2)}) %collective-permute-start.10) | collective-permute-done | bytes 524320 | tf_op jit(solution)/shard_map/ppermute | solution.py:47
  48.9 0.4 collective-permute-done.11
  49.3 3.0 %near_tiles.1.refs_2_ = f32[4,128,128]{2,1,0:T(8,128)S(1)} custom-call(s32[384]{0:T(512)S(1)} %add_select_fusion.table, s32[9]{0:T(128)S(1)} %select_reduce_fusion.4.bounds, bf16[192,128,128]{2,1,0:T(8,128)(2,1)S(1)} %copy-done, bf16[16,128,128]{2,1,0:T(8,128)(2,1)S(1)} %bitcast.31, bf16[16,128,128]{2,1,0:T(8,128)(2,1)S(1)} %bitcast.30, ...), custom_call_target="tpu_custom_call" | custom-call | flops 268435456 | bytes 8388608 | tf_op jit(solution)/shard_map/near_tiles/pallas_call | solution.py:208
  52.3 2.3 %collective-permute-done.8 = bf16[2,4,256,128]{3,2,1,0:T(8,128)(2,1)S(1)} collective-permute-done((bf16[2,4,256,128]{3,2,1,0:T(8,128)(2,1)S(1)}, bf16[2,4,256,128]{3,2,1,0:T(8,128)(2,1)S(1)}, u32[]{:S(2)}, u32[]{:S(2)}) %collective-permute-start.8) | collective-permute-done | bytes 524320 | tf_op jit(solution)/shard_map/ppermute | solution.py:37
  54.6 2.8 %collective-permute-done.9 = bf16[2,4,256,128]{3,2,1,0:T(8,128)(2,1)S(1)} collective-permute-done((bf16[2,4,256,128]{3,2,1,0:T(8,128)(2,1)S(1)}, bf16[2,4,256,128]{3,2,1,0:T(8,128)(2,1)S(1)}, u32[]{:S(2)}, u32[]{:S(2)}) %collective-permute-start.9) | collective-permute-done | bytes 524320 | tf_op jit(solution)/shard_map/ppermute | solution.py:37
  57.4 0.0 copy-done.1
  57.4 3.1 %far_tiles.1 = (bf16[320,128]{1,0:T(8,128)(2,1)S(1)}, bf16[320,128]{1,0:T(8,128)(2,1)S(1)}, bf16[320,128]{1,0:T(8,128)(2,1)S(1)}, bf16[320,128]{1,0:T(8,128)(2,1)S(1)}, f32[64,2,128]{2,1,0:T(2,128)}) custom-call(s32[384]{0:T(512)S(1)} %add_select_fusion.table, s32[9]{0:T(128)S(1)} %select_reduce_fusion.4.bounds, bf16[192,128,128]{2,1,0:T(8,128)(2,1)S(1)} %copy-done, ...), custom_call_target="tpu_custom_call" | custom-call | flops 268435456 | bytes 8388608 | tf_op jit(solution)/shard_map/far_tiles/pallas_call | solution.py:208
  60.5 0.0 collective-permute-start.12
  60.5 0.1 fusion.43
  60.6 7.8 %all-to-all-start = ((f32[64,2,128]{2,1,0:T(2,128)}), f32[64,2,128]{2,1,0:T(2,128)S(1)}, u32[]{:S(2)}, u32[]{:S(2)}) async-start(f32[64,2,128]{2,1,0:T(2,128)} %get-tuple-element.35), calls=%async_computation | async-start | bytes 131072 | tf_op jit(solution)/shard_map/all_to_all | solution.py:245
  68.4 0.8 %collective-permute-start.13 = (bf16[320,128]{1,0:T(8,128)(2,1)S(1)}, bf16[320,128]{1,0:T(8,128)(2,1)S(1)}, u32[]{:S(2)}, u32[]{:S(2)}) collective-permute-start(bf16[320,128]{1,0:T(8,128)(2,1)S(1)} %get-tuple-element.33), channel_id=1, source_target_pairs={{0,2},{2,0},{1,3},{3,1},{4,6},{6,4},{5,7},{7,5},{8,10},{10,8},{9,1... | collective-permute-start | bytes 245768 | tf_op jit(solution)/shard_map/ppermute | solution.py:246
  69.3 0.8 %collective-permute-start.14 = (bf16[320,128]{1,0:T(8,128)(2,1)S(1)}, bf16[320,128]{1,0:T(8,128)(2,1)S(1)}, u32[]{:S(2)}, u32[]{:S(2)}) collective-permute-start(bf16[320,128]{1,0:T(8,128)(2,1)S(1)} %get-tuple-element.34), channel_id=1, source_target_pairs={{0,3},{3,0},{1,2},{2,1},{4,7},{7,4},{5,6},{6,5},{8,11},{11,8},{9,1... | collective-permute-start | bytes 245768 | tf_op jit(solution)/shard_map/ppermute | solution.py:246
  70.1 0.0 collective-permute-done.12
  70.1 0.1 fusion.44
  70.2 3.8 %collective-permute-done.13 = bf16[320,128]{1,0:T(8,128)(2,1)S(1)} collective-permute-done((bf16[320,128]{1,0:T(8,128)(2,1)S(1)}, bf16[320,128]{1,0:T(8,128)(2,1)S(1)}, u32[]{:S(2)}, u32[]{:S(2)}) %collective-permute-start.13) | collective-permute-done | bytes 81952 | tf_op jit(solution)/shard_map/ppermute | solution.py:246
  74.0 0.1 fusion.45
  74.1 0.4 collective-permute-done.14
  74.5 0.1 fusion.46
  74.6 1.0 %convolution_convert_fusion = bf16[512,64]{0,1:T(8,128)(2,1)} fusion(bf16[256,64]{1,0:T(8,128)(2,1)S(1)} %get-tuple-element.50, bf16[256,64]{1,0:T(8,128)(2,1)S(1)} %get-tuple-element.49, bf16[256,64]{1,0:T(8,128)(2,1)S(1)} %get-tuple-element.48, bf16[256,64]{1,0:T(8,128)(2,1)S(1)} %get-tuple-element.47, bf16[256,64]{1,0:T(8,128)(2,1)S(1)} %get-tuple-element.46, ...), kind=kOutput, calls=%fused_computation | convolution fusion | flops 19038208 | bytes 360448 | tf_op jit(solution)/shard_map/rs,si->ri/dot_general | solution.py:249
  75.6 4.9 %all-to-all-done = f32[64,2,128]{2,1,0:T(2,128)S(1)} async-done(((f32[64,2,128]{2,1,0:T(2,128)}), f32[64,2,128]{2,1,0:T(2,128)S(1)}, u32[]{:S(2)}, u32[]{:S(2)}) %all-to-all-start) | async-done | bytes 65568 | tf_op jit(solution)/shard_map/all_to_all | solution.py:245
  80.5 0.1 reduce_sum.89
  80.5 0.1 fusion.47
  80.6 0.6 pad_maximum_fusion.3
  (12 shorter events, 0.2 us)
Async XLA Ops:
  2.3 14.9 %collective-permute-start.1 = (bf16[256,128]{1,0:T(8,128)(2,1)}, bf16[256,128]{1,0:T(8,128)(2,1)S(1)}, u32[]{:S(2)}, u32[]{:S(2)}) collective-permute-start(bf16[256,128]{1,0:T(8,128)(2,1)} %masked.1), channel_id=1, source_target_pairs={{128,0},{129,1},{130,2},{131,3},{132,4},{133,5},{134,6},{135,7},{1... | collective-permute-start | bytes 196616 | tf_op jit(solution)/shard_map/ppermute | solution.py:27
  9.5 10.8 %collective-permute-start.2 = (bf16[256,128]{1,0:T(8,128)(2,1)}, bf16[256,128]{1,0:T(8,128)(2,1)S(1)}, u32[]{:S(2)}, u32[]{:S(2)}) collective-permute-start(bf16[256,128]{1,0:T(8,128)(2,1)} %masked.1), channel_id=1, source_target_pairs={{144,0},{145,1},{146,2},{147,3},{148,4},{149,5},{150,6},{151,7},{1... | collective-permute-start | bytes 196616 | tf_op jit(solution)/shard_map/ppermute | solution.py:27
  11.2 6.0 %collective-permute-start = (bf16[256,128]{1,0:T(8,128)(2,1)}, bf16[256,128]{1,0:T(8,128)(2,1)S(1)}, u32[]{:S(2)}, u32[]{:S(2)}) collective-permute-start(bf16[256,128]{1,0:T(8,128)(2,1)} %masked.1), channel_id=1, source_target_pairs={{16,0},{17,1},{18,2},{19,3},{20,4},{21,5},{22,6},{23,7},{24,8},{25... | collective-permute-start | bytes 196616 | tf_op jit(solution)/shard_map/ppermute | solution.py:27
  21.2 7.7 %collective-permute-start.4 = (bf16[4,256,128]{2,1,0:T(8,128)(2,1)S(1)}, bf16[4,256,128]{2,1,0:T(8,128)(2,1)S(1)}, u32[]{:S(2)}, u32[]{:S(2)}) collective-permute-start(bf16[4,256,128]{2,1,0:T(8,128)(2,1)S(1)} %pad_maximum_fusion.2), channel_id=1, source_target_pairs={{12,0},{225,1},{14,2},{227,3},{0,4},{229,5},{2,6},{231,7},{4,8},{2... | collective-permute-start | bytes 786440 | tf_op jit(solution)/shard_map/ppermute | solution.py:37
  22.7 10.4 %collective-permute-start.5 = (bf16[4,256,128]{2,1,0:T(8,128)(2,1)S(1)}, bf16[4,256,128]{2,1,0:T(8,128)(2,1)S(1)}, u32[]{:S(2)}, u32[]{:S(2)}) collective-permute-start(bf16[4,256,128]{2,1,0:T(8,128)(2,1)S(1)} %pad_maximum_fusion.2), channel_id=1, source_target_pairs={{8,0},{65,1},{10,2},{67,3},{12,4},{69,5},{14,6},{71,7},{0,8},{73,9... | collective-permute-start | bytes 786440 | tf_op jit(solution)/shard_map/ppermute | solution.py:37
  25.5 8.5 %collective-permute-start.3 = (bf16[4,256,128]{2,1,0:T(8,128)(2,1)S(1)}, bf16[4,256,128]{2,1,0:T(8,128)(2,1)S(1)}, u32[]{:S(2)}, u32[]{:S(2)}) collective-permute-start(bf16[4,256,128]{2,1,0:T(8,128)(2,1)S(1)} %pad_maximum_fusion.2), channel_id=1, source_target_pairs={{4,0},{33,1},{6,2},{35,3},{8,4},{37,5},{10,6},{39,7},{12,8},{41,9}... | collective-permute-start | bytes 786440 | tf_op jit(solution)/shard_map/ppermute | solution.py:37
  33.2 10.5 %collective-permute-start.7 = (bf16[2,4,256,128]{3,2,1,0:T(8,128)(2,1)S(1)}, bf16[2,4,256,128]{3,2,1,0:T(8,128)(2,1)S(1)}, u32[]{:S(2)}, u32[]{:S(2)}) collective-permute-start(bf16[2,4,256,128]{3,2,1,0:T(8,128)(2,1)S(1)} %pad_maximum_fusion.1), channel_id=1, source_target_pairs={{224,0},{13,1},{226,2},{15,3},{228,4},{1,5},{230,6},{3,7},{232,8},... | collective-permute-start | bytes 1572872 | tf_op jit(solution)/shard_map/ppermute | solution.py:37
  34.0 9.7 %collective-permute-start.6 = (bf16[2,4,256,128]{3,2,1,0:T(8,128)(2,1)S(1)}, bf16[2,4,256,128]{3,2,1,0:T(8,128)(2,1)S(1)}, u32[]{:S(2)}, u32[]{:S(2)}) collective-permute-start(bf16[2,4,256,128]{3,2,1,0:T(8,128)(2,1)S(1)} %pad_maximum_fusion), channel_id=1, source_target_pairs={{32,0},{5,1},{34,2},{7,3},{36,4},{9,5},{38,6},{11,7},{40,8},{13,9}... | collective-permute-start | bytes 1572872 | tf_op jit(solution)/shard_map/ppermute | solution.py:37
  36.7 12.2 %collective-permute-start.10 = (bf16[2,4,256,128]{3,2,1,0:T(8,128)(2,1)S(1)}, bf16[2,4,256,128]{3,2,1,0:T(8,128)(2,1)S(1)}, u32[]{:S(2)}, u32[]{:S(2)}) collective-permute-start(bf16[2,4,256,128]{3,2,1,0:T(8,128)(2,1)S(1)} %get-tuple-element.42), channel_id=1, source_target_pairs={{32,0},{5,1},{34,2},{7,3},{36,4},{1,5},{38,6},{3,7},{40,8},{13,9},... | collective-permute-start | bytes 1572872 | tf_op jit(solution)/shard_map/ppermute | solution.py:47
  36.8 12.5 %collective-permute-start.11 = (bf16[2,4,256,128]{3,2,1,0:T(8,128)(2,1)S(1)}, bf16[2,4,256,128]{3,2,1,0:T(8,128)(2,1)S(1)}, u32[]{:S(2)}, u32[]{:S(2)}) collective-permute-start(bf16[2,4,256,128]{3,2,1,0:T(8,128)(2,1)S(1)} %get-tuple-element.41), channel_id=1, source_target_pairs={{224,0},{13,1},{226,2},{15,3},{228,4},{9,5},{230,6},{11,7},{232,8}... | collective-permute-start | bytes 1572872 | tf_op jit(solution)/shard_map/ppermute | solution.py:47
  38.6 2.8 %copy-start = (bf16[192,128,128]{2,1,0:T(8,128)(2,1)S(1)}, bf16[192,128,128]{2,1,0:T(8,128)(2,1)}, u32[]{:S(2)}) copy-start(bf16[192,128,128]{2,1,0:T(8,128)(2,1)} %adj.5) | copy-start | bytes 18874372
  43.2 14.2 %copy-start.1 = (bf16[256,64]{0,1:T(8,128)(2,1)S(1)}, bf16[256,64]{0,1:T(8,128)(2,1)}, u32[]{:S(2)}) copy-start(bf16[256,64]{0,1:T(8,128)(2,1)} %param.11) | copy-start | bytes 98308
  43.7 10.9 %collective-permute-start.8 = (bf16[2,4,256,128]{3,2,1,0:T(8,128)(2,1)S(1)}, bf16[2,4,256,128]{3,2,1,0:T(8,128)(2,1)S(1)}, u32[]{:S(2)}, u32[]{:S(2)}) collective-permute-start(bf16[2,4,256,128]{3,2,1,0:T(8,128)(2,1)S(1)} %collective-permute-done.6), channel_id=1, source_target_pairs={{32,0},{5,1},{34,2},{7,3},{36,4},{9,5},{38,6},{11,7},{40,8},{13,9}... | collective-permute-start | bytes 1572872 | tf_op jit(solution)/shard_map/ppermute | solution.py:37
  47.0 10.4 %collective-permute-start.9 = (bf16[2,4,256,128]{3,2,1,0:T(8,128)(2,1)S(1)}, bf16[2,4,256,128]{3,2,1,0:T(8,128)(2,1)S(1)}, u32[]{:S(2)}, u32[]{:S(2)}) collective-permute-start(bf16[2,4,256,128]{3,2,1,0:T(8,128)(2,1)S(1)} %collective-permute-done.7), channel_id=1, source_target_pairs={{224,0},{13,1},{226,2},{15,3},{228,4},{1,5},{230,6},{3,7},{232,8},... | collective-permute-start | bytes 1572872 | tf_op jit(solution)/shard_map/ppermute | solution.py:37
  60.5 9.5 %collective-permute-start.12 = (bf16[320,128]{1,0:T(8,128)(2,1)S(1)}, bf16[320,128]{1,0:T(8,128)(2,1)S(1)}, u32[]{:S(2)}, u32[]{:S(2)}) collective-permute-start(bf16[320,128]{1,0:T(8,128)(2,1)S(1)} %get-tuple-element.32), channel_id=1, source_target_pairs={{0,1},{1,0},{2,3},{3,2},{4,5},{5,4},{6,7},{7,6},{8,9},{9,8},{10,11... | collective-permute-start | bytes 245768 | tf_op jit(solution)/shard_map/ppermute | solution.py:246
  60.6 19.8 %all-to-all-start = ((f32[64,2,128]{2,1,0:T(2,128)}), f32[64,2,128]{2,1,0:T(2,128)S(1)}, u32[]{:S(2)}, u32[]{:S(2)}) async-start(f32[64,2,128]{2,1,0:T(2,128)} %get-tuple-element.35), calls=%async_computation | async-start | bytes 131072 | tf_op jit(solution)/shard_map/all_to_all | solution.py:245
  68.4 5.6 %collective-permute-start.13 = (bf16[320,128]{1,0:T(8,128)(2,1)S(1)}, bf16[320,128]{1,0:T(8,128)(2,1)S(1)}, u32[]{:S(2)}, u32[]{:S(2)}) collective-permute-start(bf16[320,128]{1,0:T(8,128)(2,1)S(1)} %get-tuple-element.33), channel_id=1, source_target_pairs={{0,2},{2,0},{1,3},{3,1},{4,6},{6,4},{5,7},{7,5},{8,10},{10,8},{9,1... | collective-permute-start | bytes 245768 | tf_op jit(solution)/shard_map/ppermute | solution.py:246
  69.3 5.2 %collective-permute-start.14 = (bf16[320,128]{1,0:T(8,128)(2,1)S(1)}, bf16[320,128]{1,0:T(8,128)(2,1)S(1)}, u32[]{:S(2)}, u32[]{:S(2)}) collective-permute-start(bf16[320,128]{1,0:T(8,128)(2,1)S(1)} %get-tuple-element.34), channel_id=1, source_target_pairs={{0,3},{3,0},{1,2},{2,1},{4,7},{7,4},{5,6},{6,5},{8,11},{11,8},{9,1... | collective-permute-start | bytes 245768 | tf_op jit(solution)/shard_map/ppermute | solution.py:246

commit v9 on v8

--- a/solution.py
+++ b/solution.py
@@ -55,14 +55,15 @@
     far_y, far = from_rows(packed, dz=4, dy=1), from_rows(packed, dz=4)
     again, position = lax.optimization_barrier((packed, position))
     four = jnp.stack([packed, from_rows(again, dy=1), far, far_y])
+    high = jnp.stack([from_axis(four, False, -1), from_axis(four, False, 2)])
     low = jnp.stack([lax.optimization_barrier(four), from_axis(four, False, 1)])
-    high = jnp.stack([from_axis(four, False, -1), from_axis(four, False, 2)])
     return low, high, position
 
 
 def gather_near(low, high):
     odd = odd_place()
-    forwarded = [from_axis(low, True, 1), from_axis(high, True, -1)]
+    minus = from_axis(high, True, -1)
+    forwarded = [from_axis(low, True, 1), minus]
     low, high = lax.optimization_barrier((low, high))
     others = [exchange(jnp.where(odd, high, low), False), exchange(jnp.where(odd, low, high), True)]
     return forwarded, others
@@ -155,6 +156,7 @@
         out_shape=jax.ShapeDtypeStruct((256, 128), jnp.bfloat16),
         in_specs=[vmem, vmem],
         out_specs=vmem,
+        compiler_params=pltpu.CompilerParams(vmem_limit_bytes=4 * 1024 * 1024),
         name="masked",
     )(grad_out.T, relu_mask.T)
 
@@ -197,7 +199,8 @@
     for k, ref in enumerate(outs):
         lanes = pl.multiple_of((lax.axis_index("yl") ^ (k >> 1)) * 128, 128)
         of_chip = weights[:, pl.ds(lanes, 128)].astype(jnp.float32)
-        of_core = jnp.where((lax.axis_index("core") ^ (k & 1)) == 0, of_chip, pltpu.roll(of_chip, 64, 1))
+        first = (lax.axis_index("core") ^ (k & 1)) == 0
+        of_core = jnp.where(low == first, of_chip, pltpu.roll(of_chip, 64, 1))
         ref[pl.ds(256, 64), :] = of_core.astype(ref.dtype)
 
 
@@ -219,8 +222,34 @@
     )(table, bounds, adj, *sources, *others)
 
 
-def halves(packed):
-    return jnp.concatenate([packed[:, :64], packed[:, 64:]], axis=0)
+def input_kernel(*refs):
+    *messages, out = refs
+    row = lax.broadcasted_iota(jnp.int32, (128, 128), 0)
+    lane = lax.broadcasted_iota(jnp.int32, (128, 128), 1)
+    factors = []
+    for m in messages:
+        block = m[pl.ds(256, 64), :].astype(jnp.float32)
+        twice = jnp.concatenate([block, block], axis=0).T
+        factors.append(jnp.where((row < 64) == (lane < 64), twice, 0.0).astype(jnp.bfloat16))
+    sums = jnp.concatenate([m[pl.ds(0, 256), :] for m in messages], axis=1)
+    result = lax.dot_general(
+        jnp.concatenate(factors, axis=1), sums, (((1,), (1,)), ((), ())), preferred_element_type=jnp.float32
+    )
+    out[:, pl.ds(0, 256)] = result[:64].astype(out.dtype)
+    out[:, pl.ds(256, 256)] = result[64:].astype(out.dtype)
+
+
+def input_gradient(messages):
+    vmem = pl.BlockSpec(memory_space=pltpu.VMEM)
+    return pl.pallas_call(
+        input_kernel,
+        out_shape=jax.ShapeDtypeStruct((64, 512), jnp.bfloat16),
+        in_specs=[vmem] * len(messages),
+        out_specs=vmem,
+        compiler_params=pltpu.CompilerParams(vmem_limit_bytes=4 * 1024 * 1024),
+        cost_estimate=pl.CostEstimate(flops=2 * 128 * 512 * 256, bytes_accessed=400 * 1024, transcendentals=0),
+        name="input_gradient",
+    )(*messages)
 
 
 def body(adj_tiles, tile_index, grad_out, relu_mask, features, weight):
@@ -244,9 +273,7 @@
 
     pieces = lax.all_to_all(partial, ROWS, 0, 0, tiled=True)
     arrived = messages[:1] + [lax.ppermute(m, SLAB, pairs) for m, pairs in zip(messages[1:], FLIPS)]
-    a_all = jnp.concatenate([halves(m[:256]) for m in arrived], axis=1)
-    w_all = jnp.concatenate([m[256:, :64] for m in arrived], axis=0)
-    grad_input = jnp.einsum("rs,si->ri", a_all, w_all, preferred_element_type=jnp.float32).astype(jnp.bfloat16)
+    grad_input = input_gradient(arrived).T
     total = jnp.sum(pieces, axis=0)
     grad_weight = jnp.concatenate([total[p : p + 1, k : k + 64] for p in range(2) for k in (0, 64)], axis=0)
     return grad_input, grad_weight

time: 82 us -> 80.6 us (0.983)
  local copies, waits for them, and re-layouts: 4.44 us -> 5.81 us
  matrix products: 0.98 us -> 0 us
  other arithmetic: 3.62 us -> 2.78 us
    unnamed x5 -> x9, local copies, waits for them, and re-layouts: 3.88 us -> 5.62 us
    pallas_call x1, Pallas kernels: 1.68 us -> 0.1 us  [masked(): pl.pallas_call(pre_kernel, out_shape=jax.ShapeDtypeStruct((256, 128), jnp...]
    dot_general x1 -> x0, matrix products: 0.98 us -> none  [body(): jnp.einsum('rs,si->ri', a_all, w_all, preferred_element_type=jnp.float32)]
    pallas_call x0 -> x1, Pallas kernels: none -> 0.86 us  [input_gradient(): pl.pallas_call(input_kernel, out_shape=jax.ShapeDtypeStruct((64, 512), jn...]
    another operation x1, other arithmetic: 0.87 us -> 0.04 us  [gather_early(): four = jnp.stack([packed, from_rows(again, dy=1), far, far_y])]
  transfers between devices with their start and end apart: 16 -> 16, of which waited for: 12 -> 12; matrix products, arithmetic and copies ran while one was open for 6% -> 4% of each run, Pallas kernels for 6% -> 7%
where the time goes in v9:
time: 80.6 us; the launch traced here: 80.3 us
  starting transfers between devices  34.7 us (43%)
  waiting for transfers between devices  27.3 us (34%)
  Pallas kernels  8.89 us (11%)
  local copies, waits for them, and re-layouts  5.81 us (7%)
  other arithmetic  2.78 us (3%)
    ppermute x7, starting transfers between devices, from_axis(): return lax.ppermute(value, ALL, pairs)  12.5 us
    ppermute x3, starting transfers between devices, from_rows(): return lax.ppermute(value, ALL, pairs)  10.3 us
    ppermute x7, waiting for transfers between devices, from_axis(): return lax.ppermute(value, ALL, pairs)  10.1 us
    all_to_all x1, starting transfers between devices, body(): pieces = lax.all_to_all(partial, ROWS, 0, 0, tiled=True)  8.05 us
    pallas_call x3, Pallas kernels, call(): pl.pallas_call(kernel, out_shape=out_shape, in_specs=[smem, smem, vmem] +...  7.93 us
    ppermute x3, waiting for transfers between devices, from_rows(): return lax.ppermute(value, ALL, pairs)  5.7 us
    unnamed x9, local copies, waits for them, and re-layouts  5.62 us
    all_to_all x1, waiting for transfers between devices, body(): pieces = lax.all_to_all(partial, ROWS, 0, 0, tiled=True)  4.74 us
  transfers between devices with their start and end apart: 16, of which 12 were waited for; matrix products, arithmetic and copies ran while one was open for 4% of the time, Pallas kernels for 7%

profile of v9, /device:TPU:8, one launch (start us, length us, event | category | flops | bytes accessed | tf_op | source)
XLA Modules:
  0.0 80.3 jit_solution(12257894910708741380)
XLA Ops:
  0.6 0.0 copy-start.1
  0.6 0.9 %copy-done.1 = s32[512,64]{0,1:T(8,128)S(1)} copy-done((s32[512,64]{0,1:T(8,128)S(1)}, s32[512,64]{0,1:T(8,128)}, u32[]{:S(2)}) %copy-start.1) | copy-done | bytes 131096
  1.5 0.0 copy-start.2
  1.5 0.8 %copy-done.2 = bf16[512,64]{0,1:T(8,128)(2,1)S(1)} copy-done((bf16[512,64]{0,1:T(8,128)(2,1)S(1)}, bf16[512,64]{0,1:T(8,128)(2,1)}, u32[]{:S(2)}) %copy-start.2) | copy-done | bytes 65560
  2.4 0.1 masked.1
  2.5 7.3 %collective-permute-start.1 = (bf16[256,128]{1,0:T(8,128)(2,1)S(1)}, bf16[256,128]{1,0:T(8,128)(2,1)S(1)}, u32[]{:S(2)}, u32[]{:S(2)}) collective-permute-start(bf16[256,128]{1,0:T(8,128)(2,1)S(1)} %masked.1), channel_id=1, source_target_pairs={{128,0},{129,1},{130,2},{131,3},{132,4},{133,5},{134,6},{135,7},{1... | collective-permute-start | bytes 196616 | tf_op jit(solution)/shard_map/ppermute | solution.py:27
  9.8 1.8 %collective-permute-start.2 = (bf16[256,128]{1,0:T(8,128)(2,1)S(1)}, bf16[256,128]{1,0:T(8,128)(2,1)S(1)}, u32[]{:S(2)}, u32[]{:S(2)}) collective-permute-start(bf16[256,128]{1,0:T(8,128)(2,1)S(1)} %masked.1), channel_id=1, source_target_pairs={{144,0},{145,1},{146,2},{147,3},{148,4},{149,5},{150,6},{151,7},{1... | collective-permute-start | bytes 196616 | tf_op jit(solution)/shard_map/ppermute | solution.py:27
  11.6 1.2 %collective-permute-start = (bf16[256,128]{1,0:T(8,128)(2,1)S(1)}, bf16[256,128]{1,0:T(8,128)(2,1)S(1)}, u32[]{:S(2)}, u32[]{:S(2)}) collective-permute-start(bf16[256,128]{1,0:T(8,128)(2,1)S(1)} %masked.1), channel_id=1, source_target_pairs={{16,0},{17,1},{18,2},{19,3},{20,4},{21,5},{22,6},{23,7},{24,8},{25... | collective-permute-start | bytes 196616 | tf_op jit(solution)/shard_map/ppermute | solution.py:27
  12.8 0.8 %fusion.15 = (s32[192,1]{0,1:T(1,128)S(1)}, s32[192,1]{0,1:T(1,128)S(1)}, s32[192,1]{0,1:T(1,128)S(1)}) fusion(pred[]{:T(512)S(6)} %eq.199, s32[]{:T(128)S(6)} %sub.146, s32[]{:T(128)S(6)} %add.279, s32[]{:T(128)S(6)} %axis_index.27, s32[]{:T(128)S(6)} %axis_index.33, s32[192,2]{0,1:T(2,128)} %param.7, s32[]{:T(128)S(6)} %mul.83), kind=kLoop, calls=%fused_computation.122 | loop fusion | flops 19200 | bytes 3861 | tf_op jit(solution)/shard_map/add | solution.py:100
  13.6 0.1 convert_reduce_fusion.1
  13.8 0.1 select_reduce_fusion.5
  13.9 0.2 select_reduce_fusion.2
  14.1 0.1 select_reduce_fusion.4.bounds
  14.2 0.1 select_reduce_fusion.3
  14.3 0.2 convert_reduce_fusion
  14.5 0.1 select_reduce_fusion.1
  14.6 2.7 %collective-permute-done = bf16[256,128]{1,0:T(8,128)(2,1)S(1)} collective-permute-done((bf16[256,128]{1,0:T(8,128)(2,1)S(1)}, bf16[256,128]{1,0:T(8,128)(2,1)S(1)}, u32[]{:S(2)}, u32[]{:S(2)}) %collective-permute-start) | collective-permute-done | bytes 65568 | tf_op jit(solution)/shard_map/ppermute | solution.py:27
  17.4 0.0 collective-permute-done.1
  17.4 3.0 %collective-permute-done.2 = bf16[256,128]{1,0:T(8,128)(2,1)S(1)} collective-permute-done((bf16[256,128]{1,0:T(8,128)(2,1)S(1)}, bf16[256,128]{1,0:T(8,128)(2,1)S(1)}, u32[]{:S(2)}, u32[]{:S(2)}) %collective-permute-start.2) | collective-permute-done | bytes 65568 | tf_op jit(solution)/shard_map/ppermute | solution.py:27
  20.4 1.6 %collective-permute-start.4 = (bf16[4,256,128]{2,1,0:T(8,128)(2,1)S(1)}, bf16[4,256,128]{2,1,0:T(8,128)(2,1)S(1)}, u32[]{:S(2)}, u32[]{:S(2)}) collective-permute-start(bf16[4,256,128]{2,1,0:T(8,128)(2,1)S(1)} %pad_maximum_fusion.2), channel_id=1, source_target_pairs={{12,0},{225,1},{14,2},{227,3},{0,4},{229,5},{2,6},{231,7},{4,8},{2... | collective-permute-start | bytes 786440 | tf_op jit(solution)/shard_map/ppermute | solution.py:37
  21.9 2.7 %collective-permute-start.5 = (bf16[4,256,128]{2,1,0:T(8,128)(2,1)S(1)}, bf16[4,256,128]{2,1,0:T(8,128)(2,1)S(1)}, u32[]{:S(2)}, u32[]{:S(2)}) collective-permute-start(bf16[4,256,128]{2,1,0:T(8,128)(2,1)S(1)} %pad_maximum_fusion.2), channel_id=1, source_target_pairs={{8,0},{65,1},{10,2},{67,3},{12,4},{69,5},{14,6},{71,7},{0,8},{73,9... | collective-permute-start | bytes 786440 | tf_op jit(solution)/shard_map/ppermute | solution.py:37
  24.7 1.4 %collective-permute-start.3 = (bf16[4,256,128]{2,1,0:T(8,128)(2,1)S(1)}, bf16[4,256,128]{2,1,0:T(8,128)(2,1)S(1)}, u32[]{:S(2)}, u32[]{:S(2)}) collective-permute-start(bf16[4,256,128]{2,1,0:T(8,128)(2,1)S(1)} %pad_maximum_fusion.2), channel_id=1, source_target_pairs={{4,0},{33,1},{6,2},{35,3},{8,4},{37,5},{10,6},{39,7},{12,8},{41,9}... | collective-permute-start | bytes 786440 | tf_op jit(solution)/shard_map/ppermute | solution.py:37
  26.1 1.1 %copy.11 = bf16[512,256]{0,1:T(8,128)(2,1)S(1)} copy(bf16[512,256]{1,0:T(8,128)(2,1)} %param.10) | data formatting | bytes 524288 | tf_op args[4]
  27.2 0.1 reshape.419
  27.3 0.1 select_reduce_fusion
  27.5 0.6 collective-permute-done.4
  28.0 4.3 %collective-permute-done.5 = bf16[4,256,128]{2,1,0:T(8,128)(2,1)S(1)} collective-permute-done((bf16[4,256,128]{2,1,0:T(8,128)(2,1)S(1)}, bf16[4,256,128]{2,1,0:T(8,128)(2,1)S(1)}, u32[]{:S(2)}, u32[]{:S(2)}) %collective-permute-start.5) | collective-permute-done | bytes 262176 | tf_op jit(solution)/shard_map/ppermute | solution.py:37
  32.4 0.1 pad_maximum_fusion.1
  32.4 0.8 collective-permute-start.7
  33.2 0.0 collective-permute-done.3
  33.2 0.1 pad_maximum_fusion
  33.2 2.6 %collective-permute-start.6 = (bf16[2,4,256,128]{3,2,1,0:T(8,128)(2,1)S(1)}, bf16[2,4,256,128]{3,2,1,0:T(8,128)(2,1)S(1)}, u32[]{:S(2)}, u32[]{:S(2)}) collective-permute-start(bf16[2,4,256,128]{3,2,1,0:T(8,128)(2,1)S(1)} %pad_maximum_fusion), channel_id=1, source_target_pairs={{32,0},{5,1},{34,2},{7,3},{36,4},{9,5},{38,6},{11,7},{40,8},{13,9}... | collective-permute-start | bytes 1572872 | tf_op jit(solution)/shard_map/ppermute | solution.py:37
  35.9 0.1 broadcast_select_fusion
  35.9 0.1 collective-permute-start.10
  36.0 1.8 %collective-permute-start.11 = (bf16[2,4,256,128]{3,2,1,0:T(8,128)(2,1)S(1)}, bf16[2,4,256,128]{3,2,1,0:T(8,128)(2,1)S(1)}, u32[]{:S(2)}, u32[]{:S(2)}) collective-permute-start(bf16[2,4,256,128]{3,2,1,0:T(8,128)(2,1)S(1)} %get-tuple-element.41), channel_id=1, source_target_pairs={{224,0},{13,1},{226,2},{15,3},{228,4},{9,5},{230,6},{11,7},{232,8}... | collective-permute-start | bytes 1572872 | tf_op jit(solution)/shard_map/ppermute | solution.py:47
  37.8 0.0 copy-start
  37.8 2.8 %copy-done = bf16[192,128,128]{2,1,0:T(8,128)(2,1)S(1)} copy-done((bf16[192,128,128]{2,1,0:T(8,128)(2,1)S(1)}, bf16[192,128,128]{2,1,0:T(8,128)(2,1)}, u32[]{:S(2)}) %copy-start) | copy-done | bytes 6291480
  40.6 1.8 %early_tiles.1.refs_4_ = f32[4,128,128]{2,1,0:T(8,128)S(1)} custom-call(s32[384]{0:T(512)S(1)} %add_select_fusion.table, s32[9]{0:T(128)S(1)} %select_reduce_fusion.4.bounds, bf16[192,128,128]{2,1,0:T(8,128)(2,1)S(1)} %copy-done, bf16[16,128,128]{2,1,0:T(8,128)(2,1)S(1)} %bitcast.29, bf16[16,128,128]{2,1,0:T(8,128)(2,1)S(1)} %bitcast.28), custom_call_target="tpu_custom_call" | custom-call | flops 268435456 | bytes 8388608 | tf_op jit(solution)/shard_map/early_tiles/pallas_call | solution.py:211
  42.5 0.0 copy-start.3
  42.5 0.4 collective-permute-done.7
  42.9 0.0 collective-permute-done.6
  42.9 3.4 %collective-permute-start.8 = (bf16[2,4,256,128]{3,2,1,0:T(8,128)(2,1)S(1)}, bf16[2,4,256,128]{3,2,1,0:T(8,128)(2,1)S(1)}, u32[]{:S(2)}, u32[]{:S(2)}) collective-permute-start(bf16[2,4,256,128]{3,2,1,0:T(8,128)(2,1)S(1)} %collective-permute-done.6), channel_id=1, source_target_pairs={{32,0},{5,1},{34,2},{7,3},{36,4},{9,5},{38,6},{11,7},{40,8},{13,9}... | collective-permute-start | bytes 1572872 | tf_op jit(solution)/shard_map/ppermute | solution.py:37
  46.3 0.0 collective-permute-start.9
  46.3 1.8 %collective-permute-done.10 = bf16[2,4,256,128]{3,2,1,0:T(8,128)(2,1)S(1)} collective-permute-done((bf16[2,4,256,128]{3,2,1,0:T(8,128)(2,1)S(1)}, bf16[2,4,256,128]{3,2,1,0:T(8,128)(2,1)S(1)}, u32[]{:S(2)}, u32[]{:S(2)}) %collective-permute-start.10) | collective-permute-done | bytes 524320 | tf_op jit(solution)/shard_map/ppermute | solution.py:47
  48.1 0.4 collective-permute-done.11
  48.5 3.3 %near_tiles.1.refs_2_ = f32[4,128,128]{2,1,0:T(8,128)S(1)} custom-call(s32[384]{0:T(512)S(1)} %add_select_fusion.table, s32[9]{0:T(128)S(1)} %select_reduce_fusion.4.bounds, bf16[192,128,128]{2,1,0:T(8,128)(2,1)S(1)} %copy-done, bf16[16,128,128]{2,1,0:T(8,128)(2,1)S(1)} %bitcast.32, bf16[16,128,128]{2,1,0:T(8,128)(2,1)S(1)} %bitcast.31, ...), custom_call_target="tpu_custom_call" | custom-call | flops 268435456 | bytes 8388608 | tf_op jit(solution)/shard_map/near_tiles/pallas_call | solution.py:211
  51.9 1.9 %collective-permute-done.8 = bf16[2,4,256,128]{3,2,1,0:T(8,128)(2,1)S(1)} collective-permute-done((bf16[2,4,256,128]{3,2,1,0:T(8,128)(2,1)S(1)}, bf16[2,4,256,128]{3,2,1,0:T(8,128)(2,1)S(1)}, u32[]{:S(2)}, u32[]{:S(2)}) %collective-permute-start.8) | collective-permute-done | bytes 524320 | tf_op jit(solution)/shard_map/ppermute | solution.py:37
  53.8 2.8 %collective-permute-done.9 = bf16[2,4,256,128]{3,2,1,0:T(8,128)(2,1)S(1)} collective-permute-done((bf16[2,4,256,128]{3,2,1,0:T(8,128)(2,1)S(1)}, bf16[2,4,256,128]{3,2,1,0:T(8,128)(2,1)S(1)}, u32[]{:S(2)}, u32[]{:S(2)}) %collective-permute-start.9) | collective-permute-done | bytes 524320 | tf_op jit(solution)/shard_map/ppermute | solution.py:37
  56.6 0.0 copy-done.3
  56.7 2.8 %far_tiles.1 = (bf16[320,128]{1,0:T(8,128)(2,1)S(1)}, bf16[320,128]{1,0:T(8,128)(2,1)S(1)}, bf16[320,128]{1,0:T(8,128)(2,1)S(1)}, bf16[320,128]{1,0:T(8,128)(2,1)S(1)}, f32[64,2,128]{2,1,0:T(2,128)}) custom-call(s32[384]{0:T(512)S(1)} %add_select_fusion.table, s32[9]{0:T(128)S(1)} %select_reduce_fusion.4.bounds, bf16[192,128,128]{2,1,0:T(8,128)(2,1)S(1)} %copy-done, ...), custom_call_target="tpu_custom_call" | custom-call | flops 268435456 | bytes 8388608 | tf_op jit(solution)/shard_map/far_tiles/pallas_call | solution.py:211
  59.4 8.1 %all-to-all-start = ((f32[64,2,128]{2,1,0:T(2,128)}), f32[64,2,128]{2,1,0:T(2,128)S(1)}, u32[]{:S(2)}, u32[]{:S(2)}) async-start(f32[64,2,128]{2,1,0:T(2,128)} %get-tuple-element.35), calls=%async_computation | async-start | bytes 131072 | tf_op jit(solution)/shard_map/all_to_all | solution.py:274
  67.5 0.1 collective-permute-start.12
  67.6 0.7 collective-permute-start.13
  68.2 1.2 %collective-permute-start.14 = (bf16[320,128]{1,0:T(8,128)(2,1)S(1)}, bf16[320,128]{1,0:T(8,128)(2,1)S(1)}, u32[]{:S(2)}, u32[]{:S(2)}) collective-permute-start(bf16[320,128]{1,0:T(8,128)(2,1)S(1)} %get-tuple-element.34), channel_id=1, source_target_pairs={{0,3},{3,0},{1,2},{2,1},{4,7},{7,4},{5,6},{6,5},{8,11},{11,8},{9,1... | collective-permute-start | bytes 245768 | tf_op jit(solution)/shard_map/ppermute | solution.py:275
  69.5 0.0 collective-permute-done.12.refs_1_
  69.5 3.6 %collective-permute-done.13.refs_2_ = bf16[320,128]{1,0:T(8,128)(2,1)S(1)} collective-permute-done((bf16[320,128]{1,0:T(8,128)(2,1)S(1)}, bf16[320,128]{1,0:T(8,128)(2,1)S(1)}, u32[]{:S(2)}, u32[]{:S(2)}) %collective-permute-start.13) | collective-permute-done | bytes 81952 | tf_op jit(solution)/shard_map/ppermute | solution.py:275
  73.1 0.9 %collective-permute-done.14.refs_3_ = bf16[320,128]{1,0:T(8,128)(2,1)S(1)} collective-permute-done((bf16[320,128]{1,0:T(8,128)(2,1)S(1)}, bf16[320,128]{1,0:T(8,128)(2,1)S(1)}, u32[]{:S(2)}, u32[]{:S(2)}) %collective-permute-start.14) | collective-permute-done | bytes 81952 | tf_op jit(solution)/shard_map/ppermute | solution.py:275
  74.0 0.9 %input_gradient.1 = bf16[64,512]{1,0:T(8,128)(2,1)} custom-call(bf16[320,128]{1,0:T(8,128)(2,1)S(1)} %get-tuple-element.31.refs_0_, bf16[320,128]{1,0:T(8,128)(2,1)S(1)} %collective-permute-done.12.refs_1_, bf16[320,128]{1,0:T(8,128)(2,1)S(1)} %collective-permute-done.13.refs_2_, bf16[320,128]{1,0:T(8,128)(2,1)S(1)} %collective-permute-done.14.refs_3_), custom_call_target="tpu_custom_call" | custom-call | flops 33554432 | bytes 409600 | tf_op jit(solution)/shard_map/input_gradient/pallas_call | solution.py:244
  74.8 4.7 %all-to-all-done = f32[64,2,128]{2,1,0:T(2,128)S(1)} async-done(((f32[64,2,128]{2,1,0:T(2,128)}), f32[64,2,128]{2,1,0:T(2,128)S(1)}, u32[]{:S(2)}, u32[]{:S(2)}) %all-to-all-start) | async-done | bytes 65568 | tf_op jit(solution)/shard_map/all_to_all | solution.py:274
  79.6 0.1 reduce_sum.89
  79.6 0.1 fusion.20
  79.7 0.6 pad_maximum_fusion.3
  (9 shorter events, 0.2 us)
Async XLA Ops:
  0.6 0.9 %copy-start.1 = (s32[512,64]{0,1:T(8,128)S(1)}, s32[512,64]{0,1:T(8,128)}, u32[]{:S(2)}) copy-start(s32[512,64]{0,1:T(8,128)} %param.9) | copy-start | bytes 393220
  1.5 0.8 %copy-start.2 = (bf16[512,64]{0,1:T(8,128)(2,1)S(1)}, bf16[512,64]{0,1:T(8,128)(2,1)}, u32[]{:S(2)}) copy-start(bf16[512,64]{0,1:T(8,128)(2,1)} %param.8) | copy-start | bytes 196612
  2.5 14.9 %collective-permute-start.1 = (bf16[256,128]{1,0:T(8,128)(2,1)S(1)}, bf16[256,128]{1,0:T(8,128)(2,1)S(1)}, u32[]{:S(2)}, u32[]{:S(2)}) collective-permute-start(bf16[256,128]{1,0:T(8,128)(2,1)S(1)} %masked.1), channel_id=1, source_target_pairs={{128,0},{129,1},{130,2},{131,3},{132,4},{133,5},{134,6},{135,7},{1... | collective-permute-start | bytes 196616 | tf_op jit(solution)/shard_map/ppermute | solution.py:27
  9.8 10.6 %collective-permute-start.2 = (bf16[256,128]{1,0:T(8,128)(2,1)S(1)}, bf16[256,128]{1,0:T(8,128)(2,1)S(1)}, u32[]{:S(2)}, u32[]{:S(2)}) collective-permute-start(bf16[256,128]{1,0:T(8,128)(2,1)S(1)} %masked.1), channel_id=1, source_target_pairs={{144,0},{145,1},{146,2},{147,3},{148,4},{149,5},{150,6},{151,7},{1... | collective-permute-start | bytes 196616 | tf_op jit(solution)/shard_map/ppermute | solution.py:27
  11.6 5.8 %collective-permute-start = (bf16[256,128]{1,0:T(8,128)(2,1)S(1)}, bf16[256,128]{1,0:T(8,128)(2,1)S(1)}, u32[]{:S(2)}, u32[]{:S(2)}) collective-permute-start(bf16[256,128]{1,0:T(8,128)(2,1)S(1)} %masked.1), channel_id=1, source_target_pairs={{16,0},{17,1},{18,2},{19,3},{20,4},{21,5},{22,6},{23,7},{24,8},{25... | collective-permute-start | bytes 196616 | tf_op jit(solution)/shard_map/ppermute | solution.py:27
  20.4 7.7 %collective-permute-start.4 = (bf16[4,256,128]{2,1,0:T(8,128)(2,1)S(1)}, bf16[4,256,128]{2,1,0:T(8,128)(2,1)S(1)}, u32[]{:S(2)}, u32[]{:S(2)}) collective-permute-start(bf16[4,256,128]{2,1,0:T(8,128)(2,1)S(1)} %pad_maximum_fusion.2), channel_id=1, source_target_pairs={{12,0},{225,1},{14,2},{227,3},{0,4},{229,5},{2,6},{231,7},{4,8},{2... | collective-permute-start | bytes 786440 | tf_op jit(solution)/shard_map/ppermute | solution.py:37
  21.9 10.4 %collective-permute-start.5 = (bf16[4,256,128]{2,1,0:T(8,128)(2,1)S(1)}, bf16[4,256,128]{2,1,0:T(8,128)(2,1)S(1)}, u32[]{:S(2)}, u32[]{:S(2)}) collective-permute-start(bf16[4,256,128]{2,1,0:T(8,128)(2,1)S(1)} %pad_maximum_fusion.2), channel_id=1, source_target_pairs={{8,0},{65,1},{10,2},{67,3},{12,4},{69,5},{14,6},{71,7},{0,8},{73,9... | collective-permute-start | bytes 786440 | tf_op jit(solution)/shard_map/ppermute | solution.py:37
  24.7 8.5 %collective-permute-start.3 = (bf16[4,256,128]{2,1,0:T(8,128)(2,1)S(1)}, bf16[4,256,128]{2,1,0:T(8,128)(2,1)S(1)}, u32[]{:S(2)}, u32[]{:S(2)}) collective-permute-start(bf16[4,256,128]{2,1,0:T(8,128)(2,1)S(1)} %pad_maximum_fusion.2), channel_id=1, source_target_pairs={{4,0},{33,1},{6,2},{35,3},{8,4},{37,5},{10,6},{39,7},{12,8},{41,9}... | collective-permute-start | bytes 786440 | tf_op jit(solution)/shard_map/ppermute | solution.py:37
  32.4 10.5 %collective-permute-start.7 = (bf16[2,4,256,128]{3,2,1,0:T(8,128)(2,1)S(1)}, bf16[2,4,256,128]{3,2,1,0:T(8,128)(2,1)S(1)}, u32[]{:S(2)}, u32[]{:S(2)}) collective-permute-start(bf16[2,4,256,128]{3,2,1,0:T(8,128)(2,1)S(1)} %pad_maximum_fusion.1), channel_id=1, source_target_pairs={{224,0},{13,1},{226,2},{15,3},{228,4},{1,5},{230,6},{3,7},{232,8},... | collective-permute-start | bytes 1572872 | tf_op jit(solution)/shard_map/ppermute | solution.py:37
  33.2 9.7 %collective-permute-start.6 = (bf16[2,4,256,128]{3,2,1,0:T(8,128)(2,1)S(1)}, bf16[2,4,256,128]{3,2,1,0:T(8,128)(2,1)S(1)}, u32[]{:S(2)}, u32[]{:S(2)}) collective-permute-start(bf16[2,4,256,128]{3,2,1,0:T(8,128)(2,1)S(1)} %pad_maximum_fusion), channel_id=1, source_target_pairs={{32,0},{5,1},{34,2},{7,3},{36,4},{9,5},{38,6},{11,7},{40,8},{13,9}... | collective-permute-start | bytes 1572872 | tf_op jit(solution)/shard_map/ppermute | solution.py:37
  35.9 12.2 %collective-permute-start.10 = (bf16[2,4,256,128]{3,2,1,0:T(8,128)(2,1)S(1)}, bf16[2,4,256,128]{3,2,1,0:T(8,128)(2,1)S(1)}, u32[]{:S(2)}, u32[]{:S(2)}) collective-permute-start(bf16[2,4,256,128]{3,2,1,0:T(8,128)(2,1)S(1)} %get-tuple-element.42), channel_id=1, source_target_pairs={{32,0},{5,1},{34,2},{7,3},{36,4},{1,5},{38,6},{3,7},{40,8},{13,9},... | collective-permute-start | bytes 1572872 | tf_op jit(solution)/shard_map/ppermute | solution.py:47
  36.0 12.5 %collective-permute-start.11 = (bf16[2,4,256,128]{3,2,1,0:T(8,128)(2,1)S(1)}, bf16[2,4,256,128]{3,2,1,0:T(8,128)(2,1)S(1)}, u32[]{:S(2)}, u32[]{:S(2)}) collective-permute-start(bf16[2,4,256,128]{3,2,1,0:T(8,128)(2,1)S(1)} %get-tuple-element.41), channel_id=1, source_target_pairs={{224,0},{13,1},{226,2},{15,3},{228,4},{9,5},{230,6},{11,7},{232,8}... | collective-permute-start | bytes 1572872 | tf_op jit(solution)/shard_map/ppermute | solution.py:47
  37.8 2.8 %copy-start = (bf16[192,128,128]{2,1,0:T(8,128)(2,1)S(1)}, bf16[192,128,128]{2,1,0:T(8,128)(2,1)}, u32[]{:S(2)}) copy-start(bf16[192,128,128]{2,1,0:T(8,128)(2,1)} %adj.5) | copy-start | bytes 18874372
  42.5 14.2 %copy-start.3 = (bf16[256,64]{0,1:T(8,128)(2,1)S(1)}, bf16[256,64]{0,1:T(8,128)(2,1)}, u32[]{:S(2)}) copy-start(bf16[256,64]{0,1:T(8,128)(2,1)} %param.11) | copy-start | bytes 98308
  42.9 10.9 %collective-permute-start.8 = (bf16[2,4,256,128]{3,2,1,0:T(8,128)(2,1)S(1)}, bf16[2,4,256,128]{3,2,1,0:T(8,128)(2,1)S(1)}, u32[]{:S(2)}, u32[]{:S(2)}) collective-permute-start(bf16[2,4,256,128]{3,2,1,0:T(8,128)(2,1)S(1)} %collective-permute-done.6), channel_id=1, source_target_pairs={{32,0},{5,1},{34,2},{7,3},{36,4},{9,5},{38,6},{11,7},{40,8},{13,9}... | collective-permute-start | bytes 1572872 | tf_op jit(solution)/shard_map/ppermute | solution.py:37
  46.3 10.4 %collective-permute-start.9 = (bf16[2,4,256,128]{3,2,1,0:T(8,128)(2,1)S(1)}, bf16[2,4,256,128]{3,2,1,0:T(8,128)(2,1)S(1)}, u32[]{:S(2)}, u32[]{:S(2)}) collective-permute-start(bf16[2,4,256,128]{3,2,1,0:T(8,128)(2,1)S(1)} %collective-permute-done.7), channel_id=1, source_target_pairs={{224,0},{13,1},{226,2},{15,3},{228,4},{1,5},{230,6},{3,7},{232,8},... | collective-permute-start | bytes 1572872 | tf_op jit(solution)/shard_map/ppermute | solution.py:37
  59.4 20.1 %all-to-all-start = ((f32[64,2,128]{2,1,0:T(2,128)}), f32[64,2,128]{2,1,0:T(2,128)S(1)}, u32[]{:S(2)}, u32[]{:S(2)}) async-start(f32[64,2,128]{2,1,0:T(2,128)} %get-tuple-element.35), calls=%async_computation | async-start | bytes 131072 | tf_op jit(solution)/shard_map/all_to_all | solution.py:274
  67.5 2.0 %collective-permute-start.12 = (bf16[320,128]{1,0:T(8,128)(2,1)S(1)}, bf16[320,128]{1,0:T(8,128)(2,1)S(1)}, u32[]{:S(2)}, u32[]{:S(2)}) collective-permute-start(bf16[320,128]{1,0:T(8,128)(2,1)S(1)} %get-tuple-element.32), channel_id=1, source_target_pairs={{0,1},{1,0},{2,3},{3,2},{4,5},{5,4},{6,7},{7,6},{8,9},{9,8},{10,11... | collective-permute-start | bytes 245768 | tf_op jit(solution)/shard_map/ppermute | solution.py:275
  67.6 5.5 %collective-permute-start.13 = (bf16[320,128]{1,0:T(8,128)(2,1)S(1)}, bf16[320,128]{1,0:T(8,128)(2,1)S(1)}, u32[]{:S(2)}, u32[]{:S(2)}) collective-permute-start(bf16[320,128]{1,0:T(8,128)(2,1)S(1)} %get-tuple-element.33), channel_id=1, source_target_pairs={{0,2},{2,0},{1,3},{3,1},{4,6},{6,4},{5,7},{7,5},{8,10},{10,8},{9,1... | collective-permute-start | bytes 245768 | tf_op jit(solution)/shard_map/ppermute | solution.py:275
  68.2 5.7 %collective-permute-start.14 = (bf16[320,128]{1,0:T(8,128)(2,1)S(1)}, bf16[320,128]{1,0:T(8,128)(2,1)S(1)}, u32[]{:S(2)}, u32[]{:S(2)}) collective-permute-start(bf16[320,128]{1,0:T(8,128)(2,1)S(1)} %get-tuple-element.34), channel_id=1, source_target_pairs={{0,3},{3,0},{1,2},{2,1},{4,7},{7,4},{5,6},{6,5},{8,11},{11,8},{9,1... | collective-permute-start | bytes 245768 | tf_op jit(solution)/shard_map/ppermute | solution.py:275

commit v10 on v9

--- a/solution.py
+++ b/solution.py
@@ -62,15 +62,14 @@
 
 def gather_near(low, high):
     odd = odd_place()
-    minus = from_axis(high, True, -1)
-    forwarded = [from_axis(low, True, 1), minus]
+    forwarded = [from_axis(high, True, -1), from_axis(low, True, 1)]
     low, high = lax.optimization_barrier((low, high))
     others = [exchange(jnp.where(odd, high, low), False), exchange(jnp.where(odd, low, high), True)]
     return forwarded, others
 
 
-def gather_far(plus, minus):
-    return [from_axis(plus, True, 1), from_axis(minus, True, -1)]
+def gather_far(minus, plus):
+    return [from_axis(minus, True, -1), from_axis(plus, True, 1)]
 
 
 def where_held(column):
@@ -86,9 +85,9 @@
     swapped = jnp.where(core == 0, (late == 2) & (a >= 2), (ring == 2) & (lax.axis_index("z") % 2 == 1))
     e = dy + 2 * (upper != swapped).astype(jnp.int32)
     high, odd = a // 2, odd_place().astype(jnp.int32)
-    after = jnp.where(high == 0, 2, 4 + odd)
-    before = jnp.where(high == 1, 3, 5 - odd)
-    source = jnp.where(late == 0, high, jnp.where(late == 1, after, jnp.where(late == 3, before, 6 + high)))
+    after = jnp.where(high == 0, 3, 4 + odd)
+    before = jnp.where(high == 1, 2, 5 - odd)
+    source = jnp.where(late == 0, 1 - high, jnp.where(late == 1, after, jnp.where(late == 3, before, 7 - high)))
     place = (a % 2 * 4 + e) * 2 + block % 2
     return source, place, block // 2
 
@@ -260,10 +259,10 @@
 
     tables = tile_table(tile_index[:, 0] - position * 4, source, place, half, 8)
     f_rows = features.reshape(512, 64, 4).transpose(2, 1, 0).reshape(256, 512)
-    low, high, tables, f_rows = lax.optimization_barrier((low, high, tables, f_rows))
+    high, low, tables, f_rows = lax.optimization_barrier((high, low, tables, f_rows))
 
     sums = jax.ShapeDtypeStruct((4, 128, 128), jnp.float32)
-    acc = call(first_kernel, *tables, adj_tiles, [low, high], [], sums, False, "early_tiles")
+    acc = call(first_kernel, *tables, adj_tiles, [high, low], [], sums, False, "early_tiles")
     forwarded, acc = lax.optimization_barrier((forwarded, acc))
     far = gather_far(*forwarded)
     acc = call(middle_kernel, *tables, adj_tiles, forwarded + others, [acc], sums, False, "near_tiles")

time: 80.6 us -> 81.8 us (1.015)
  starting transfers between devices: 34.7 us -> 37.1 us
  waiting for transfers between devices: 27.3 us -> 26.3 us
    all_to_all x1, starting transfers between devices: 8.05 us -> 10.4 us  [body(): pieces = lax.all_to_all(partial, ROWS, 0, 0, tiled=True)]
    ppermute x2, starting transfers between devices: 1.89 us -> 3.14 us  [exchange(): return lax.ppermute(value, ALL, pairs)]
    ppermute x7, starting transfers between devices: 12.5 us -> 11.3 us  [from_axis(): return lax.ppermute(value, ALL, pairs)]
    ppermute x7, waiting for transfers between devices: 10.1 us -> 8.97 us  [from_axis(): return lax.ppermute(value, ALL, pairs)]
  transfers between devices with their start and end apart: 16 -> 16, of which waited for: 12 -> 10; matrix products, arithmetic and copies ran while one was open for 4% -> 4% of each run, Pallas kernels for 7% -> 7%
where the time goes in v10:
time: 81.8 us; the launch traced here: 81.7 us
  starting transfers between devices  37.1 us (45%)
  waiting for transfers between devices  26.3 us (32%)
  Pallas kernels  8.89 us (11%)
  local copies, waits for them, and re-layouts  5.81 us (7%)
  other arithmetic  2.78 us (3%)
    ppermute x7, starting transfers between devices, from_axis(): return lax.ppermute(value, ALL, pairs)  11.3 us
    all_to_all x1, starting transfers between devices, body(): pieces = lax.all_to_all(partial, ROWS, 0, 0, tiled=True)  10.4 us
    ppermute x3, starting transfers between devices, from_rows(): return lax.ppermute(value, ALL, pairs)  10.3 us
    ppermute x7, waiting for transfers between devices, from_axis(): return lax.ppermute(value, ALL, pairs)  8.97 us
    pallas_call x3, Pallas kernels, call(): pl.pallas_call(kernel, out_shape=out_shape, in_specs=[smem, smem, vmem] +...  7.93 us
    ppermute x3, waiting for transfers between devices, from_rows(): return lax.ppermute(value, ALL, pairs)  5.7 us
    unnamed x9, local copies, waits for them, and re-layouts  5.62 us
    all_to_all x1, waiting for transfers between devices, body(): pieces = lax.all_to_all(partial, ROWS, 0, 0, tiled=True)  4.79 us
  transfers between devices with their start and end apart: 16, of which 10 were waited for; matrix products, arithmetic and copies ran while one was open for 4% of the time, Pallas kernels for 7%

profile of v10, /device:TPU:8, one launch (start us, length us, event | category | flops | bytes accessed | tf_op | source)
XLA Modules:
  0.0 81.7 jit_solution(6684103180130513428)
XLA Ops:
  0.6 0.0 copy-start.1
  0.6 0.9 %copy-done.1 = s32[512,64]{0,1:T(8,128)S(1)} copy-done((s32[512,64]{0,1:T(8,128)S(1)}, s32[512,64]{0,1:T(8,128)}, u32[]{:S(2)}) %copy-start.1) | copy-done | bytes 131096
  1.5 0.0 copy-start.2
  1.5 0.8 %copy-done.2 = bf16[512,64]{0,1:T(8,128)(2,1)S(1)} copy-done((bf16[512,64]{0,1:T(8,128)(2,1)S(1)}, bf16[512,64]{0,1:T(8,128)(2,1)}, u32[]{:S(2)}) %copy-start.2) | copy-done | bytes 65560
  2.4 0.1 masked.1
  2.5 7.3 %collective-permute-start.1 = (bf16[256,128]{1,0:T(8,128)(2,1)S(1)}, bf16[256,128]{1,0:T(8,128)(2,1)S(1)}, u32[]{:S(2)}, u32[]{:S(2)}) collective-permute-start(bf16[256,128]{1,0:T(8,128)(2,1)S(1)} %masked.1), channel_id=1, source_target_pairs={{128,0},{129,1},{130,2},{131,3},{132,4},{133,5},{134,6},{135,7},{1... | collective-permute-start | bytes 196616 | tf_op jit(solution)/shard_map/ppermute | solution.py:27
  9.8 1.8 %collective-permute-start.2 = (bf16[256,128]{1,0:T(8,128)(2,1)S(1)}, bf16[256,128]{1,0:T(8,128)(2,1)S(1)}, u32[]{:S(2)}, u32[]{:S(2)}) collective-permute-start(bf16[256,128]{1,0:T(8,128)(2,1)S(1)} %masked.1), channel_id=1, source_target_pairs={{144,0},{145,1},{146,2},{147,3},{148,4},{149,5},{150,6},{151,7},{1... | collective-permute-start | bytes 196616 | tf_op jit(solution)/shard_map/ppermute | solution.py:27
  11.6 1.2 %collective-permute-start = (bf16[256,128]{1,0:T(8,128)(2,1)S(1)}, bf16[256,128]{1,0:T(8,128)(2,1)S(1)}, u32[]{:S(2)}, u32[]{:S(2)}) collective-permute-start(bf16[256,128]{1,0:T(8,128)(2,1)S(1)} %masked.1), channel_id=1, source_target_pairs={{16,0},{17,1},{18,2},{19,3},{20,4},{21,5},{22,6},{23,7},{24,8},{25... | collective-permute-start | bytes 196616 | tf_op jit(solution)/shard_map/ppermute | solution.py:27
  12.8 0.8 fusion.15
  13.6 0.1 convert_reduce_fusion.1
  13.8 0.1 select_reduce_fusion.5
  13.9 0.2 select_reduce_fusion.2
  14.1 0.1 select_reduce_fusion.4.bounds
  14.2 0.1 select_reduce_fusion.3
  14.3 0.2 convert_reduce_fusion
  14.5 0.1 select_reduce_fusion.1
  14.6 2.7 %collective-permute-done = bf16[256,128]{1,0:T(8,128)(2,1)S(1)} collective-permute-done((bf16[256,128]{1,0:T(8,128)(2,1)S(1)}, bf16[256,128]{1,0:T(8,128)(2,1)S(1)}, u32[]{:S(2)}, u32[]{:S(2)}) %collective-permute-start) | collective-permute-done | bytes 65568 | tf_op jit(solution)/shard_map/ppermute | solution.py:27
  17.4 0.0 collective-permute-done.1
  17.4 3.0 %collective-permute-done.2 = bf16[256,128]{1,0:T(8,128)(2,1)S(1)} collective-permute-done((bf16[256,128]{1,0:T(8,128)(2,1)S(1)}, bf16[256,128]{1,0:T(8,128)(2,1)S(1)}, u32[]{:S(2)}, u32[]{:S(2)}) %collective-permute-start.2) | collective-permute-done | bytes 65568 | tf_op jit(solution)/shard_map/ppermute | solution.py:27
  20.4 2.8 %collective-permute-start.5 = (bf16[4,256,128]{2,1,0:T(8,128)(2,1)S(1)}, bf16[4,256,128]{2,1,0:T(8,128)(2,1)S(1)}, u32[]{:S(2)}, u32[]{:S(2)}) collective-permute-start(bf16[4,256,128]{2,1,0:T(8,128)(2,1)S(1)} %pad_maximum_fusion.2), channel_id=1, source_target_pairs={{4,0},{33,1},{6,2},{35,3},{8,4},{37,5},{10,6},{39,7},{12,8},{41,9}... | collective-permute-start | bytes 786440 | tf_op jit(solution)/shard_map/ppermute | solution.py:37
  23.2 0.0 collective-permute-start.3
  23.2 2.3 %collective-permute-start.4 = (bf16[4,256,128]{2,1,0:T(8,128)(2,1)S(1)}, bf16[4,256,128]{2,1,0:T(8,128)(2,1)S(1)}, u32[]{:S(2)}, u32[]{:S(2)}) collective-permute-start(bf16[4,256,128]{2,1,0:T(8,128)(2,1)S(1)} %pad_maximum_fusion.2), channel_id=1, source_target_pairs={{8,0},{65,1},{10,2},{67,3},{12,4},{69,5},{14,6},{71,7},{0,8},{73,9... | collective-permute-start | bytes 786440 | tf_op jit(solution)/shard_map/ppermute | solution.py:37
  25.5 1.1 %copy.11 = bf16[512,256]{0,1:T(8,128)(2,1)S(1)} copy(bf16[512,256]{1,0:T(8,128)(2,1)} %param.10) | data formatting | bytes 524288 | tf_op args[4]
  26.6 0.1 reshape.420
  26.7 0.1 select_reduce_fusion
  26.9 0.2 collective-permute-done.5
  27.1 0.1 pad_maximum_fusion.1
  27.2 1.6 %collective-permute-start.7 = (bf16[2,4,256,128]{3,2,1,0:T(8,128)(2,1)S(1)}, bf16[2,4,256,128]{3,2,1,0:T(8,128)(2,1)S(1)}, u32[]{:S(2)}, u32[]{:S(2)}) collective-permute-start(bf16[2,4,256,128]{3,2,1,0:T(8,128)(2,1)S(1)} %pad_maximum_fusion.1), channel_id=1, source_target_pairs={{32,0},{5,1},{34,2},{7,3},{36,4},{9,5},{38,6},{11,7},{40,8},{13,9}... | collective-permute-start | bytes 1572872 | tf_op jit(solution)/shard_map/ppermute | solution.py:37
  28.8 4.8 %collective-permute-done.3 = bf16[4,256,128]{2,1,0:T(8,128)(2,1)S(1)} collective-permute-done((bf16[4,256,128]{2,1,0:T(8,128)(2,1)S(1)}, bf16[4,256,128]{2,1,0:T(8,128)(2,1)S(1)}, u32[]{:S(2)}, u32[]{:S(2)}) %collective-permute-start.3) | collective-permute-done | bytes 262176 | tf_op jit(solution)/shard_map/ppermute | solution.py:37
  33.6 0.0 collective-permute-done.4
  33.6 0.1 pad_maximum_fusion
  33.7 1.3 %collective-permute-start.6 = (bf16[2,4,256,128]{3,2,1,0:T(8,128)(2,1)S(1)}, bf16[2,4,256,128]{3,2,1,0:T(8,128)(2,1)S(1)}, u32[]{:S(2)}, u32[]{:S(2)}) collective-permute-start(bf16[2,4,256,128]{3,2,1,0:T(8,128)(2,1)S(1)} %pad_maximum_fusion), channel_id=1, source_target_pairs={{224,0},{13,1},{226,2},{15,3},{228,4},{1,5},{230,6},{3,7},{232,8},... | collective-permute-start | bytes 1572872 | tf_op jit(solution)/shard_map/ppermute | solution.py:37
  35.0 0.1 broadcast_select_fusion
  35.0 1.7 %collective-permute-start.10 = (bf16[2,4,256,128]{3,2,1,0:T(8,128)(2,1)S(1)}, bf16[2,4,256,128]{3,2,1,0:T(8,128)(2,1)S(1)}, u32[]{:S(2)}, u32[]{:S(2)}) collective-permute-start(bf16[2,4,256,128]{3,2,1,0:T(8,128)(2,1)S(1)} %get-tuple-element.42), channel_id=1, source_target_pairs={{32,0},{5,1},{34,2},{7,3},{36,4},{1,5},{38,6},{3,7},{40,8},{13,9},... | collective-permute-start | bytes 1572872 | tf_op jit(solution)/shard_map/ppermute | solution.py:47
  36.8 1.4 %collective-permute-start.11 = (bf16[2,4,256,128]{3,2,1,0:T(8,128)(2,1)S(1)}, bf16[2,4,256,128]{3,2,1,0:T(8,128)(2,1)S(1)}, u32[]{:S(2)}, u32[]{:S(2)}) collective-permute-start(bf16[2,4,256,128]{3,2,1,0:T(8,128)(2,1)S(1)} %get-tuple-element.41), channel_id=1, source_target_pairs={{224,0},{13,1},{226,2},{15,3},{228,4},{9,5},{230,6},{11,7},{232,8}... | collective-permute-start | bytes 1572872 | tf_op jit(solution)/shard_map/ppermute | solution.py:47
  38.2 0.0 copy-start
  38.2 2.8 %copy-done = bf16[192,128,128]{2,1,0:T(8,128)(2,1)S(1)} copy-done((bf16[192,128,128]{2,1,0:T(8,128)(2,1)S(1)}, bf16[192,128,128]{2,1,0:T(8,128)(2,1)}, u32[]{:S(2)}) %copy-start) | copy-done | bytes 6291480
  40.9 1.8 %early_tiles.1.refs_4_ = f32[4,128,128]{2,1,0:T(8,128)S(1)} custom-call(s32[384]{0:T(512)S(1)} %add_select_fusion.table, s32[9]{0:T(128)S(1)} %select_reduce_fusion.4.bounds, bf16[192,128,128]{2,1,0:T(8,128)(2,1)S(1)} %copy-done, bf16[16,128,128]{2,1,0:T(8,128)(2,1)S(1)} %bitcast.29, bf16[16,128,128]{2,1,0:T(8,128)(2,1)S(1)} %bitcast.28), custom_call_target="tpu_custom_call" | custom-call | flops 268435456 | bytes 8388608 | tf_op jit(solution)/shard_map/early_tiles/pallas_call | solution.py:210
  42.8 0.0 copy-start.3
  42.8 0.0 collective-permute-done.7
  42.8 1.3 %collective-permute-done.6 = bf16[2,4,256,128]{3,2,1,0:T(8,128)(2,1)S(1)} collective-permute-done((bf16[2,4,256,128]{3,2,1,0:T(8,128)(2,1)S(1)}, bf16[2,4,256,128]{3,2,1,0:T(8,128)(2,1)S(1)}, u32[]{:S(2)}, u32[]{:S(2)}) %collective-permute-start.6) | collective-permute-done | bytes 524320 | tf_op jit(solution)/shard_map/ppermute | solution.py:37
  44.1 0.1 collective-permute-start.8
  44.3 3.1 %collective-permute-start.9 = (bf16[2,4,256,128]{3,2,1,0:T(8,128)(2,1)S(1)}, bf16[2,4,256,128]{3,2,1,0:T(8,128)(2,1)S(1)}, u32[]{:S(2)}, u32[]{:S(2)}) collective-permute-start(bf16[2,4,256,128]{3,2,1,0:T(8,128)(2,1)S(1)} %collective-permute-done.7), channel_id=1, source_target_pairs={{32,0},{5,1},{34,2},{7,3},{36,4},{9,5},{38,6},{11,7},{40,8},{13,9}... | collective-permute-start | bytes 1572872 | tf_op jit(solution)/shard_map/ppermute | solution.py:37
  47.4 0.0 collective-permute-done.10
  47.4 2.4 %collective-permute-done.11 = bf16[2,4,256,128]{3,2,1,0:T(8,128)(2,1)S(1)} collective-permute-done((bf16[2,4,256,128]{3,2,1,0:T(8,128)(2,1)S(1)}, bf16[2,4,256,128]{3,2,1,0:T(8,128)(2,1)S(1)}, u32[]{:S(2)}, u32[]{:S(2)}) %collective-permute-start.11) | collective-permute-done | bytes 524320 | tf_op jit(solution)/shard_map/ppermute | solution.py:47
  49.7 3.0 %near_tiles.1.refs_2_ = f32[4,128,128]{2,1,0:T(8,128)S(1)} custom-call(s32[384]{0:T(512)S(1)} %add_select_fusion.table, s32[9]{0:T(128)S(1)} %select_reduce_fusion.4.bounds, bf16[192,128,128]{2,1,0:T(8,128)(2,1)S(1)} %copy-done, bf16[16,128,128]{2,1,0:T(8,128)(2,1)S(1)} %bitcast.32, bf16[16,128,128]{2,1,0:T(8,128)(2,1)S(1)} %bitcast.31, ...), custom_call_target="tpu_custom_call" | custom-call | flops 268435456 | bytes 8388608 | tf_op jit(solution)/shard_map/near_tiles/pallas_call | solution.py:210
  52.8 2.6 %collective-permute-done.8 = bf16[2,4,256,128]{3,2,1,0:T(8,128)(2,1)S(1)} collective-permute-done((bf16[2,4,256,128]{3,2,1,0:T(8,128)(2,1)S(1)}, bf16[2,4,256,128]{3,2,1,0:T(8,128)(2,1)S(1)}, u32[]{:S(2)}, u32[]{:S(2)}) %collective-permute-start.8) | collective-permute-done | bytes 524320 | tf_op jit(solution)/shard_map/ppermute | solution.py:37
  55.4 0.0 collective-permute-done.9
  55.4 0.0 copy-done.3
  55.4 3.1 %far_tiles.1 = (bf16[320,128]{1,0:T(8,128)(2,1)S(1)}, bf16[320,128]{1,0:T(8,128)(2,1)S(1)}, bf16[320,128]{1,0:T(8,128)(2,1)S(1)}, bf16[320,128]{1,0:T(8,128)(2,1)S(1)}, f32[64,2,128]{2,1,0:T(2,128)}) custom-call(s32[384]{0:T(512)S(1)} %add_select_fusion.table, s32[9]{0:T(128)S(1)} %select_reduce_fusion.4.bounds, bf16[192,128,128]{2,1,0:T(8,128)(2,1)S(1)} %copy-done, ...), custom_call_target="tpu_custom_call" | custom-call | flops 268435456 | bytes 8388608 | tf_op jit(solution)/shard_map/far_tiles/pallas_call | solution.py:210
  58.4 10.4 %all-to-all-start = ((f32[64,2,128]{2,1,0:T(2,128)}), f32[64,2,128]{2,1,0:T(2,128)S(1)}, u32[]{:S(2)}, u32[]{:S(2)}) async-start(f32[64,2,128]{2,1,0:T(2,128)} %get-tuple-element.35), calls=%async_computation | async-start | bytes 131072 | tf_op jit(solution)/shard_map/all_to_all | solution.py:273
  68.8 0.1 collective-permute-start.12
  68.9 1.2 %collective-permute-start.13 = (bf16[320,128]{1,0:T(8,128)(2,1)S(1)}, bf16[320,128]{1,0:T(8,128)(2,1)S(1)}, u32[]{:S(2)}, u32[]{:S(2)}) collective-permute-start(bf16[320,128]{1,0:T(8,128)(2,1)S(1)} %get-tuple-element.33), channel_id=1, source_target_pairs={{0,2},{2,0},{1,3},{3,1},{4,6},{6,4},{5,7},{7,5},{8,10},{10,8},{9,1... | collective-permute-start | bytes 245768 | tf_op jit(solution)/shard_map/ppermute | solution.py:274
  70.1 0.7 collective-permute-start.14
  70.8 0.0 collective-permute-done.12.refs_1_
  70.8 3.5 %collective-permute-done.13.refs_2_ = bf16[320,128]{1,0:T(8,128)(2,1)S(1)} collective-permute-done((bf16[320,128]{1,0:T(8,128)(2,1)S(1)}, bf16[320,128]{1,0:T(8,128)(2,1)S(1)}, u32[]{:S(2)}, u32[]{:S(2)}) %collective-permute-start.13) | collective-permute-done | bytes 81952 | tf_op jit(solution)/shard_map/ppermute | solution.py:274
  74.4 0.9 %collective-permute-done.14.refs_3_ = bf16[320,128]{1,0:T(8,128)(2,1)S(1)} collective-permute-done((bf16[320,128]{1,0:T(8,128)(2,1)S(1)}, bf16[320,128]{1,0:T(8,128)(2,1)S(1)}, u32[]{:S(2)}, u32[]{:S(2)}) %collective-permute-start.14) | collective-permute-done | bytes 81952 | tf_op jit(solution)/shard_map/ppermute | solution.py:274
  75.3 0.9 %input_gradient.1 = bf16[64,512]{1,0:T(8,128)(2,1)} custom-call(bf16[320,128]{1,0:T(8,128)(2,1)S(1)} %get-tuple-element.31.refs_0_, bf16[320,128]{1,0:T(8,128)(2,1)S(1)} %collective-permute-done.12.refs_1_, bf16[320,128]{1,0:T(8,128)(2,1)S(1)} %collective-permute-done.13.refs_2_, bf16[320,128]{1,0:T(8,128)(2,1)S(1)} %collective-permute-done.14.refs_3_), custom_call_target="tpu_custom_call" | custom-call | flops 33554432 | bytes 409600 | tf_op jit(solution)/shard_map/input_gradient/pallas_call | solution.py:243
  76.1 4.8 %all-to-all-done = f32[64,2,128]{2,1,0:T(2,128)S(1)} async-done(((f32[64,2,128]{2,1,0:T(2,128)}), f32[64,2,128]{2,1,0:T(2,128)S(1)}, u32[]{:S(2)}, u32[]{:S(2)}) %all-to-all-start) | async-done | bytes 65568 | tf_op jit(solution)/shard_map/all_to_all | solution.py:273
  80.9 0.1 reduce_sum.89
  81.0 0.1 fusion.20
  81.1 0.6 pad_maximum_fusion.3
  (9 shorter events, 0.2 us)
Async XLA Ops:
  0.6 0.9 %copy-start.1 = (s32[512,64]{0,1:T(8,128)S(1)}, s32[512,64]{0,1:T(8,128)}, u32[]{:S(2)}) copy-start(s32[512,64]{0,1:T(8,128)} %param.9) | copy-start | bytes 393220
  1.5 0.8 %copy-start.2 = (bf16[512,64]{0,1:T(8,128)(2,1)S(1)}, bf16[512,64]{0,1:T(8,128)(2,1)}, u32[]{:S(2)}) copy-start(bf16[512,64]{0,1:T(8,128)(2,1)} %param.8) | copy-start | bytes 196612
  2.5 14.9 %collective-permute-start.1 = (bf16[256,128]{1,0:T(8,128)(2,1)S(1)}, bf16[256,128]{1,0:T(8,128)(2,1)S(1)}, u32[]{:S(2)}, u32[]{:S(2)}) collective-permute-start(bf16[256,128]{1,0:T(8,128)(2,1)S(1)} %masked.1), channel_id=1, source_target_pairs={{128,0},{129,1},{130,2},{131,3},{132,4},{133,5},{134,6},{135,7},{1... | collective-permute-start | bytes 196616 | tf_op jit(solution)/shard_map/ppermute | solution.py:27
  9.8 10.6 %collective-permute-start.2 = (bf16[256,128]{1,0:T(8,128)(2,1)S(1)}, bf16[256,128]{1,0:T(8,128)(2,1)S(1)}, u32[]{:S(2)}, u32[]{:S(2)}) collective-permute-start(bf16[256,128]{1,0:T(8,128)(2,1)S(1)} %masked.1), channel_id=1, source_target_pairs={{144,0},{145,1},{146,2},{147,3},{148,4},{149,5},{150,6},{151,7},{1... | collective-permute-start | bytes 196616 | tf_op jit(solution)/shard_map/ppermute | solution.py:27
  11.6 5.8 %collective-permute-start = (bf16[256,128]{1,0:T(8,128)(2,1)S(1)}, bf16[256,128]{1,0:T(8,128)(2,1)S(1)}, u32[]{:S(2)}, u32[]{:S(2)}) collective-permute-start(bf16[256,128]{1,0:T(8,128)(2,1)S(1)} %masked.1), channel_id=1, source_target_pairs={{16,0},{17,1},{18,2},{19,3},{20,4},{21,5},{22,6},{23,7},{24,8},{25... | collective-permute-start | bytes 196616 | tf_op jit(solution)/shard_map/ppermute | solution.py:27
  20.4 6.7 %collective-permute-start.5 = (bf16[4,256,128]{2,1,0:T(8,128)(2,1)S(1)}, bf16[4,256,128]{2,1,0:T(8,128)(2,1)S(1)}, u32[]{:S(2)}, u32[]{:S(2)}) collective-permute-start(bf16[4,256,128]{2,1,0:T(8,128)(2,1)S(1)} %pad_maximum_fusion.2), channel_id=1, source_target_pairs={{4,0},{33,1},{6,2},{35,3},{8,4},{37,5},{10,6},{39,7},{12,8},{41,9}... | collective-permute-start | bytes 786440 | tf_op jit(solution)/shard_map/ppermute | solution.py:37
  23.2 10.4 %collective-permute-start.3 = (bf16[4,256,128]{2,1,0:T(8,128)(2,1)S(1)}, bf16[4,256,128]{2,1,0:T(8,128)(2,1)S(1)}, u32[]{:S(2)}, u32[]{:S(2)}) collective-permute-start(bf16[4,256,128]{2,1,0:T(8,128)(2,1)S(1)} %pad_maximum_fusion.2), channel_id=1, source_target_pairs={{12,0},{225,1},{14,2},{227,3},{0,4},{229,5},{2,6},{231,7},{4,8},{2... | collective-permute-start | bytes 786440 | tf_op jit(solution)/shard_map/ppermute | solution.py:37
  23.2 10.4 %collective-permute-start.4 = (bf16[4,256,128]{2,1,0:T(8,128)(2,1)S(1)}, bf16[4,256,128]{2,1,0:T(8,128)(2,1)S(1)}, u32[]{:S(2)}, u32[]{:S(2)}) collective-permute-start(bf16[4,256,128]{2,1,0:T(8,128)(2,1)S(1)} %pad_maximum_fusion.2), channel_id=1, source_target_pairs={{8,0},{65,1},{10,2},{67,3},{12,4},{69,5},{14,6},{71,7},{0,8},{73,9... | collective-permute-start | bytes 786440 | tf_op jit(solution)/shard_map/ppermute | solution.py:37
  27.2 15.6 %collective-permute-start.7 = (bf16[2,4,256,128]{3,2,1,0:T(8,128)(2,1)S(1)}, bf16[2,4,256,128]{3,2,1,0:T(8,128)(2,1)S(1)}, u32[]{:S(2)}, u32[]{:S(2)}) collective-permute-start(bf16[2,4,256,128]{3,2,1,0:T(8,128)(2,1)S(1)} %pad_maximum_fusion.1), channel_id=1, source_target_pairs={{32,0},{5,1},{34,2},{7,3},{36,4},{9,5},{38,6},{11,7},{40,8},{13,9}... | collective-permute-start | bytes 1572872 | tf_op jit(solution)/shard_map/ppermute | solution.py:37
  33.7 10.5 %collective-permute-start.6 = (bf16[2,4,256,128]{3,2,1,0:T(8,128)(2,1)S(1)}, bf16[2,4,256,128]{3,2,1,0:T(8,128)(2,1)S(1)}, u32[]{:S(2)}, u32[]{:S(2)}) collective-permute-start(bf16[2,4,256,128]{3,2,1,0:T(8,128)(2,1)S(1)} %pad_maximum_fusion), channel_id=1, source_target_pairs={{224,0},{13,1},{226,2},{15,3},{228,4},{1,5},{230,6},{3,7},{232,8},... | collective-permute-start | bytes 1572872 | tf_op jit(solution)/shard_map/ppermute | solution.py:37
  35.0 12.3 %collective-permute-start.10 = (bf16[2,4,256,128]{3,2,1,0:T(8,128)(2,1)S(1)}, bf16[2,4,256,128]{3,2,1,0:T(8,128)(2,1)S(1)}, u32[]{:S(2)}, u32[]{:S(2)}) collective-permute-start(bf16[2,4,256,128]{3,2,1,0:T(8,128)(2,1)S(1)} %get-tuple-element.42), channel_id=1, source_target_pairs={{32,0},{5,1},{34,2},{7,3},{36,4},{1,5},{38,6},{3,7},{40,8},{13,9},... | collective-permute-start | bytes 1572872 | tf_op jit(solution)/shard_map/ppermute | solution.py:47
  36.8 13.0 %collective-permute-start.11 = (bf16[2,4,256,128]{3,2,1,0:T(8,128)(2,1)S(1)}, bf16[2,4,256,128]{3,2,1,0:T(8,128)(2,1)S(1)}, u32[]{:S(2)}, u32[]{:S(2)}) collective-permute-start(bf16[2,4,256,128]{3,2,1,0:T(8,128)(2,1)S(1)} %get-tuple-element.41), channel_id=1, source_target_pairs={{224,0},{13,1},{226,2},{15,3},{228,4},{9,5},{230,6},{11,7},{232,8}... | collective-permute-start | bytes 1572872 | tf_op jit(solution)/shard_map/ppermute | solution.py:47
  38.2 2.8 %copy-start = (bf16[192,128,128]{2,1,0:T(8,128)(2,1)S(1)}, bf16[192,128,128]{2,1,0:T(8,128)(2,1)}, u32[]{:S(2)}) copy-start(bf16[192,128,128]{2,1,0:T(8,128)(2,1)} %adj.5) | copy-start | bytes 18874372
  42.8 12.6 %copy-start.3 = (bf16[256,64]{0,1:T(8,128)(2,1)S(1)}, bf16[256,64]{0,1:T(8,128)(2,1)}, u32[]{:S(2)}) copy-start(bf16[256,64]{0,1:T(8,128)(2,1)} %param.11) | copy-start | bytes 98308
  44.1 11.2 %collective-permute-start.8 = (bf16[2,4,256,128]{3,2,1,0:T(8,128)(2,1)S(1)}, bf16[2,4,256,128]{3,2,1,0:T(8,128)(2,1)S(1)}, u32[]{:S(2)}, u32[]{:S(2)}) collective-permute-start(bf16[2,4,256,128]{3,2,1,0:T(8,128)(2,1)S(1)} %collective-permute-done.6), channel_id=1, source_target_pairs={{224,0},{13,1},{226,2},{15,3},{228,4},{1,5},{230,6},{3,7},{232,8},... | collective-permute-start | bytes 1572872 | tf_op jit(solution)/shard_map/ppermute | solution.py:37
  44.3 11.1 %collective-permute-start.9 = (bf16[2,4,256,128]{3,2,1,0:T(8,128)(2,1)S(1)}, bf16[2,4,256,128]{3,2,1,0:T(8,128)(2,1)S(1)}, u32[]{:S(2)}, u32[]{:S(2)}) collective-permute-start(bf16[2,4,256,128]{3,2,1,0:T(8,128)(2,1)S(1)} %collective-permute-done.7), channel_id=1, source_target_pairs={{32,0},{5,1},{34,2},{7,3},{36,4},{9,5},{38,6},{11,7},{40,8},{13,9}... | collective-permute-start | bytes 1572872 | tf_op jit(solution)/shard_map/ppermute | solution.py:37
  58.4 22.5 %all-to-all-start = ((f32[64,2,128]{2,1,0:T(2,128)}), f32[64,2,128]{2,1,0:T(2,128)S(1)}, u32[]{:S(2)}, u32[]{:S(2)}) async-start(f32[64,2,128]{2,1,0:T(2,128)} %get-tuple-element.35), calls=%async_computation | async-start | bytes 131072 | tf_op jit(solution)/shard_map/all_to_all | solution.py:273
  68.8 2.0 %collective-permute-start.12 = (bf16[320,128]{1,0:T(8,128)(2,1)S(1)}, bf16[320,128]{1,0:T(8,128)(2,1)S(1)}, u32[]{:S(2)}, u32[]{:S(2)}) collective-permute-start(bf16[320,128]{1,0:T(8,128)(2,1)S(1)} %get-tuple-element.32), channel_id=1, source_target_pairs={{0,1},{1,0},{2,3},{3,2},{4,5},{5,4},{6,7},{7,6},{8,9},{9,8},{10,11... | collective-permute-start | bytes 245768 | tf_op jit(solution)/shard_map/ppermute | solution.py:274
  68.9 5.4 %collective-permute-start.13 = (bf16[320,128]{1,0:T(8,128)(2,1)S(1)}, bf16[320,128]{1,0:T(8,128)(2,1)S(1)}, u32[]{:S(2)}, u32[]{:S(2)}) collective-permute-start(bf16[320,128]{1,0:T(8,128)(2,1)S(1)} %get-tuple-element.33), channel_id=1, source_target_pairs={{0,2},{2,0},{1,3},{3,1},{4,6},{6,4},{5,7},{7,5},{8,10},{10,8},{9,1... | collective-permute-start | bytes 245768 | tf_op jit(solution)/shard_map/ppermute | solution.py:274
  70.1 5.1 %collective-permute-start.14 = (bf16[320,128]{1,0:T(8,128)(2,1)S(1)}, bf16[320,128]{1,0:T(8,128)(2,1)S(1)}, u32[]{:S(2)}, u32[]{:S(2)}) collective-permute-start(bf16[320,128]{1,0:T(8,128)(2,1)S(1)} %get-tuple-element.34), channel_id=1, source_target_pairs={{0,3},{3,0},{1,2},{2,1},{4,7},{7,4},{5,6},{6,5},{8,11},{11,8},{9,1... | collective-permute-start | bytes 245768 | tf_op jit(solution)/shard_map/ppermute | solution.py:274

commit v11 on v10

--- a/solution.py
+++ b/solution.py
@@ -3,6 +3,7 @@
 from jax import lax
 from jax.experimental import pallas as pl
 from jax.experimental.pallas import tpu as pltpu
+from jax.experimental.layout import Layout, with_layout_constraint
 from jax.sharding import Mesh, PartitionSpec as P
 
 NZ, NY, NX, NL, NC = 8, 2, 4, 2, 2
@@ -143,21 +144,10 @@
     return lax.broadcasted_iota(jnp.int32, (128, 128), 1)
 
 
-def pre_kernel(grad_out, relu_mask, out):
-    g = grad_out[...].astype(jnp.float32) * relu_mask[...].astype(jnp.float32)
-    out[...] = jnp.concatenate([g[:, :256], g[:, 256:]], axis=0).T.astype(out.dtype)
-
-
 def masked(grad_out, relu_mask):
-    vmem = pl.BlockSpec(memory_space=pltpu.VMEM)
-    return pl.pallas_call(
-        pre_kernel,
-        out_shape=jax.ShapeDtypeStruct((256, 128), jnp.bfloat16),
-        in_specs=[vmem, vmem],
-        out_specs=vmem,
-        compiler_params=pltpu.CompilerParams(vmem_limit_bytes=4 * 1024 * 1024),
-        name="masked",
-    )(grad_out.T, relu_mask.T)
+    g_pre = (grad_out.T.astype(jnp.float32) * relu_mask.T.astype(jnp.float32)).astype(jnp.bfloat16)
+    turned = with_layout_constraint(jnp.concatenate([g_pre[:, :256], g_pre[:, 256:]], axis=0), Layout((0, 1)))
+    return with_layout_constraint(turned.T, Layout((0, 1)))
 
 
 def add_sources(table, bounds, adj, sources, first, acc, masks):

time: 81.8 us -> 81 us (level)
  local copies, waits for them, and re-layouts: 5.81 us -> 4.19 us
  other arithmetic: 2.78 us -> 3.72 us
    unnamed x9 -> x5, local copies, waits for them, and re-layouts: 5.62 us -> 3.88 us
    convert_element_type x0 -> x1, other arithmetic: none -> 0.93 us  [masked(): (grad_out.T.astype(jnp.float32) * relu_mask.T.astype(jnp.float32)).astype...]
where the time goes in v11:
time: 81 us; the launch traced here: 80.9 us
  starting transfers between devices  37.4 us (46%)
  waiting for transfers between devices  26 us (32%)
  Pallas kernels  8.8 us (11%)
  local copies, waits for them, and re-layouts  4.19 us (5%)
  other arithmetic  3.72 us (5%)
    ppermute x7, starting transfers between devices, from_axis(): return lax.ppermute(value, ALL, pairs)  11.3 us
    all_to_all x1, starting transfers between devices, body(): pieces = lax.all_to_all(partial, ROWS, 0, 0, tiled=True)  10.7 us
    ppermute x3, starting transfers between devices, from_rows(): return lax.ppermute(value, ALL, pairs)  10.3 us
    ppermute x7, waiting for transfers between devices, from_axis(): return lax.ppermute(value, ALL, pairs)  8.68 us
    pallas_call x3, Pallas kernels, call(): pl.pallas_call(kernel, out_shape=out_shape, in_specs=[smem, smem, vmem] +...  7.94 us
    ppermute x3, waiting for transfers between devices, from_rows(): return lax.ppermute(value, ALL, pairs)  5.7 us
    all_to_all x1, waiting for transfers between devices, body(): pieces = lax.all_to_all(partial, ROWS, 0, 0, tiled=True)  4.79 us
    ppermute x3, waiting for transfers between devices, body(): lax.ppermute(m, SLAB, pairs)  4.44 us
  transfers between devices with their start and end apart: 16, of which 10 were waited for; matrix products, arithmetic and copies ran while one was open for 4% of the time, Pallas kernels for 7%

profile of v11, /device:TPU:8, one launch (start us, length us, event | category | flops | bytes accessed | tf_op | source)
XLA Modules:
  0.0 80.9 jit_solution(15365995002949680180)
XLA Ops:
  0.6 0.9 %fusion.1 = bf16[64,512]{1,0:T(8,128)(2,1)S(1)} fusion(s32[512,64]{0,1:T(8,128)} %param.9, bf16[512,64]{0,1:T(8,128)(2,1)} %param.8), kind=kLoop, calls=%fused_computation.11 | loop fusion | flops 131072 | bytes 262144 | tf_op jit(solution)/shard_map/convert_element_type | solution.py:148
  1.6 0.1 copy.13
  1.7 7.3 %collective-permute-start.1 = (bf16[256,128]{1,0:T(8,128)(2,1)S(1)}, bf16[256,128]{1,0:T(8,128)(2,1)S(1)}, u32[]{:S(2)}, u32[]{:S(2)}) collective-permute-start(bf16[256,128]{1,0:T(8,128)(2,1)S(1)} %bitcast.46), channel_id=1, source_target_pairs={{128,0},{129,1},{130,2},{131,3},{132,4},{133,5},{134,6},{135,7},{1... | collective-permute-start | bytes 196616 | tf_op jit(solution)/shard_map/ppermute | solution.py:28
  9.0 1.8 %collective-permute-start.2 = (bf16[256,128]{1,0:T(8,128)(2,1)S(1)}, bf16[256,128]{1,0:T(8,128)(2,1)S(1)}, u32[]{:S(2)}, u32[]{:S(2)}) collective-permute-start(bf16[256,128]{1,0:T(8,128)(2,1)S(1)} %bitcast.47), channel_id=1, source_target_pairs={{144,0},{145,1},{146,2},{147,3},{148,4},{149,5},{150,6},{151,7},{1... | collective-permute-start | bytes 196616 | tf_op jit(solution)/shard_map/ppermute | solution.py:28
  10.8 1.2 %collective-permute-start = (bf16[256,128]{1,0:T(8,128)(2,1)S(1)}, bf16[256,128]{1,0:T(8,128)(2,1)S(1)}, u32[]{:S(2)}, u32[]{:S(2)}) collective-permute-start(bf16[256,128]{1,0:T(8,128)(2,1)S(1)} %bitcast.48), channel_id=1, source_target_pairs={{16,0},{17,1},{18,2},{19,3},{20,4},{21,5},{22,6},{23,7},{24,8},{25... | collective-permute-start | bytes 196616 | tf_op jit(solution)/shard_map/ppermute | solution.py:28
  12.1 0.8 fusion.16
  12.9 0.1 convert_reduce_fusion.1
  13.0 0.1 select_reduce_fusion.5
  13.1 0.2 select_reduce_fusion.2
  13.3 0.1 select_reduce_fusion.4.bounds
  13.4 0.1 select_reduce_fusion.3
  13.5 0.2 convert_reduce_fusion
  13.8 0.1 select_reduce_fusion.1
  13.9 2.7 %collective-permute-done = bf16[256,128]{1,0:T(8,128)(2,1)S(1)} collective-permute-done((bf16[256,128]{1,0:T(8,128)(2,1)S(1)}, bf16[256,128]{1,0:T(8,128)(2,1)S(1)}, u32[]{:S(2)}, u32[]{:S(2)}) %collective-permute-start) | collective-permute-done | bytes 65568 | tf_op jit(solution)/shard_map/ppermute | solution.py:28
  16.6 0.0 collective-permute-done.1
  16.6 3.0 %collective-permute-done.2 = bf16[256,128]{1,0:T(8,128)(2,1)S(1)} collective-permute-done((bf16[256,128]{1,0:T(8,128)(2,1)S(1)}, bf16[256,128]{1,0:T(8,128)(2,1)S(1)}, u32[]{:S(2)}, u32[]{:S(2)}) %collective-permute-start.2) | collective-permute-done | bytes 65568 | tf_op jit(solution)/shard_map/ppermute | solution.py:28
  19.6 2.8 %collective-permute-start.5 = (bf16[4,256,128]{2,1,0:T(8,128)(2,1)S(1)}, bf16[4,256,128]{2,1,0:T(8,128)(2,1)S(1)}, u32[]{:S(2)}, u32[]{:S(2)}) collective-permute-start(bf16[4,256,128]{2,1,0:T(8,128)(2,1)S(1)} %pad_maximum_fusion.2), channel_id=1, source_target_pairs={{4,0},{33,1},{6,2},{35,3},{8,4},{37,5},{10,6},{39,7},{12,8},{41,9}... | collective-permute-start | bytes 786440 | tf_op jit(solution)/shard_map/ppermute | solution.py:38
  22.4 0.0 collective-permute-start.3
  22.4 2.3 %collective-permute-start.4 = (bf16[4,256,128]{2,1,0:T(8,128)(2,1)S(1)}, bf16[4,256,128]{2,1,0:T(8,128)(2,1)S(1)}, u32[]{:S(2)}, u32[]{:S(2)}) collective-permute-start(bf16[4,256,128]{2,1,0:T(8,128)(2,1)S(1)} %pad_maximum_fusion.2), channel_id=1, source_target_pairs={{8,0},{65,1},{10,2},{67,3},{12,4},{69,5},{14,6},{71,7},{0,8},{73,9... | collective-permute-start | bytes 786440 | tf_op jit(solution)/shard_map/ppermute | solution.py:38
  24.7 1.1 %copy.14 = bf16[512,256]{0,1:T(8,128)(2,1)S(1)} copy(bf16[512,256]{1,0:T(8,128)(2,1)} %param.10) | data formatting | bytes 524288 | tf_op args[4]
  25.8 0.1 reshape.420
  26.0 0.1 select_reduce_fusion
  26.1 0.2 collective-permute-done.5
  26.3 0.1 pad_maximum_fusion.1
  26.4 1.6 %collective-permute-start.7 = (bf16[2,4,256,128]{3,2,1,0:T(8,128)(2,1)S(1)}, bf16[2,4,256,128]{3,2,1,0:T(8,128)(2,1)S(1)}, u32[]{:S(2)}, u32[]{:S(2)}) collective-permute-start(bf16[2,4,256,128]{3,2,1,0:T(8,128)(2,1)S(1)} %pad_maximum_fusion.1), channel_id=1, source_target_pairs={{32,0},{5,1},{34,2},{7,3},{36,4},{9,5},{38,6},{11,7},{40,8},{13,9}... | collective-permute-start | bytes 1572872 | tf_op jit(solution)/shard_map/ppermute | solution.py:38
  28.0 4.8 %collective-permute-done.3 = bf16[4,256,128]{2,1,0:T(8,128)(2,1)S(1)} collective-permute-done((bf16[4,256,128]{2,1,0:T(8,128)(2,1)S(1)}, bf16[4,256,128]{2,1,0:T(8,128)(2,1)S(1)}, u32[]{:S(2)}, u32[]{:S(2)}) %collective-permute-start.3) | collective-permute-done | bytes 262176 | tf_op jit(solution)/shard_map/ppermute | solution.py:38
  32.8 0.0 collective-permute-done.4
  32.8 0.1 pad_maximum_fusion
  32.9 1.3 %collective-permute-start.6 = (bf16[2,4,256,128]{3,2,1,0:T(8,128)(2,1)S(1)}, bf16[2,4,256,128]{3,2,1,0:T(8,128)(2,1)S(1)}, u32[]{:S(2)}, u32[]{:S(2)}) collective-permute-start(bf16[2,4,256,128]{3,2,1,0:T(8,128)(2,1)S(1)} %pad_maximum_fusion), channel_id=1, source_target_pairs={{224,0},{13,1},{226,2},{15,3},{228,4},{1,5},{230,6},{3,7},{232,8},... | collective-permute-start | bytes 1572872 | tf_op jit(solution)/shard_map/ppermute | solution.py:38
  34.2 0.1 broadcast_select_fusion
  34.3 1.7 %collective-permute-start.10 = (bf16[2,4,256,128]{3,2,1,0:T(8,128)(2,1)S(1)}, bf16[2,4,256,128]{3,2,1,0:T(8,128)(2,1)S(1)}, u32[]{:S(2)}, u32[]{:S(2)}) collective-permute-start(bf16[2,4,256,128]{3,2,1,0:T(8,128)(2,1)S(1)} %get-tuple-element.42), channel_id=1, source_target_pairs={{32,0},{5,1},{34,2},{7,3},{36,4},{1,5},{38,6},{3,7},{40,8},{13,9},... | collective-permute-start | bytes 1572872 | tf_op jit(solution)/shard_map/ppermute | solution.py:48
  36.0 1.4 %collective-permute-start.11 = (bf16[2,4,256,128]{3,2,1,0:T(8,128)(2,1)S(1)}, bf16[2,4,256,128]{3,2,1,0:T(8,128)(2,1)S(1)}, u32[]{:S(2)}, u32[]{:S(2)}) collective-permute-start(bf16[2,4,256,128]{3,2,1,0:T(8,128)(2,1)S(1)} %get-tuple-element.41), channel_id=1, source_target_pairs={{224,0},{13,1},{226,2},{15,3},{228,4},{9,5},{230,6},{11,7},{232,8}... | collective-permute-start | bytes 1572872 | tf_op jit(solution)/shard_map/ppermute | solution.py:48
  37.4 0.0 copy-start
  37.4 2.8 %copy-done = bf16[192,128,128]{2,1,0:T(8,128)(2,1)S(1)} copy-done((bf16[192,128,128]{2,1,0:T(8,128)(2,1)S(1)}, bf16[192,128,128]{2,1,0:T(8,128)(2,1)}, u32[]{:S(2)}) %copy-start) | copy-done | bytes 6291480
  40.2 1.8 %early_tiles.1.refs_4_ = f32[4,128,128]{2,1,0:T(8,128)S(1)} custom-call(s32[384]{0:T(512)S(1)} %add_select_fusion.table, s32[9]{0:T(128)S(1)} %select_reduce_fusion.4.bounds, bf16[192,128,128]{2,1,0:T(8,128)(2,1)S(1)} %copy-done, bf16[16,128,128]{2,1,0:T(8,128)(2,1)S(1)} %bitcast.31, bf16[16,128,128]{2,1,0:T(8,128)(2,1)S(1)} %bitcast.30), custom_call_target="tpu_custom_call" | custom-call | flops 268435456 | bytes 8388608 | tf_op jit(solution)/shard_map/early_tiles/pallas_call | solution.py:200
  42.0 0.0 copy-start.1
  42.0 0.0 collective-permute-done.7
  42.0 1.3 %collective-permute-done.6 = bf16[2,4,256,128]{3,2,1,0:T(8,128)(2,1)S(1)} collective-permute-done((bf16[2,4,256,128]{3,2,1,0:T(8,128)(2,1)S(1)}, bf16[2,4,256,128]{3,2,1,0:T(8,128)(2,1)S(1)}, u32[]{:S(2)}, u32[]{:S(2)}) %collective-permute-start.6) | collective-permute-done | bytes 524320 | tf_op jit(solution)/shard_map/ppermute | solution.py:38
  43.4 0.1 collective-permute-start.8
  43.5 3.1 %collective-permute-start.9 = (bf16[2,4,256,128]{3,2,1,0:T(8,128)(2,1)S(1)}, bf16[2,4,256,128]{3,2,1,0:T(8,128)(2,1)S(1)}, u32[]{:S(2)}, u32[]{:S(2)}) collective-permute-start(bf16[2,4,256,128]{3,2,1,0:T(8,128)(2,1)S(1)} %collective-permute-done.7), channel_id=1, source_target_pairs={{32,0},{5,1},{34,2},{7,3},{36,4},{9,5},{38,6},{11,7},{40,8},{13,9}... | collective-permute-start | bytes 1572872 | tf_op jit(solution)/shard_map/ppermute | solution.py:38
  46.6 0.0 collective-permute-done.10
  46.6 2.4 %collective-permute-done.11 = bf16[2,4,256,128]{3,2,1,0:T(8,128)(2,1)S(1)} collective-permute-done((bf16[2,4,256,128]{3,2,1,0:T(8,128)(2,1)S(1)}, bf16[2,4,256,128]{3,2,1,0:T(8,128)(2,1)S(1)}, u32[]{:S(2)}, u32[]{:S(2)}) %collective-permute-start.11) | collective-permute-done | bytes 524320 | tf_op jit(solution)/shard_map/ppermute | solution.py:48
  49.0 3.3 %near_tiles.1.refs_2_ = f32[4,128,128]{2,1,0:T(8,128)S(1)} custom-call(s32[384]{0:T(512)S(1)} %add_select_fusion.table, s32[9]{0:T(128)S(1)} %select_reduce_fusion.4.bounds, bf16[192,128,128]{2,1,0:T(8,128)(2,1)S(1)} %copy-done, bf16[16,128,128]{2,1,0:T(8,128)(2,1)S(1)} %bitcast.34, bf16[16,128,128]{2,1,0:T(8,128)(2,1)S(1)} %bitcast.33, ...), custom_call_target="tpu_custom_call" | custom-call | flops 268435456 | bytes 8388608 | tf_op jit(solution)/shard_map/near_tiles/pallas_call | solution.py:200
  52.3 2.3 %collective-permute-done.8 = bf16[2,4,256,128]{3,2,1,0:T(8,128)(2,1)S(1)} collective-permute-done((bf16[2,4,256,128]{3,2,1,0:T(8,128)(2,1)S(1)}, bf16[2,4,256,128]{3,2,1,0:T(8,128)(2,1)S(1)}, u32[]{:S(2)}, u32[]{:S(2)}) %collective-permute-start.8) | collective-permute-done | bytes 524320 | tf_op jit(solution)/shard_map/ppermute | solution.py:38
  54.6 0.0 collective-permute-done.9
  54.6 0.0 copy-done.1
  54.6 2.8 %far_tiles.1 = (bf16[320,128]{1,0:T(8,128)(2,1)S(1)}, bf16[320,128]{1,0:T(8,128)(2,1)S(1)}, bf16[320,128]{1,0:T(8,128)(2,1)S(1)}, bf16[320,128]{1,0:T(8,128)(2,1)S(1)}, f32[64,2,128]{2,1,0:T(2,128)}) custom-call(s32[384]{0:T(512)S(1)} %add_select_fusion.table, s32[9]{0:T(128)S(1)} %select_reduce_fusion.4.bounds, bf16[192,128,128]{2,1,0:T(8,128)(2,1)S(1)} %copy-done, ...), custom_call_target="tpu_custom_call" | custom-call | flops 268435456 | bytes 8388608 | tf_op jit(solution)/shard_map/far_tiles/pallas_call | solution.py:200
  57.4 10.7 %all-to-all-start = ((f32[64,2,128]{2,1,0:T(2,128)}), f32[64,2,128]{2,1,0:T(2,128)S(1)}, u32[]{:S(2)}, u32[]{:S(2)}) async-start(f32[64,2,128]{2,1,0:T(2,128)} %get-tuple-element.35), calls=%async_computation | async-start | bytes 131072 | tf_op jit(solution)/shard_map/all_to_all | solution.py:263
  68.1 0.1 collective-permute-start.12
  68.2 1.2 %collective-permute-start.13 = (bf16[320,128]{1,0:T(8,128)(2,1)S(1)}, bf16[320,128]{1,0:T(8,128)(2,1)S(1)}, u32[]{:S(2)}, u32[]{:S(2)}) collective-permute-start(bf16[320,128]{1,0:T(8,128)(2,1)S(1)} %get-tuple-element.33), channel_id=1, source_target_pairs={{0,2},{2,0},{1,3},{3,1},{4,6},{6,4},{5,7},{7,5},{8,10},{10,8},{9,1... | collective-permute-start | bytes 245768 | tf_op jit(solution)/shard_map/ppermute | solution.py:264
  69.3 0.7 collective-permute-start.14
  70.0 0.0 collective-permute-done.12.refs_1_
  70.0 3.5 %collective-permute-done.13.refs_2_ = bf16[320,128]{1,0:T(8,128)(2,1)S(1)} collective-permute-done((bf16[320,128]{1,0:T(8,128)(2,1)S(1)}, bf16[320,128]{1,0:T(8,128)(2,1)S(1)}, u32[]{:S(2)}, u32[]{:S(2)}) %collective-permute-start.13) | collective-permute-done | bytes 81952 | tf_op jit(solution)/shard_map/ppermute | solution.py:264
  73.6 0.9 %collective-permute-done.14.refs_3_ = bf16[320,128]{1,0:T(8,128)(2,1)S(1)} collective-permute-done((bf16[320,128]{1,0:T(8,128)(2,1)S(1)}, bf16[320,128]{1,0:T(8,128)(2,1)S(1)}, u32[]{:S(2)}, u32[]{:S(2)}) %collective-permute-start.14) | collective-permute-done | bytes 81952 | tf_op jit(solution)/shard_map/ppermute | solution.py:264
  74.5 0.9 %input_gradient.1 = bf16[64,512]{1,0:T(8,128)(2,1)} custom-call(bf16[320,128]{1,0:T(8,128)(2,1)S(1)} %get-tuple-element.31.refs_0_, bf16[320,128]{1,0:T(8,128)(2,1)S(1)} %collective-permute-done.12.refs_1_, bf16[320,128]{1,0:T(8,128)(2,1)S(1)} %collective-permute-done.13.refs_2_, bf16[320,128]{1,0:T(8,128)(2,1)S(1)} %collective-permute-done.14.refs_3_), custom_call_target="tpu_custom_call" | custom-call | flops 33554432 | bytes 409600 | tf_op jit(solution)/shard_map/input_gradient/pallas_call | solution.py:233
  75.3 4.8 %all-to-all-done = f32[64,2,128]{2,1,0:T(2,128)S(1)} async-done(((f32[64,2,128]{2,1,0:T(2,128)}), f32[64,2,128]{2,1,0:T(2,128)S(1)}, u32[]{:S(2)}, u32[]{:S(2)}) %all-to-all-start) | async-done | bytes 65568 | tf_op jit(solution)/shard_map/all_to_all | solution.py:263
  80.1 0.1 reduce_sum.89
  80.2 0.1 fusion.22
  80.3 0.6 pad_maximum_fusion.4
  (11 shorter events, 0.2 us)
Async XLA Ops:
  1.7 14.9 %collective-permute-start.1 = (bf16[256,128]{1,0:T(8,128)(2,1)S(1)}, bf16[256,128]{1,0:T(8,128)(2,1)S(1)}, u32[]{:S(2)}, u32[]{:S(2)}) collective-permute-start(bf16[256,128]{1,0:T(8,128)(2,1)S(1)} %bitcast.46), channel_id=1, source_target_pairs={{128,0},{129,1},{130,2},{131,3},{132,4},{133,5},{134,6},{135,7},{1... | collective-permute-start | bytes 196616 | tf_op jit(solution)/shard_map/ppermute | solution.py:28
  9.0 10.6 %collective-permute-start.2 = (bf16[256,128]{1,0:T(8,128)(2,1)S(1)}, bf16[256,128]{1,0:T(8,128)(2,1)S(1)}, u32[]{:S(2)}, u32[]{:S(2)}) collective-permute-start(bf16[256,128]{1,0:T(8,128)(2,1)S(1)} %bitcast.47), channel_id=1, source_target_pairs={{144,0},{145,1},{146,2},{147,3},{148,4},{149,5},{150,6},{151,7},{1... | collective-permute-start | bytes 196616 | tf_op jit(solution)/shard_map/ppermute | solution.py:28
  10.8 5.8 %collective-permute-start = (bf16[256,128]{1,0:T(8,128)(2,1)S(1)}, bf16[256,128]{1,0:T(8,128)(2,1)S(1)}, u32[]{:S(2)}, u32[]{:S(2)}) collective-permute-start(bf16[256,128]{1,0:T(8,128)(2,1)S(1)} %bitcast.48), channel_id=1, source_target_pairs={{16,0},{17,1},{18,2},{19,3},{20,4},{21,5},{22,6},{23,7},{24,8},{25... | collective-permute-start | bytes 196616 | tf_op jit(solution)/shard_map/ppermute | solution.py:28
  19.6 6.7 %collective-permute-start.5 = (bf16[4,256,128]{2,1,0:T(8,128)(2,1)S(1)}, bf16[4,256,128]{2,1,0:T(8,128)(2,1)S(1)}, u32[]{:S(2)}, u32[]{:S(2)}) collective-permute-start(bf16[4,256,128]{2,1,0:T(8,128)(2,1)S(1)} %pad_maximum_fusion.2), channel_id=1, source_target_pairs={{4,0},{33,1},{6,2},{35,3},{8,4},{37,5},{10,6},{39,7},{12,8},{41,9}... | collective-permute-start | bytes 786440 | tf_op jit(solution)/shard_map/ppermute | solution.py:38
  22.4 10.4 %collective-permute-start.3 = (bf16[4,256,128]{2,1,0:T(8,128)(2,1)S(1)}, bf16[4,256,128]{2,1,0:T(8,128)(2,1)S(1)}, u32[]{:S(2)}, u32[]{:S(2)}) collective-permute-start(bf16[4,256,128]{2,1,0:T(8,128)(2,1)S(1)} %pad_maximum_fusion.2), channel_id=1, source_target_pairs={{12,0},{225,1},{14,2},{227,3},{0,4},{229,5},{2,6},{231,7},{4,8},{2... | collective-permute-start | bytes 786440 | tf_op jit(solution)/shard_map/ppermute | solution.py:38
  22.4 10.4 %collective-permute-start.4 = (bf16[4,256,128]{2,1,0:T(8,128)(2,1)S(1)}, bf16[4,256,128]{2,1,0:T(8,128)(2,1)S(1)}, u32[]{:S(2)}, u32[]{:S(2)}) collective-permute-start(bf16[4,256,128]{2,1,0:T(8,128)(2,1)S(1)} %pad_maximum_fusion.2), channel_id=1, source_target_pairs={{8,0},{65,1},{10,2},{67,3},{12,4},{69,5},{14,6},{71,7},{0,8},{73,9... | collective-permute-start | bytes 786440 | tf_op jit(solution)/shard_map/ppermute | solution.py:38
  26.4 15.6 %collective-permute-start.7 = (bf16[2,4,256,128]{3,2,1,0:T(8,128)(2,1)S(1)}, bf16[2,4,256,128]{3,2,1,0:T(8,128)(2,1)S(1)}, u32[]{:S(2)}, u32[]{:S(2)}) collective-permute-start(bf16[2,4,256,128]{3,2,1,0:T(8,128)(2,1)S(1)} %pad_maximum_fusion.1), channel_id=1, source_target_pairs={{32,0},{5,1},{34,2},{7,3},{36,4},{9,5},{38,6},{11,7},{40,8},{13,9}... | collective-permute-start | bytes 1572872 | tf_op jit(solution)/shard_map/ppermute | solution.py:38
  32.9 10.5 %collective-permute-start.6 = (bf16[2,4,256,128]{3,2,1,0:T(8,128)(2,1)S(1)}, bf16[2,4,256,128]{3,2,1,0:T(8,128)(2,1)S(1)}, u32[]{:S(2)}, u32[]{:S(2)}) collective-permute-start(bf16[2,4,256,128]{3,2,1,0:T(8,128)(2,1)S(1)} %pad_maximum_fusion), channel_id=1, source_target_pairs={{224,0},{13,1},{226,2},{15,3},{228,4},{1,5},{230,6},{3,7},{232,8},... | collective-permute-start | bytes 1572872 | tf_op jit(solution)/shard_map/ppermute | solution.py:38
  34.3 12.3 %collective-permute-start.10 = (bf16[2,4,256,128]{3,2,1,0:T(8,128)(2,1)S(1)}, bf16[2,4,256,128]{3,2,1,0:T(8,128)(2,1)S(1)}, u32[]{:S(2)}, u32[]{:S(2)}) collective-permute-start(bf16[2,4,256,128]{3,2,1,0:T(8,128)(2,1)S(1)} %get-tuple-element.42), channel_id=1, source_target_pairs={{32,0},{5,1},{34,2},{7,3},{36,4},{1,5},{38,6},{3,7},{40,8},{13,9},... | collective-permute-start | bytes 1572872 | tf_op jit(solution)/shard_map/ppermute | solution.py:48
  36.0 13.0 %collective-permute-start.11 = (bf16[2,4,256,128]{3,2,1,0:T(8,128)(2,1)S(1)}, bf16[2,4,256,128]{3,2,1,0:T(8,128)(2,1)S(1)}, u32[]{:S(2)}, u32[]{:S(2)}) collective-permute-start(bf16[2,4,256,128]{3,2,1,0:T(8,128)(2,1)S(1)} %get-tuple-element.41), channel_id=1, source_target_pairs={{224,0},{13,1},{226,2},{15,3},{228,4},{9,5},{230,6},{11,7},{232,8}... | collective-permute-start | bytes 1572872 | tf_op jit(solution)/shard_map/ppermute | solution.py:48
  37.4 2.8 %copy-start = (bf16[192,128,128]{2,1,0:T(8,128)(2,1)S(1)}, bf16[192,128,128]{2,1,0:T(8,128)(2,1)}, u32[]{:S(2)}) copy-start(bf16[192,128,128]{2,1,0:T(8,128)(2,1)} %adj.5) | copy-start | bytes 18874372
  42.0 12.6 %copy-start.1 = (bf16[256,64]{0,1:T(8,128)(2,1)S(1)}, bf16[256,64]{0,1:T(8,128)(2,1)}, u32[]{:S(2)}) copy-start(bf16[256,64]{0,1:T(8,128)(2,1)} %param.11) | copy-start | bytes 98308
  43.4 11.2 %collective-permute-start.8 = (bf16[2,4,256,128]{3,2,1,0:T(8,128)(2,1)S(1)}, bf16[2,4,256,128]{3,2,1,0:T(8,128)(2,1)S(1)}, u32[]{:S(2)}, u32[]{:S(2)}) collective-permute-start(bf16[2,4,256,128]{3,2,1,0:T(8,128)(2,1)S(1)} %collective-permute-done.6), channel_id=1, source_target_pairs={{224,0},{13,1},{226,2},{15,3},{228,4},{1,5},{230,6},{3,7},{232,8},... | collective-permute-start | bytes 1572872 | tf_op jit(solution)/shard_map/ppermute | solution.py:38
  43.5 11.1 %collective-permute-start.9 = (bf16[2,4,256,128]{3,2,1,0:T(8,128)(2,1)S(1)}, bf16[2,4,256,128]{3,2,1,0:T(8,128)(2,1)S(1)}, u32[]{:S(2)}, u32[]{:S(2)}) collective-permute-start(bf16[2,4,256,128]{3,2,1,0:T(8,128)(2,1)S(1)} %collective-permute-done.7), channel_id=1, source_target_pairs={{32,0},{5,1},{34,2},{7,3},{36,4},{9,5},{38,6},{11,7},{40,8},{13,9}... | collective-permute-start | bytes 1572872 | tf_op jit(solution)/shard_map/ppermute | solution.py:38
  57.4 22.8 %all-to-all-start = ((f32[64,2,128]{2,1,0:T(2,128)}), f32[64,2,128]{2,1,0:T(2,128)S(1)}, u32[]{:S(2)}, u32[]{:S(2)}) async-start(f32[64,2,128]{2,1,0:T(2,128)} %get-tuple-element.35), calls=%async_computation | async-start | bytes 131072 | tf_op jit(solution)/shard_map/all_to_all | solution.py:263
  68.1 2.0 %collective-permute-start.12 = (bf16[320,128]{1,0:T(8,128)(2,1)S(1)}, bf16[320,128]{1,0:T(8,128)(2,1)S(1)}, u32[]{:S(2)}, u32[]{:S(2)}) collective-permute-start(bf16[320,128]{1,0:T(8,128)(2,1)S(1)} %get-tuple-element.32), channel_id=1, source_target_pairs={{0,1},{1,0},{2,3},{3,2},{4,5},{5,4},{6,7},{7,6},{8,9},{9,8},{10,11... | collective-permute-start | bytes 245768 | tf_op jit(solution)/shard_map/ppermute | solution.py:264
  68.2 5.4 %collective-permute-start.13 = (bf16[320,128]{1,0:T(8,128)(2,1)S(1)}, bf16[320,128]{1,0:T(8,128)(2,1)S(1)}, u32[]{:S(2)}, u32[]{:S(2)}) collective-permute-start(bf16[320,128]{1,0:T(8,128)(2,1)S(1)} %get-tuple-element.33), channel_id=1, source_target_pairs={{0,2},{2,0},{1,3},{3,1},{4,6},{6,4},{5,7},{7,5},{8,10},{10,8},{9,1... | collective-permute-start | bytes 245768 | tf_op jit(solution)/shard_map/ppermute | solution.py:264
  69.3 5.1 %collective-permute-start.14 = (bf16[320,128]{1,0:T(8,128)(2,1)S(1)}, bf16[320,128]{1,0:T(8,128)(2,1)S(1)}, u32[]{:S(2)}, u32[]{:S(2)}) collective-permute-start(bf16[320,128]{1,0:T(8,128)(2,1)S(1)} %get-tuple-element.34), channel_id=1, source_target_pairs={{0,3},{3,0},{1,2},{2,1},{4,7},{7,4},{5,6},{6,5},{8,11},{11,8},{9,1... | collective-permute-start | bytes 245768 | tf_op jit(solution)/shard_map/ppermute | solution.py:264

commit v12 on v9

--- a/solution.py
+++ b/solution.py
@@ -3,6 +3,7 @@
 from jax import lax
 from jax.experimental import pallas as pl
 from jax.experimental.pallas import tpu as pltpu
+from jax.experimental.layout import Layout, with_layout_constraint
 from jax.sharding import Mesh, PartitionSpec as P
 
 NZ, NY, NX, NL, NC = 8, 2, 4, 2, 2
@@ -144,21 +145,10 @@
     return lax.broadcasted_iota(jnp.int32, (128, 128), 1)
 
 
-def pre_kernel(grad_out, relu_mask, out):
-    g = grad_out[...].astype(jnp.float32) * relu_mask[...].astype(jnp.float32)
-    out[...] = jnp.concatenate([g[:, :256], g[:, 256:]], axis=0).T.astype(out.dtype)
-
-
 def masked(grad_out, relu_mask):
-    vmem = pl.BlockSpec(memory_space=pltpu.VMEM)
-    return pl.pallas_call(
-        pre_kernel,
-        out_shape=jax.ShapeDtypeStruct((256, 128), jnp.bfloat16),
-        in_specs=[vmem, vmem],
-        out_specs=vmem,
-        compiler_params=pltpu.CompilerParams(vmem_limit_bytes=4 * 1024 * 1024),
-        name="masked",
-    )(grad_out.T, relu_mask.T)
+    g_pre = (grad_out.T.astype(jnp.float32) * relu_mask.T.astype(jnp.float32)).astype(jnp.bfloat16)
+    turned = with_layout_constraint(jnp.concatenate([g_pre[:, :256], g_pre[:, 256:]], axis=0), Layout((0, 1)))
+    return with_layout_constraint(turned.T, Layout((0, 1)))
 
 
 def add_sources(table, bounds, adj, sources, first, acc, masks):

time: 80.6 us -> 79.8 us (0.990)
  local copies, waits for them, and re-layouts: 5.81 us -> 4.19 us
  other arithmetic: 2.78 us -> 3.71 us
    unnamed x9 -> x5, local copies, waits for them, and re-layouts: 5.62 us -> 3.88 us
    convert_element_type x0 -> x1, other arithmetic: none -> 0.93 us  [masked(): (grad_out.T.astype(jnp.float32) * relu_mask.T.astype(jnp.float32)).astype...]
  transfers between devices with their start and end apart: 16 -> 16, of which waited for: 12 -> 12; matrix products, arithmetic and copies ran while one was open for 4% -> 4% of each run, Pallas kernels for 7% -> 8%
where the time goes in v12:
time: 79.8 us; the launch traced here: 79.5 us
  starting transfers between devices  34.8 us (44%)
  waiting for transfers between devices  27.3 us (34%)
  Pallas kernels  8.79 us (11%)
  local copies, waits for them, and re-layouts  4.19 us (5%)
  other arithmetic  3.71 us (5%)
  between operations  0.8 us (1%)
    ppermute x7, starting transfers between devices, from_axis(): return lax.ppermute(value, ALL, pairs)  12.5 us
    ppermute x3, starting transfers between devices, from_rows(): return lax.ppermute(value, ALL, pairs)  10.3 us
    ppermute x7, waiting for transfers between devices, from_axis(): return lax.ppermute(value, ALL, pairs)  10.1 us
    all_to_all x1, starting transfers between devices, body(): pieces = lax.all_to_all(partial, ROWS, 0, 0, tiled=True)  8.07 us
    pallas_call x3, Pallas kernels, call(): pl.pallas_call(kernel, out_shape=out_shape, in_specs=[smem, smem, vmem] +...  7.93 us
    ppermute x3, waiting for transfers between devices, from_rows(): return lax.ppermute(value, ALL, pairs)  5.7 us
    all_to_all x1, waiting for transfers between devices, body(): pieces = lax.all_to_all(partial, ROWS, 0, 0, tiled=True)  4.74 us
    ppermute x3, waiting for transfers between devices, body(): lax.ppermute(m, SLAB, pairs)  4.49 us
  transfers between devices with their start and end apart: 16, of which 12 were waited for; matrix products, arithmetic and copies ran while one was open for 4% of the time, Pallas kernels for 8%

profile of v12, /device:TPU:8, one launch (start us, length us, event | category | flops | bytes accessed | tf_op | source)
XLA Modules:
  0.0 79.5 jit_solution(9761503342578427233)
XLA Ops:
  0.6 0.9 %fusion.1 = bf16[64,512]{1,0:T(8,128)(2,1)S(1)} fusion(s32[512,64]{0,1:T(8,128)} %param.9, bf16[512,64]{0,1:T(8,128)(2,1)} %param.8), kind=kLoop, calls=%fused_computation.11 | loop fusion | flops 131072 | bytes 262144 | tf_op jit(solution)/shard_map/convert_element_type | solution.py:149
  1.6 0.1 copy.13
  1.7 7.3 %collective-permute-start.1 = (bf16[256,128]{1,0:T(8,128)(2,1)S(1)}, bf16[256,128]{1,0:T(8,128)(2,1)S(1)}, u32[]{:S(2)}, u32[]{:S(2)}) collective-permute-start(bf16[256,128]{1,0:T(8,128)(2,1)S(1)} %bitcast.46), channel_id=1, source_target_pairs={{128,0},{129,1},{130,2},{131,3},{132,4},{133,5},{134,6},{135,7},{1... | collective-permute-start | bytes 196616 | tf_op jit(solution)/shard_map/ppermute | solution.py:28
  9.0 1.8 %collective-permute-start.2 = (bf16[256,128]{1,0:T(8,128)(2,1)S(1)}, bf16[256,128]{1,0:T(8,128)(2,1)S(1)}, u32[]{:S(2)}, u32[]{:S(2)}) collective-permute-start(bf16[256,128]{1,0:T(8,128)(2,1)S(1)} %bitcast.47), channel_id=1, source_target_pairs={{144,0},{145,1},{146,2},{147,3},{148,4},{149,5},{150,6},{151,7},{1... | collective-permute-start | bytes 196616 | tf_op jit(solution)/shard_map/ppermute | solution.py:28
  10.8 1.2 %collective-permute-start = (bf16[256,128]{1,0:T(8,128)(2,1)S(1)}, bf16[256,128]{1,0:T(8,128)(2,1)S(1)}, u32[]{:S(2)}, u32[]{:S(2)}) collective-permute-start(bf16[256,128]{1,0:T(8,128)(2,1)S(1)} %bitcast.48), channel_id=1, source_target_pairs={{16,0},{17,1},{18,2},{19,3},{20,4},{21,5},{22,6},{23,7},{24,8},{25... | collective-permute-start | bytes 196616 | tf_op jit(solution)/shard_map/ppermute | solution.py:28
  12.1 0.8 %fusion.16 = (s32[192,1]{0,1:T(1,128)S(1)}, s32[192,1]{0,1:T(1,128)S(1)}, s32[192,1]{0,1:T(1,128)S(1)}) fusion(pred[]{:T(512)S(6)} %eq.199, s32[]{:T(128)S(6)} %sub.146, s32[]{:T(128)S(6)} %add.279, s32[]{:T(128)S(6)} %axis_index.27, s32[]{:T(128)S(6)} %axis_index.33, s32[192,2]{0,1:T(2,128)} %param.7, s32[]{:T(128)S(6)} %mul.88), kind=kLoop, calls=%fused_computation.125 | loop fusion | flops 19200 | bytes 3861 | tf_op jit(solution)/shard_map/add | solution.py:101
  12.9 0.1 convert_reduce_fusion.1
  13.0 0.1 select_reduce_fusion.5
  13.1 0.2 select_reduce_fusion.2
  13.3 0.1 select_reduce_fusion.4.bounds
  13.4 0.1 select_reduce_fusion.3
  13.5 0.2 convert_reduce_fusion
  13.8 0.1 select_reduce_fusion.1
  13.9 2.7 %collective-permute-done = bf16[256,128]{1,0:T(8,128)(2,1)S(1)} collective-permute-done((bf16[256,128]{1,0:T(8,128)(2,1)S(1)}, bf16[256,128]{1,0:T(8,128)(2,1)S(1)}, u32[]{:S(2)}, u32[]{:S(2)}) %collective-permute-start) | collective-permute-done | bytes 65568 | tf_op jit(solution)/shard_map/ppermute | solution.py:28
  16.6 0.0 collective-permute-done.1
  16.6 3.0 %collective-permute-done.2 = bf16[256,128]{1,0:T(8,128)(2,1)S(1)} collective-permute-done((bf16[256,128]{1,0:T(8,128)(2,1)S(1)}, bf16[256,128]{1,0:T(8,128)(2,1)S(1)}, u32[]{:S(2)}, u32[]{:S(2)}) %collective-permute-start.2) | collective-permute-done | bytes 65568 | tf_op jit(solution)/shard_map/ppermute | solution.py:28
  19.6 1.6 %collective-permute-start.4 = (bf16[4,256,128]{2,1,0:T(8,128)(2,1)S(1)}, bf16[4,256,128]{2,1,0:T(8,128)(2,1)S(1)}, u32[]{:S(2)}, u32[]{:S(2)}) collective-permute-start(bf16[4,256,128]{2,1,0:T(8,128)(2,1)S(1)} %pad_maximum_fusion.2), channel_id=1, source_target_pairs={{12,0},{225,1},{14,2},{227,3},{0,4},{229,5},{2,6},{231,7},{4,8},{2... | collective-permute-start | bytes 786440 | tf_op jit(solution)/shard_map/ppermute | solution.py:38
  21.2 2.7 %collective-permute-start.5 = (bf16[4,256,128]{2,1,0:T(8,128)(2,1)S(1)}, bf16[4,256,128]{2,1,0:T(8,128)(2,1)S(1)}, u32[]{:S(2)}, u32[]{:S(2)}) collective-permute-start(bf16[4,256,128]{2,1,0:T(8,128)(2,1)S(1)} %pad_maximum_fusion.2), channel_id=1, source_target_pairs={{8,0},{65,1},{10,2},{67,3},{12,4},{69,5},{14,6},{71,7},{0,8},{73,9... | collective-permute-start | bytes 786440 | tf_op jit(solution)/shard_map/ppermute | solution.py:38
  23.9 1.4 %collective-permute-start.3 = (bf16[4,256,128]{2,1,0:T(8,128)(2,1)S(1)}, bf16[4,256,128]{2,1,0:T(8,128)(2,1)S(1)}, u32[]{:S(2)}, u32[]{:S(2)}) collective-permute-start(bf16[4,256,128]{2,1,0:T(8,128)(2,1)S(1)} %pad_maximum_fusion.2), channel_id=1, source_target_pairs={{4,0},{33,1},{6,2},{35,3},{8,4},{37,5},{10,6},{39,7},{12,8},{41,9}... | collective-permute-start | bytes 786440 | tf_op jit(solution)/shard_map/ppermute | solution.py:38
  25.3 1.1 %copy.14 = bf16[512,256]{0,1:T(8,128)(2,1)S(1)} copy(bf16[512,256]{1,0:T(8,128)(2,1)} %param.10) | data formatting | bytes 524288 | tf_op args[4]
  26.4 0.1 reshape.419
  26.6 0.1 select_reduce_fusion
  26.7 0.6 collective-permute-done.4
  27.3 4.3 %collective-permute-done.5 = bf16[4,256,128]{2,1,0:T(8,128)(2,1)S(1)} collective-permute-done((bf16[4,256,128]{2,1,0:T(8,128)(2,1)S(1)}, bf16[4,256,128]{2,1,0:T(8,128)(2,1)S(1)}, u32[]{:S(2)}, u32[]{:S(2)}) %collective-permute-start.5) | collective-permute-done | bytes 262176 | tf_op jit(solution)/shard_map/ppermute | solution.py:38
  31.6 0.1 pad_maximum_fusion.1
  31.6 0.8 collective-permute-start.7
  32.4 0.0 collective-permute-done.3
  32.4 0.1 pad_maximum_fusion
  32.5 2.6 %collective-permute-start.6 = (bf16[2,4,256,128]{3,2,1,0:T(8,128)(2,1)S(1)}, bf16[2,4,256,128]{3,2,1,0:T(8,128)(2,1)S(1)}, u32[]{:S(2)}, u32[]{:S(2)}) collective-permute-start(bf16[2,4,256,128]{3,2,1,0:T(8,128)(2,1)S(1)} %pad_maximum_fusion), channel_id=1, source_target_pairs={{32,0},{5,1},{34,2},{7,3},{36,4},{9,5},{38,6},{11,7},{40,8},{13,9}... | collective-permute-start | bytes 1572872 | tf_op jit(solution)/shard_map/ppermute | solution.py:38
  35.1 0.1 broadcast_select_fusion
  35.2 0.1 collective-permute-start.10
  35.3 1.8 %collective-permute-start.11 = (bf16[2,4,256,128]{3,2,1,0:T(8,128)(2,1)S(1)}, bf16[2,4,256,128]{3,2,1,0:T(8,128)(2,1)S(1)}, u32[]{:S(2)}, u32[]{:S(2)}) collective-permute-start(bf16[2,4,256,128]{3,2,1,0:T(8,128)(2,1)S(1)} %get-tuple-element.41), channel_id=1, source_target_pairs={{224,0},{13,1},{226,2},{15,3},{228,4},{9,5},{230,6},{11,7},{232,8}... | collective-permute-start | bytes 1572872 | tf_op jit(solution)/shard_map/ppermute | solution.py:48
  37.1 0.0 copy-start
  37.1 2.8 %copy-done = bf16[192,128,128]{2,1,0:T(8,128)(2,1)S(1)} copy-done((bf16[192,128,128]{2,1,0:T(8,128)(2,1)S(1)}, bf16[192,128,128]{2,1,0:T(8,128)(2,1)}, u32[]{:S(2)}) %copy-start) | copy-done | bytes 6291480
  39.9 1.8 %early_tiles.1.refs_4_ = f32[4,128,128]{2,1,0:T(8,128)S(1)} custom-call(s32[384]{0:T(512)S(1)} %add_select_fusion.table, s32[9]{0:T(128)S(1)} %select_reduce_fusion.4.bounds, bf16[192,128,128]{2,1,0:T(8,128)(2,1)S(1)} %copy-done, bf16[16,128,128]{2,1,0:T(8,128)(2,1)S(1)} %bitcast.31, bf16[16,128,128]{2,1,0:T(8,128)(2,1)S(1)} %bitcast.30), custom_call_target="tpu_custom_call" | custom-call | flops 268435456 | bytes 8388608 | tf_op jit(solution)/shard_map/early_tiles/pallas_call | solution.py:201
  41.7 0.0 copy-start.1
  41.7 0.4 collective-permute-done.7
  42.1 0.0 collective-permute-done.6
  42.1 3.4 %collective-permute-start.8 = (bf16[2,4,256,128]{3,2,1,0:T(8,128)(2,1)S(1)}, bf16[2,4,256,128]{3,2,1,0:T(8,128)(2,1)S(1)}, u32[]{:S(2)}, u32[]{:S(2)}) collective-permute-start(bf16[2,4,256,128]{3,2,1,0:T(8,128)(2,1)S(1)} %collective-permute-done.6), channel_id=1, source_target_pairs={{32,0},{5,1},{34,2},{7,3},{36,4},{9,5},{38,6},{11,7},{40,8},{13,9}... | collective-permute-start | bytes 1572872 | tf_op jit(solution)/shard_map/ppermute | solution.py:38
  45.5 0.0 collective-permute-start.9
  45.5 1.8 %collective-permute-done.10 = bf16[2,4,256,128]{3,2,1,0:T(8,128)(2,1)S(1)} collective-permute-done((bf16[2,4,256,128]{3,2,1,0:T(8,128)(2,1)S(1)}, bf16[2,4,256,128]{3,2,1,0:T(8,128)(2,1)S(1)}, u32[]{:S(2)}, u32[]{:S(2)}) %collective-permute-start.10) | collective-permute-done | bytes 524320 | tf_op jit(solution)/shard_map/ppermute | solution.py:48
  47.3 0.4 collective-permute-done.11
  47.7 3.3 %near_tiles.1.refs_2_ = f32[4,128,128]{2,1,0:T(8,128)S(1)} custom-call(s32[384]{0:T(512)S(1)} %add_select_fusion.table, s32[9]{0:T(128)S(1)} %select_reduce_fusion.4.bounds, bf16[192,128,128]{2,1,0:T(8,128)(2,1)S(1)} %copy-done, bf16[16,128,128]{2,1,0:T(8,128)(2,1)S(1)} %bitcast.34, bf16[16,128,128]{2,1,0:T(8,128)(2,1)S(1)} %bitcast.33, ...), custom_call_target="tpu_custom_call" | custom-call | flops 268435456 | bytes 8388608 | tf_op jit(solution)/shard_map/near_tiles/pallas_call | solution.py:201
  51.1 1.9 %collective-permute-done.8 = bf16[2,4,256,128]{3,2,1,0:T(8,128)(2,1)S(1)} collective-permute-done((bf16[2,4,256,128]{3,2,1,0:T(8,128)(2,1)S(1)}, bf16[2,4,256,128]{3,2,1,0:T(8,128)(2,1)S(1)}, u32[]{:S(2)}, u32[]{:S(2)}) %collective-permute-start.8) | collective-permute-done | bytes 524320 | tf_op jit(solution)/shard_map/ppermute | solution.py:38
  53.0 2.8 %collective-permute-done.9 = bf16[2,4,256,128]{3,2,1,0:T(8,128)(2,1)S(1)} collective-permute-done((bf16[2,4,256,128]{3,2,1,0:T(8,128)(2,1)S(1)}, bf16[2,4,256,128]{3,2,1,0:T(8,128)(2,1)S(1)}, u32[]{:S(2)}, u32[]{:S(2)}) %collective-permute-start.9) | collective-permute-done | bytes 524320 | tf_op jit(solution)/shard_map/ppermute | solution.py:38
  55.9 0.0 copy-done.1
  55.9 2.8 %far_tiles.1 = (bf16[320,128]{1,0:T(8,128)(2,1)S(1)}, bf16[320,128]{1,0:T(8,128)(2,1)S(1)}, bf16[320,128]{1,0:T(8,128)(2,1)S(1)}, bf16[320,128]{1,0:T(8,128)(2,1)S(1)}, f32[64,2,128]{2,1,0:T(2,128)}) custom-call(s32[384]{0:T(512)S(1)} %add_select_fusion.table, s32[9]{0:T(128)S(1)} %select_reduce_fusion.4.bounds, bf16[192,128,128]{2,1,0:T(8,128)(2,1)S(1)} %copy-done, ...), custom_call_target="tpu_custom_call" | custom-call | flops 268435456 | bytes 8388608 | tf_op jit(solution)/shard_map/far_tiles/pallas_call | solution.py:201
  58.7 8.1 %all-to-all-start = ((f32[64,2,128]{2,1,0:T(2,128)}), f32[64,2,128]{2,1,0:T(2,128)S(1)}, u32[]{:S(2)}, u32[]{:S(2)}) async-start(f32[64,2,128]{2,1,0:T(2,128)} %get-tuple-element.35), calls=%async_computation | async-start | bytes 131072 | tf_op jit(solution)/shard_map/all_to_all | solution.py:264
  66.7 0.1 collective-permute-start.12
  66.8 0.7 collective-permute-start.13
  67.5 1.2 %collective-permute-start.14 = (bf16[320,128]{1,0:T(8,128)(2,1)S(1)}, bf16[320,128]{1,0:T(8,128)(2,1)S(1)}, u32[]{:S(2)}, u32[]{:S(2)}) collective-permute-start(bf16[320,128]{1,0:T(8,128)(2,1)S(1)} %get-tuple-element.34), channel_id=1, source_target_pairs={{0,3},{3,0},{1,2},{2,1},{4,7},{7,4},{5,6},{6,5},{8,11},{11,8},{9,1... | collective-permute-start | bytes 245768 | tf_op jit(solution)/shard_map/ppermute | solution.py:265
  68.7 0.0 collective-permute-done.12.refs_1_
  68.7 3.6 %collective-permute-done.13.refs_2_ = bf16[320,128]{1,0:T(8,128)(2,1)S(1)} collective-permute-done((bf16[320,128]{1,0:T(8,128)(2,1)S(1)}, bf16[320,128]{1,0:T(8,128)(2,1)S(1)}, u32[]{:S(2)}, u32[]{:S(2)}) %collective-permute-start.13) | collective-permute-done | bytes 81952 | tf_op jit(solution)/shard_map/ppermute | solution.py:265
  72.3 0.9 %collective-permute-done.14.refs_3_ = bf16[320,128]{1,0:T(8,128)(2,1)S(1)} collective-permute-done((bf16[320,128]{1,0:T(8,128)(2,1)S(1)}, bf16[320,128]{1,0:T(8,128)(2,1)S(1)}, u32[]{:S(2)}, u32[]{:S(2)}) %collective-permute-start.14) | collective-permute-done | bytes 81952 | tf_op jit(solution)/shard_map/ppermute | solution.py:265
  73.2 0.9 %input_gradient.1 = bf16[64,512]{1,0:T(8,128)(2,1)} custom-call(bf16[320,128]{1,0:T(8,128)(2,1)S(1)} %get-tuple-element.31.refs_0_, bf16[320,128]{1,0:T(8,128)(2,1)S(1)} %collective-permute-done.12.refs_1_, bf16[320,128]{1,0:T(8,128)(2,1)S(1)} %collective-permute-done.13.refs_2_, bf16[320,128]{1,0:T(8,128)(2,1)S(1)} %collective-permute-done.14.refs_3_), custom_call_target="tpu_custom_call" | custom-call | flops 33554432 | bytes 409600 | tf_op jit(solution)/shard_map/input_gradient/pallas_call | solution.py:234
  74.1 4.7 %all-to-all-done = f32[64,2,128]{2,1,0:T(2,128)S(1)} async-done(((f32[64,2,128]{2,1,0:T(2,128)}), f32[64,2,128]{2,1,0:T(2,128)S(1)}, u32[]{:S(2)}, u32[]{:S(2)}) %all-to-all-start) | async-done | bytes 65568 | tf_op jit(solution)/shard_map/all_to_all | solution.py:264
  78.8 0.1 reduce_sum.89
  78.9 0.1 fusion.22
  78.9 0.6 pad_maximum_fusion.4
  (11 shorter events, 0.2 us)
Async XLA Ops:
  1.7 14.9 %collective-permute-start.1 = (bf16[256,128]{1,0:T(8,128)(2,1)S(1)}, bf16[256,128]{1,0:T(8,128)(2,1)S(1)}, u32[]{:S(2)}, u32[]{:S(2)}) collective-permute-start(bf16[256,128]{1,0:T(8,128)(2,1)S(1)} %bitcast.46), channel_id=1, source_target_pairs={{128,0},{129,1},{130,2},{131,3},{132,4},{133,5},{134,6},{135,7},{1... | collective-permute-start | bytes 196616 | tf_op jit(solution)/shard_map/ppermute | solution.py:28
  9.0 10.6 %collective-permute-start.2 = (bf16[256,128]{1,0:T(8,128)(2,1)S(1)}, bf16[256,128]{1,0:T(8,128)(2,1)S(1)}, u32[]{:S(2)}, u32[]{:S(2)}) collective-permute-start(bf16[256,128]{1,0:T(8,128)(2,1)S(1)} %bitcast.47), channel_id=1, source_target_pairs={{144,0},{145,1},{146,2},{147,3},{148,4},{149,5},{150,6},{151,7},{1... | collective-permute-start | bytes 196616 | tf_op jit(solution)/shard_map/ppermute | solution.py:28
  10.8 5.8 %collective-permute-start = (bf16[256,128]{1,0:T(8,128)(2,1)S(1)}, bf16[256,128]{1,0:T(8,128)(2,1)S(1)}, u32[]{:S(2)}, u32[]{:S(2)}) collective-permute-start(bf16[256,128]{1,0:T(8,128)(2,1)S(1)} %bitcast.48), channel_id=1, source_target_pairs={{16,0},{17,1},{18,2},{19,3},{20,4},{21,5},{22,6},{23,7},{24,8},{25... | collective-permute-start | bytes 196616 | tf_op jit(solution)/shard_map/ppermute | solution.py:28
  19.6 7.7 %collective-permute-start.4 = (bf16[4,256,128]{2,1,0:T(8,128)(2,1)S(1)}, bf16[4,256,128]{2,1,0:T(8,128)(2,1)S(1)}, u32[]{:S(2)}, u32[]{:S(2)}) collective-permute-start(bf16[4,256,128]{2,1,0:T(8,128)(2,1)S(1)} %pad_maximum_fusion.2), channel_id=1, source_target_pairs={{12,0},{225,1},{14,2},{227,3},{0,4},{229,5},{2,6},{231,7},{4,8},{2... | collective-permute-start | bytes 786440 | tf_op jit(solution)/shard_map/ppermute | solution.py:38
  21.2 10.4 %collective-permute-start.5 = (bf16[4,256,128]{2,1,0:T(8,128)(2,1)S(1)}, bf16[4,256,128]{2,1,0:T(8,128)(2,1)S(1)}, u32[]{:S(2)}, u32[]{:S(2)}) collective-permute-start(bf16[4,256,128]{2,1,0:T(8,128)(2,1)S(1)} %pad_maximum_fusion.2), channel_id=1, source_target_pairs={{8,0},{65,1},{10,2},{67,3},{12,4},{69,5},{14,6},{71,7},{0,8},{73,9... | collective-permute-start | bytes 786440 | tf_op jit(solution)/shard_map/ppermute | solution.py:38
  23.9 8.5 %collective-permute-start.3 = (bf16[4,256,128]{2,1,0:T(8,128)(2,1)S(1)}, bf16[4,256,128]{2,1,0:T(8,128)(2,1)S(1)}, u32[]{:S(2)}, u32[]{:S(2)}) collective-permute-start(bf16[4,256,128]{2,1,0:T(8,128)(2,1)S(1)} %pad_maximum_fusion.2), channel_id=1, source_target_pairs={{4,0},{33,1},{6,2},{35,3},{8,4},{37,5},{10,6},{39,7},{12,8},{41,9}... | collective-permute-start | bytes 786440 | tf_op jit(solution)/shard_map/ppermute | solution.py:38
  31.6 10.5 %collective-permute-start.7 = (bf16[2,4,256,128]{3,2,1,0:T(8,128)(2,1)S(1)}, bf16[2,4,256,128]{3,2,1,0:T(8,128)(2,1)S(1)}, u32[]{:S(2)}, u32[]{:S(2)}) collective-permute-start(bf16[2,4,256,128]{3,2,1,0:T(8,128)(2,1)S(1)} %pad_maximum_fusion.1), channel_id=1, source_target_pairs={{224,0},{13,1},{226,2},{15,3},{228,4},{1,5},{230,6},{3,7},{232,8},... | collective-permute-start | bytes 1572872 | tf_op jit(solution)/shard_map/ppermute | solution.py:38
  32.5 9.7 %collective-permute-start.6 = (bf16[2,4,256,128]{3,2,1,0:T(8,128)(2,1)S(1)}, bf16[2,4,256,128]{3,2,1,0:T(8,128)(2,1)S(1)}, u32[]{:S(2)}, u32[]{:S(2)}) collective-permute-start(bf16[2,4,256,128]{3,2,1,0:T(8,128)(2,1)S(1)} %pad_maximum_fusion), channel_id=1, source_target_pairs={{32,0},{5,1},{34,2},{7,3},{36,4},{9,5},{38,6},{11,7},{40,8},{13,9}... | collective-permute-start | bytes 1572872 | tf_op jit(solution)/shard_map/ppermute | solution.py:38
  35.2 12.2 %collective-permute-start.10 = (bf16[2,4,256,128]{3,2,1,0:T(8,128)(2,1)S(1)}, bf16[2,4,256,128]{3,2,1,0:T(8,128)(2,1)S(1)}, u32[]{:S(2)}, u32[]{:S(2)}) collective-permute-start(bf16[2,4,256,128]{3,2,1,0:T(8,128)(2,1)S(1)} %get-tuple-element.42), channel_id=1, source_target_pairs={{32,0},{5,1},{34,2},{7,3},{36,4},{1,5},{38,6},{3,7},{40,8},{13,9},... | collective-permute-start | bytes 1572872 | tf_op jit(solution)/shard_map/ppermute | solution.py:48
  35.3 12.5 %collective-permute-start.11 = (bf16[2,4,256,128]{3,2,1,0:T(8,128)(2,1)S(1)}, bf16[2,4,256,128]{3,2,1,0:T(8,128)(2,1)S(1)}, u32[]{:S(2)}, u32[]{:S(2)}) collective-permute-start(bf16[2,4,256,128]{3,2,1,0:T(8,128)(2,1)S(1)} %get-tuple-element.41), channel_id=1, source_target_pairs={{224,0},{13,1},{226,2},{15,3},{228,4},{9,5},{230,6},{11,7},{232,8}... | collective-permute-start | bytes 1572872 | tf_op jit(solution)/shard_map/ppermute | solution.py:48
  37.1 2.8 %copy-start = (bf16[192,128,128]{2,1,0:T(8,128)(2,1)S(1)}, bf16[192,128,128]{2,1,0:T(8,128)(2,1)}, u32[]{:S(2)}) copy-start(bf16[192,128,128]{2,1,0:T(8,128)(2,1)} %adj.5) | copy-start | bytes 18874372
  41.7 14.2 %copy-start.1 = (bf16[256,64]{0,1:T(8,128)(2,1)S(1)}, bf16[256,64]{0,1:T(8,128)(2,1)}, u32[]{:S(2)}) copy-start(bf16[256,64]{0,1:T(8,128)(2,1)} %param.11) | copy-start | bytes 98308
  42.1 10.9 %collective-permute-start.8 = (bf16[2,4,256,128]{3,2,1,0:T(8,128)(2,1)S(1)}, bf16[2,4,256,128]{3,2,1,0:T(8,128)(2,1)S(1)}, u32[]{:S(2)}, u32[]{:S(2)}) collective-permute-start(bf16[2,4,256,128]{3,2,1,0:T(8,128)(2,1)S(1)} %collective-permute-done.6), channel_id=1, source_target_pairs={{32,0},{5,1},{34,2},{7,3},{36,4},{9,5},{38,6},{11,7},{40,8},{13,9}... | collective-permute-start | bytes 1572872 | tf_op jit(solution)/shard_map/ppermute | solution.py:38
  45.5 10.4 %collective-permute-start.9 = (bf16[2,4,256,128]{3,2,1,0:T(8,128)(2,1)S(1)}, bf16[2,4,256,128]{3,2,1,0:T(8,128)(2,1)S(1)}, u32[]{:S(2)}, u32[]{:S(2)}) collective-permute-start(bf16[2,4,256,128]{3,2,1,0:T(8,128)(2,1)S(1)} %collective-permute-done.7), channel_id=1, source_target_pairs={{224,0},{13,1},{226,2},{15,3},{228,4},{1,5},{230,6},{3,7},{232,8},... | collective-permute-start | bytes 1572872 | tf_op jit(solution)/shard_map/ppermute | solution.py:38
  58.7 20.1 %all-to-all-start = ((f32[64,2,128]{2,1,0:T(2,128)}), f32[64,2,128]{2,1,0:T(2,128)S(1)}, u32[]{:S(2)}, u32[]{:S(2)}) async-start(f32[64,2,128]{2,1,0:T(2,128)} %get-tuple-element.35), calls=%async_computation | async-start | bytes 131072 | tf_op jit(solution)/shard_map/all_to_all | solution.py:264
  66.7 2.0 %collective-permute-start.12 = (bf16[320,128]{1,0:T(8,128)(2,1)S(1)}, bf16[320,128]{1,0:T(8,128)(2,1)S(1)}, u32[]{:S(2)}, u32[]{:S(2)}) collective-permute-start(bf16[320,128]{1,0:T(8,128)(2,1)S(1)} %get-tuple-element.32), channel_id=1, source_target_pairs={{0,1},{1,0},{2,3},{3,2},{4,5},{5,4},{6,7},{7,6},{8,9},{9,8},{10,11... | collective-permute-start | bytes 245768 | tf_op jit(solution)/shard_map/ppermute | solution.py:265
  66.8 5.5 %collective-permute-start.13 = (bf16[320,128]{1,0:T(8,128)(2,1)S(1)}, bf16[320,128]{1,0:T(8,128)(2,1)S(1)}, u32[]{:S(2)}, u32[]{:S(2)}) collective-permute-start(bf16[320,128]{1,0:T(8,128)(2,1)S(1)} %get-tuple-element.33), channel_id=1, source_target_pairs={{0,2},{2,0},{1,3},{3,1},{4,6},{6,4},{5,7},{7,5},{8,10},{10,8},{9,1... | collective-permute-start | bytes 245768 | tf_op jit(solution)/shard_map/ppermute | solution.py:265
  67.5 5.7 %collective-permute-start.14 = (bf16[320,128]{1,0:T(8,128)(2,1)S(1)}, bf16[320,128]{1,0:T(8,128)(2,1)S(1)}, u32[]{:S(2)}, u32[]{:S(2)}) collective-permute-start(bf16[320,128]{1,0:T(8,128)(2,1)S(1)} %get-tuple-element.34), channel_id=1, source_target_pairs={{0,3},{3,0},{1,2},{2,1},{4,7},{7,4},{5,6},{6,5},{8,11},{11,8},{9,1... | collective-permute-start | bytes 245768 | tf_op jit(solution)/shard_map/ppermute | solution.py:265

commit v13 on v12

--- a/solution.py
+++ b/solution.py
@@ -164,9 +164,16 @@
 
 
 def middle_kernel(table, bounds, adj, *refs):
-    *sources, before, acc, masks = refs
+    *sources, before, weights, acc, turned, masks = refs
     set_masks(masks)
     acc[...] = before[...]
+    low = lax.broadcasted_iota(jnp.int32, (64, 128), 1) < 64
+    for k in range(4):
+        lanes = pl.multiple_of((lax.axis_index("yl") ^ (k >> 1)) * 128, 128)
+        of_chip = weights[:, pl.ds(lanes, 128)].astype(jnp.float32)
+        first = (lax.axis_index("core") ^ (k & 1)) == 0
+        of_core = jnp.where(low == first, of_chip, pltpu.roll(of_chip, 64, 1))
+        turned[k] = of_core.astype(turned.dtype)
     add_sources(table, bounds, adj, sources, 2, acc, masks)
 
 
@@ -187,11 +194,7 @@
         for ref in outs:
             ref[pl.ds(r * 128, 128), :] = packed
     for k, ref in enumerate(outs):
-        lanes = pl.multiple_of((lax.axis_index("yl") ^ (k >> 1)) * 128, 128)
-        of_chip = weights[:, pl.ds(lanes, 128)].astype(jnp.float32)
-        first = (lax.axis_index("core") ^ (k & 1)) == 0
-        of_core = jnp.where(low == first, of_chip, pltpu.roll(of_chip, 64, 1))
-        ref[pl.ds(256, 64), :] = of_core.astype(ref.dtype)
+        ref[pl.ds(256, 64), :] = weights[k]
 
 
 def call(kernel, table, bounds, adj, sources, others, out_shape, keep_acc, name):
@@ -256,10 +259,11 @@
     acc = call(first_kernel, *tables, adj_tiles, [low, high], [], sums, False, "early_tiles")
     forwarded, acc = lax.optimization_barrier((forwarded, acc))
     far = gather_far(*forwarded)
-    acc = call(middle_kernel, *tables, adj_tiles, forwarded + others, [acc], sums, False, "near_tiles")
+    blocks = jax.ShapeDtypeStruct((4, 64, 128), jnp.bfloat16)
+    acc, turned = call(middle_kernel, *tables, adj_tiles, forwarded + others, [acc, weight.T], (sums, blocks), False, "near_tiles")
     message = jax.ShapeDtypeStruct((320, 128), jnp.bfloat16)
     outs = (message, message, message, message, jax.ShapeDtypeStruct((64, 2, 128), jnp.float32))
-    *messages, partial = call(last_kernel, *tables, adj_tiles, far, [acc, f_rows, weight.T], outs, True, "far_tiles")
+    *messages, partial = call(last_kernel, *tables, adj_tiles, far, [acc, f_rows, turned], outs, True, "far_tiles")
 
     pieces = lax.all_to_all(partial, ROWS, 0, 0, tiled=True)
     arrived = messages[:1] + [lax.ppermute(m, SLAB, pairs) for m, pairs in zip(messages[1:], FLIPS)]

time: 79.8 us -> 80.1 us (level)
  no operation moved by 1% of the time
where the time goes in v13:
time: 80.1 us; the launch traced here: 79.7 us
  starting transfers between devices  34.9 us (44%)
  waiting for transfers between devices  27.2 us (34%)
  Pallas kernels  8.88 us (11%)
  local copies, waits for them, and re-layouts  4.19 us (5%)
  other arithmetic  3.71 us (5%)
    ppermute x7, starting transfers between devices, from_axis(): return lax.ppermute(value, ALL, pairs)  12.5 us
    ppermute x3, starting transfers between devices, from_rows(): return lax.ppermute(value, ALL, pairs)  10.3 us
    ppermute x7, waiting for transfers between devices, from_axis(): return lax.ppermute(value, ALL, pairs)  10 us
    all_to_all x1, starting transfers between devices, body(): pieces = lax.all_to_all(partial, ROWS, 0, 0, tiled=True)  8.24 us
    pallas_call x3, Pallas kernels, call(): pl.pallas_call(kernel, out_shape=out_shape, in_specs=[smem, smem, vmem] +...  8.01 us
    ppermute x3, waiting for transfers between devices, from_rows(): return lax.ppermute(value, ALL, pairs)  5.7 us
    all_to_all x1, waiting for transfers between devices, body(): pieces = lax.all_to_all(partial, ROWS, 0, 0, tiled=True)  4.74 us
    ppermute x3, waiting for transfers between devices, body(): lax.ppermute(m, SLAB, pairs)  4.49 us
  transfers between devices with their start and end apart: 16, of which 12 were waited for; matrix products, arithmetic and copies ran while one was open for 4% of the time, Pallas kernels for 8%

profile of v13, /device:TPU:8, one launch (start us, length us, event | category | flops | bytes accessed | tf_op | source)
XLA Modules:
  0.0 79.7 jit_solution(6979732785680245258)
XLA Ops:
  0.6 0.9 %fusion.1 = bf16[64,512]{1,0:T(8,128)(2,1)S(1)} fusion(s32[512,64]{0,1:T(8,128)} %param.9, bf16[512,64]{0,1:T(8,128)(2,1)} %param.8), kind=kLoop, calls=%fused_computation.11 | loop fusion | flops 131072 | bytes 262144 | tf_op jit(solution)/shard_map/convert_element_type | solution.py:149
  1.6 0.1 copy.13
  1.7 7.3 %collective-permute-start.1 = (bf16[256,128]{1,0:T(8,128)(2,1)S(1)}, bf16[256,128]{1,0:T(8,128)(2,1)S(1)}, u32[]{:S(2)}, u32[]{:S(2)}) collective-permute-start(bf16[256,128]{1,0:T(8,128)(2,1)S(1)} %bitcast.46), channel_id=1, source_target_pairs={{128,0},{129,1},{130,2},{131,3},{132,4},{133,5},{134,6},{135,7},{1... | collective-permute-start | bytes 196616 | tf_op jit(solution)/shard_map/ppermute | solution.py:28
  9.0 1.8 %collective-permute-start.2 = (bf16[256,128]{1,0:T(8,128)(2,1)S(1)}, bf16[256,128]{1,0:T(8,128)(2,1)S(1)}, u32[]{:S(2)}, u32[]{:S(2)}) collective-permute-start(bf16[256,128]{1,0:T(8,128)(2,1)S(1)} %bitcast.47), channel_id=1, source_target_pairs={{144,0},{145,1},{146,2},{147,3},{148,4},{149,5},{150,6},{151,7},{1... | collective-permute-start | bytes 196616 | tf_op jit(solution)/shard_map/ppermute | solution.py:28
  10.8 1.2 %collective-permute-start = (bf16[256,128]{1,0:T(8,128)(2,1)S(1)}, bf16[256,128]{1,0:T(8,128)(2,1)S(1)}, u32[]{:S(2)}, u32[]{:S(2)}) collective-permute-start(bf16[256,128]{1,0:T(8,128)(2,1)S(1)} %bitcast.48), channel_id=1, source_target_pairs={{16,0},{17,1},{18,2},{19,3},{20,4},{21,5},{22,6},{23,7},{24,8},{25... | collective-permute-start | bytes 196616 | tf_op jit(solution)/shard_map/ppermute | solution.py:28
  12.1 0.8 %fusion.16 = (s32[192,1]{0,1:T(1,128)S(1)}, s32[192,1]{0,1:T(1,128)S(1)}, s32[192,1]{0,1:T(1,128)S(1)}) fusion(pred[]{:T(512)S(6)} %eq.199, s32[]{:T(128)S(6)} %sub.146, s32[]{:T(128)S(6)} %add.279, s32[]{:T(128)S(6)} %axis_index.27, s32[]{:T(128)S(6)} %axis_index.33, s32[192,2]{0,1:T(2,128)} %param.7, s32[]{:T(128)S(6)} %mul.88), kind=kLoop, calls=%fused_computation.125 | loop fusion | flops 19200 | bytes 3861 | tf_op jit(solution)/shard_map/add | solution.py:101
  12.9 0.1 convert_reduce_fusion.1
  13.0 0.1 select_reduce_fusion.5
  13.1 0.2 select_reduce_fusion.2
  13.3 0.1 select_reduce_fusion.4.bounds
  13.4 0.1 select_reduce_fusion.3
  13.5 0.2 convert_reduce_fusion
  13.8 0.1 select_reduce_fusion.1
  13.9 2.7 %collective-permute-done = bf16[256,128]{1,0:T(8,128)(2,1)S(1)} collective-permute-done((bf16[256,128]{1,0:T(8,128)(2,1)S(1)}, bf16[256,128]{1,0:T(8,128)(2,1)S(1)}, u32[]{:S(2)}, u32[]{:S(2)}) %collective-permute-start) | collective-permute-done | bytes 65568 | tf_op jit(solution)/shard_map/ppermute | solution.py:28
  16.6 0.0 collective-permute-done.1
  16.6 3.0 %collective-permute-done.2 = bf16[256,128]{1,0:T(8,128)(2,1)S(1)} collective-permute-done((bf16[256,128]{1,0:T(8,128)(2,1)S(1)}, bf16[256,128]{1,0:T(8,128)(2,1)S(1)}, u32[]{:S(2)}, u32[]{:S(2)}) %collective-permute-start.2) | collective-permute-done | bytes 65568 | tf_op jit(solution)/shard_map/ppermute | solution.py:28
  19.6 1.6 %collective-permute-start.4 = (bf16[4,256,128]{2,1,0:T(8,128)(2,1)S(1)}, bf16[4,256,128]{2,1,0:T(8,128)(2,1)S(1)}, u32[]{:S(2)}, u32[]{:S(2)}) collective-permute-start(bf16[4,256,128]{2,1,0:T(8,128)(2,1)S(1)} %pad_maximum_fusion.2), channel_id=1, source_target_pairs={{12,0},{225,1},{14,2},{227,3},{0,4},{229,5},{2,6},{231,7},{4,8},{2... | collective-permute-start | bytes 786440 | tf_op jit(solution)/shard_map/ppermute | solution.py:38
  21.2 2.7 %collective-permute-start.5 = (bf16[4,256,128]{2,1,0:T(8,128)(2,1)S(1)}, bf16[4,256,128]{2,1,0:T(8,128)(2,1)S(1)}, u32[]{:S(2)}, u32[]{:S(2)}) collective-permute-start(bf16[4,256,128]{2,1,0:T(8,128)(2,1)S(1)} %pad_maximum_fusion.2), channel_id=1, source_target_pairs={{8,0},{65,1},{10,2},{67,3},{12,4},{69,5},{14,6},{71,7},{0,8},{73,9... | collective-permute-start | bytes 786440 | tf_op jit(solution)/shard_map/ppermute | solution.py:38
  23.9 1.4 %collective-permute-start.3 = (bf16[4,256,128]{2,1,0:T(8,128)(2,1)S(1)}, bf16[4,256,128]{2,1,0:T(8,128)(2,1)S(1)}, u32[]{:S(2)}, u32[]{:S(2)}) collective-permute-start(bf16[4,256,128]{2,1,0:T(8,128)(2,1)S(1)} %pad_maximum_fusion.2), channel_id=1, source_target_pairs={{4,0},{33,1},{6,2},{35,3},{8,4},{37,5},{10,6},{39,7},{12,8},{41,9}... | collective-permute-start | bytes 786440 | tf_op jit(solution)/shard_map/ppermute | solution.py:38
  25.3 1.1 %copy.14 = bf16[512,256]{0,1:T(8,128)(2,1)S(1)} copy(bf16[512,256]{1,0:T(8,128)(2,1)} %param.10) | data formatting | bytes 524288 | tf_op args[4]
  26.4 0.1 reshape.419
  26.5 0.0 copy-start.1
  26.6 0.1 select_reduce_fusion
  26.7 0.5 collective-permute-done.4
  27.3 4.3 %collective-permute-done.5 = bf16[4,256,128]{2,1,0:T(8,128)(2,1)S(1)} collective-permute-done((bf16[4,256,128]{2,1,0:T(8,128)(2,1)S(1)}, bf16[4,256,128]{2,1,0:T(8,128)(2,1)S(1)}, u32[]{:S(2)}, u32[]{:S(2)}) %collective-permute-start.5) | collective-permute-done | bytes 262176 | tf_op jit(solution)/shard_map/ppermute | solution.py:38
  31.6 0.1 pad_maximum_fusion.1
  31.6 0.8 collective-permute-start.7
  32.4 0.0 collective-permute-done.3
  32.4 0.1 pad_maximum_fusion
  32.5 2.6 %collective-permute-start.6 = (bf16[2,4,256,128]{3,2,1,0:T(8,128)(2,1)S(1)}, bf16[2,4,256,128]{3,2,1,0:T(8,128)(2,1)S(1)}, u32[]{:S(2)}, u32[]{:S(2)}) collective-permute-start(bf16[2,4,256,128]{3,2,1,0:T(8,128)(2,1)S(1)} %pad_maximum_fusion), channel_id=1, source_target_pairs={{32,0},{5,1},{34,2},{7,3},{36,4},{9,5},{38,6},{11,7},{40,8},{13,9}... | collective-permute-start | bytes 1572872 | tf_op jit(solution)/shard_map/ppermute | solution.py:38
  35.1 0.1 broadcast_select_fusion
  35.2 0.1 collective-permute-start.10
  35.3 1.8 %collective-permute-start.11 = (bf16[2,4,256,128]{3,2,1,0:T(8,128)(2,1)S(1)}, bf16[2,4,256,128]{3,2,1,0:T(8,128)(2,1)S(1)}, u32[]{:S(2)}, u32[]{:S(2)}) collective-permute-start(bf16[2,4,256,128]{3,2,1,0:T(8,128)(2,1)S(1)} %get-tuple-element.45), channel_id=1, source_target_pairs={{224,0},{13,1},{226,2},{15,3},{228,4},{9,5},{230,6},{11,7},{232,8}... | collective-permute-start | bytes 1572872 | tf_op jit(solution)/shard_map/ppermute | solution.py:48
  37.1 0.0 copy-start
  37.1 2.8 %copy-done = bf16[192,128,128]{2,1,0:T(8,128)(2,1)S(1)} copy-done((bf16[192,128,128]{2,1,0:T(8,128)(2,1)S(1)}, bf16[192,128,128]{2,1,0:T(8,128)(2,1)}, u32[]{:S(2)}) %copy-start) | copy-done | bytes 6291480
  39.9 1.8 %early_tiles.1.refs_4_ = f32[4,128,128]{2,1,0:T(8,128)S(1)} custom-call(s32[384]{0:T(512)S(1)} %add_select_fusion.table, s32[9]{0:T(128)S(1)} %select_reduce_fusion.4.bounds, bf16[192,128,128]{2,1,0:T(8,128)(2,1)S(1)} %copy-done, bf16[16,128,128]{2,1,0:T(8,128)(2,1)S(1)} %bitcast.31, bf16[16,128,128]{2,1,0:T(8,128)(2,1)S(1)} %bitcast.30), custom_call_target="tpu_custom_call" | custom-call | flops 268435456 | bytes 8388608 | tf_op jit(solution)/shard_map/early_tiles/pallas_call | solution.py:204
  41.7 0.4 collective-permute-done.7
  42.1 0.0 collective-permute-done.6
  42.1 3.4 %collective-permute-start.8 = (bf16[2,4,256,128]{3,2,1,0:T(8,128)(2,1)S(1)}, bf16[2,4,256,128]{3,2,1,0:T(8,128)(2,1)S(1)}, u32[]{:S(2)}, u32[]{:S(2)}) collective-permute-start(bf16[2,4,256,128]{3,2,1,0:T(8,128)(2,1)S(1)} %collective-permute-done.6), channel_id=1, source_target_pairs={{32,0},{5,1},{34,2},{7,3},{36,4},{9,5},{38,6},{11,7},{40,8},{13,9}... | collective-permute-start | bytes 1572872 | tf_op jit(solution)/shard_map/ppermute | solution.py:38
  45.5 0.0 collective-permute-start.9
  45.5 1.8 %collective-permute-done.10 = bf16[2,4,256,128]{3,2,1,0:T(8,128)(2,1)S(1)} collective-permute-done((bf16[2,4,256,128]{3,2,1,0:T(8,128)(2,1)S(1)}, bf16[2,4,256,128]{3,2,1,0:T(8,128)(2,1)S(1)}, u32[]{:S(2)}, u32[]{:S(2)}) %collective-permute-start.10) | collective-permute-done | bytes 524320 | tf_op jit(solution)/shard_map/ppermute | solution.py:48
  47.3 0.4 collective-permute-done.11
  47.7 0.0 copy-done.1
  47.7 3.4 %near_tiles.1 = (f32[4,128,128]{2,1,0:T(8,128)S(1)}, bf16[4,64,128]{2,1,0:T(8,128)(2,1)S(1)}) custom-call(s32[384]{0:T(512)S(1)} %add_select_fusion.table, s32[9]{0:T(128)S(1)} %select_reduce_fusion.4.bounds, bf16[192,128,128]{2,1,0:T(8,128)(2,1)S(1)} %copy-done, bf16[16,128,128]{2,1,0:T(8,128)(2,1)S(1)} %bitcast.34, bf16[16,128,128]{2,1,0:T(8,128)(2,1)S(1)} %bitcast.33, ...), custom_call_target="tpu_custom_call" | custom-call | flops 268435456 | bytes 8388608 | tf_op jit(solution)/shard_map/near_tiles/pallas_call | solution.py:204
  51.2 1.9 %collective-permute-done.8 = bf16[2,4,256,128]{3,2,1,0:T(8,128)(2,1)S(1)} collective-permute-done((bf16[2,4,256,128]{3,2,1,0:T(8,128)(2,1)S(1)}, bf16[2,4,256,128]{3,2,1,0:T(8,128)(2,1)S(1)}, u32[]{:S(2)}, u32[]{:S(2)}) %collective-permute-start.8) | collective-permute-done | bytes 524320 | tf_op jit(solution)/shard_map/ppermute | solution.py:38
  53.0 2.8 %collective-permute-done.9 = bf16[2,4,256,128]{3,2,1,0:T(8,128)(2,1)S(1)} collective-permute-done((bf16[2,4,256,128]{3,2,1,0:T(8,128)(2,1)S(1)}, bf16[2,4,256,128]{3,2,1,0:T(8,128)(2,1)S(1)}, u32[]{:S(2)}, u32[]{:S(2)}) %collective-permute-start.9) | collective-permute-done | bytes 524320 | tf_op jit(solution)/shard_map/ppermute | solution.py:38
  55.9 2.8 %far_tiles.1 = (bf16[320,128]{1,0:T(8,128)(2,1)S(1)}, bf16[320,128]{1,0:T(8,128)(2,1)S(1)}, bf16[320,128]{1,0:T(8,128)(2,1)S(1)}, bf16[320,128]{1,0:T(8,128)(2,1)S(1)}, f32[64,2,128]{2,1,0:T(2,128)}) custom-call(s32[384]{0:T(512)S(1)} %add_select_fusion.table, s32[9]{0:T(128)S(1)} %select_reduce_fusion.4.bounds, bf16[192,128,128]{2,1,0:T(8,128)(2,1)S(1)} %copy-done, ...), custom_call_target="tpu_custom_call" | custom-call | flops 268435456 | bytes 8388608 | tf_op jit(solution)/shard_map/far_tiles/pallas_call | solution.py:204
  58.6 8.2 %all-to-all-start = ((f32[64,2,128]{2,1,0:T(2,128)}), f32[64,2,128]{2,1,0:T(2,128)S(1)}, u32[]{:S(2)}, u32[]{:S(2)}) async-start(f32[64,2,128]{2,1,0:T(2,128)} %get-tuple-element.39), calls=%async_computation | async-start | bytes 131072 | tf_op jit(solution)/shard_map/all_to_all | solution.py:268
  66.9 0.1 collective-permute-start.12
  67.0 0.7 collective-permute-start.13
  67.7 1.2 %collective-permute-start.14 = (bf16[320,128]{1,0:T(8,128)(2,1)S(1)}, bf16[320,128]{1,0:T(8,128)(2,1)S(1)}, u32[]{:S(2)}, u32[]{:S(2)}) collective-permute-start(bf16[320,128]{1,0:T(8,128)(2,1)S(1)} %get-tuple-element.38), channel_id=1, source_target_pairs={{0,3},{3,0},{1,2},{2,1},{4,7},{7,4},{5,6},{6,5},{8,11},{11,8},{9,1... | collective-permute-start | bytes 245768 | tf_op jit(solution)/shard_map/ppermute | solution.py:269
  68.9 0.0 collective-permute-done.12.refs_1_
  68.9 3.6 %collective-permute-done.13.refs_2_ = bf16[320,128]{1,0:T(8,128)(2,1)S(1)} collective-permute-done((bf16[320,128]{1,0:T(8,128)(2,1)S(1)}, bf16[320,128]{1,0:T(8,128)(2,1)S(1)}, u32[]{:S(2)}, u32[]{:S(2)}) %collective-permute-start.13) | collective-permute-done | bytes 81952 | tf_op jit(solution)/shard_map/ppermute | solution.py:269
  72.5 0.9 %collective-permute-done.14.refs_3_ = bf16[320,128]{1,0:T(8,128)(2,1)S(1)} collective-permute-done((bf16[320,128]{1,0:T(8,128)(2,1)S(1)}, bf16[320,128]{1,0:T(8,128)(2,1)S(1)}, u32[]{:S(2)}, u32[]{:S(2)}) %collective-permute-start.14) | collective-permute-done | bytes 81952 | tf_op jit(solution)/shard_map/ppermute | solution.py:269
  73.4 0.9 %input_gradient.1 = bf16[64,512]{1,0:T(8,128)(2,1)} custom-call(bf16[320,128]{1,0:T(8,128)(2,1)S(1)} %get-tuple-element.35.refs_0_, bf16[320,128]{1,0:T(8,128)(2,1)S(1)} %collective-permute-done.12.refs_1_, bf16[320,128]{1,0:T(8,128)(2,1)S(1)} %collective-permute-done.13.refs_2_, bf16[320,128]{1,0:T(8,128)(2,1)S(1)} %collective-permute-done.14.refs_3_), custom_call_target="tpu_custom_call" | custom-call | flops 33554432 | bytes 409600 | tf_op jit(solution)/shard_map/input_gradient/pallas_call | solution.py:237
  74.2 4.7 %all-to-all-done = f32[64,2,128]{2,1,0:T(2,128)S(1)} async-done(((f32[64,2,128]{2,1,0:T(2,128)}), f32[64,2,128]{2,1,0:T(2,128)S(1)}, u32[]{:S(2)}, u32[]{:S(2)}) %all-to-all-start) | async-done | bytes 65568 | tf_op jit(solution)/shard_map/all_to_all | solution.py:268
  79.0 0.1 reduce_sum.89
  79.0 0.1 fusion.22
  79.1 0.6 pad_maximum_fusion.4
  (11 shorter events, 0.2 us)
Async XLA Ops:
  1.7 14.9 %collective-permute-start.1 = (bf16[256,128]{1,0:T(8,128)(2,1)S(1)}, bf16[256,128]{1,0:T(8,128)(2,1)S(1)}, u32[]{:S(2)}, u32[]{:S(2)}) collective-permute-start(bf16[256,128]{1,0:T(8,128)(2,1)S(1)} %bitcast.46), channel_id=1, source_target_pairs={{128,0},{129,1},{130,2},{131,3},{132,4},{133,5},{134,6},{135,7},{1... | collective-permute-start | bytes 196616 | tf_op jit(solution)/shard_map/ppermute | solution.py:28
  9.0 10.6 %collective-permute-start.2 = (bf16[256,128]{1,0:T(8,128)(2,1)S(1)}, bf16[256,128]{1,0:T(8,128)(2,1)S(1)}, u32[]{:S(2)}, u32[]{:S(2)}) collective-permute-start(bf16[256,128]{1,0:T(8,128)(2,1)S(1)} %bitcast.47), channel_id=1, source_target_pairs={{144,0},{145,1},{146,2},{147,3},{148,4},{149,5},{150,6},{151,7},{1... | collective-permute-start | bytes 196616 | tf_op jit(solution)/shard_map/ppermute | solution.py:28
  10.8 5.8 %collective-permute-start = (bf16[256,128]{1,0:T(8,128)(2,1)S(1)}, bf16[256,128]{1,0:T(8,128)(2,1)S(1)}, u32[]{:S(2)}, u32[]{:S(2)}) collective-permute-start(bf16[256,128]{1,0:T(8,128)(2,1)S(1)} %bitcast.48), channel_id=1, source_target_pairs={{16,0},{17,1},{18,2},{19,3},{20,4},{21,5},{22,6},{23,7},{24,8},{25... | collective-permute-start | bytes 196616 | tf_op jit(solution)/shard_map/ppermute | solution.py:28
  19.6 7.7 %collective-permute-start.4 = (bf16[4,256,128]{2,1,0:T(8,128)(2,1)S(1)}, bf16[4,256,128]{2,1,0:T(8,128)(2,1)S(1)}, u32[]{:S(2)}, u32[]{:S(2)}) collective-permute-start(bf16[4,256,128]{2,1,0:T(8,128)(2,1)S(1)} %pad_maximum_fusion.2), channel_id=1, source_target_pairs={{12,0},{225,1},{14,2},{227,3},{0,4},{229,5},{2,6},{231,7},{4,8},{2... | collective-permute-start | bytes 786440 | tf_op jit(solution)/shard_map/ppermute | solution.py:38
  21.2 10.4 %collective-permute-start.5 = (bf16[4,256,128]{2,1,0:T(8,128)(2,1)S(1)}, bf16[4,256,128]{2,1,0:T(8,128)(2,1)S(1)}, u32[]{:S(2)}, u32[]{:S(2)}) collective-permute-start(bf16[4,256,128]{2,1,0:T(8,128)(2,1)S(1)} %pad_maximum_fusion.2), channel_id=1, source_target_pairs={{8,0},{65,1},{10,2},{67,3},{12,4},{69,5},{14,6},{71,7},{0,8},{73,9... | collective-permute-start | bytes 786440 | tf_op jit(solution)/shard_map/ppermute | solution.py:38
  23.9 8.5 %collective-permute-start.3 = (bf16[4,256,128]{2,1,0:T(8,128)(2,1)S(1)}, bf16[4,256,128]{2,1,0:T(8,128)(2,1)S(1)}, u32[]{:S(2)}, u32[]{:S(2)}) collective-permute-start(bf16[4,256,128]{2,1,0:T(8,128)(2,1)S(1)} %pad_maximum_fusion.2), channel_id=1, source_target_pairs={{4,0},{33,1},{6,2},{35,3},{8,4},{37,5},{10,6},{39,7},{12,8},{41,9}... | collective-permute-start | bytes 786440 | tf_op jit(solution)/shard_map/ppermute | solution.py:38
  26.5 21.2 %copy-start.1 = (bf16[256,64]{0,1:T(8,128)(2,1)S(1)}, bf16[256,64]{0,1:T(8,128)(2,1)}, u32[]{:S(2)}) copy-start(bf16[256,64]{0,1:T(8,128)(2,1)} %param.11) | copy-start | bytes 98308
  31.6 10.5 %collective-permute-start.7 = (bf16[2,4,256,128]{3,2,1,0:T(8,128)(2,1)S(1)}, bf16[2,4,256,128]{3,2,1,0:T(8,128)(2,1)S(1)}, u32[]{:S(2)}, u32[]{:S(2)}) collective-permute-start(bf16[2,4,256,128]{3,2,1,0:T(8,128)(2,1)S(1)} %pad_maximum_fusion.1), channel_id=1, source_target_pairs={{224,0},{13,1},{226,2},{15,3},{228,4},{1,5},{230,6},{3,7},{232,8},... | collective-permute-start | bytes 1572872 | tf_op jit(solution)/shard_map/ppermute | solution.py:38
  32.5 9.7 %collective-permute-start.6 = (bf16[2,4,256,128]{3,2,1,0:T(8,128)(2,1)S(1)}, bf16[2,4,256,128]{3,2,1,0:T(8,128)(2,1)S(1)}, u32[]{:S(2)}, u32[]{:S(2)}) collective-permute-start(bf16[2,4,256,128]{3,2,1,0:T(8,128)(2,1)S(1)} %pad_maximum_fusion), channel_id=1, source_target_pairs={{32,0},{5,1},{34,2},{7,3},{36,4},{9,5},{38,6},{11,7},{40,8},{13,9}... | collective-permute-start | bytes 1572872 | tf_op jit(solution)/shard_map/ppermute | solution.py:38
  35.2 12.2 %collective-permute-start.10 = (bf16[2,4,256,128]{3,2,1,0:T(8,128)(2,1)S(1)}, bf16[2,4,256,128]{3,2,1,0:T(8,128)(2,1)S(1)}, u32[]{:S(2)}, u32[]{:S(2)}) collective-permute-start(bf16[2,4,256,128]{3,2,1,0:T(8,128)(2,1)S(1)} %get-tuple-element.46), channel_id=1, source_target_pairs={{32,0},{5,1},{34,2},{7,3},{36,4},{1,5},{38,6},{3,7},{40,8},{13,9},... | collective-permute-start | bytes 1572872 | tf_op jit(solution)/shard_map/ppermute | solution.py:48
  35.3 12.5 %collective-permute-start.11 = (bf16[2,4,256,128]{3,2,1,0:T(8,128)(2,1)S(1)}, bf16[2,4,256,128]{3,2,1,0:T(8,128)(2,1)S(1)}, u32[]{:S(2)}, u32[]{:S(2)}) collective-permute-start(bf16[2,4,256,128]{3,2,1,0:T(8,128)(2,1)S(1)} %get-tuple-element.45), channel_id=1, source_target_pairs={{224,0},{13,1},{226,2},{15,3},{228,4},{9,5},{230,6},{11,7},{232,8}... | collective-permute-start | bytes 1572872 | tf_op jit(solution)/shard_map/ppermute | solution.py:48
  37.1 2.8 %copy-start = (bf16[192,128,128]{2,1,0:T(8,128)(2,1)S(1)}, bf16[192,128,128]{2,1,0:T(8,128)(2,1)}, u32[]{:S(2)}) copy-start(bf16[192,128,128]{2,1,0:T(8,128)(2,1)} %adj.5) | copy-start | bytes 18874372
  42.1 10.9 %collective-permute-start.8 = (bf16[2,4,256,128]{3,2,1,0:T(8,128)(2,1)S(1)}, bf16[2,4,256,128]{3,2,1,0:T(8,128)(2,1)S(1)}, u32[]{:S(2)}, u32[]{:S(2)}) collective-permute-start(bf16[2,4,256,128]{3,2,1,0:T(8,128)(2,1)S(1)} %collective-permute-done.6), channel_id=1, source_target_pairs={{32,0},{5,1},{34,2},{7,3},{36,4},{9,5},{38,6},{11,7},{40,8},{13,9}... | collective-permute-start | bytes 1572872 | tf_op jit(solution)/shard_map/ppermute | solution.py:38
  45.5 10.4 %collective-permute-start.9 = (bf16[2,4,256,128]{3,2,1,0:T(8,128)(2,1)S(1)}, bf16[2,4,256,128]{3,2,1,0:T(8,128)(2,1)S(1)}, u32[]{:S(2)}, u32[]{:S(2)}) collective-permute-start(bf16[2,4,256,128]{3,2,1,0:T(8,128)(2,1)S(1)} %collective-permute-done.7), channel_id=1, source_target_pairs={{224,0},{13,1},{226,2},{15,3},{228,4},{1,5},{230,6},{3,7},{232,8},... | collective-permute-start | bytes 1572872 | tf_op jit(solution)/shard_map/ppermute | solution.py:38
  58.6 20.3 %all-to-all-start = ((f32[64,2,128]{2,1,0:T(2,128)}), f32[64,2,128]{2,1,0:T(2,128)S(1)}, u32[]{:S(2)}, u32[]{:S(2)}) async-start(f32[64,2,128]{2,1,0:T(2,128)} %get-tuple-element.39), calls=%async_computation | async-start | bytes 131072 | tf_op jit(solution)/shard_map/all_to_all | solution.py:268
  66.9 2.0 %collective-permute-start.12 = (bf16[320,128]{1,0:T(8,128)(2,1)S(1)}, bf16[320,128]{1,0:T(8,128)(2,1)S(1)}, u32[]{:S(2)}, u32[]{:S(2)}) collective-permute-start(bf16[320,128]{1,0:T(8,128)(2,1)S(1)} %get-tuple-element.36), channel_id=1, source_target_pairs={{0,1},{1,0},{2,3},{3,2},{4,5},{5,4},{6,7},{7,6},{8,9},{9,8},{10,11... | collective-permute-start | bytes 245768 | tf_op jit(solution)/shard_map/ppermute | solution.py:269
  67.0 5.5 %collective-permute-start.13 = (bf16[320,128]{1,0:T(8,128)(2,1)S(1)}, bf16[320,128]{1,0:T(8,128)(2,1)S(1)}, u32[]{:S(2)}, u32[]{:S(2)}) collective-permute-start(bf16[320,128]{1,0:T(8,128)(2,1)S(1)} %get-tuple-element.37), channel_id=1, source_target_pairs={{0,2},{2,0},{1,3},{3,1},{4,6},{6,4},{5,7},{7,5},{8,10},{10,8},{9,1... | collective-permute-start | bytes 245768 | tf_op jit(solution)/shard_map/ppermute | solution.py:269
  67.7 5.7 %collective-permute-start.14 = (bf16[320,128]{1,0:T(8,128)(2,1)S(1)}, bf16[320,128]{1,0:T(8,128)(2,1)S(1)}, u32[]{:S(2)}, u32[]{:S(2)}) collective-permute-start(bf16[320,128]{1,0:T(8,128)(2,1)S(1)} %get-tuple-element.38), channel_id=1, source_target_pairs={{0,3},{3,0},{1,2},{2,1},{4,7},{7,4},{5,6},{6,5},{8,11},{11,8},{9,1... | collective-permute-start | bytes 245768 | tf_op jit(solution)/shard_map/ppermute | solution.py:269
